TPU v7x, 32 devices: a whole 2x2x4 slice. The times are simulated.
32 devices in a mesh: section: 2 (over core), expert: 8 (over z, y), dp: 2 (over x).
Axes of the slice: x: 2, y: 2, z: 4, core: 2. Of those that a mesh axis runs over, the one named last changes fastest.
Arguments:
- layer_input: bfloat16 [2, 2048, 1536], P(None, ('expert', 'dp')), may hold values from -6 to 6
- cotangent: bfloat16 [2, 2048, 1536], P(None, ('expert', 'dp')), may hold values from -6 to 6
- segments: int32 [2, 2048], P(None, ('expert', 'dp')), may hold values from 0 to 31, never falling along the last dimension, each value on 1 to 128 neighbouring positions
- routes: int32 [2, 2, 2048, 8], P('section', None, ('expert', 'dp')), may hold values from 0 to 23, all different within a row; in each aligned block of 128 rows (0 to 127, 128 to 255, ..., all dimensions but the last counted through in order) at most 64 rows name the same one
- gain_attn: bfloat16 [2, 1536], P('section', 'dp'), may hold values from 0.099609375 to 1.8984375
- w_query: bfloat16 [2, 1536, 1536], P('section', 'dp'), may hold values from -0.15625 to 0.15625
- key_matrix: bfloat16 [2, 1536, 512], P('section', 'dp'), may hold values from -0.15625 to 0.15625
- value_matrix: bfloat16 [2, 1536, 512], P('section', 'dp'), may hold values from -0.15625 to 0.15625
- w_out: bfloat16 [2, 1536, 1536], P('section', 'dp'), may hold values from -0.875 to 0.875
- gain_moe: bfloat16 [2, 1536], P('section', 'dp'), may hold values from 0.099609375 to 1.8984375
- w_router: bfloat16 [2, 1536, 24], P('section', 'dp'), may hold values from -0.078125 to 0.078125
- w_gate: bfloat16 [2, 24, 1536, 512], P('section', 'expert'), may hold values from -0.15625 to 0.15625
- w_up: bfloat16 [2, 24, 1536, 512], P('section', 'expert'), may hold values from -0.15625 to 0.15625
- w_down: bfloat16 [2, 24, 512, 1536], P('section', 'expert'), may hold values from -1 to 1
Outputs:
- section_outputs: bfloat16 [2, 2, 2048, 1536], P('section', None, ('expert', 'dp'))
- section_input_grads: bfloat16 [2, 2, 2048, 1536], P('section', None, ('expert', 'dp'))
- grad_gain_attn: float32 [2, 1536], P('section', 'dp')
- grad_w_query: float32 [2, 1536, 1536], P('section', 'dp')
- grad_w_key: float32 [2, 1536, 512], P('section', 'dp')
- grad_w_value: float32 [2, 1536, 512], P('section', 'dp')
- grad_w_out: float32 [2, 1536, 1536], P('section', 'dp')
- grad_gain_moe: float32 [2, 1536], P('section', 'dp')
- grad_w_router: float32 [2, 1536, 24], P('section', 'dp')
- grad_w_gate: float32 [2, 24, 1536, 512], P('section', 'expert', 'dp')
- grad_w_up: float32 [2, 24, 1536, 512], P('section', 'expert', 'dp')
- grad_w_down: float32 [2, 24, 512, 1536], P('section', 'expert', 'dp')
Inputs may be any that keep to these rules, and one draw needn't show every extreme that they name: `segments`: document numbers never fall along a row of 2048 tokens; a document may run on into the next sequence, where it counts as a new one. `routes`: each token names 8 different experts in each layer. Among the 128 tokens of one device in one micro-batch no expert is named by more than 64 rows, and in every draw some expert is named by exactly 64 of them.
All inputs are finite; a program needn't handle non-finite values.
Results may differ from a plain program's by a relative error of at most 0.028.
Values may be sent and summed in bfloat16 or wider, within the bound.
A program may use at most 320 MiB of HBM per device.

v0:
```python
import jax
import jax.numpy as jnp
from jax import lax
from jax.sharding import PartitionSpec as P

QUERY_HEADS = 24
KEY_VALUE_HEADS = 8
HEAD_SIZE = 64
TOPK = 8
EXP_DEV = 3


EPS = 1e-06
THETA = 10000.0
NEG = -1e30


def passed_along(shard, axis, by):
    length = lax.axis_size(axis)
    pairs = [(i, i + by) for i in range(length) if 0 <= i + by < length]
    return lax.ppermute(shard, axis, pairs)


def rope_tables(length, head_dim):
    places = jnp.arange(length, dtype=jnp.float32)
    rates = THETA ** (-2.0 * jnp.arange(head_dim // 2, dtype=jnp.float32) / head_dim)
    angle = places[:, None] * rates[None, :]
    return (jnp.cos(angle)[:, None, :], jnp.sin(angle)[:, None, :])


def apply_rotary(value_rows, cosine_table, sine_table):
    half_size = value_rows.shape[-1] // 2
    first = value_rows[..., :half_size]
    second = value_rows[..., half_size:]
    return jnp.concatenate(
        [first * cosine_table - second * sine_table, second * cosine_table + first * sine_table],
        axis=-1,
    )


def reverse_rotary(value_rows, cosine_table, sine_table):
    half_size = value_rows.shape[-1] // 2
    first = value_rows[..., :half_size]
    second = value_rows[..., half_size:]
    return jnp.concatenate(
        [first * cosine_table + second * sine_table, second * cosine_table - first * sine_table],
        axis=-1,
    )


def norm_scale(value_rows):
    return lax.rsqrt(jnp.mean(value_rows * value_rows, axis=-1, keepdims=True) + EPS)


def norm_back(grad_rows, value_rows, inverse, gain):
    scaled = value_rows * inverse
    weighted = grad_rows * gain
    gain_grad = jnp.sum(grad_rows * scaled, axis=0)
    value_grad = inverse * (weighted - scaled * jnp.mean(weighted * scaled, axis=-1, keepdims=True))
    return (value_grad, gain_grad)


def mask_for(seg_row):
    places = jnp.arange(seg_row.shape[0])
    return (seg_row[:, None] == seg_row[None, :]) & (places[:, None] >= places[None, :])


def attend_scores(query_rows, key_rows, allowed):
    scale = HEAD_SIZE ** (-0.5)
    scores = scale * jnp.einsum(
        "qkgd,pkd->kgqp", query_rows, key_rows, preferred_element_type=jnp.float32
    )
    return jnp.where(allowed[None, None], scores, NEG)


def slot_table(route_rows, n_owner, capacity):
    flattened = route_rows.reshape(-1)
    markers = (
        flattened[:, None] == jnp.arange(EXP_DEV * n_owner, dtype=jnp.int32)[None, :]
    ).astype(jnp.int32)
    position = jnp.sum((jnp.cumsum(markers, axis=0) - 1) * markers, axis=1)
    return flattened % EXP_DEV * (n_owner * capacity) + flattened // EXP_DEV * capacity + position


def expert_picks(route_rows, n_owner):
    return (
        route_rows[:, :, None] == jnp.arange(EXP_DEV * n_owner, dtype=jnp.int32)[None, None, :]
    ).astype(jnp.float32)


def forward_layer(h_in, seg_row, route_rows, shared, experts, n_owner):
    gain_attn, w_query, key_matrix, value_matrix, w_out, gain_moe, w_router = shared
    w_gate, w_up, w_down = experts
    token_count = h_in.shape[0]
    query_group = QUERY_HEADS // KEY_VALUE_HEADS
    capacity = 3 * token_count * TOPK // (2 * EXP_DEV * n_owner)
    cosine_table, sine_table = rope_tables(token_count, HEAD_SIZE)
    hidden = h_in.astype(jnp.float32)
    inv_one = norm_scale(hidden)
    normalized_input = (hidden * inv_one * gain_attn.astype(jnp.float32)).astype(jnp.bfloat16)
    query_rows = jnp.dot(normalized_input, w_query, preferred_element_type=jnp.float32).reshape(
        token_count, QUERY_HEADS, HEAD_SIZE
    )
    query_rows = (
        apply_rotary(query_rows, cosine_table, sine_table)
        .astype(jnp.bfloat16)
        .reshape(token_count, KEY_VALUE_HEADS, query_group, HEAD_SIZE)
    )
    key_rows = jnp.dot(normalized_input, key_matrix, preferred_element_type=jnp.float32).reshape(
        token_count, KEY_VALUE_HEADS, HEAD_SIZE
    )
    key_rows = apply_rotary(key_rows, cosine_table, sine_table).astype(jnp.bfloat16)
    value_rows = (
        jnp.dot(normalized_input, value_matrix, preferred_element_type=jnp.float32)
        .astype(jnp.bfloat16)
        .reshape(token_count, KEY_VALUE_HEADS, HEAD_SIZE)
    )
    scores = attend_scores(query_rows, key_rows, mask_for(seg_row))
    highest = jnp.max(scores, axis=-1, keepdims=True)
    exponent = jnp.exp(scores - highest)
    row_total = jnp.sum(exponent, axis=-1, keepdims=True)
    probs = exponent / row_total
    log_total = highest + jnp.log(row_total)
    context = jnp.einsum(
        "kgqp,pkd->qkgd", probs.astype(jnp.bfloat16), value_rows, preferred_element_type=jnp.float32
    )
    context = context.reshape(token_count, QUERY_HEADS * HEAD_SIZE).astype(jnp.bfloat16)
    middle = hidden + jnp.dot(context, w_out, preferred_element_type=jnp.float32)
    inv_two = norm_scale(middle)
    normed_two = (middle * inv_two * gain_moe.astype(jnp.float32)).astype(jnp.bfloat16)
    logits = jnp.dot(normed_two, w_router, preferred_element_type=jnp.float32)
    picks = expert_picks(route_rows, n_owner)
    chosen = jnp.sum(picks * logits[:, None, :], axis=-1)
    gates = jax.nn.softmax(chosen, axis=-1)
    slots = slot_table(route_rows, n_owner, capacity)
    rows_total = EXP_DEV * n_owner * capacity
    sending = jnp.zeros((rows_total, normed_two.shape[1]), jnp.bfloat16)
    sending = (
        sending.at[slots]
        .set(jnp.repeat(normed_two, TOPK, axis=0))
        .reshape(EXP_DEV, n_owner * capacity, -1)
    )
    received = lax.all_to_all(sending, "expert", split_axis=1, concat_axis=1, tiled=True)
    gate_pre = jnp.einsum("lrd,ldf->lrf", received, w_gate, preferred_element_type=jnp.float32)
    up_pre = jnp.einsum("lrd,ldf->lrf", received, w_up, preferred_element_type=jnp.float32)
    active = (jax.nn.silu(gate_pre) * up_pre).astype(jnp.bfloat16)
    produced = jnp.einsum(
        "lrf,lfd->lrd", active, w_down, preferred_element_type=jnp.float32
    ).astype(jnp.bfloat16)
    returned = lax.all_to_all(produced, "expert", split_axis=1, concat_axis=1, tiled=True).reshape(
        rows_total, -1
    )
    pair_out = returned[slots].reshape(token_count, TOPK, -1)
    mixed = jnp.sum(gates[:, :, None] * pair_out, axis=1)
    result = (middle + mixed).astype(jnp.bfloat16)
    kept = {
        "h_in": h_in,
        "inv_one": inv_one,
        "normed": normalized_input,
        "query": query_rows,
        "keys": key_rows,
        "values": value_rows,
        "seg_row": seg_row,
        "log_total": log_total,
        "context": context,
        "middle": middle,
        "inv_two": inv_two,
        "normed_two": normed_two,
        "route_rows": route_rows,
        "gates": gates,
        "slots": slots,
        "received": received,
        "gate_pre": gate_pre,
        "up_pre": up_pre,
        "active": active,
        "pair_out": pair_out,
    }
    return (result, kept)


def backward_layer(d_out, kept, shared, experts, n_owner):
    gain_attn, w_query, key_matrix, value_matrix, w_out, gain_moe, w_router = shared
    w_gate, w_up, w_down = experts
    token_count = d_out.shape[0]
    query_group = QUERY_HEADS // KEY_VALUE_HEADS
    received = kept["received"]
    rows_total = received.shape[0] * received.shape[1]
    gates = kept["gates"]
    slots = kept["slots"]
    d_gates = jnp.sum(d_out[:, None, :] * kept["pair_out"], axis=-1)
    d_pair = (
        (gates[:, :, None] * d_out[:, None, :]).astype(jnp.bfloat16).reshape(token_count * TOPK, -1)
    )
    d_sending = (
        jnp.zeros((rows_total, d_pair.shape[1]), jnp.bfloat16)
        .at[slots]
        .set(d_pair)
        .reshape(received.shape)
    )
    d_produced = lax.all_to_all(d_sending, "expert", split_axis=1, concat_axis=1, tiled=True)
    gate_pre = kept["gate_pre"]
    up_pre = kept["up_pre"]
    grad_down = jnp.einsum(
        "lrf,lrd->lfd", kept["active"], d_produced, preferred_element_type=jnp.float32
    )
    d_active = jnp.einsum("lrd,lfd->lrf", d_produced, w_down, preferred_element_type=jnp.float32)
    sigmoid_gate = jax.nn.sigmoid(gate_pre)
    d_gate_pre = (
        d_active * up_pre * sigmoid_gate * (1.0 + gate_pre * (1.0 - sigmoid_gate))
    ).astype(jnp.bfloat16)
    d_up_pre = (d_active * gate_pre * sigmoid_gate).astype(jnp.bfloat16)
    grad_gate = jnp.einsum("lrd,lrf->ldf", received, d_gate_pre, preferred_element_type=jnp.float32)
    grad_up = jnp.einsum("lrd,lrf->ldf", received, d_up_pre, preferred_element_type=jnp.float32)
    d_received = jnp.einsum("lrf,ldf->lrd", d_gate_pre, w_gate, preferred_element_type=jnp.float32)
    d_received = (
        d_received + jnp.einsum("lrf,ldf->lrd", d_up_pre, w_up, preferred_element_type=jnp.float32)
    ).astype(jnp.bfloat16)
    d_returned = lax.all_to_all(
        d_received, "expert", split_axis=1, concat_axis=1, tiled=True
    ).reshape(rows_total, -1)
    d_normed_two = jnp.sum(
        d_returned[slots].reshape(token_count, TOPK, -1), axis=1, dtype=jnp.float32
    )
    picks = expert_picks(kept["route_rows"], n_owner)
    d_chosen = gates * (d_gates - jnp.sum(gates * d_gates, axis=-1, keepdims=True))
    d_logits = jnp.sum(picks * d_chosen[:, :, None], axis=1).astype(jnp.bfloat16)
    normed_two = kept["normed_two"]
    grad_router = jnp.dot(normed_two.T, d_logits, preferred_element_type=jnp.float32)
    d_normed_two = d_normed_two + jnp.dot(d_logits, w_router.T, preferred_element_type=jnp.float32)
    d_middle, grad_gain_moe = norm_back(
        d_normed_two, kept["middle"], kept["inv_two"], gain_moe.astype(jnp.float32)
    )
    d_middle = d_middle + d_out
    d_attn = d_middle.astype(jnp.bfloat16)
    grad_out = jnp.dot(kept["context"].T, d_attn, preferred_element_type=jnp.float32)
    d_context = (
        jnp.dot(d_attn, w_out.T, preferred_element_type=jnp.float32)
        .astype(jnp.bfloat16)
        .reshape(token_count, KEY_VALUE_HEADS, query_group, HEAD_SIZE)
    )
    query_rows = kept["query"]
    key_rows = kept["keys"]
    value_rows = kept["values"]
    scores = attend_scores(query_rows, key_rows, mask_for(kept["seg_row"]))
    probs = jnp.exp(scores - kept["log_total"])
    d_probs = jnp.einsum(
        "qkgd,pkd->kgqp", d_context, value_rows, preferred_element_type=jnp.float32
    )
    row_inner = jnp.sum(probs * d_probs, axis=-1, keepdims=True)
    d_scores = (probs * (d_probs - row_inner)).astype(jnp.bfloat16)
    scale = HEAD_SIZE ** (-0.5)
    cosine_table, sine_table = rope_tables(token_count, HEAD_SIZE)
    d_query = scale * jnp.einsum(
        "kgqp,pkd->qkgd", d_scores, key_rows, preferred_element_type=jnp.float32
    )
    d_query = (
        reverse_rotary(
            d_query.reshape(token_count, QUERY_HEADS, HEAD_SIZE), cosine_table, sine_table
        )
        .astype(jnp.bfloat16)
        .reshape(token_count, QUERY_HEADS * HEAD_SIZE)
    )
    key_gradient = scale * jnp.einsum(
        "kgqp,qkgd->pkd", d_scores, query_rows, preferred_element_type=jnp.float32
    )
    key_gradient = (
        reverse_rotary(key_gradient, cosine_table, sine_table)
        .astype(jnp.bfloat16)
        .reshape(token_count, KEY_VALUE_HEADS * HEAD_SIZE)
    )
    value_gradient = jnp.einsum(
        "kgqp,qkgd->pkd", probs.astype(jnp.bfloat16), d_context, preferred_element_type=jnp.float32
    )
    value_gradient = value_gradient.astype(jnp.bfloat16).reshape(
        token_count, KEY_VALUE_HEADS * HEAD_SIZE
    )
    normalized_input = kept["normed"]
    grad_query = jnp.dot(normalized_input.T, d_query, preferred_element_type=jnp.float32)
    grad_key = jnp.dot(normalized_input.T, key_gradient, preferred_element_type=jnp.float32)
    grad_value = jnp.dot(normalized_input.T, value_gradient, preferred_element_type=jnp.float32)
    d_normed = jnp.dot(d_query, w_query.T, preferred_element_type=jnp.float32)
    d_normed = d_normed + jnp.dot(key_gradient, key_matrix.T, preferred_element_type=jnp.float32)
    d_normed = d_normed + jnp.dot(
        value_gradient, value_matrix.T, preferred_element_type=jnp.float32
    )
    d_hidden, grad_gain_attn = norm_back(
        d_normed, kept["h_in"].astype(jnp.float32), kept["inv_one"], gain_attn.astype(jnp.float32)
    )
    d_in = (d_hidden + d_middle).astype(jnp.bfloat16)
    shared_grads = (
        grad_gain_attn,
        grad_query,
        grad_key,
        grad_value,
        grad_out,
        grad_gain_moe,
        grad_router,
    )
    return (d_in, shared_grads, (grad_gate, grad_up, grad_down))


def fetch_each(gain_attn, w_query, key_matrix, value_matrix, w_out, gain_moe, w_router):
    pieces = (
        lax.all_gather(gain_attn, "dp", axis=1, tiled=True),
        lax.all_gather(w_query, "dp", axis=1, tiled=True),
        lax.all_gather(key_matrix, "dp", axis=1, tiled=True),
        lax.all_gather(value_matrix, "dp", axis=1, tiled=True),
        lax.all_gather(w_out, "dp", axis=1, tiled=True),
        lax.all_gather(gain_moe, "dp", axis=1, tiled=True),
        lax.all_gather(w_router, "dp", axis=1, tiled=True),
    )
    return tuple((piece[0] for piece in pieces))


def shards(
    layer_input,
    cotangent,
    segments,
    routes,
    gain_attn,
    w_query,
    key_matrix,
    value_matrix,
    w_out,
    gain_moe,
    w_router,
    w_gate,
    w_up,
    w_down,
):
    sections = lax.axis_size("section")
    section_index = lax.axis_index("section")
    n_owner = lax.axis_size("expert")
    micro_count = layer_input.shape[0]
    steps_total = micro_count + sections - 1
    experts = (w_gate[0], w_up[0], w_down[0])
    route_all = routes[0]

    def current_weights():
        return fetch_each(gain_attn, w_query, key_matrix, value_matrix, w_out, gain_moe, w_router)

    incoming = jnp.zeros_like(layer_input[0])
    kept_list = []
    out_list = []
    for step_number in range(steps_total):
        micro_index = jnp.clip(step_number - section_index, 0, micro_count - 1)
        h_in = jnp.where(
            section_index == 0, layer_input[min(step_number, micro_count - 1)], incoming
        )
        seg_row = lax.dynamic_index_in_dim(segments, micro_index, 0, keepdims=False)
        route_rows = lax.dynamic_index_in_dim(route_all, micro_index, 0, keepdims=False)
        result, kept = forward_layer(h_in, seg_row, route_rows, current_weights(), experts, n_owner)
        kept_list.append(kept)
        out_list.append(result)
        if step_number + 1 < steps_total:
            incoming = passed_along(result, "section", 1)
    kept_stack = jax.tree.map(lambda *leaves: jnp.stack(leaves), *kept_list)
    section_outputs = lax.dynamic_slice_in_dim(jnp.stack(out_list), section_index, micro_count, 0)
    incoming_grad = jnp.zeros_like(layer_input[0])
    grad_list = []
    shared_sum = None
    expert_sum = None
    for step_number in range(steps_total):
        shifted = step_number - (sections - 1 - section_index)
        valid = (shifted >= 0) & (shifted < micro_count)
        micro_index = jnp.clip(shifted, 0, micro_count - 1)
        forward_step = jnp.clip(micro_index + section_index, 0, steps_total - 1)
        kept = jax.tree.map(
            lambda leaf: lax.dynamic_index_in_dim(leaf, forward_step, 0, keepdims=False), kept_stack
        )
        d_out = jnp.where(
            section_index == sections - 1,
            cotangent[min(step_number, micro_count - 1)],
            incoming_grad,
        ).astype(jnp.float32)
        d_in, shared_grads, expert_grads = backward_layer(
            d_out, kept, current_weights(), experts, n_owner
        )
        shared_grads = jax.tree.map(
            lambda grad_part: jnp.where(valid, grad_part, 0.0), shared_grads
        )
        expert_grads = jax.tree.map(
            lambda grad_part: jnp.where(valid, grad_part, 0.0), expert_grads
        )
        if shared_sum is None:
            shared_sum, expert_sum = (shared_grads, expert_grads)
        else:
            shared_sum = jax.tree.map(
                lambda first_sum, second_sum: first_sum + second_sum, shared_sum, shared_grads
            )
            expert_sum = jax.tree.map(
                lambda first_sum, second_sum: first_sum + second_sum, expert_sum, expert_grads
            )
        grad_list.append(d_in)
        if step_number + 1 < steps_total:
            incoming_grad = passed_along(d_in, "section", -1)
    section_input_grads = lax.dynamic_slice_in_dim(
        jnp.stack(grad_list), sections - 1 - section_index, micro_count, 0
    )
    summed = (
        lax.psum(shared_sum[0].astype(jnp.bfloat16), "expert").astype(jnp.float32),
        lax.psum(shared_sum[1].astype(jnp.bfloat16), "expert").astype(jnp.float32),
        lax.psum(shared_sum[2].astype(jnp.bfloat16), "expert").astype(jnp.float32),
        lax.psum(shared_sum[3].astype(jnp.bfloat16), "expert").astype(jnp.float32),
        lax.psum(shared_sum[4].astype(jnp.bfloat16), "expert").astype(jnp.float32),
        lax.psum(shared_sum[5].astype(jnp.bfloat16), "expert").astype(jnp.float32),
        lax.psum(shared_sum[6].astype(jnp.bfloat16), "expert").astype(jnp.float32),
    )
    finals = (
        lax.psum_scatter(
            summed[0].astype(jnp.bfloat16), "dp", scatter_dimension=0, tiled=True
        ).astype(jnp.float32),
        lax.psum_scatter(
            summed[1].astype(jnp.bfloat16), "dp", scatter_dimension=0, tiled=True
        ).astype(jnp.float32),
        lax.psum_scatter(
            summed[2].astype(jnp.bfloat16), "dp", scatter_dimension=0, tiled=True
        ).astype(jnp.float32),
        lax.psum_scatter(
            summed[3].astype(jnp.bfloat16), "dp", scatter_dimension=0, tiled=True
        ).astype(jnp.float32),
        lax.psum_scatter(
            summed[4].astype(jnp.bfloat16), "dp", scatter_dimension=0, tiled=True
        ).astype(jnp.float32),
        lax.psum_scatter(
            summed[5].astype(jnp.bfloat16), "dp", scatter_dimension=0, tiled=True
        ).astype(jnp.float32),
        lax.psum_scatter(
            summed[6].astype(jnp.bfloat16), "dp", scatter_dimension=0, tiled=True
        ).astype(jnp.float32),
        lax.psum_scatter(
            expert_sum[0].astype(jnp.bfloat16), "dp", scatter_dimension=1, tiled=True
        ).astype(jnp.float32),
        lax.psum_scatter(
            expert_sum[1].astype(jnp.bfloat16), "dp", scatter_dimension=1, tiled=True
        ).astype(jnp.float32),
        lax.psum_scatter(
            expert_sum[2].astype(jnp.bfloat16), "dp", scatter_dimension=1, tiled=True
        ).astype(jnp.float32),
    )
    return (
        section_outputs[None],
        section_input_grads[None],
        finals[0][None],
        finals[1][None],
        finals[2][None],
        finals[3][None],
        finals[4][None],
        finals[5][None],
        finals[6][None],
        finals[7][None],
        finals[8][None],
        finals[9][None],
    )


def solution(mesh):
    placed = (
        P(None, ("expert", "dp"), None),
        P(None, ("expert", "dp"), None),
        P(None, ("expert", "dp")),
        P("section", None, ("expert", "dp"), None),
        P("section", "dp"),
        P("section", "dp", None),
        P("section", "dp", None),
        P("section", "dp", None),
        P("section", "dp", None),
        P("section", "dp"),
        P("section", "dp", None),
        P("section", "expert", None, None),
        P("section", "expert", None, None),
        P("section", "expert", None, None),
    )
    return jax.shard_map(
        shards,
        mesh=mesh,
        in_specs=placed,
        out_specs=(
            P("section", None, ("expert", "dp"), None),
            P("section", None, ("expert", "dp"), None),
            P("section", "dp"),
            P("section", "dp", None),
            P("section", "dp", None),
            P("section", "dp", None),
            P("section", "dp", None),
            P("section", "dp"),
            P("section", "dp", None),
            P("section", "expert", "dp", None),
            P("section", "expert", "dp", None),
            P("section", "expert", "dp", None),
        ),
        check_vma=False,
    )
```

profile of v0, /device:TPU:17, one launch (start us, length us, event | category | flops | bytes accessed | tf_op | source)
XLA Modules:
  0.0 2969.5 jit_solution(11932852618926203947)
XLA Ops:
  27.8 10.2 all-gather.5.cloned.1.call-done
  40.0 26.9 all-gather.7.cloned.1.call-done
  69.2 61.8 %all-gather.9.cloned.1.call-done = bf16[1,1536,1536]{2,1,0:T(8,128)(2,1)} async-done(((bf16[1,768,1536]{2,1,0:T(8,128)(2,1)}), bf16[1,1536,1536]{2,1,0:T(8,128)(2,1)}) %all-gather.9.cloned.1.call-update) | async-done | bytes 4718608 | tf_op jit(solution)/shard_map/all_gather | solution.py:305
  143.3 51.8 %all-gather.11.cloned.1.call-done = bf16[1,1536,1536]{2,1,0:T(8,128)(2,1)} async-done(((bf16[1,768,1536]{2,1,0:T(8,128)(2,1)}), bf16[1,1536,1536]{2,1,0:T(8,128)(2,1)}) %all-gather.11.cloned.1.call-update) | async-done | bytes 4718608 | tf_op jit(solution)/shard_map/all_gather | solution.py:308
  199.5 8.6 scatter_custom_fusion
  214.5 141.5 %all_to_all.60 = bf16[3,512,1536]{2,0,1:T(4,128)(2,1)S(1)} all-to-all(bf16[3,512,1536]{2,0,1:T(4,128)(2,1)S(1)} %copy.587), channel_id=1, replica_groups=mesh['section'=2,'expert'=8,'dp'=2] {'expert'}, dimensions={1} | all-to-all | bytes 9437184 | tf_op jit(solution)/shard_map/all_to_all | solution.py:143
  408.0 107.3 %all-to-all-done.1 = bf16[3,512,1536]{2,0,1:T(4,128)(2,1)} async-done(((bf16[3,512,1536]{2,0,1:T(4,128)(2,1)}), bf16[3,512,1536]{2,0,1:T(4,128)(2,1)}, u32[]{:S(2)}, u32[]{:S(2)}) %all-to-all-start.1) | async-done | bytes 4718624 | tf_op jit(solution)/shard_map/all_to_all | solution.py:150
  521.4 9.6 gather_fusion
  563.0 8.6 scatter_custom_fusion.1
  578.0 144.4 %all_to_all.61 = bf16[3,512,1536]{2,0,1:T(4,128)(2,1)S(1)} all-to-all(bf16[3,512,1536]{2,0,1:T(4,128)(2,1)S(1)} %copy.602), channel_id=1, replica_groups=mesh['section'=2,'expert'=8,'dp'=2] {'expert'}, dimensions={1} | all-to-all | bytes 9437184 | tf_op jit(solution)/shard_map/all_to_all | solution.py:143
  750.8 131.5 %all-to-all-done.3 = bf16[3,512,1536]{2,0,1:T(4,128)(2,1)} async-done(((bf16[3,512,1536]{2,0,1:T(4,128)(2,1)}), bf16[3,512,1536]{2,0,1:T(4,128)(2,1)}, u32[]{:S(2)}, u32[]{:S(2)}) %all-to-all-start.3) | async-done | bytes 4718624 | tf_op jit(solution)/shard_map/all_to_all | solution.py:150
  888.3 9.7 gather_fusion.1
  919.9 8.7 scatter_custom_fusion.2
  928.6 9.0 copy.617
  949.2 8.8 scatter_custom_fusion.3
  958.0 9.0 copy.635
  967.1 113.8 %all-to-all-done.4 = bf16[3,512,1536]{2,0,1:T(4,128)(2,1)} async-done(((bf16[3,512,1536]{2,0,1:T(4,128)(2,1)}), bf16[3,512,1536]{2,0,1:T(4,128)(2,1)}, u32[]{:S(2)}, u32[]{:S(2)}) %all-to-all-start.4) | async-done | bytes 4718624 | tf_op jit(solution)/shard_map/all_to_all | solution.py:143
  1112.9 110.3 %all-to-all-done.6 = bf16[3,512,1536]{2,0,1:T(4,128)(2,1)} async-done(((bf16[3,512,1536]{2,0,1:T(4,128)(2,1)}), bf16[3,512,1536]{2,0,1:T(4,128)(2,1)}, u32[]{:S(2)}, u32[]{:S(2)}) %all-to-all-start.6) | async-done | bytes 4718624 | tf_op jit(solution)/shard_map/all_to_all | solution.py:200
  1223.3 10.8 fusion.132
  1271.5 121.3 %all-to-all-done.7 = bf16[3,512,1536]{2,0,1:T(4,128)(2,1)} async-done(((bf16[3,512,1536]{2,0,1:T(4,128)(2,1)}), bf16[3,512,1536]{2,0,1:T(4,128)(2,1)}, u32[]{:S(2)}, u32[]{:S(2)}) %all-to-all-start.7) | async-done | bytes 4718624 | tf_op jit(solution)/shard_map/all_to_all | solution.py:218
  1392.8 9.0 all-to-all-start.5
  1419.3 9.7 gather_fusion.3
  1432.0 103.1 %all-to-all-done.5 = bf16[3,512,1536]{2,0,1:T(4,128)(2,1)} async-done(((bf16[3,512,1536]{2,0,1:T(4,128)(2,1)}), bf16[3,512,1536]{2,0,1:T(4,128)(2,1)}, u32[]{:S(2)}, u32[]{:S(2)}) %all-to-all-start.5) | async-done | bytes 4718624 | tf_op jit(solution)/shard_map/all_to_all | solution.py:150
  1541.2 9.7 gather_fusion.2
  1594.1 9.5 scatter_custom_fusion.4
  1603.6 9.1 copy.646
  1612.7 145.3 %all_to_all.62 = bf16[3,512,1536]{2,0,1:T(4,128)(2,1)} all-to-all(bf16[3,512,1536]{2,0,1:T(4,128)(2,1)} %copy.646), channel_id=1, replica_groups=mesh['section'=2,'expert'=8,'dp'=2] {'expert'}, dimensions={1} | all-to-all | bytes 9437184 | tf_op jit(solution)/shard_map/all_to_all | solution.py:200
  1758.0 11.4 fusion.123
  1782.7 8.9 copy.648
  1802.0 131.5 %all-to-all-done.9 = bf16[3,512,1536]{2,0,1:T(4,128)(2,1)} async-done(((bf16[3,512,1536]{2,0,1:T(4,128)(2,1)}), bf16[3,512,1536]{2,0,1:T(4,128)(2,1)}, u32[]{:S(2)}, u32[]{:S(2)}) %all-to-all-start.9) | async-done | bytes 4718624 | tf_op jit(solution)/shard_map/all_to_all | solution.py:218
  1939.6 10.2 gather_fusion.4
  1978.1 8.8 scatter_custom_fusion.5
  1986.9 9.1 copy.657
  1996.1 146.0 %all_to_all.63 = bf16[3,512,1536]{2,0,1:T(4,128)(2,1)} all-to-all(bf16[3,512,1536]{2,0,1:T(4,128)(2,1)} %copy.657), channel_id=1, replica_groups=mesh['section'=2,'expert'=8,'dp'=2] {'expert'}, dimensions={1} | all-to-all | bytes 9437184 | tf_op jit(solution)/shard_map/all_to_all | solution.py:200
  2142.0 11.4 fusion.114
  2166.7 9.0 copy.659
  2188.6 127.2 %all-to-all-done.11 = bf16[3,512,1536]{2,0,1:T(4,128)(2,1)} async-done(((bf16[3,512,1536]{2,0,1:T(4,128)(2,1)}), bf16[3,512,1536]{2,0,1:T(4,128)(2,1)}, u32[]{:S(2)}, u32[]{:S(2)}) %all-to-all-start.11) | async-done | bytes 4718624 | tf_op jit(solution)/shard_map/all_to_all | solution.py:218
  2321.8 10.2 gather_fusion.5
  2413.1 12.2 add_convert_fusion.2
  2443.5 11.8 add_convert_fusion.1
  2458.2 8.7 fusion.98
  2472.4 12.7 add_convert_fusion
  2485.5 47.7 %reduce-scatter.21.cloned.1.call-done = bf16[768,1536]{1,0:T(8,128)(2,1)} async-done(((bf16[1536,1536]{1,0:T(8,128)(2,1)}), bf16[768,1536]{1,0:T(8,128)(2,1)}) %reduce-scatter.21.cloned.1.call-update) | async-done | bytes 2359312 | tf_op jit(solution)/shard_map/reduce_scatter | solution.py:422
  2551.5 27.7 all-reduce.2
  2586.0 22.7 reduce-scatter.9.cloned.1.call-done
  2613.2 58.5 %reduce-scatter.11.cloned.1.call-done = bf16[3,768,512]{2,1,0:T(8,128)(2,1)} async-done(((bf16[3,1536,512]{2,1,0:T(8,128)(2,1)}), bf16[3,768,512]{2,1,0:T(8,128)(2,1)}) %reduce-scatter.11.cloned.1.call-update) | async-done | bytes 2359312 | tf_op jit(solution)/shard_map/reduce_scatter | solution.py:434
  2676.3 58.2 %reduce-scatter.13.cloned.1.call-done = bf16[3,256,1536]{2,1,0:T(8,128)(2,1)} async-done(((bf16[3,512,1536]{2,1,0:T(8,128)(2,1)}), bf16[3,256,1536]{2,1,0:T(8,128)(2,1)}) %reduce-scatter.13.cloned.1.call-update) | async-done | bytes 2359312 | tf_op jit(solution)/shard_map/reduce_scatter | solution.py:437
  2739.0 213.6 %all-reduce.7.cloned.1.call-done = (bf16[768,1536]{1,0:T(8,128)(2,1)}, bf16[768,512]{1,0:T(8,128)(2,1)}, bf16[768,512]{1,0:T(8,128)(2,1)}, bf16[768,1536]{1,0:T(8,128)(2,1)}) async-done(((bf16[768,1536]{1,0:T(8,128)(2,1)}, bf16[768,512]{1,0:T(8,128)(2,1)}, bf16[768,512]{1,0:T(8,128)(2,1)}, bf16[768,1536]{1,0:T(8,128)(2,1)}), (bf16[768,1536]{1,0:T(8,128)(2,1)}, bf16[768,512]{1,0:T(8,128)(2,1)}, ...) | async-done | bytes 6291472 | tf_op jit(solution)/shard_map/psum | solution.py:402
  (1064 shorter events, 593.5 us)
Async XLA Ops:
  7.2 30.8 %all-gather.5.cloned.1.call-start = ((), (), s32[]{:S(2)}) async-start(), calls=%async_computation.20 | async-start | bytes 2359296 | tf_op jit(solution)/shard_map/all_gather | solution.py:307
  7.9 58.9 %all-gather.7.cloned.1.call-start = ((), (), s32[]{:S(2)}) async-start(), calls=%async_computation.21 | async-start | bytes 2359296 | tf_op jit(solution)/shard_map/all_gather | solution.py:306
  8.7 122.4 %all-gather.9.cloned.1.call-start = ((), (), s32[]{:S(2)}) async-start(), calls=%async_computation.22 | async-start | bytes 7077888 | tf_op jit(solution)/shard_map/all_gather | solution.py:305
  9.4 185.7 %all-gather.11.cloned.1.call-start = ((), (), s32[]{:S(2)}) async-start(), calls=%async_computation.23 | async-start | bytes 7077888 | tf_op jit(solution)/shard_map/all_gather | solution.py:308
  10.7 392.5 %copy-start.191 = (s32[1,1,128,8]{2,3,1,0:T(8,128)}, s32[1,1,128,8]{2,3,1,0:T(8,128)S(1)}, u32[]{:S(2)}) copy-start(s32[1,1,128,8]{2,3,1,0:T(8,128)S(1)} %get-tuple-element.34) | copy-start | bytes 12292
  10.7 393.1 %copy-start.183 = (s32[1,1,128,8]{2,3,1,0:T(8,128)}, s32[1,1,128,8]{2,3,1,0:T(8,128)S(1)}, u32[]{:S(2)}) copy-start(s32[1,1,128,8]{2,3,1,0:T(8,128)S(1)} %get-tuple-element.94) | copy-start | bytes 12292
  10.7 396.1 %copy-start.181 = (s32[1,1,128,8]{2,3,1,0:T(8,128)}, s32[1,1,128,8]{2,3,1,0:T(8,128)S(1)}, u32[]{:S(2)}) copy-start(s32[1,1,128,8]{2,3,1,0:T(8,128)S(1)} %get-tuple-element.92) | copy-start | bytes 12292
  26.3 378.1 %copy-start.248 = (s32[1,128]{1,0:T(1,128)}, s32[1,128]{1,0:T(1,128)S(1)}, u32[]{:S(2)}) copy-start(s32[1,128]{1,0:T(1,128)S(1)} %get-tuple-element.106) | copy-start | bytes 1540
  26.4 172.7 %copy-start.116 = (f32[1536]{0:T(1024)}, f32[1536]{0:T(1024)S(1)}, u32[]{:S(2)}) copy-start(f32[1536]{0:T(1024)S(1)} %convert_reduce_fusion.3) | copy-start | bytes 18436
  26.8 168.4 %copy-start.58 = (bf16[1,128,1536]{2,1,0:T(8,128)(2,1)}, bf16[1,128,1536]{2,1,0:T(8,128)(2,1)S(1)}, u32[]{:S(2)}) copy-start(bf16[1,128,1536]{2,1,0:T(8,128)(2,1)S(1)} %get-tuple-element.44) | copy-start | bytes 1179652
  208.0 148.0 %slice-start.10 = ((s8[4718592]{0:T(1024)(128)(4,1)}), s8[524288]{0:T(1024)(128)(4,1)S(1)}, s32[]{:S(2)}) async-start(s8[4718592]{0:T(1024)(128)(4,1)} %bitcast.1063), calls=%async_computation.43 | async-start | bytes 1048576
  214.5 141.6 %slice-start.11 = ((s8[4718592]{0:T(1024)(128)(4,1)}), s8[4194304]{0:T(1024)(128)(4,1)S(1)}, s32[]{:S(2)}) async-start(s8[4718592]{0:T(1024)(128)(4,1)} %bitcast.1063), calls=%async_computation.44 | async-start | bytes 8388608
  214.5 144.2 %slice-start.18 = ((s8[4718592]{0:T(1024)(128)(4,1)}), s8[4194304]{0:T(1024)(128)(4,1)S(1)}, s32[]{:S(2)}) async-start(s8[4718592]{0:T(1024)(128)(4,1)} %bitcast.1071), calls=%async_computation.51 | async-start | bytes 8388608
  375.8 139.5 %all-to-all-start.1 = ((bf16[3,512,1536]{2,0,1:T(4,128)(2,1)}), bf16[3,512,1536]{2,0,1:T(4,128)(2,1)}, u32[]{:S(2)}, u32[]{:S(2)}) async-start(bf16[3,512,1536]{2,0,1:T(4,128)(2,1)} %copy.590), calls=%async_computation.1 | async-start | bytes 12582912 | tf_op jit(solution)/shard_map/all_to_all | solution.py:150
  534.0 16.1 collective-permute-start
  571.5 150.9 %slice-start.12 = ((s8[4718592]{0:T(1024)(128)(4,1)}), s8[524288]{0:T(1024)(128)(4,1)S(1)}, s32[]{:S(2)}) async-start(s8[4718592]{0:T(1024)(128)(4,1)} %bitcast.1065), calls=%async_computation.45 | async-start | bytes 1048576
  578.0 144.4 %slice-start.13 = ((s8[4718592]{0:T(1024)(128)(4,1)}), s8[4194304]{0:T(1024)(128)(4,1)S(1)}, s32[]{:S(2)}) async-start(s8[4718592]{0:T(1024)(128)(4,1)} %bitcast.1065), calls=%async_computation.46 | async-start | bytes 8388608
  578.0 147.0 %slice-start.20 = ((s8[4718592]{0:T(1024)(128)(4,1)}), s8[4194304]{0:T(1024)(128)(4,1)S(1)}, s32[]{:S(2)}) async-start(s8[4718592]{0:T(1024)(128)(4,1)} %bitcast.1073), calls=%async_computation.53 | async-start | bytes 8388608
  742.1 140.1 %all-to-all-start.3 = ((bf16[3,512,1536]{2,0,1:T(4,128)(2,1)}), bf16[3,512,1536]{2,0,1:T(4,128)(2,1)}, u32[]{:S(2)}, u32[]{:S(2)}) async-start(bf16[3,512,1536]{2,0,1:T(4,128)(2,1)} %copy.605), calls=%async_computation.3 | async-start | bytes 12582912 | tf_op jit(solution)/shard_map/all_to_all | solution.py:150
  749.9 138.4 %copy-start.197 = (f32[128,8]{0,1:T(8,128)}, f32[128,8]{0,1:T(8,128)S(1)}, u32[]{:S(2)}) copy-start(f32[128,8]{0,1:T(8,128)S(1)} %select_reduce_fusion.4) | copy-start | bytes 12292
  750.0 138.3 %copy-start.252 = (f32[128]{0:T(128)}, f32[128]{0:T(128)S(1)}, u32[]{:S(2)}) copy-start(f32[128]{0:T(128)S(1)} %reduce_max.57) | copy-start | bytes 1540
  750.0 138.3 %copy-start.262 = (f32[128]{0:T(128)}, f32[128]{0:T(128)S(1)}, u32[]{:S(2)}) copy-start(f32[128]{0:T(128)S(1)} %fusion.483) | copy-start | bytes 1540
  902.4 5.4 collective-permute-start.1
  937.8 143.0 %all-to-all-start.4 = ((bf16[3,512,1536]{2,0,1:T(4,128)(2,1)}), bf16[3,512,1536]{2,0,1:T(4,128)(2,1)}, u32[]{:S(2)}, u32[]{:S(2)}) async-start(bf16[3,512,1536]{2,0,1:T(4,128)(2,1)} %copy.617), calls=%async_computation.4 | async-start | bytes 12582912 | tf_op jit(solution)/shard_map/all_to_all | solution.py:143
  949.0 456.0 %copy-start.216 = (f32[1,128,8]{1,2,0:T(8,128)}, f32[1,128,8]{1,2,0:T(8,128)S(1)}, u32[]{:S(2)}) copy-start(f32[1,128,8]{1,2,0:T(8,128)S(1)} %get-tuple-element.86) | copy-start | bytes 12292
  1080.9 142.4 %all-to-all-start.6 = ((bf16[3,512,1536]{2,0,1:T(4,128)(2,1)}), bf16[3,512,1536]{2,0,1:T(4,128)(2,1)}, u32[]{:S(2)}, u32[]{:S(2)}) async-start(bf16[3,512,1536]{2,0,1:T(4,128)(2,1)} %copy.635), calls=%async_computation.6 | async-start | bytes 12582912 | tf_op jit(solution)/shard_map/all_to_all | solution.py:200
  1251.5 141.3 %all-to-all-start.7 = ((bf16[3,512,1536]{2,0,1:T(4,128)(2,1)}), bf16[3,512,1536]{2,0,1:T(4,128)(2,1)}, u32[]{:S(2)}, u32[]{:S(2)}) async-start(bf16[3,512,1536]{2,0,1:T(4,128)(2,1)} %copy.637), calls=%async_computation.7 | async-start | bytes 12582912 | tf_op jit(solution)/shard_map/all_to_all | solution.py:218
  1271.4 137.8 %copy-start.138 = (bf16[128,24,32]{0,2,1:T(8,128)(2,1)S(1)}, bf16[128,24,32]{0,2,1:T(8,128)(2,1)}, u32[]{:S(2)}) copy-start(bf16[128,24,32]{0,2,1:T(8,128)(2,1)} %copy-done.137) | copy-start | bytes 589828
  1392.8 142.3 %all-to-all-start.5 = ((bf16[3,512,1536]{2,0,1:T(4,128)(2,1)}), bf16[3,512,1536]{2,0,1:T(4,128)(2,1)}, u32[]{:S(2)}, u32[]{:S(2)}) async-start(bf16[3,512,1536]{2,0,1:T(4,128)(2,1)} %copy.620), calls=%async_computation.5 | async-start | bytes 12582912 | tf_op jit(solution)/shard_map/all_to_all | solution.py:150
  1583.8 8.3 collective-permute-start.2
  1612.7 156.7 %slice-start.14 = ((s8[4718592]{0:T(1024)(128)(4,1)}), s8[4194304]{0:T(1024)(128)(4,1)S(1)}, s32[]{:S(2)}) async-start(s8[4718592]{0:T(1024)(128)(4,1)} %bitcast.1067), calls=%async_computation.47 | async-start | bytes 8388608
  1612.7 163.3 %slice-start.24 = ((s8[4718592]{0:T(1024)(128)(4,1)}), s8[4194304]{0:T(1024)(128)(4,1)S(1)}, s32[]{:S(2)}) async-start(s8[4718592]{0:T(1024)(128)(4,1)} %bitcast.1077), calls=%async_computation.57 | async-start | bytes 8388608
  1791.6 141.9 %all-to-all-start.9 = ((bf16[3,512,1536]{2,0,1:T(4,128)(2,1)}), bf16[3,512,1536]{2,0,1:T(4,128)(2,1)}, u32[]{:S(2)}, u32[]{:S(2)}) async-start(bf16[3,512,1536]{2,0,1:T(4,128)(2,1)} %copy.648), calls=%async_computation.9 | async-start | bytes 12582912 | tf_op jit(solution)/shard_map/all_to_all | solution.py:218
  1802.0 152.0 %copy-start.219 = (bf16[128,24]{0,1:T(8,128)(2,1)}, bf16[128,24]{0,1:T(8,128)(2,1)S(1)}, u32[]{:S(2)}) copy-start(bf16[128,24]{0,1:T(8,128)(2,1)S(1)} %select_reduce_fusion.1) | copy-start | bytes 18436
  1974.1 4.0 collective-permute-start.3
  1996.0 157.4 %slice-start.16 = ((s8[4718592]{0:T(1024)(128)(4,1)}), s8[4194304]{0:T(1024)(128)(4,1)S(1)}, s32[]{:S(2)}) async-start(s8[4718592]{0:T(1024)(128)(4,1)} %bitcast.1069), calls=%async_computation.49 | async-start | bytes 8388608
  1996.0 164.0 %slice-start.26 = ((s8[4718592]{0:T(1024)(128)(4,1)}), s8[4194304]{0:T(1024)(128)(4,1)S(1)}, s32[]{:S(2)}) async-start(s8[4718592]{0:T(1024)(128)(4,1)} %bitcast.1079), calls=%async_computation.59 | async-start | bytes 8388608
  2175.8 140.0 %all-to-all-start.11 = ((bf16[3,512,1536]{2,0,1:T(4,128)(2,1)}), bf16[3,512,1536]{2,0,1:T(4,128)(2,1)}, u32[]{:S(2)}, u32[]{:S(2)}) async-start(bf16[3,512,1536]{2,0,1:T(4,128)(2,1)} %copy.659), calls=%async_computation.11 | async-start | bytes 12582912 | tf_op jit(solution)/shard_map/all_to_all | solution.py:218
  2181.7 303.7 %reduce-scatter.17.cloned.1.call-start = ((), (), s32[]{:S(2)}) async-start(), calls=%async_computation.28 | async-start | bytes 2359296 | tf_op jit(solution)/shard_map/reduce_scatter | solution.py:416
  2188.6 147.7 %copy-start.221 = (bf16[128,24]{0,1:T(8,128)(2,1)}, bf16[128,24]{0,1:T(8,128)(2,1)S(1)}, u32[]{:S(2)}) copy-start(bf16[128,24]{0,1:T(8,128)(2,1)S(1)} %select_reduce_fusion) | copy-start | bytes 18436
  2350.4 135.1 %reduce-scatter.19.cloned.1.call-start = ((), (), s32[]{:S(2)}) async-start(), calls=%async_computation.29 | async-start | bytes 2359296 | tf_op jit(solution)/shard_map/reduce_scatter | solution.py:419
  2356.2 129.3 %reduce-scatter.15.cloned.1.call-start = ((), (), s32[]{:S(2)}) async-start(), calls=%async_computation.27 | async-start | bytes 7077888 | tf_op jit(solution)/shard_map/reduce_scatter | solution.py:413
  2364.4 168.9 %reduce-scatter.21.cloned.1.call-start = ((), (), s32[]{:S(2)}) async-start(), calls=%async_computation.30 | async-start | bytes 7077888 | tf_op jit(solution)/shard_map/reduce_scatter | solution.py:422
  2373.3 178.2 %reduce-scatter.23.cloned.1.call-start = ((), (), s32[]{:S(2)}) async-start(), calls=%async_computation.31 | async-start | bytes 110592 | tf_op jit(solution)/shard_map/reduce_scatter | solution.py:428
  2413.0 195.7 %reduce-scatter.9.cloned.1.call-start = ((), (), s32[]{:S(2)}) async-start(), calls=%async_computation.24 | async-start | bytes 7077888 | tf_op jit(solution)/shard_map/reduce_scatter | solution.py:431
  2425.3 246.4 %reduce-scatter.11.cloned.1.call-start = ((), (), s32[]{:S(2)}) async-start(), calls=%async_computation.25 | async-start | bytes 7077888 | tf_op jit(solution)/shard_map/reduce_scatter | solution.py:434
  2455.3 279.2 %reduce-scatter.13.cloned.1.call-start = ((), (), s32[]{:S(2)}) async-start(), calls=%async_computation.26 | async-start | bytes 7077888 | tf_op jit(solution)/shard_map/reduce_scatter | solution.py:437
  2485.2 467.4 %all-reduce.7.cloned.1.call-start = ((), (), s32[]{:S(2)}) async-start(), calls=%async_computation.32 | async-start | bytes 12582912 | tf_op jit(solution)/shard_map/psum | solution.py:402
  (300 other events, 6465.2 us)
Sparse Core Ops, SparseCore 0:
  9.6 28.4 all-gather.4
  39.6 27.2 all-gather.6
  68.4 62.6 all-gather.8
  132.5 62.6 all-gather.10
  2350.5 28.4 reduce-scatter.16
  2381.2 26.0 reduce-scatter.18
  2410.2 59.9 reduce-scatter.14
  2473.2 59.9 reduce-scatter.20
  2536.0 9.4 reduce-scatter.22
  2548.3 60.4 reduce-scatter.8
  2611.7 60.0 reduce-scatter.10
  2674.5 59.9 reduce-scatter.12
  2739.6 212.9 all-reduce.6
where the time goes:
time: 2980 us; the launch traced here: 2970 us
  waiting for transfers between devices  1500 us (50%)
  blocking collectives  621 us (21%)
  local copies, waits for them, and re-layouts  294 us (10%)
  matrix products  292 us (10%)
  other arithmetic  168 us (6%)
  starting transfers between devices  71.1 us (2%)
    all_to_all x3, waiting for transfers between devices, backward_layer(): lax.all_to_all(d_received, 'expert', split_axis=1, concat_axis=1, tiled=T...  380 us
    all_to_all x3, waiting for transfers between devices, forward_layer(): lax.all_to_all(produced, 'expert', split_axis=1, concat_axis=1, tiled=True)  342 us
    all_to_all x2, blocking collectives, backward_layer(): lax.all_to_all(d_sending, 'expert', split_axis=1, concat_axis=1, tiled=True)  291 us
    all_to_all x2, blocking collectives, forward_layer(): lax.all_to_all(sending, 'expert', split_axis=1, concat_axis=1, tiled=True)  286 us
    psum x1, waiting for transfers between devices, shards(): lax.psum(shared_sum[1].astype(jnp.bfloat16), 'expert').astype(jnp.float32)  214 us
    all_to_all x1, waiting for transfers between devices, forward_layer(): lax.all_to_all(sending, 'expert', split_axis=1, concat_axis=1, tiled=True)  114 us
    all_to_all x1, waiting for transfers between devices, backward_layer(): lax.all_to_all(d_sending, 'expert', split_axis=1, concat_axis=1, tiled=True)  110 us
    all_gather x1, waiting for transfers between devices, fetch_each(): lax.all_gather(w_query, 'dp', axis=1, tiled=True)  61.8 us
  transfers between devices with their start and end apart: 25, of which 19 were waited for; matrix products, arithmetic and copies ran while one was open for 11% of the time, Pallas kernels for 0%

commit v1 on v0

v1 whole, which is shorter than its diff:
```python
import functools

import jax
import jax.numpy as jnp
from jax import lax
from jax.experimental import pallas as pl
from jax.experimental.pallas import tpu as pltpu
from jax.sharding import PartitionSpec as P

QUERY_HEADS = 24
KEY_VALUE_HEADS = 8
HEAD_SIZE = 64
TOPK = 8
EXP_DEV = 3
LINE = 4
LANES = 128

EPS = 1e-06
THETA = 10000.0
NEG = -1e30

MESH = pl.DeviceIdType.MESH
DMA = pltpu.SemaphoreType.DMA
VM = pl.BlockSpec(memory_space=pltpu.VMEM)
HB = pl.BlockSpec(memory_space=pl.ANY)
F32 = jnp.float32
BF16 = jnp.bfloat16
MIB = 1 << 20


def place(e, ls):
    if ls == 2:
        return e // 2, e % 2
    return e % LINE, e // LINE


def index_of(l, p, ls):
    return l * 2 + p if ls == 2 else p * LINE + l


def near_first(l, k):
    inner = jnp.where(k < 2, 1 - k, k)
    return jnp.where(
        l == 0, k, jnp.where(l == 1, inner, jnp.where(l == 2, 3 - inner, 3 - k))
    )


def signal(**where):
    pl.semaphore_signal(
        pltpu.get_barrier_semaphore(), inc=1, device_id=where, device_id_type=MESH
    )


def greet_all(peers):
    count = 0
    for wanted, where in peers:

        @pl.when(wanted)
        def _(where=where):
            signal(**where)

        count = count + jnp.where(wanted, 1, 0)
    pl.semaphore_wait(pltpu.get_barrier_semaphore(), count)


def greet(l, p, ls, extra=()):
    greet_all(
        (
            (l >= 0, {"expert": index_of(l, 1 - p, ls)}),
            (l > 0, {"expert": index_of(l - 1, p, ls)}),
            (l < LINE - 1, {"expert": index_of(l + 1, p, ls)}),
        )
        + tuple(extra)
    )


def remote(src, dst, ssem, rsem, **where):
    return pltpu.make_async_remote_copy(
        src, dst, ssem, rsem, device_id=where, device_id_type=MESH
    )


class Gather:
    def __init__(self, l, p, ls, buf, sems, chunks):
        self.l, self.p, self.ls, self.buf, self.chunks = l, p, ls, buf, chunks
        self.us, self.ur, self.ds, self.dr, self.ps, self.pr = sems
        self.half = buf.shape[1] // 2
        self.rows = self.half // chunks

    def view(self, L, p, c):
        start = pl.multiple_of(p * self.half + c * self.rows, self.rows)
        return self.buf.at[L, pl.ds(start, self.rows)]

    def copy(self, L, p, c, ssem, rsem, dev):
        v = self.view(L, p, c)
        return remote(v, v, ssem, rsem, expert=dev)

    def up(self, s, c):
        dev = index_of(self.l + 1, self.p, self.ls)
        return self.copy(self.l - s, self.p, c, self.us.at[s, c], self.ur.at[s, c], dev)

    def dn(self, s, c):
        dev = index_of(self.l - 1, self.p, self.ls)
        return self.copy(self.l + s, self.p, c, self.ds.at[s, c], self.dr.at[s, c], dev)

    def pair(self, L, c):
        dev = index_of(self.l, 1 - self.p, self.ls)
        return self.copy(L, self.p, c, self.ps.at[L, c], self.pr.at[L, c], dev)

    def up_in(self, s, c):
        dev = index_of(self.l, self.p, self.ls)
        return self.copy(self.l - 1 - s, self.p, c, self.us.at[s, c], self.ur.at[s, c], dev)

    def dn_in(self, s, c):
        dev = index_of(self.l, self.p, self.ls)
        return self.copy(self.l + 1 + s, self.p, c, self.ds.at[s, c], self.dr.at[s, c], dev)

    def pair_in(self, L, c):
        dev = index_of(self.l, self.p, self.ls)
        return self.copy(L, 1 - self.p, c, self.ps.at[L, c], self.pr.at[L, c], dev)

    def begin(self):
        l = self.l
        for c in range(self.chunks):

            @pl.when(l < LINE - 1)
            def _():
                self.up(0, c).start()

            @pl.when(l > 0)
            def _():
                self.dn(0, c).start()

            self.pair(l, c).start()

    def arrive(self, s):
        l = self.l
        for c in range(self.chunks):

            @pl.when(l - s >= 0)
            def _():
                self.up_in(s - 1, c).wait_recv()

                @pl.when(l < LINE - 1)
                def _():
                    self.up(s, c).start()

                self.pair(l - s, c).start()

            @pl.when(l + s < LINE)
            def _():
                self.dn_in(s - 1, c).wait_recv()

                @pl.when(l > 0)
                def _():
                    self.dn(s, c).start()

                self.pair(l + s, c).start()

    def from_pair(self, L):
        for c in range(self.chunks):
            self.pair_in(L, c).wait_recv()

    def end(self):
        l = self.l
        for c in range(self.chunks):
            for L in range(LINE):
                self.pair(L, c).wait_send()
            for s in range(LINE - 1):

                @pl.when((l - s >= 0) & (l < LINE - 1))
                def _():
                    self.up(s, c).wait_send()

                @pl.when((l + s < LINE) & (l > 0))
                def _():
                    self.dn(s, c).wait_send()


class Sum:
    def __init__(self, l, p, ls, buf, pairb, upb, dnb, sems, chunks):
        self.l, self.p, self.ls, self.buf, self.chunks = l, p, ls, buf, chunks
        self.pairb, self.upb, self.dnb = pairb, upb, dnb
        self.us, self.ur, self.ds, self.dr, self.ps, self.pr = sems
        self.half = buf.shape[1] // 2
        self.rows = self.half // chunks

    def mine(self, p, c):
        return pl.ds(pl.multiple_of(p * self.half + c * self.rows, self.rows), self.rows)

    def part(self, c):
        return pl.ds(c * self.rows, self.rows)

    def pair(self, L, c):
        return remote(
            self.buf.at[L, self.mine(1 - self.p, c)],
            self.pairb.at[L, self.part(c)],
            self.ps.at[L, c],
            self.pr.at[L, c],
            expert=index_of(self.l, 1 - self.p, self.ls),
        )

    def up(self, L, c):
        return remote(
            self.buf.at[L, self.mine(self.p, c)],
            self.upb.at[L, self.part(c)],
            self.us.at[L, c],
            self.ur.at[L, c],
            expert=index_of(self.l + 1, self.p, self.ls),
        )

    def dn(self, L, c):
        return remote(
            self.buf.at[L, self.mine(self.p, c)],
            self.dnb.at[L, self.part(c)],
            self.ds.at[L, c],
            self.dr.at[L, c],
            expert=index_of(self.l - 1, self.p, self.ls),
        )

    def give(self, L):
        for c in range(self.chunks):
            self.pair(L, c).start()

    def total(self, L, c):
        return self.buf[L, self.mine(self.p, c)].astype(F32) + self.pairb[
            L, self.part(c)
        ].astype(F32)

    def pass_on(self, L, write):
        l = self.l
        for c in range(self.chunks):
            self.pair(L, c).wait_recv()

            @pl.when(L > l)
            def _():
                @pl.when(l == 0)
                def _():
                    self.buf[L, self.mine(self.p, c)] = self.total(L, c).astype(BF16)

                @pl.when(l > 0)
                def _():
                    self.up(L, c).wait_recv()
                    here = self.total(L, c) + self.upb[L, self.part(c)].astype(F32)
                    self.buf[L, self.mine(self.p, c)] = here.astype(BF16)

                self.up(L, c).start()

            @pl.when(L < l)
            def _():
                @pl.when(l == LINE - 1)
                def _():
                    self.buf[L, self.mine(self.p, c)] = self.total(L, c).astype(BF16)

                @pl.when(l < LINE - 1)
                def _():
                    self.dn(L, c).wait_recv()
                    here = self.total(L, c) + self.dnb[L, self.part(c)].astype(F32)
                    self.buf[L, self.mine(self.p, c)] = here.astype(BF16)

                self.dn(L, c).start()

            @pl.when(L == l)
            def _():
                @pl.when(l == 0)
                def _():
                    self.dn(L, c).wait_recv()
                    write(c, self.total(L, c) + self.dnb[L, self.part(c)].astype(F32))

                @pl.when(l == LINE - 1)
                def _():
                    self.up(L, c).wait_recv()
                    write(c, self.total(L, c) + self.upb[L, self.part(c)].astype(F32))

                @pl.when((l > 0) & (l < LINE - 1))
                def _():
                    self.up(L, c).wait_recv()
                    self.dn(L, c).wait_recv()
                    write(
                        c,
                        self.total(L, c)
                        + self.upb[L, self.part(c)].astype(F32)
                        + self.dnb[L, self.part(c)].astype(F32),
                    )

    def end(self):
        l = self.l
        for c in range(self.chunks):
            for L in range(LINE):
                self.pair(L, c).wait_send()
                if L > 0:

                    @pl.when(l < L)
                    def _():
                        self.up(L, c).wait_send()

                if L < LINE - 1:

                    @pl.when(l > L)
                    def _():
                        self.dn(L, c).wait_send()


def link_sems(chunks):
    return [DMA((LINE, chunks))] * 6


class Spread:
    def __init__(self, src, shards, wholes, sems):
        self.src, self.shards, self.wholes = src, shards, wholes
        self.own, self.xs, self.xr, self.cs, self.cr = sems
        self.s, self.x = lax.axis_index("section"), lax.axis_index("dp")

    def rows(self, i, x):
        size = self.shards[i].shape[0]
        return self.wholes[i].at[pl.ds(pl.multiple_of(x * size, size), size)]

    def local(self, i):
        return pltpu.make_async_copy(self.shards[i], self.rows(i, self.x), self.own.at[i])

    def across(self, i):
        return remote(
            self.shards[i], self.rows(i, self.x), self.xs.at[i], self.xr.at[i], dp=1 - self.x
        )

    def core_own(self, i):
        return remote(
            self.shards[i],
            self.rows(i, self.x),
            self.cs.at[0, i],
            self.cr.at[0, i],
            section=1 - self.s,
        )

    def core_other(self, i):
        v = self.rows(i, 1 - self.x)
        return remote(v, v, self.cs.at[1, i], self.cr.at[1, i], section=1 - self.s)

    def greetings(self):
        return (
            (self.s == self.src, {"dp": 1 - self.x}),
            (self.s >= 0, {"section": 1 - self.s}),
        )

    def begin(self):
        @pl.when(self.s == self.src)
        def _():
            for i in range(len(self.shards)):
                self.across(i).start()
                self.core_own(i).start()
                self.local(i).start()

    def end(self):
        @pl.when(self.s == self.src)
        def _():
            for i in range(len(self.shards)):
                self.across(i).wait_recv()
                self.core_other(i).start()
            for i in range(len(self.shards)):
                self.across(i).wait_send()
                self.core_own(i).wait_send()
                self.core_other(i).wait_send()
                self.local(i).wait()

        @pl.when(self.s != self.src)
        def _():
            for i in range(len(self.shards)):
                self.core_own(i).wait_recv()
                self.core_other(i).wait_recv()


def spread_sems(count):
    return [DMA((count,)), DMA((count,)), DMA((count,)), DMA((2, count)), DMA((2, count))]


def spread_shapes(shards):
    return [jax.ShapeDtypeStruct((2 * w.shape[0], w.shape[1]), w.dtype) for w in shards]


def spread_kernel(src, count, *refs):
    shards, wholes, sems = refs[:count], refs[count : 2 * count], refs[2 * count :]
    spread = Spread(src, shards, wholes, sems)
    greet_all(spread.greetings())
    spread.begin()
    spread.end()


def spread_weights(src, shards, cid):
    count = len(shards)
    return pl.pallas_call(
        functools.partial(spread_kernel, src, count),
        out_shape=spread_shapes(shards),
        in_specs=[HB] * count,
        out_specs=[HB] * count,
        scratch_shapes=spread_sems(count),
        compiler_params=pltpu.CompilerParams(collective_id=cid, has_side_effects=True),
        cost_estimate=pl.CostEstimate(flops=0, bytes_accessed=200 * MIB, transcendentals=0),
        name="spread_weights",
    )(*shards)


def fetch(mine, theirs, own_layer, dst, sems, wait=False):
    for i in range(len(dst)):
        a = pltpu.make_async_copy(mine[i], dst[i], sems.at[i])
        b = pltpu.make_async_copy(theirs[i], dst[i], sems.at[i])

        @pl.when(own_layer)
        def _():
            a.wait() if wait else a.start()

        @pl.when(jnp.logical_not(own_layer))
        def _():
            b.wait() if wait else b.start()


def dot(a, b):
    return jnp.dot(a, b, preferred_element_type=F32)


def dot_nt(a, b):
    return lax.dot_general(a, b, (((1,), (1,)), ((), ())), preferred_element_type=F32)


def dot_tn(a, b):
    return lax.dot_general(a, b, (((0,), (0,)), ((), ())), preferred_element_type=F32)


def experts_forward_kernel(ls, layer, chunks, n_spread, *refs):
    n2_ref, h1_ref, mask_ref, wr_ref = refs[:4]
    mine, theirs = refs[4:7], refs[7:10]
    shards = refs[10 : 10 + n_spread]
    at = 10 + n_spread
    out_ref, x_out, gp_out, up_out, gates_ref = refs[at : at + 5]
    wholes = refs[at + 5 : at + 5 + n_spread]
    at = at + 5 + n_spread
    xb, gpb, upre, part, pairb, upb, dnb, wg, wu, wd, act = refs[at : at + 11]
    at += 11
    ag_sems, rs_sems = refs[at : at + 6], refs[at + 6 : at + 12]
    at += 12
    w_sem, own_sem, save_sem = refs[at : at + 3]
    spread_sem = refs[at + 3 :]

    e = lax.axis_index("expert")
    s = lax.axis_index("section")
    l, p = place(e, ls)
    half = n2_ref.shape[0]
    own_layer = s == layer
    fetch(mine, theirs, own_layer, (wg, wu, wd), w_sem)
    own = pltpu.make_async_copy(
        n2_ref, xb.at[l, pl.ds(pl.multiple_of(p * half, half), half)], own_sem
    )
    own.start()
    own.wait()
    extra = ()
    if n_spread:
        spread = Spread(1 - layer, shards, wholes, spread_sem)
        extra = spread.greetings()
    greet(l, p, ls, extra)
    gather = Gather(l, p, ls, xb, ag_sems, chunks)
    total = Sum(l, p, ls, part, pairb, upb, dnb, rs_sems, chunks)
    gather.begin()
    if n_spread:
        spread.begin()
    fetch(mine, theirs, own_layer, (wg, wu, wd), w_sem, wait=True)

    def save(L):
        return (
            pltpu.make_async_copy(xb.at[L], x_out.at[L], save_sem.at[0, L]),
            pltpu.make_async_copy(gpb.at[L], gp_out.at[L], save_sem.at[1, L]),
            pltpu.make_async_copy(upre.at[L], up_out.at[L], save_sem.at[2, L]),
        )

    def step(k, carry):
        @pl.when(k > 0)
        def _():
            gather.arrive(k)

        L = near_first(l, k)
        gather.from_pair(L)
        x = xb[L]
        logits = dot(x, wr_ref[...])
        mask = mask_ref[L]
        z = jnp.where(mask > 0, logits, NEG)
        top = jnp.max(z, axis=-1, keepdims=True)
        ex = jnp.exp(z - top) * mask
        gates = ex / jnp.sum(ex, axis=-1, keepdims=True)
        gates_ref[L] = gates
        for j in range(EXP_DEV):
            width = wg.shape[2]
            cols = slice(j * width, (j + 1) * width)
            gp = dot(xb[L], wg[j])
            up = dot(xb[L], wu[j])
            gpb[L, :, cols] = gp.astype(BF16)
            upre[L, :, cols] = up.astype(BF16)
            a = gp * jax.nn.sigmoid(gp) * up
            act[:, cols] = (gates[:, j : j + 1] * a).astype(BF16)
        for copy in save(L):
            copy.start()
        tile = 512
        for n in range(wd.shape[1] // tile):
            cols = slice(n * tile, (n + 1) * tile)
            part[L, :, cols] = dot(act[...], wd[:, cols]).astype(BF16)
        total.give(L)
        return carry

    lax.fori_loop(0, LINE, step, 0)

    def write(c, value):
        rows = pl.ds(c * (half // chunks), half // chunks)
        out_ref[rows, :] = (h1_ref[rows, :] + value).astype(BF16)

    def back(j, carry):
        total.pass_on(near_first(l, LINE - 1 - j), write)
        return carry

    lax.fori_loop(0, LINE, back, 0)
    if n_spread:
        spread.end()
    gather.end()
    total.end()
    for L in range(LINE):
        for copy in save(L):
            copy.wait()


def experts_forward(ls, layer, cid, n2, h1, mask, wr, mine, theirs, shards=(), chunks=2):
    tokens, width = n2.shape
    hidden = mine[0].shape[2]
    wide = EXP_DEV * hidden
    two = 2 * tokens
    mine = (mine[0], mine[1], mine[2].reshape(wide, width))
    theirs = (theirs[0], theirs[1], theirs[2].reshape(wide, width))
    n = len(shards)
    outs = [
        jax.ShapeDtypeStruct((tokens, width), BF16),
        jax.ShapeDtypeStruct((LINE, two, width), BF16),
        jax.ShapeDtypeStruct((LINE, two, wide), BF16),
        jax.ShapeDtypeStruct((LINE, two, wide), BF16),
        jax.ShapeDtypeStruct((LINE, two, LANES), F32),
    ] + spread_shapes(shards)
    scratch = [
        pltpu.VMEM((LINE, two, width), BF16),
        pltpu.VMEM((LINE, two, wide), BF16),
        pltpu.VMEM((LINE, two, wide), BF16),
        pltpu.VMEM((LINE, two, width), BF16),
        pltpu.VMEM((LINE, tokens, width), BF16),
        pltpu.VMEM((LINE, tokens, width), BF16),
        pltpu.VMEM((LINE, tokens, width), BF16),
        pltpu.VMEM(mine[0].shape, BF16),
        pltpu.VMEM(mine[1].shape, BF16),
        pltpu.VMEM(mine[2].shape, BF16),
        pltpu.VMEM((two, wide), BF16),
    ]
    scratch += link_sems(chunks) + link_sems(chunks)
    scratch += [DMA((3,)), DMA(()), DMA((3, LINE))]
    if n:
        scratch += spread_sems(n)
    return pl.pallas_call(
        functools.partial(experts_forward_kernel, ls, layer, chunks, n),
        out_shape=outs,
        in_specs=[VM] * 4 + [HB] * (6 + n),
        out_specs=[VM, HB, HB, HB, VM] + [HB] * n,
        scratch_shapes=scratch,
        compiler_params=pltpu.CompilerParams(
            collective_id=cid, has_side_effects=True, vmem_limit_bytes=56 * MIB
        ),
        cost_estimate=pl.CostEstimate(
            flops=6 * LINE * two * width * wide, bytes_accessed=60 * MIB, transcendentals=0
        ),
        name="experts_forward",
    )(n2, h1, mask, wr, *mine, *theirs, *shards)


def experts_backward_kernel(ls, layer, chunks, *refs):
    g_ref = refs[0]
    mine, theirs = refs[1:4], refs[4:7]
    x_in, gp_in, up_in, gates_ref = refs[7:11]
    dn_ref, dgate_ref, grads = refs[11:14]
    (xb, gb, gpb, upre, act, part, pairb, upb, dnb, wg, wu, wd, stage) = refs[14:27]
    ag_sems, rs_sems = refs[27:33], refs[33:39]
    w_sem, own_sem, load_sem, stage_sem = refs[39:]

    e = lax.axis_index("expert")
    s = lax.axis_index("section")
    l, p = place(e, ls)
    half, width = g_ref.shape
    hidden = wg.shape[2]
    two = 2 * half
    own_layer = s == layer
    fetch(mine, theirs, own_layer, (wg, wu, wd), w_sem)
    loads = (
        pltpu.make_async_copy(x_in, xb, load_sem.at[0]),
        pltpu.make_async_copy(gp_in, gpb, load_sem.at[1]),
        pltpu.make_async_copy(up_in, upre, load_sem.at[2]),
    )
    for copy in loads:
        copy.start()
    own = pltpu.make_async_copy(
        g_ref, gb.at[l, pl.ds(pl.multiple_of(p * half, half), half)], own_sem
    )
    own.start()
    own.wait()
    greet(l, p, ls)
    gather = Gather(l, p, ls, gb, ag_sems, chunks)
    total = Sum(l, p, ls, part, pairb, upb, dnb, rs_sems, chunks)
    gather.begin()
    fetch(mine, theirs, own_layer, (wg, wu, wd), w_sem, wait=True)
    for copy in loads:
        copy.wait()

    def step(k, carry):
        @pl.when(k > 0)
        def _():
            gather.arrive(k)

        L = near_first(l, k)
        gather.from_pair(L)
        gates = gates_ref[L]
        lane = lax.broadcasted_iota(jnp.int32, (two, LANES), 1)
        dgates = jnp.zeros((two, LANES), F32)
        for j in range(EXP_DEV):
            cols = slice(j * hidden, (j + 1) * hidden)
            da = dot_nt(gb[L], wd[cols, :])
            gp = gpb[L, :, cols].astype(F32)
            up = upre[L, :, cols].astype(F32)
            sig = jax.nn.sigmoid(gp)
            silu = gp * sig
            a = silu * up
            gate = gates[:, j : j + 1]
            dgate = jnp.sum(a * da, axis=-1, keepdims=True)
            high = dgate.astype(BF16).astype(F32)
            dgates = dgates + jnp.where(lane == EXP_DEV * e + j, high, 0.0)
            dgates = dgates + jnp.where(lane == 32 + EXP_DEV * e + j, dgate - high, 0.0)
            da = da * gate
            act[L, :, cols] = (gate * a).astype(BF16)
            gpb[L, :, cols] = (da * up * sig * (1.0 + gp * (1.0 - sig))).astype(BF16)
            upre[L, :, cols] = (da * silu).astype(BF16)
        part[L, :, width:] = dgates.astype(BF16)
        tile = 512
        for n in range(width // tile):
            cols = slice(n * tile, (n + 1) * tile)
            acc = jnp.zeros((two, tile), F32)
            for j in range(EXP_DEV):
                sub = slice(j * hidden, (j + 1) * hidden)
                acc = acc + dot_nt(gpb[L, :, sub], wg[j, cols, :])
                acc = acc + dot_nt(upre[L, :, sub], wu[j, cols, :])
            part[L, :, cols] = acc.astype(BF16)
        total.give(L)
        return carry

    lax.fori_loop(0, LINE, step, 0)

    def write(c, value):
        rows = pl.ds(c * (half // chunks), half // chunks)
        dn_ref[rows, :] = value[:, :width]
        dgate_ref[rows, :] = value[:, width:]

    height = 256
    tiles = width // height

    def stored(t, kind):
        rows = pl.ds(pl.multiple_of(t * height, height), height)
        return pltpu.make_async_copy(
            stage.at[kind], grads.at[kind, rows], stage_sem.at[kind]
        )

    def weight_grads(t, carry):
        cols = pl.ds(pl.multiple_of(t * height, height), height)
        for kind, (lhs, rhs) in enumerate(((xb, gpb), (xb, upre), (act, gb))):
            acc = dot_tn(lhs[0, :, cols], rhs[0])
            for L in range(1, LINE):
                acc = acc + dot_tn(lhs[L, :, cols], rhs[L])

            @pl.when(t > 0)
            def _():
                stored(t - 1, kind).wait()

            stage[kind] = acc.astype(BF16)
            stored(t, kind).start()
        return carry

    def back(j, carry):
        total.pass_on(near_first(l, LINE - 1 - j), write)
        first = j * tiles // (LINE - 1)
        last = jnp.minimum((j + 1) * tiles // (LINE - 1), tiles)
        lax.fori_loop(first, last, weight_grads, 0)
        return carry

    lax.fori_loop(0, LINE, back, 0)
    for kind in range(3):
        stored(tiles - 1, kind).wait()
    gather.end()
    total.end()


def experts_backward(ls, layer, cid, g, mine, theirs, x, gp, up, gates, chunks=2):
    tokens, width = g.shape
    hidden = mine[0].shape[2]
    wide = EXP_DEV * hidden
    two = 2 * tokens
    mine = (mine[0], mine[1], mine[2].reshape(wide, width))
    theirs = (theirs[0], theirs[1], theirs[2].reshape(wide, width))
    sent = width + LANES
    scratch = [
        pltpu.VMEM((LINE, two, width), BF16),
        pltpu.VMEM((LINE, two, width), BF16),
        pltpu.VMEM((LINE, two, wide), BF16),
        pltpu.VMEM((LINE, two, wide), BF16),
        pltpu.VMEM((LINE, two, wide), BF16),
        pltpu.VMEM((LINE, two, sent), BF16),
        pltpu.VMEM((LINE, tokens, sent), BF16),
        pltpu.VMEM((LINE, tokens, sent), BF16),
        pltpu.VMEM((LINE, tokens, sent), BF16),
        pltpu.VMEM(mine[0].shape, BF16),
        pltpu.VMEM(mine[1].shape, BF16),
        pltpu.VMEM(mine[2].shape, BF16),
        pltpu.VMEM((3, 256, width), BF16),
    ]
    scratch += link_sems(chunks) + link_sems(chunks)
    scratch += [DMA((3,)), DMA(()), DMA((3,)), DMA((3,))]
    return pl.pallas_call(
        functools.partial(experts_backward_kernel, ls, layer, chunks),
        out_shape=[
            jax.ShapeDtypeStruct((tokens, width), F32),
            jax.ShapeDtypeStruct((tokens, LANES), F32),
            jax.ShapeDtypeStruct((3, width, wide), BF16),
        ],
        in_specs=[VM] + [HB] * 9 + [VM],
        out_specs=[VM, VM, HB],
        scratch_shapes=scratch,
        compiler_params=pltpu.CompilerParams(
            collective_id=cid, has_side_effects=True, vmem_limit_bytes=60 * MIB
        ),
        cost_estimate=pl.CostEstimate(
            flops=12 * LINE * two * width * wide, bytes_accessed=100 * MIB, transcendentals=0
        ),
        name="experts_backward",
    )(g, *mine, *theirs, x, gp, up, gates)


def sum_kernel(ls, chunks, p_ref, o_ref, part, pairb, upb, dnb, load_sem, *sems):
    l, p = place(lax.axis_index("expert"), ls)
    load = pltpu.make_async_copy(p_ref, part, load_sem)
    load.start()
    greet(l, p, ls)
    total = Sum(l, p, ls, part, pairb, upb, dnb, sems, chunks)
    rows = pairb.shape[1] // chunks
    load.wait()
    for k in range(LINE):
        total.give(near_first(l, LINE - 1 - k))

    def write(c, value):
        o_ref[pl.ds(c * rows, rows), :] = value.astype(BF16)

    def back(j, carry):
        total.pass_on(near_first(l, LINE - 1 - j), write)
        return carry

    lax.fori_loop(0, LINE, back, 0)
    total.end()


def sum_scattered(ls, cid, parts, chunks=2):
    n, two, width = parts.shape
    rows = two // 2
    buf = pltpu.VMEM((LINE, rows, width), BF16)
    return pl.pallas_call(
        functools.partial(sum_kernel, ls, chunks),
        out_shape=jax.ShapeDtypeStruct((rows, width), BF16),
        in_specs=[HB],
        out_specs=VM,
        scratch_shapes=[pltpu.VMEM((LINE, two, width), BF16), buf, buf, buf, DMA(())]
        + link_sems(chunks),
        compiler_params=pltpu.CompilerParams(
            collective_id=cid, has_side_effects=True, vmem_limit_bytes=40 * MIB
        ),
        cost_estimate=pl.CostEstimate(flops=0, bytes_accessed=200 * MIB, transcendentals=0),
        name="sum_scattered",
    )(parts)


def gather_kernel(ls, chunks, x_ref, o_ref, own_sem, *sems):
    l, p = place(lax.axis_index("expert"), ls)
    rows = x_ref.shape[0]
    own = pltpu.make_async_copy(
        x_ref, o_ref.at[l, pl.ds(pl.multiple_of(p * rows, rows), rows)], own_sem
    )
    own.start()
    own.wait()
    greet(l, p, ls)
    gather = Gather(l, p, ls, o_ref, sems, chunks)
    gather.begin()

    def step(k, carry):
        gather.arrive(k)
        return carry

    lax.fori_loop(1, LINE, step, 0)
    for L in range(LINE):
        gather.from_pair(L)
    gather.end()


def gather_all(ls, cid, rows, chunks=2):
    count, width = rows.shape
    return pl.pallas_call(
        functools.partial(gather_kernel, ls, chunks),
        out_shape=jax.ShapeDtypeStruct((LINE, 2 * count, width), BF16),
        in_specs=[VM],
        out_specs=VM,
        scratch_shapes=[DMA(())] + link_sems(chunks),
        compiler_params=pltpu.CompilerParams(
            collective_id=cid, has_side_effects=True, vmem_limit_bytes=40 * MIB
        ),
        cost_estimate=pl.CostEstimate(flops=0, bytes_accessed=200 * MIB, transcendentals=0),
        name="gather_all",
    )(rows)


def rope_tables(length, head_dim):
    places = jnp.arange(length, dtype=F32)
    rates = THETA ** (-2.0 * jnp.arange(head_dim // 2, dtype=F32) / head_dim)
    angle = places[:, None] * rates[None, :]
    return (jnp.cos(angle)[:, None, :], jnp.sin(angle)[:, None, :])


def apply_rotary(value_rows, cosine_table, sine_table):
    half_size = value_rows.shape[-1] // 2
    first = value_rows[..., :half_size]
    second = value_rows[..., half_size:]
    return jnp.concatenate(
        [first * cosine_table - second * sine_table, second * cosine_table + first * sine_table],
        axis=-1,
    )


def norm_scale(value_rows):
    return lax.rsqrt(jnp.mean(value_rows * value_rows, axis=-1, keepdims=True) + EPS)


def norm_back(grad_rows, value_rows, inverse, gain):
    scaled = value_rows * inverse
    weighted = grad_rows * gain
    gain_grad = jnp.sum(grad_rows * scaled, axis=0)
    value_grad = inverse * (weighted - scaled * jnp.mean(weighted * scaled, axis=-1, keepdims=True))
    return (value_grad, gain_grad)


def mask_for(seg_row):
    places = jnp.arange(seg_row.shape[0])
    return (seg_row[:, None] == seg_row[None, :]) & (places[:, None] >= places[None, :])


def attend_scores(query_rows, key_rows, allowed):
    scale = HEAD_SIZE ** (-0.5)
    scores = scale * jnp.einsum("qkgd,pkd->kgqp", query_rows, key_rows, preferred_element_type=F32)
    return jnp.where(allowed[None, None], scores, NEG)


def attention_forward(hidden, allowed, gain_attn, gain_moe, weights):
    w_query, key_matrix, value_matrix, w_out = weights
    token_count = hidden.shape[0]
    query_group = QUERY_HEADS // KEY_VALUE_HEADS
    cosine_table, sine_table = rope_tables(token_count, HEAD_SIZE)
    inv_one = norm_scale(hidden)
    normed = (hidden * inv_one * gain_attn).astype(BF16)
    query = dot(normed, w_query).reshape(token_count, QUERY_HEADS, HEAD_SIZE)
    query = (
        apply_rotary(query, cosine_table, sine_table)
        .astype(BF16)
        .reshape(token_count, KEY_VALUE_HEADS, query_group, HEAD_SIZE)
    )
    keys = dot(normed, key_matrix).reshape(token_count, KEY_VALUE_HEADS, HEAD_SIZE)
    keys = apply_rotary(keys, cosine_table, sine_table).astype(BF16)
    values = (
        dot(normed, value_matrix).astype(BF16).reshape(token_count, KEY_VALUE_HEADS, HEAD_SIZE)
    )
    scores = attend_scores(query, keys, allowed)
    highest = jnp.max(scores, axis=-1, keepdims=True)
    exponent = jnp.exp(scores - highest)
    row_total = jnp.sum(exponent, axis=-1, keepdims=True)
    probs = exponent / row_total
    log_total = highest + jnp.log(row_total)
    context = jnp.einsum(
        "kgqp,pkd->qkgd", probs.astype(BF16), values, preferred_element_type=F32
    )
    context = context.reshape(token_count, QUERY_HEADS * HEAD_SIZE).astype(BF16)
    middle = hidden + dot(context, w_out)
    inv_two = norm_scale(middle)
    normed_two = (middle * inv_two * gain_moe).astype(BF16)
    kept = dict(
        hidden=hidden,
        inv_one=inv_one,
        normed=normed,
        query=query,
        keys=keys,
        values=values,
        log_total=log_total,
        context=context,
        middle=middle,
        inv_two=inv_two,
        normed_two=normed_two,
    )
    return middle, normed_two, kept


def attention_backward(d_out, d_normed_two, d_gates, gates, kept, allowed, gains, weights, w_router):
    gain_attn, gain_moe = gains
    w_query, key_matrix, value_matrix, w_out = weights
    token_count = d_out.shape[0]
    query_group = QUERY_HEADS // KEY_VALUE_HEADS
    d_logits = (gates * (d_gates - jnp.sum(gates * d_gates, axis=-1, keepdims=True))).astype(BF16)
    d_normed_two = d_normed_two + dot(d_logits, w_router.T)
    d_middle, grad_gain_moe = norm_back(d_normed_two, kept["middle"], kept["inv_two"], gain_moe)
    d_middle = d_middle + d_out
    d_attn = d_middle.astype(BF16)
    d_context = (
        dot(d_attn, w_out.T)
        .astype(BF16)
        .reshape(token_count, KEY_VALUE_HEADS, query_group, HEAD_SIZE)
    )
    query, keys, values = kept["query"], kept["keys"], kept["values"]
    scores = attend_scores(query, keys, allowed)
    probs = jnp.exp(scores - kept["log_total"])
    d_probs = jnp.einsum("qkgd,pkd->kgqp", d_context, values, preferred_element_type=F32)
    row_inner = jnp.sum(probs * d_probs, axis=-1, keepdims=True)
    d_scores = (probs * (d_probs - row_inner)).astype(BF16)
    scale = HEAD_SIZE ** (-0.5)
    cosine_table, sine_table = rope_tables(token_count, HEAD_SIZE)
    d_query = scale * jnp.einsum("kgqp,pkd->qkgd", d_scores, keys, preferred_element_type=F32)
    d_query = (
        apply_rotary(
            d_query.reshape(token_count, QUERY_HEADS, HEAD_SIZE), cosine_table, -sine_table
        )
        .astype(BF16)
        .reshape(token_count, QUERY_HEADS * HEAD_SIZE)
    )
    d_keys = scale * jnp.einsum("kgqp,qkgd->pkd", d_scores, query, preferred_element_type=F32)
    d_keys = (
        apply_rotary(d_keys, cosine_table, -sine_table)
        .astype(BF16)
        .reshape(token_count, KEY_VALUE_HEADS * HEAD_SIZE)
    )
    d_values = jnp.einsum(
        "kgqp,qkgd->pkd", probs.astype(BF16), d_context, preferred_element_type=F32
    )
    d_values = d_values.astype(BF16).reshape(token_count, KEY_VALUE_HEADS * HEAD_SIZE)
    d_normed = dot(d_query, w_query.T) + dot(d_keys, key_matrix.T) + dot(d_values, value_matrix.T)
    d_hidden, grad_gain_attn = norm_back(d_normed, kept["hidden"], kept["inv_one"], gain_attn)
    d_in = (d_hidden + d_middle).astype(BF16)
    acts = dict(dq=d_query, dk=d_keys, dv=d_values, dat=d_attn, dr=d_logits)
    return d_in, acts, (grad_gain_attn, grad_gain_moe)


def swap(value, axis):
    return lax.ppermute(value, axis, [(0, 1), (1, 0)])


def half_of(value, axis, index, size):
    return lax.dynamic_slice_in_dim(value, index * size, size, axis)


def sum_over_dp(value, axis, size):
    n = lax.axis_size("dp")
    x = lax.axis_index("dp")
    if n == 2:
        there = half_of(value, axis, 1 - x, size)
        here = half_of(value, axis, x, size)
        return here.astype(F32) + swap(there, "dp").astype(F32)
    return lax.psum_scatter(value, "dp", scatter_dimension=axis, tiled=True).astype(F32)


def shards(
    layer_input,
    cotangent,
    segments,
    routes,
    gain_attn,
    w_query,
    key_matrix,
    value_matrix,
    w_out,
    gain_moe,
    w_router,
    w_gate,
    w_up,
    w_down,
):
    n_dp = lax.axis_size("dp")
    n_exp = lax.axis_size("expert")
    ls = 2 if n_dp == 2 else 1
    s = lax.axis_index("section")
    e = lax.axis_index("expert")
    x = lax.axis_index("dp")
    tokens, width = layer_input.shape[1:]
    n_experts = EXP_DEV * n_exp
    shard_rows = width // n_dp

    def micro(value):
        return lax.dynamic_index_in_dim(value, s, 0, keepdims=False)

    small = jnp.concatenate([w_router[0], gain_attn[0][:, None], gain_moe[0][:, None]], axis=1)
    small = lax.all_gather(small, ("section", "dp"), axis=0, tiled=True).reshape(2, width, -1)
    routers = small[:, :, :n_experts]
    gains = [
        (small[k, :, n_experts].astype(F32), small[k, :, n_experts + 1].astype(F32))
        for k in range(2)
    ]
    all_routes = lax.all_gather(routes[0], ("section", "expert"), axis=0)
    all_routes = all_routes.reshape(2, n_exp, 2, tokens, TOPK)
    all_routes = lax.dynamic_index_in_dim(all_routes, s, 2, keepdims=False)
    picks = jnp.max(
        (all_routes[..., None] == jnp.arange(n_experts, dtype=jnp.int32)).astype(F32), axis=-2
    )
    own_picks = lax.dynamic_index_in_dim(picks, e, 1, keepdims=False)

    def rolled(value):
        twice = jnp.concatenate([value, value], axis=-1)
        cut = lax.dynamic_slice_in_dim(twice, EXP_DEV * e, n_experts, value.ndim - 1)
        pad = [(0, 0)] * (value.ndim - 1) + [(0, LANES - n_experts)]
        return jnp.pad(cut, pad)

    masks = rolled(picks)
    if ls == 1:
        masks = masks.reshape(2, 2, LINE, tokens, LANES).swapaxes(1, 2)
    masks = masks.reshape(2, LINE, 2 * tokens, LANES)

    mine = (w_gate[0], w_up[0], w_down[0])
    theirs = tuple(swap(w, "section") for w in mine)
    own = (w_query[0], key_matrix[0], value_matrix[0], w_out[0])
    if n_dp == 2:
        layer_weights = [spread_weights(0, own, 0), None]
    else:
        wholes = [
            lax.all_gather(w, ("section", "dp"), axis=0, tiled=True).reshape(2, width, -1)
            for w in own
        ]
        layer_weights = [tuple(w[k] for w in wholes) for k in range(2)]

    allowed = mask_for(micro(segments))
    current = micro(layer_input)
    kept_list, outs = [], []
    for k in range(2):
        middle, normed_two, kept = attention_forward(
            current.astype(F32), allowed, gains[k][0], gains[k][1], layer_weights[k]
        )
        logits = dot(normed_two, routers[k])
        z = jnp.where(own_picks[k] > 0, logits, NEG)
        kept["gates"] = jax.nn.softmax(z, axis=-1) * own_picks[k]
        riders = own if (n_dp == 2 and k == 0) else ()
        result = experts_forward(
            ls, k, 1 + k, normed_two, middle, masks[k], rolled(routers[k]), mine, theirs, riders
        )
        current = result[0]
        kept["saved"] = result[1:5]
        if riders:
            layer_weights[1] = result[5:]
        kept_list.append(kept)
        outs.append(current)

    d_out = micro(cotangent)
    d_ins, act_list, gain_list, expert_list = [None] * 2, [None] * 2, [None] * 2, [None] * 2
    for k in (1, 0):
        kept = kept_list[k]
        d_normed_two, d_gates, grads = experts_backward(
            ls, k, 3 + k, d_out, mine, theirs, *kept["saved"]
        )
        mid = grads.shape[2] // 2
        there = half_of(grads, 2, 1 - s, mid)
        here = half_of(grads, 2, s, mid)
        both = (here.astype(F32) + swap(there, "section").astype(F32)).astype(BF16)
        gate_up = sum_over_dp(both[:2], 1, shard_rows)
        down = both[2].reshape(EXP_DEV, -1, mid)
        down = sum_over_dp(down, 1, down.shape[1] // n_dp)
        expert_list[k] = (gate_up.astype(BF16), down.astype(BF16))

        d_gates = d_gates[:, :n_experts] + d_gates[:, 32 : 32 + n_experts]
        d_out, acts, gain_grads = attention_backward(
            d_out.astype(F32),
            d_normed_two,
            d_gates,
            kept["gates"],
            kept,
            allowed,
            gains[k],
            layer_weights[k],
            routers[k],
        )
        d_ins[k] = d_out
        lhs = jnp.concatenate(
            [kept["normed"], kept["context"], kept["normed_two"]], axis=1
        ).reshape(tokens, 3, width)
        rhs = jnp.concatenate(
            [acts["dq"], acts["dk"], acts["dv"], acts["dat"]]
            + [jnp.pad(acts["dr"], ((0, 0), (0, LANES - n_experts)))],
            axis=1,
        )
        gain_rows = jnp.stack(gain_grads)
        if n_dp == 2:
            pack_there = half_of(lhs, 2, 1 - x, shard_rows).reshape(tokens, -1)
            pack_here = half_of(lhs, 2, x, shard_rows).reshape(tokens, -1)
            sent = jnp.concatenate([pack_there, rhs], axis=1)
            kept_here = jnp.concatenate([pack_here, rhs], axis=1)
            pack = jnp.concatenate([kept_here, swap(sent, "dp")], axis=0)
        else:
            pack = jnp.concatenate([lhs.reshape(tokens, -1), rhs], axis=1)
        act_list[k] = pack
        gain_list[k] = sum_over_dp(gain_rows, 1, shard_rows)

    first = s == 0

    def own_layer(zero, one):
        kept_part = jnp.where(first, zero, one)
        sent_part = jnp.where(first, one, zero)
        return kept_part, swap(sent_part, "section")

    acts_mine = jnp.concatenate(own_layer(act_list[0], act_list[1]), axis=0)
    gain_mine = sum(own_layer(gain_list[0], gain_list[1]))
    lhs_rows = shard_rows if n_dp == 2 else width
    lhs = [acts_mine[:, i * lhs_rows : (i + 1) * lhs_rows] for i in range(3)]
    rhs = acts_mine[:, 3 * lhs_rows :]
    n_qkv = own[0].shape[1] + own[1].shape[1] + own[2].shape[1]
    parts = jnp.concatenate(
        [
            dot_tn(lhs[0], rhs[:, :n_qkv]),
            dot_tn(lhs[1], rhs[:, n_qkv : n_qkv + width]),
            dot_tn(lhs[2], rhs[:, n_qkv + width :]),
        ],
        axis=1,
    ).astype(BF16)
    if n_dp != 2:
        parts = lax.psum_scatter(parts, "dp", scatter_dimension=0, tiled=True)
    gain_cols = jnp.pad(gain_mine.T, ((0, 0), (LANES - 2, 0)))
    parts = jnp.concatenate(
        [parts[:, :-LANES], (parts[:, -LANES:].astype(F32) + gain_cols).astype(BF16)], axis=1
    )
    if n_dp == 2:
        block = shard_rows // n_exp
        blocks = parts.reshape(LINE, 2 * block, -1)
        spread = gather_all(ls, 6, sum_scattered(ls, 5, blocks))
        spread = spread.reshape(shard_rows, -1).astype(F32)
    else:
        spread = lax.psum(parts, "expert").astype(F32)

    def joined(zero, one):
        kept_part, got = own_layer(zero, one)
        return jnp.where(
            first,
            jnp.concatenate([kept_part, got], axis=-1),
            jnp.concatenate([got, kept_part], axis=-1),
        ).astype(F32)

    gate_up = joined(expert_list[0][0], expert_list[1][0])
    gate_up = gate_up.reshape(2, shard_rows, EXP_DEV, -1).swapaxes(1, 2)
    down = joined(expert_list[0][1], expert_list[1][1])

    def both_micros(zero, one):
        kept_part, got = own_layer(zero, one)
        return jnp.where(first, jnp.stack([kept_part, got]), jnp.stack([got, kept_part]))

    section_outputs = both_micros(outs[0], outs[1])
    section_input_grads = both_micros(d_ins[0], d_ins[1])
    cut = [0]
    for w in own:
        cut.append(cut[-1] + w.shape[1])
    return (
        section_outputs[None],
        section_input_grads[None],
        spread[:, -2][None],
        spread[:, cut[0] : cut[1]][None],
        spread[:, cut[1] : cut[2]][None],
        spread[:, cut[2] : cut[3]][None],
        spread[:, cut[3] : cut[4]][None],
        spread[:, -1][None],
        spread[:, cut[4] : cut[4] + n_experts][None],
        gate_up[0][None],
        gate_up[1][None],
        down[None],
    )


def solution(mesh):
    placed = (
        P(None, ("expert", "dp"), None),
        P(None, ("expert", "dp"), None),
        P(None, ("expert", "dp")),
        P("section", None, ("expert", "dp"), None),
        P("section", "dp"),
        P("section", "dp", None),
        P("section", "dp", None),
        P("section", "dp", None),
        P("section", "dp", None),
        P("section", "dp"),
        P("section", "dp", None),
        P("section", "expert", None, None),
        P("section", "expert", None, None),
        P("section", "expert", None, None),
    )
    return jax.shard_map(
        shards,
        mesh=mesh,
        in_specs=placed,
        out_specs=(
            P("section", None, ("expert", "dp"), None),
            P("section", None, ("expert", "dp"), None),
            P("section", "dp"),
            P("section", "dp", None),
            P("section", "dp", None),
            P("section", "dp", None),
            P("section", "dp", None),
            P("section", "dp"),
            P("section", "dp", None),
            P("section", "expert", "dp", None),
            P("section", "expert", "dp", None),
            P("section", "expert", "dp", None),
        ),
        check_vma=False,
    )
```

time: 2980 us -> 1250 us (0.42)
  waiting for transfers between devices: 1500 us -> 91.9 us
  Pallas kernels: 0 us -> 709 us
  blocking collectives: 621 us -> 153 us
  matrix products: 292 us -> 59.8 us
  local copies, waits for them, and re-layouts: 294 us -> 124 us
  other arithmetic: 168 us -> 79.6 us
  starting transfers between devices: 71.1 us -> 16 us
    all_to_all x8 -> x0, waiting for transfers between devices: 946 us -> none  [the longest x3 380 us: backward_layer(): lax.all_to_all(d_received, 'expert', split_axis=1, concat_axis=1, tiled=T...]
    pallas_call x0 -> x7, Pallas kernels: none -> 709 us  [the longest x2 294 us: experts_forward(): pl.pallas_call(functools.partial(experts_forward_kernel, ls, layer, chunk...]
    all_to_all x4 -> x0, blocking collectives: 577 us -> none  [the longest x2 291 us: backward_layer(): lax.all_to_all(d_sending, 'expert', split_axis=1, concat_axis=1, tiled=True)]
    dot_general x87 -> x33, matrix products: 285 us -> 58.9 us  [the longest x20 41.8 us: dot(): return jnp.dot(a, b, preferred_element_type=F32)]
    psum x1 -> x0, waiting for transfers between devices: 214 us -> none  [shards(): lax.psum(shared_sum[1].astype(jnp.bfloat16), 'expert').astype(jnp.float32)]
    reduce_scatter x8 -> x0, waiting for transfers between devices: 187 us -> none  [the longest x1 58.5 us: shards(): lax.psum_scatter(expert_sum[1].astype(jnp.bfloat16), 'dp', scatter_dimens...]
    all_gather x4 -> x0, waiting for transfers between devices: 151 us -> none  [the longest x1 61.8 us: fetch_each(): lax.all_gather(w_query, 'dp', axis=1, tiled=True)]
    all_gather x3 -> x2, blocking collectives: 11.3 us -> 153 us  [the longest x1 143 us: shards(): all_routes = lax.all_gather(routes[0], ('section', 'expert'), axis=0)]
  transfers between devices with their start and end apart: 25 -> 19, of which waited for: 19 -> 5; matrix products, arithmetic and copies ran while one was open for 11% -> 13% of each run, Pallas kernels for 0% -> 18%
where the time goes in v1:
time: 1250 us; the launch traced here: 1240 us
  Pallas kernels  709 us (57%)
  blocking collectives  153 us (12%)
  local copies, waits for them, and re-layouts  124 us (10%)
  waiting for transfers between devices  91.9 us (7%)
  other arithmetic  79.6 us (6%)
  matrix products  59.8 us (5%)
  starting transfers between devices  16 us (1%)
    pallas_call x2, Pallas kernels, experts_forward(): pl.pallas_call(functools.partial(experts_forward_kernel, ls, layer, chunk...  294 us
    pallas_call x2, Pallas kernels, experts_backward(): pl.pallas_call(functools.partial(experts_backward_kernel, ls, layer, chun...  195 us
    all_gather x1, blocking collectives, shards(): all_routes = lax.all_gather(routes[0], ('section', 'expert'), axis=0)  143 us
    ppermute x19, waiting for transfers between devices, swap(): return lax.ppermute(value, axis, [(0, 1), (1, 0)])  91.9 us
    pallas_call x1, Pallas kernels, spread_weights(): pl.pallas_call(functools.partial(spread_kernel, src, count), out_shape=sp...  76.5 us
    pallas_call x1, Pallas kernels, sum_scattered(): pl.pallas_call(functools.partial(sum_kernel, ls, chunks), out_shape=jax.S...  72.4 us
    pallas_call x1, Pallas kernels, gather_all(): pl.pallas_call(functools.partial(gather_kernel, ls, chunks), out_shape=ja...  70.8 us
    dot_general x20, matrix products, dot(): return jnp.dot(a, b, preferred_element_type=F32)  41.8 us
  transfers between devices with their start and end apart: 19, of which 5 were waited for; matrix products, arithmetic and copies ran while one was open for 13% of the time, Pallas kernels for 18%

profile of v1, /device:TPU:17, one launch (start us, length us, event | category | flops | bytes accessed | tf_op | source)
XLA Modules:
  0.0 1236.2 jit_solution(2703903381303716094)
XLA Ops:
  2.7 9.7 all_gather.6
  15.2 76.5 %spread_weights.1 = (bf16[1536,1536]{1,0:T(8,128)(2,1)}, bf16[1536,512]{1,0:T(8,128)(2,1)}, bf16[1536,512]{1,0:T(8,128)(2,1)}, bf16[1536,1536]{1,0:T(8,128)(2,1)}) custom-call(bf16[768,1536]{1,0:T(8,128)(2,1)} %bitcast.311, bf16[768,512]{1,0:T(8,128)(2,1)} %bitcast.339, bf16[768,512]{1,0:T(8,128)(2,1)} %bitcast.341, bf16[768,1536]{1,0:T(8,128)(2,1)} %bitcast.313), custom_call_target="tpu_custom_call" | custom-call | bytes 209715200 | tf_op jit(solution)/shard_map/spread_weights/pallas_call | solution.py:390
  91.7 6.6 copy.247
  99.0 2.7 copy.246
  105.8 143.5 %all_gather.7 = s32[16,2,128,8]{2,3,1,0:T(8,128)S(1)} all-gather(s32[1,2,128,8]{2,3,1,0:T(8,128)S(1)} %copy-done.113), channel_id=1, replica_groups=mesh['section'=2,'expert'=8,'dp'=2] {'section','expert'}, dimensions={0}, use_global_device_ids=true | all-gather | bytes 139264 | tf_op jit(solution)/shard_map/all_gather | solution.py:1009
  255.5 3.9 fusion.71
  261.9 3.4 multiply_reduce_fusion.5
  274.0 199.4 %experts_forward.2 = (bf16[128,1536]{1,0:T(8,128)(2,1)}, bf16[4,256,1536]{2,1,0:T(8,128)(2,1)}, bf16[4,256,1536]{2,1,0:T(8,128)(2,1)}, bf16[4,256,1536]{2,1,0:T(...) custom-call(bf16[128,1536]{1,0:T(8,128)(2,1)} %copy-done.26, ...), custom_call_target="tpu_custom_call" | custom-call | flops 14495514624 | bytes 62914560 | tf_op jit(solution)/shard_map/experts_forward/pallas_call | solution.py:558
  475.8 2.3 fusion.109
  478.2 4.4 fusion.110
  487.4 3.4 multiply_reduce_fusion.4
  491.8 94.5 %experts_forward.3 = (bf16[128,1536]{1,0:T(8,128)(2,1)}, bf16[4,256,1536]{2,1,0:T(8,128)(2,1)}, bf16[4,256,1536]{2,1,0:T(8,128)(2,1)}, bf16[4,256,1536]{2,1,0:T(8,128)(2,1)}, f32[4,256,128]{2,1,0:T(8,128)}) custom-call(bf16[128,1536]{1,0:T(8,128)(2,1)} %copy-done.24, f32[128,1536]{1,0:T(8,128)} %copy-done.6, f32[4,256,128]{2,1,0:T(8,128)} %bitcast.355, ...), custom_call_target="tpu_custom_call" | custom-call | flops 14495514624 | bytes 62914560 | tf_op jit(solution)/shard_map/experts_forward/pallas_call | solution.py:558
  586.4 95.0 %experts_backward.2 = (f32[128,1536]{1,0:T(8,128)}, f32[128,128]{1,0:T(8,128)}, bf16[3,1536,1536]{2,1,0:T(8,128)(2,1)}) custom-call(bf16[128,1536]{1,0:T(8,128)(2,1)} %dynamic-slice_bitcast_fusion.refs_0_, bf16[3,1536,512]{2,1,0:T(8,128)(2,1)} %bitcast.365, bf16[3,1536,512]{2,1,0:T(8,128)(2,1)} %bitcast.370, bf16[1536,1536]{1,0:T(8,128)(2,1)} %bitcast.375, ...), custom_call_target="tpu_custom_call" | custom-call | flops 28991029248 | bytes 104857600 | tf_op jit(solution)/shard_map/experts_backward/pallas_call | solution.py:721
  683.6 2.4 multiply_reduce_fusion
  688.0 4.7 convolution_convert_fusion.3
  701.1 2.4 fusion.55
  704.6 100.4 %experts_backward.3 = (f32[128,1536]{1,0:T(8,128)}, f32[128,128]{1,0:T(8,128)}, bf16[3,1536,1536]{2,1,0:T(8,128)(2,1)}) custom-call(bf16[128,1536]{1,0:T(8,128)(2,1)} %fusion.54.refs_0_, bf16[3,1536,512]{2,1,0:T(8,128)(2,1)} %bitcast.366, bf16[3,1536,512]{2,1,0:T(8,128)(2,1)} %bitcast.371, bf16[1536,1536]{1,0:T(8,128)(2,1)} %bitcast.376, ...), custom_call_target="tpu_custom_call" | custom-call | flops 28991029248 | bytes 104857600 | tf_op jit(solution)/shard_map/experts_backward/pallas_call | solution.py:721
  810.7 4.0 convolution_convert_fusion.2
  824.6 6.3 constant_dynamic-slice_fusion.6
  830.9 6.5 constant_dynamic-slice_fusion.4
  860.5 20.0 %collective-permute-done.5 = bf16[128,6528]{0,1:T(8,128)(2,1)} collective-permute-done((bf16[128,6528]{0,1:T(8,128)(2,1)}, bf16[128,6528]{0,1:T(8,128)(2,1)}, u32[]{:S(2)}, u32[]{:S(2)}) %collective-permute-start.5) | collective-permute-done | bytes 1671200 | tf_op jit(solution)/shard_map/ppermute | solution.py:956
  880.8 35.6 %collective-permute-done.6 = bf16[128,6528]{0,1:T(8,128)(2,1)} collective-permute-done((bf16[128,6528]{0,1:T(8,128)(2,1)}, bf16[128,6528]{0,1:T(8,128)(2,1)}, u32[]{:S(2)}, u32[]{:S(2)}) %collective-permute-start.6) | collective-permute-done | bytes 1671200 | tf_op jit(solution)/shard_map/ppermute | solution.py:956
  916.4 4.6 broadcast_select_fusion
  926.0 7.2 collective-permute-done.9
  936.2 9.7 add_convert_fusion.1
  945.9 2.6 slice.256
  951.4 9.5 add_convert_fusion
  960.9 2.6 slice.257
  973.6 2.7 convolution_convert_fusion.1
  976.3 3.7 convolution_convert_fusion
  980.5 72.4 %sum_scattered.1.x_ref = bf16[96,4224]{1,0:T(8,128)(2,1)S(1)} custom-call(bf16[4,192,4224]{2,1,0:T(8,128)(2,1)S(1)} %bitcast.282), custom_call_target="tpu_custom_call" | custom-call | bytes 209715200 | tf_op jit(solution)/shard_map/sum_scattered/pallas_call | solution.py:767
  1052.9 70.8 %gather_all.1 = bf16[4,192,4224]{2,1,0:T(8,128)(2,1)S(1)} custom-call(bf16[96,4224]{1,0:T(8,128)(2,1)S(1)} %sum_scattered.1.x_ref), custom_call_target="tpu_custom_call" | custom-call | bytes 209715200 | tf_op jit(solution)/shard_map/gather_all/pallas_call | solution.py:806
  1125.7 2.7 slice.261
  1132.2 5.2 broadcast_select_fusion.3
  1137.4 3.1 collective-permute-start.15
  1140.4 6.0 bitcast_convert_fusion
  1151.1 3.8 collective-permute-done.16
  1154.8 25.3 %collective-permute-done.17 = bf16[3,256,768]{2,1,0:T(8,128)(2,1)} collective-permute-done((bf16[3,256,768]{2,1,0:T(8,128)(2,1)}, bf16[3,256,768]{2,1,0:T(8,128)(2,1)}, u32[]{:S(2)}, u32[]{:S(2)}) %collective-permute-start.17) | collective-permute-done | bytes 1179680 | tf_op jit(solution)/shard_map/ppermute | solution.py:956
  1180.1 3.2 select_bitcast_fusion
  1183.3 3.5 collective-permute-start.18
  1186.8 3.9 slice_bitcast_fusion.2
  1190.7 5.1 slice_bitcast_fusion
  1195.8 2.9 fusion.4
  1198.7 6.8 fusion
  1205.5 9.6 copy.286
  1215.0 8.7 fusion.103
  1223.7 6.0 copy.287
  1229.8 6.1 copy.288
  (431 shorter events, 118.5 us)
Async XLA Ops:
  0.6 103.3 %copy-start = (s32[2,128]{1,0:T(2,128)S(1)}, s32[2,128]{1,0:T(2,128)}, u32[]{:S(2)}) copy-start(s32[2,128]{1,0:T(2,128)} %param.16) | copy-start | bytes 3076
  0.7 273.3 %collective-permute-start = (bf16[3,1536,512]{2,1,0:T(8,128)(2,1)}, bf16[3,1536,512]{2,1,0:T(8,128)(2,1)}, u32[]{:S(2)}, u32[]{:S(2)}) collective-permute-start(bf16[3,1536,512]{2,1,0:T(8,128)(2,1)} %bitcast.362), channel_id=1, source_target_pairs={{0,16},{16,0},{1,17},{17,1},{2,18},{18,2},{3,19},{19,3},{4,20},{20... | collective-permute-start | bytes 14155784 | tf_op jit(solution)/shard_map/ppermute | solution.py:956
  1.4 272.6 %collective-permute-start.1 = (bf16[3,1536,512]{2,1,0:T(8,128)(2,1)}, bf16[3,1536,512]{2,1,0:T(8,128)(2,1)}, u32[]{:S(2)}, u32[]{:S(2)}) collective-permute-start(bf16[3,1536,512]{2,1,0:T(8,128)(2,1)} %bitcast.367), channel_id=1, source_target_pairs={{0,16},{16,0},{1,17},{17,1},{2,18},{18,2},{3,19},{19,3},{4,20},{20... | collective-permute-start | bytes 14155784 | tf_op jit(solution)/shard_map/ppermute | solution.py:956
  1.5 272.5 %collective-permute-start.2 = (bf16[3,512,1536]{2,1,0:T(8,128)(2,1)}, bf16[3,512,1536]{2,1,0:T(8,128)(2,1)}, u32[]{:S(2)}, u32[]{:S(2)}) collective-permute-start(bf16[3,512,1536]{2,1,0:T(8,128)(2,1)} %bitcast.372), channel_id=1, source_target_pairs={{0,16},{16,0},{1,17},{17,1},{2,18},{18,2},{3,19},{19,3},{4,20},{20... | collective-permute-start | bytes 14155784 | tf_op jit(solution)/shard_map/ppermute | solution.py:956
  99.0 160.3 %copy-start.46 = (f32[128,32]{0,1:T(8,128)}, f32[128,32]{0,1:T(8,128)S(1)}, u32[]{:S(2)}) copy-start(f32[128,32]{0,1:T(8,128)S(1)} %get-tuple-element.206) | copy-start | bytes 49156
  99.0 160.3 %copy-start.81 = (f32[128,32]{0,1:T(8,128)}, f32[128,32]{0,1:T(8,128)S(1)}, u32[]{:S(2)}) copy-start(f32[128,32]{0,1:T(8,128)S(1)} %get-tuple-element.205) | copy-start | bytes 49156
  99.0 5.6 copy-start.16
  105.0 145.6 %copy-start.77 = (bf16[1,1536,24]{1,0,2:T(2,128)(2,1)S(1)}, bf16[1,1536,24]{1,0,2:T(2,128)(2,1)}, u32[]{:S(2)}) copy-start(bf16[1,1536,24]{1,0,2:T(2,128)(2,1)} %get-tuple-element.186) | copy-start | bytes 221188
  250.7 8.7 copy-start.58
  274.0 200.7 %copy-start.100 = (f32[1536]{0:T(1024)S(1)}, f32[1536]{0:T(1024)}, u32[]{:S(2)}) copy-start(f32[1536]{0:T(1024)} %get-tuple-element.131) | copy-start | bytes 18436
  475.8 9.0 copy-start.10
  704.5 100.5 %copy-start.63 = (f32[1,1,128,24]{3,2,1,0:T(8,128)S(1)}, f32[1,1,128,24]{3,2,1,0:T(8,128)}, u32[]{:S(2)}) copy-start(f32[1,1,128,24]{3,2,1,0:T(8,128)} %copy.316) | copy-start | bytes 36868
  704.5 100.5 %copy-start.65 = (f32[128,24]{1,0:T(8,128)S(1)}, f32[128,24]{1,0:T(8,128)}, u32[]{:S(2)}) copy-start(f32[128,24]{1,0:T(8,128)} %copy-done.64) | copy-start | bytes 36868
  704.5 100.5 %copy-start.116 = (f32[128]{0:T(128)S(1)}, f32[128]{0:T(128)}, u32[]{:S(2)}) copy-start(f32[128]{0:T(128)} %fusion.76) | copy-start | bytes 1540
  704.6 102.8 %copy-start.9 = (f32[128,1536]{1,0:T(8,128)S(1)}, f32[128,1536]{1,0:T(8,128)}, u32[]{:S(2)}) copy-start(f32[128,1536]{1,0:T(8,128)} %copy-done.8) | copy-start | bytes 2359300
  704.6 102.8 %copy-start.59 = (bf16[1,1536,24]{1,2,0:T(8,128)(2,1)S(1)}, bf16[1,1536,24]{1,2,0:T(8,128)(2,1)}, u32[]{:S(2)}) copy-start(bf16[1,1536,24]{1,2,0:T(8,128)(2,1)} %copy-done.58) | copy-start | bytes 221188
  704.6 102.8 %copy-start.98 = (f32[1536]{0:T(1024)S(1)}, f32[1536]{0:T(1024)}, u32[]{:S(2)}) copy-start(f32[1536]{0:T(1024)} %get-tuple-element.132) | copy-start | bytes 18436
  704.6 102.8 %copy-start.115 = (f32[128]{0:T(128)S(1)}, f32[128]{0:T(128)}, u32[]{:S(2)}) copy-start(f32[128]{0:T(128)} %copy-done.114) | copy-start | bytes 1540
  830.9 105.3 %collective-permute-start.11 = (bf16[3,1536,768]{2,1,0:T(8,128)(2,1)}, bf16[3,1536,768]{2,1,0:T(8,128)(2,1)}, u32[]{:S(2)}, u32[]{:S(2)}) collective-permute-start(bf16[3,1536,768]{2,1,0:T(8,128)(2,1)} %constant_dynamic-slice_fusion.6), channel_id=1, source_target_pairs={{0,16},{16,0},{1,17},{17,1},{2,18},{18,2},{3,19},{19,3},{4,20},{20... | collective-permute-start | bytes 21233672 | tf_op jit(solution)/shard_map/ppermute | solution.py:956
  830.9 7.0 copy-start.31
  830.9 7.0 copy-start.49
  830.9 7.0 copy-start.80
  830.9 7.1 copy-start.62
  837.4 114.0 %collective-permute-start.13 = (bf16[3,1536,768]{2,1,0:T(8,128)(2,1)}, bf16[3,1536,768]{2,1,0:T(8,128)(2,1)}, u32[]{:S(2)}, u32[]{:S(2)}) collective-permute-start(bf16[3,1536,768]{2,1,0:T(8,128)(2,1)} %constant_dynamic-slice_fusion.4), channel_id=1, source_target_pairs={{0,16},{16,0},{1,17},{17,1},{2,18},{18,2},{3,19},{19,3},{4,20},{20... | collective-permute-start | bytes 21233672 | tf_op jit(solution)/shard_map/ppermute | solution.py:956
  842.1 38.4 %collective-permute-start.5 = (bf16[128,6528]{0,1:T(8,128)(2,1)}, bf16[128,6528]{0,1:T(8,128)(2,1)}, u32[]{:S(2)}, u32[]{:S(2)}) collective-permute-start(bf16[128,6528]{0,1:T(8,128)(2,1)} %get-tuple-element.201), channel_id=1, source_target_pairs={{0,1},{1,0},{2,3},{3,2},{4,5},{5,4},{6,7},{7,6},{8,9},{9,8},{10,11... | collective-permute-start | bytes 5013512 | tf_op jit(solution)/shard_map/ppermute | solution.py:956
  842.2 10.1 slice-start.2
  843.7 8.6 slice-start.3
  850.8 65.5 %collective-permute-start.6 = (bf16[128,6528]{0,1:T(8,128)(2,1)}, bf16[128,6528]{0,1:T(8,128)(2,1)}, u32[]{:S(2)}, u32[]{:S(2)}) collective-permute-start(bf16[128,6528]{0,1:T(8,128)(2,1)} %get-tuple-element.203), channel_id=1, source_target_pairs={{0,1},{1,0},{2,3},{3,2},{4,5},{5,4},{6,7},{7,6},{8,9},{9,8},{10,11... | collective-permute-start | bytes 5013512 | tf_op jit(solution)/shard_map/ppermute | solution.py:956
  857.5 67.6 %collective-permute-start.8 = (f32[2,768]{0,1:T(8,128)}, f32[2,768]{0,1:T(8,128)}, u32[]{:S(2)}, u32[]{:S(2)}) collective-permute-start(f32[2,768]{0,1:T(8,128)} %copy.318), channel_id=1, source_target_pairs={{0,1},{1,0},{2,3},{3,2},{4,5},{5,4},{6,7},{7,6},{8,9},{9,8},{10,11... | collective-permute-start | bytes 18440 | tf_op jit(solution)/shard_map/ppermute | solution.py:956
  858.6 57.8 %copy-start.37 = (bf16[128,6528]{0,1:T(8,128)(2,1)S(1)}, bf16[128,6528]{0,1:T(8,128)(2,1)}, u32[]{:S(2)}) copy-start(bf16[128,6528]{0,1:T(8,128)(2,1)} %copy-done.36) | copy-start | bytes 5013508
  858.6 57.8 %copy-start.38 = (bf16[128,6528]{0,1:T(8,128)(2,1)S(1)}, bf16[128,6528]{0,1:T(8,128)(2,1)}, u32[]{:S(2)}) copy-start(bf16[128,6528]{0,1:T(8,128)(2,1)} %get-tuple-element.200) | copy-start | bytes 5013508
  880.6 52.7 %collective-permute-start.9 = (f32[2,768]{0,1:T(8,128)}, f32[2,768]{0,1:T(8,128)}, u32[]{:S(2)}, u32[]{:S(2)}) collective-permute-start(f32[2,768]{0,1:T(8,128)} %copy.320), channel_id=1, source_target_pairs={{0,1},{1,0},{2,3},{3,2},{4,5},{5,4},{6,7},{7,6},{8,9},{9,8},{10,11... | collective-permute-start | bytes 18440 | tf_op jit(solution)/shard_map/ppermute | solution.py:956
  916.4 5.9 copy-start.5
  916.4 5.9 copy-start.83
  921.0 51.3 %collective-permute-start.7 = (bf16[256,6528]{0,1:T(8,128)(2,1)}, bf16[256,6528]{0,1:T(8,128)(2,1)}, u32[]{:S(2)}, u32[]{:S(2)}) collective-permute-start(bf16[256,6528]{0,1:T(8,128)(2,1)} %get-tuple-element.150), channel_id=1, source_target_pairs={{0,16},{16,0},{1,17},{17,1},{2,18},{18,2},{3,19},{19,3},{4,20},{20... | collective-permute-start | bytes 10027016 | tf_op jit(solution)/shard_map/ppermute | solution.py:956
  925.1 42.9 %collective-permute-start.4 = (bf16[128,1536]{1,0:T(8,128)(2,1)}, bf16[128,1536]{1,0:T(8,128)(2,1)}, u32[]{:S(2)}, u32[]{:S(2)}) collective-permute-start(bf16[128,1536]{1,0:T(8,128)(2,1)} %broadcast_select_fusion.5), channel_id=1, source_target_pairs={{0,16},{16,0},{1,17},{17,1},{2,18},{18,2},{3,19},{19,3},{4,20},{20... | collective-permute-start | bytes 1179656 | tf_op jit(solution)/shard_map/ppermute | solution.py:956
  933.2 36.9 %collective-permute-start.3 = (bf16[128,1536]{1,0:T(8,128)(2,1)}, bf16[128,1536]{1,0:T(8,128)(2,1)}, u32[]{:S(2)}, u32[]{:S(2)}) collective-permute-start(bf16[128,1536]{1,0:T(8,128)(2,1)} %get-tuple-element.165), channel_id=1, source_target_pairs={{0,16},{16,0},{1,17},{17,1},{2,18},{18,2},{3,19},{19,3},{4,20},{20... | collective-permute-start | bytes 1179656 | tf_op jit(solution)/shard_map/ppermute | solution.py:956
  936.2 29.0 %collective-permute-start.10 = (f32[2,768]{0,1:T(8,128)}, f32[2,768]{0,1:T(8,128)}, u32[]{:S(2)}, u32[]{:S(2)}) collective-permute-start(f32[2,768]{0,1:T(8,128)} %broadcast_select_fusion.7), channel_id=1, source_target_pairs={{0,16},{16,0},{1,17},{17,1},{2,18},{18,2},{3,19},{19,3},{4,20},{20... | collective-permute-start | bytes 18440 | tf_op jit(solution)/shard_map/ppermute | solution.py:956
  951.4 180.7 %collective-permute-start.12 = (bf16[2,768,768]{2,1,0:T(8,128)(2,1)}, bf16[2,768,768]{2,1,0:T(8,128)(2,1)}, u32[]{:S(2)}, u32[]{:S(2)}) collective-permute-start(bf16[2,768,768]{2,1,0:T(8,128)(2,1)} %constant_dynamic-slice_fusion.5), channel_id=1, source_target_pairs={{0,1},{1,0},{2,3},{3,2},{4,5},{5,4},{6,7},{7,6},{8,9},{9,8},{10,11... | collective-permute-start | bytes 7077896 | tf_op jit(solution)/shard_map/ppermute | solution.py:956
  965.2 167.0 %collective-permute-start.14 = (bf16[2,768,768]{2,1,0:T(8,128)(2,1)}, bf16[2,768,768]{2,1,0:T(8,128)(2,1)}, u32[]{:S(2)}, u32[]{:S(2)}) collective-permute-start(bf16[2,768,768]{2,1,0:T(8,128)(2,1)} %constant_dynamic-slice_fusion.3), channel_id=1, source_target_pairs={{0,1},{1,0},{2,3},{3,2},{4,5},{5,4},{6,7},{7,6},{8,9},{9,8},{10,11... | collective-permute-start | bytes 7077896 | tf_op jit(solution)/shard_map/ppermute | solution.py:956
  1123.7 8.5 slice-start
  1125.7 6.5 slice-start.1
  1129.6 25.3 %collective-permute-start.16 = (bf16[3,256,768]{2,1,0:T(8,128)(2,1)}, bf16[3,256,768]{2,1,0:T(8,128)(2,1)}, u32[]{:S(2)}, u32[]{:S(2)}) collective-permute-start(bf16[3,256,768]{2,1,0:T(8,128)(2,1)} %constant_dynamic-slice_fusion.2), channel_id=1, source_target_pairs={{0,1},{1,0},{2,3},{3,2},{4,5},{5,4},{6,7},{7,6},{8,9},{9,8},{10,11... | collective-permute-start | bytes 3538952 | tf_op jit(solution)/shard_map/ppermute | solution.py:956
  1131.1 49.0 %collective-permute-start.17 = (bf16[3,256,768]{2,1,0:T(8,128)(2,1)}, bf16[3,256,768]{2,1,0:T(8,128)(2,1)}, u32[]{:S(2)}, u32[]{:S(2)}) collective-permute-start(bf16[3,256,768]{2,1,0:T(8,128)(2,1)} %constant_dynamic-slice_fusion.1), channel_id=1, source_target_pairs={{0,1},{1,0},{2,3},{3,2},{4,5},{5,4},{6,7},{7,6},{8,9},{9,8},{10,11... | collective-permute-start | bytes 3538952 | tf_op jit(solution)/shard_map/ppermute | solution.py:956
  1137.4 61.3 %collective-permute-start.15 = (bf16[2,768,768]{2,1,0:T(8,128)(2,1)}, bf16[2,768,768]{2,1,0:T(8,128)(2,1)}, u32[]{:S(2)}, u32[]{:S(2)}) collective-permute-start(bf16[2,768,768]{2,1,0:T(8,128)(2,1)} %get-tuple-element.141), channel_id=1, source_target_pairs={{0,16},{16,0},{1,17},{17,1},{2,18},{18,2},{3,19},{19,3},{4,20},{20... | collective-permute-start | bytes 7077896 | tf_op jit(solution)/shard_map/ppermute | solution.py:956
  1180.1 10.6 copy-start.2
  1183.3 12.4 %collective-permute-start.18 = (bf16[3,256,768]{2,1,0:T(8,128)(2,1)S(1)}, bf16[3,256,768]{2,1,0:T(8,128)(2,1)S(1)}, u32[]{:S(2)}, u32[]{:S(2)}) collective-permute-start(bf16[3,256,768]{2,1,0:T(8,128)(2,1)S(1)} %get-tuple-element.149), channel_id=1, source_target_pairs={{0,16},{16,0},{1,17},{17,1},{2,18},{18,2},{3,19},{19,3},{4,20},{20... | collective-permute-start | bytes 3538952 | tf_op jit(solution)/shard_map/ppermute | solution.py:956
  1229.7 6.1 copy-start.1
  (96 other events, 248.4 us)

commit v2 on v1

--- a/solution.py
+++ b/solution.py
@@ -51,27 +51,27 @@
     )
 
 
-def greet_all(peers):
-    count = 0
-    for wanted, where in peers:
+def greet_all(signals, waits):
+    for wanted, where in signals:
 
         @pl.when(wanted)
         def _(where=where):
             signal(**where)
 
-        count = count + jnp.where(wanted, 1, 0)
-    pl.semaphore_wait(pltpu.get_barrier_semaphore(), count)
-
-
-def greet(l, p, ls, extra=()):
-    greet_all(
-        (
-            (l >= 0, {"expert": index_of(l, 1 - p, ls)}),
-            (l > 0, {"expert": index_of(l - 1, p, ls)}),
-            (l < LINE - 1, {"expert": index_of(l + 1, p, ls)}),
-        )
-        + tuple(extra)
-    )
+    count = sum(jnp.where(wanted, 1, 0) for wanted in waits)
+
+    @pl.when(count > 0)
+    def _():
+        pl.semaphore_wait(pltpu.get_barrier_semaphore(), count)
+
+
+def greet(l, p, ls, signals=(), waits=()):
+    near = (
+        (l >= 0, {"expert": index_of(l, 1 - p, ls)}),
+        (l > 0, {"expert": index_of(l - 1, p, ls)}),
+        (l < LINE - 1, {"expert": index_of(l + 1, p, ls)}),
+    )
+    greet_all(near + tuple(signals), tuple(w for w, _ in near) + tuple(waits))
 
 
 def remote(src, dst, ssem, rsem, **where):
@@ -306,17 +306,21 @@
 
 
 class Spread:
-    def __init__(self, src, shards, wholes, sems):
+    def __init__(self, src, shards, wholes, scratch):
         self.src, self.shards, self.wholes = src, shards, wholes
-        self.own, self.xs, self.xr, self.cs, self.cr = sems
+        self.own, self.xs, self.xr, self.cs, self.cr = scratch[:5]
+        self.bounce = scratch[5:]
         self.s, self.x = lax.axis_index("section"), lax.axis_index("dp")
 
     def rows(self, i, x):
         size = self.shards[i].shape[0]
         return self.wholes[i].at[pl.ds(pl.multiple_of(x * size, size), size)]
 
-    def local(self, i):
-        return pltpu.make_async_copy(self.shards[i], self.rows(i, self.x), self.own.at[i])
+    def local_in(self, i):
+        return pltpu.make_async_copy(self.shards[i], self.bounce[i], self.own.at[0, i])
+
+    def local_out(self, i):
+        return pltpu.make_async_copy(self.bounce[i], self.rows(i, self.x), self.own.at[1, i])
 
     def across(self, i):
         return remote(
@@ -336,19 +340,26 @@
         v = self.rows(i, 1 - self.x)
         return remote(v, v, self.cs.at[1, i], self.cr.at[1, i], section=1 - self.s)
 
-    def greetings(self):
+    def signals(self):
         return (
             (self.s == self.src, {"dp": 1 - self.x}),
-            (self.s >= 0, {"section": 1 - self.s}),
-        )
+            (self.s != self.src, {"section": 1 - self.s}),
+        )
+
+    def waits(self):
+        return (self.s == self.src, self.s == self.src)
 
     def begin(self):
         @pl.when(self.s == self.src)
         def _():
-            for i in range(len(self.shards)):
+            count = len(self.shards)
+            for i in range(count):
                 self.across(i).start()
+                self.local_in(i).start()
+            for i in range(count):
                 self.core_own(i).start()
-                self.local(i).start()
+                self.local_in(i).wait()
+                self.local_out(i).start()
 
     def end(self):
         @pl.when(self.s == self.src)
@@ -360,7 +371,7 @@
                 self.across(i).wait_send()
                 self.core_own(i).wait_send()
                 self.core_other(i).wait_send()
-                self.local(i).wait()
+                self.local_out(i).wait()
 
         @pl.when(self.s != self.src)
         def _():
@@ -369,8 +380,10 @@
                 self.core_other(i).wait_recv()
 
 
-def spread_sems(count):
-    return [DMA((count,)), DMA((count,)), DMA((count,)), DMA((2, count)), DMA((2, count))]
+def spread_scratch(shards):
+    count = len(shards)
+    sems = [DMA((2, count)), DMA((count,)), DMA((count,)), DMA((2, count)), DMA((2, count))]
+    return sems + [pltpu.VMEM(w.shape, w.dtype) for w in shards]
 
 
 def spread_shapes(shards):
@@ -378,9 +391,9 @@
 
 
 def spread_kernel(src, count, *refs):
-    shards, wholes, sems = refs[:count], refs[count : 2 * count], refs[2 * count :]
-    spread = Spread(src, shards, wholes, sems)
-    greet_all(spread.greetings())
+    shards, wholes, scratch = refs[:count], refs[count : 2 * count], refs[2 * count :]
+    spread = Spread(src, shards, wholes, scratch)
+    greet_all(spread.signals(), spread.waits())
     spread.begin()
     spread.end()
 
@@ -392,8 +405,10 @@
         out_shape=spread_shapes(shards),
         in_specs=[HB] * count,
         out_specs=[HB] * count,
-        scratch_shapes=spread_sems(count),
-        compiler_params=pltpu.CompilerParams(collective_id=cid, has_side_effects=True),
+        scratch_shapes=spread_scratch(shards),
+        compiler_params=pltpu.CompilerParams(
+            collective_id=cid, has_side_effects=True, vmem_limit_bytes=32 * MIB
+        ),
         cost_estimate=pl.CostEstimate(flops=0, bytes_accessed=200 * MIB, transcendentals=0),
         name="spread_weights",
     )(*shards)
@@ -451,11 +466,11 @@
     )
     own.start()
     own.wait()
-    extra = ()
+    signals = waits = ()
     if n_spread:
         spread = Spread(1 - layer, shards, wholes, spread_sem)
-        extra = spread.greetings()
-    greet(l, p, ls, extra)
+        signals, waits = spread.signals(), spread.waits()
+    greet(l, p, ls, signals, waits)
     gather = Gather(l, p, ls, xb, ag_sems, chunks)
     total = Sum(l, p, ls, part, pairb, upb, dnb, rs_sems, chunks)
     gather.begin()
@@ -554,7 +569,7 @@
     scratch += link_sems(chunks) + link_sems(chunks)
     scratch += [DMA((3,)), DMA(()), DMA((3, LINE))]
     if n:
-        scratch += spread_sems(n)
+        scratch += spread_scratch(shards)
     return pl.pallas_call(
         functools.partial(experts_forward_kernel, ls, layer, chunks, n),
         out_shape=outs,
@@ -562,7 +577,7 @@
         out_specs=[VM, HB, HB, HB, VM] + [HB] * n,
         scratch_shapes=scratch,
         compiler_params=pltpu.CompilerParams(
-            collective_id=cid, has_side_effects=True, vmem_limit_bytes=56 * MIB
+            collective_id=cid, has_side_effects=True, vmem_limit_bytes=60 * MIB
         ),
         cost_estimate=pl.CostEstimate(
             flops=6 * LINE * two * width * wide, bytes_accessed=60 * MIB, transcendentals=0
@@ -571,14 +586,108 @@
     )(n2, h1, mask, wr, *mine, *theirs, *shards)
 
 
-def experts_backward_kernel(ls, layer, chunks, *refs):
+class Deliver:
+    def __init__(self, layer, sums, near, far, sems):
+        self.layer, self.sums, self.near, self.far = layer, sums, near, far
+        self.ns, self.nr, self.fs, self.fr = sems
+        self.s, self.x = lax.axis_index("section"), lax.axis_index("dp")
+
+    def signals(self, met_section):
+        owner = self.s == self.layer
+        out = [
+            (owner, {"dp": 1 - self.x}),
+            (owner, {"dp": 1 - self.x, "section": 1 - self.layer}),
+        ]
+        if not met_section:
+            out.append((owner, {"section": 1 - self.layer}))
+        return tuple(out)
+
+    def waits(self, met_section):
+        away = self.s != self.layer
+        return (self.s >= 0,) + (() if met_section else (away,))
+
+    def to_far(self, i):
+        return remote(
+            self.sums.at[i, 1 - self.x],
+            self.far.at[self.s, i],
+            self.fs.at[i],
+            self.fr.at[self.s, i],
+            dp=1 - self.x,
+            section=self.layer,
+        )
+
+    def to_near(self, i):
+        return remote(
+            self.sums.at[i, self.x],
+            self.near.at[i],
+            self.ns.at[i],
+            self.nr.at[i],
+            section=self.layer,
+        )
+
+    def from_far(self, h, i):
+        return remote(
+            self.sums.at[i, 1 - self.x],
+            self.far.at[h, i],
+            self.fs.at[i],
+            self.fr.at[h, i],
+            dp=1 - self.x,
+            section=self.layer,
+        )
+
+    def begin(self):
+        for i in range(3):
+            self.to_far(i).start()
+
+        @pl.when(self.s != self.layer)
+        def _():
+            for i in range(3):
+                self.to_near(i).start()
+
+    def end(self):
+        for i in range(3):
+            self.to_far(i).wait_send()
+
+        @pl.when(self.s != self.layer)
+        def _():
+            for i in range(3):
+                self.to_near(i).wait_send()
+
+        @pl.when(self.s == self.layer)
+        def _():
+            for i in range(3):
+                self.to_near(i).wait_recv()
+                for h in range(2):
+                    self.from_far(h, i).wait_recv()
+
+
+def deliver_sems():
+    return [DMA((3,)), DMA((3,)), DMA((3,)), DMA((2, 3))]
+
+
+def deliver_shapes(sums):
+    kinds, _, rows, width = sums.shape
+    return [
+        jax.ShapeDtypeStruct((kinds, rows, width), BF16),
+        jax.ShapeDtypeStruct((2, kinds, rows, width), BF16),
+    ]
+
+
+def experts_backward_kernel(ls, layer, chunks, exchange, n_deliver, *refs):
     g_ref = refs[0]
     mine, theirs = refs[1:4], refs[4:7]
     x_in, gp_in, up_in, gates_ref = refs[7:11]
-    dn_ref, dgate_ref, grads = refs[11:14]
-    (xb, gb, gpb, upre, act, part, pairb, upb, dnb, wg, wu, wd, stage) = refs[14:27]
-    ag_sems, rs_sems = refs[27:33], refs[33:39]
-    w_sem, own_sem, load_sem, stage_sem = refs[39:]
+    sums_in = refs[11 : 11 + n_deliver]
+    at = 11 + n_deliver
+    dn_ref, dgate_ref, grads, got = refs[at : at + 4]
+    near_far = refs[at + 4 : at + 4 + 2 * n_deliver]
+    at = at + 4 + 2 * n_deliver
+    (xb, gb, gpb, upre, act, part, pairb, upb, dnb, wg, wu, wd, stage, extra) = refs[at : at + 14]
+    at += 14
+    ag_sems, rs_sems = refs[at : at + 6], refs[at + 6 : at + 12]
+    at += 12
+    w_sem, own_sem, load_sem, stage_sem, got_sem, extra_sem = refs[at : at + 6]
+    deliver_sem = refs[at + 6 :]
 
     e = lax.axis_index("expert")
     s = lax.axis_index("section")
@@ -600,10 +709,19 @@
     )
     own.start()
     own.wait()
-    greet(l, p, ls)
+    signals = waits = ()
+    if exchange:
+        signals, waits = ((s >= 0, {"section": 1 - s}),), (s >= 0,)
+    if n_deliver:
+        deliver = Deliver(1 - layer, sums_in[0], *near_far, deliver_sem)
+        signals += deliver.signals(True)
+        waits += deliver.waits(True)
+    greet(l, p, ls, signals, waits)
     gather = Gather(l, p, ls, gb, ag_sems, chunks)
     total = Sum(l, p, ls, part, pairb, upb, dnb, rs_sems, chunks)
     gather.begin()
+    if n_deliver:
+        deliver.begin()
     fetch(mine, theirs, own_layer, (wg, wu, wd), w_sem, wait=True)
     for copy in loads:
         copy.wait()
@@ -655,45 +773,99 @@
         dn_ref[rows, :] = value[:, :width]
         dgate_ref[rows, :] = value[:, width:]
 
-    height = 256
-    tiles = width // height
-
-    def stored(t, kind):
-        rows = pl.ds(pl.multiple_of(t * height, height), height)
-        return pltpu.make_async_copy(
-            stage.at[kind], grads.at[kind, rows], stage_sem.at[kind]
-        )
+    def stored(kind, t):
+        if exchange:
+            return pltpu.make_async_copy(
+                stage.at[kind], grads.at[kind, t % 2], stage_sem.at[0, kind]
+            )
+        return pltpu.make_async_copy(stage.at[kind], grads.at[kind, t], stage_sem.at[0, kind])
+
+    def handed(kind, t):
+        return remote(
+            stage.at[kind],
+            got.at[kind, t % 2],
+            stage_sem.at[1, kind],
+            got_sem.at[kind, t % 2],
+            section=1 - s,
+        )
+
+    def product(lhs, rhs, cuts):
+        def rows(L):
+            return jnp.concatenate([lhs[L, :, cut] for cut in cuts], axis=1)
+
+        acc = dot_tn(rows(0), rhs[0])
+        for L in range(1, LINE):
+            acc = acc + dot_tn(rows(L), rhs[L])
+        return acc
 
     def weight_grads(t, carry):
-        cols = pl.ds(pl.multiple_of(t * height, height), height)
-        for kind, (lhs, rhs) in enumerate(((xb, gpb), (xb, upre), (act, gb))):
-            acc = dot_tn(lhs[0, :, cols], rhs[0])
-            for L in range(1, LINE):
-                acc = acc + dot_tn(lhs[L, :, cols], rhs[L])
-
-            @pl.when(t > 0)
-            def _():
-                stored(t - 1, kind).wait()
-
-            stage[kind] = acc.astype(BF16)
-            stored(t, kind).start()
+        if exchange:
+            part_x = t % 2
+            part_h = jnp.where(t < 2, 1 - s, s)
+        else:
+            part_x, part_h = t // 2, t % 2
+        quarter = width // 4
+        start = pl.multiple_of((part_x * 2 + part_h) * quarter, quarter)
+        wide_cut = [pl.ds(start, quarter)]
+        small = hidden // 4
+        down_cut = [
+            pl.ds(pl.multiple_of(j * hidden + (part_x * 2 + part_h) * small, small), small)
+            for j in range(EXP_DEV)
+        ]
+        for kind, (lhs, rhs, cuts) in enumerate(
+            ((xb, gpb, wide_cut), (xb, upre, wide_cut), (act, gb, down_cut))
+        ):
+            acc = product(lhs, rhs, cuts)
+            if exchange:
+
+                @pl.when((t > 0) & (t <= 2))
+                def _():
+                    handed(kind, t - 1).wait_send()
+
+                @pl.when(t > 2)
+                def _():
+                    stored(kind, t - 1).wait()
+
+                @pl.when(t < 2)
+                def _():
+                    stage[kind] = acc.astype(BF16)
+                    handed(kind, t).start()
+
+                @pl.when(t >= 2)
+                def _():
+                    handed(kind, t).wait_recv()
+                    load = pltpu.make_async_copy(got.at[kind, t % 2], extra, extra_sem)
+                    load.start()
+                    load.wait()
+                    stage[kind] = (acc + extra[...].astype(F32)).astype(BF16)
+                    stored(kind, t).start()
+            else:
+
+                @pl.when(t > 0)
+                def _():
+                    stored(kind, t - 1).wait()
+
+                stage[kind] = acc.astype(BF16)
+                stored(kind, t).start()
         return carry
 
     def back(j, carry):
+        weight_grads(j, carry)
         total.pass_on(near_first(l, LINE - 1 - j), write)
-        first = j * tiles // (LINE - 1)
-        last = jnp.minimum((j + 1) * tiles // (LINE - 1), tiles)
-        lax.fori_loop(first, last, weight_grads, 0)
         return carry
 
     lax.fori_loop(0, LINE, back, 0)
     for kind in range(3):
-        stored(tiles - 1, kind).wait()
+        stored(kind, 3).wait()
     gather.end()
     total.end()
-
-
-def experts_backward(ls, layer, cid, g, mine, theirs, x, gp, up, gates, chunks=2):
+    if n_deliver:
+        deliver.end()
+
+
+def experts_backward(
+    ls, layer, cid, g, mine, theirs, x, gp, up, gates, exchange, sums=(), chunks=2
+):
     tokens, width = g.shape
     hidden = mine[0].shape[2]
     wide = EXP_DEV * hidden
@@ -701,6 +873,7 @@
     mine = (mine[0], mine[1], mine[2].reshape(wide, width))
     theirs = (theirs[0], theirs[1], theirs[2].reshape(wide, width))
     sent = width + LANES
+    quarter = width // 4
     scratch = [
         pltpu.VMEM((LINE, two, width), BF16),
         pltpu.VMEM((LINE, two, width), BF16),
@@ -714,81 +887,98 @@
         pltpu.VMEM(mine[0].shape, BF16),
         pltpu.VMEM(mine[1].shape, BF16),
         pltpu.VMEM(mine[2].shape, BF16),
-        pltpu.VMEM((3, 256, width), BF16),
+        pltpu.VMEM((3, quarter, width), BF16),
+        pltpu.VMEM((quarter, width), BF16),
     ]
     scratch += link_sems(chunks) + link_sems(chunks)
-    scratch += [DMA((3,)), DMA(()), DMA((3,)), DMA((3,))]
+    scratch += [DMA((3,)), DMA(()), DMA((3,)), DMA((2, 3)), DMA((3, 2)), DMA(())]
+    n = len(sums)
+    shapes = [
+        jax.ShapeDtypeStruct((tokens, width), F32),
+        jax.ShapeDtypeStruct((tokens, LANES), F32),
+        jax.ShapeDtypeStruct((3, 2 if exchange else 4, quarter, width), BF16),
+        jax.ShapeDtypeStruct((3, 2, quarter, width), BF16),
+    ]
+    if n:
+        shapes += deliver_shapes(sums[0])
+        scratch += deliver_sems()
     return pl.pallas_call(
-        functools.partial(experts_backward_kernel, ls, layer, chunks),
-        out_shape=[
-            jax.ShapeDtypeStruct((tokens, width), F32),
-            jax.ShapeDtypeStruct((tokens, LANES), F32),
-            jax.ShapeDtypeStruct((3, width, wide), BF16),
-        ],
-        in_specs=[VM] + [HB] * 9 + [VM],
-        out_specs=[VM, VM, HB],
+        functools.partial(experts_backward_kernel, ls, layer, chunks, exchange, n),
+        out_shape=shapes,
+        in_specs=[VM] + [HB] * 9 + [VM] + [HB] * n,
+        out_specs=[VM, VM, HB, HB] + [HB] * (2 * n),
         scratch_shapes=scratch,
         compiler_params=pltpu.CompilerParams(
-            collective_id=cid, has_side_effects=True, vmem_limit_bytes=60 * MIB
+            collective_id=cid, has_side_effects=True, vmem_limit_bytes=62 * MIB
         ),
         cost_estimate=pl.CostEstimate(
             flops=12 * LINE * two * width * wide, bytes_accessed=100 * MIB, transcendentals=0
         ),
         name="experts_backward",
-    )(g, *mine, *theirs, x, gp, up, gates)
-
-
-def sum_kernel(ls, chunks, p_ref, o_ref, part, pairb, upb, dnb, load_sem, *sems):
+    )(g, *mine, *theirs, x, gp, up, gates, *sums)
+
+
+def shared_grads_kernel(ls, chunks, *refs):
+    lhs_ref, rhs_ref, gain_ref, sums_ref = refs[:4]
+    out, near, far = refs[4:7]
+    part, pairb, upb, dnb, small = refs[7:12]
+    ag_sems, rs_sems, deliver_sem = refs[12:18], refs[18:24], refs[24:]
     l, p = place(lax.axis_index("expert"), ls)
-    load = pltpu.make_async_copy(p_ref, part, load_sem)
-    load.start()
-    greet(l, p, ls)
-    total = Sum(l, p, ls, part, pairb, upb, dnb, sems, chunks)
-    rows = pairb.shape[1] // chunks
-    load.wait()
-    for k in range(LINE):
-        total.give(near_first(l, LINE - 1 - k))
+    tokens, rows = lhs_ref.shape[1:]
+    half, width = pairb.shape[1:]
+    deliver = Deliver(0, sums_ref, near, far, deliver_sem)
+    greet(l, p, ls, deliver.signals(False), deliver.waits(False))
+    gather = Gather(l, p, ls, out, ag_sems, chunks)
+    total = Sum(l, p, ls, part, pairb, upb, dnb, rs_sems, chunks)
+    n_first = 5
+    small[...] = dot_tn(lhs_ref[2], rhs_ref[:, 8 * width :]) + gain_ref[...]
+    n_rows = rows // 8
+    quarter = n_rows // 4
+
+    def fill(k, carry):
+        L = near_first(l, LINE - 1 - k)
+
+        def one(q, carry):
+            b = 2 * L + q
+            cols = pl.ds(pl.multiple_of(b * width, width), width)
+            which = jnp.where(b < n_first, 0, 1)
+            acc = dot_tn(lhs_ref[which], rhs_ref[:, cols])
+            start = pl.multiple_of(q * half, half)
+            part[L, pl.ds(start, rows), :] = acc.astype(BF16)
+            for g in range(width // LANES):
+                top = pl.multiple_of(b * n_rows + g * quarter, 8)
+                piece = small[pl.ds(top, quarter), :]
+                piece = jnp.concatenate(
+                    [piece, jnp.zeros((half - rows - quarter, LANES), F32)], axis=0
+                )
+                part[
+                    L,
+                    pl.ds(pl.multiple_of(start + rows, half - rows), half - rows),
+                    g * LANES : (g + 1) * LANES,
+                ] = piece.astype(BF16)
+            return carry
+
+        lax.fori_loop(0, 2, one, 0)
+        total.give(L)
+
+        @pl.when(k == 0)
+        def _():
+            deliver.begin()
+
+        return carry
+
+    lax.fori_loop(0, LINE, fill, 0)
 
     def write(c, value):
-        o_ref[pl.ds(c * rows, rows), :] = value.astype(BF16)
+        size = half // chunks
+        start = pl.multiple_of(p * half + c * size, size)
+        out[l, pl.ds(start, size), :] = value.astype(BF16)
 
     def back(j, carry):
         total.pass_on(near_first(l, LINE - 1 - j), write)
         return carry
 
     lax.fori_loop(0, LINE, back, 0)
-    total.end()
-
-
-def sum_scattered(ls, cid, parts, chunks=2):
-    n, two, width = parts.shape
-    rows = two // 2
-    buf = pltpu.VMEM((LINE, rows, width), BF16)
-    return pl.pallas_call(
-        functools.partial(sum_kernel, ls, chunks),
-        out_shape=jax.ShapeDtypeStruct((rows, width), BF16),
-        in_specs=[HB],
-        out_specs=VM,
-        scratch_shapes=[pltpu.VMEM((LINE, two, width), BF16), buf, buf, buf, DMA(())]
-        + link_sems(chunks),
-        compiler_params=pltpu.CompilerParams(
-            collective_id=cid, has_side_effects=True, vmem_limit_bytes=40 * MIB
-        ),
-        cost_estimate=pl.CostEstimate(flops=0, bytes_accessed=200 * MIB, transcendentals=0),
-        name="sum_scattered",
-    )(parts)
-
-
-def gather_kernel(ls, chunks, x_ref, o_ref, own_sem, *sems):
-    l, p = place(lax.axis_index("expert"), ls)
-    rows = x_ref.shape[0]
-    own = pltpu.make_async_copy(
-        x_ref, o_ref.at[l, pl.ds(pl.multiple_of(p * rows, rows), rows)], own_sem
-    )
-    own.start()
-    own.wait()
-    greet(l, p, ls)
-    gather = Gather(l, p, ls, o_ref, sems, chunks)
     gather.begin()
 
     def step(k, carry):
@@ -799,22 +989,155 @@
     for L in range(LINE):
         gather.from_pair(L)
     gather.end()
-
-
-def gather_all(ls, cid, rows, chunks=2):
-    count, width = rows.shape
+    total.end()
+    deliver.end()
+
+
+def shared_grads(ls, cid, lhs, rhs, gain_cols, sums, chunks=2):
+    _, tokens, rows = lhs.shape
+    width = 512
+    half = rows + 32
+    buf = pltpu.VMEM((LINE, half, width), BF16)
     return pl.pallas_call(
-        functools.partial(gather_kernel, ls, chunks),
-        out_shape=jax.ShapeDtypeStruct((LINE, 2 * count, width), BF16),
-        in_specs=[VM],
-        out_specs=VM,
-        scratch_shapes=[DMA(())] + link_sems(chunks),
+        functools.partial(shared_grads_kernel, ls, chunks),
+        out_shape=[jax.ShapeDtypeStruct((LINE, 2 * half, width), BF16)] + deliver_shapes(sums),
+        in_specs=[VM, VM, VM, HB],
+        out_specs=[VM, HB, HB],
+        scratch_shapes=[
+            pltpu.VMEM((LINE, 2 * half, width), BF16),
+            buf,
+            buf,
+            buf,
+            pltpu.VMEM((rows, LANES), F32),
+        ]
+        + link_sems(chunks)
+        + link_sems(chunks)
+        + deliver_sems(),
         compiler_params=pltpu.CompilerParams(
-            collective_id=cid, has_side_effects=True, vmem_limit_bytes=40 * MIB
+            collective_id=cid, has_side_effects=True, vmem_limit_bytes=60 * MIB
         ),
-        cost_estimate=pl.CostEstimate(flops=0, bytes_accessed=200 * MIB, transcendentals=0),
-        name="gather_all",
-    )(rows)
+        cost_estimate=pl.CostEstimate(flops=0, bytes_accessed=400 * MIB, transcendentals=0),
+        name="shared_grads",
+    )(lhs, rhs, gain_cols, sums)
+
+
+def finish_kernel(*refs):
+    sums, near, far = refs[0:2], refs[2:4], refs[4:6]
+    blocks = refs[6]
+    gate_out, up_out, down_out = refs[7:10]
+    wides = refs[10:14]
+    left, right, wide, cols_in, cols_out, in_sem, out_sem, col_in_sem, col_out_sem = refs[14:]
+    s, x = lax.axis_index("section"), lax.axis_index("dp")
+    quarter, width = left.shape[1:]
+    hidden = gate_out.shape[2]
+    small = quarter // EXP_DEV
+    units = [(kind, h) for kind in range(3) for h in range(2)]
+
+    def load(u, wait):
+        kind, h = units[u]
+        slot = u % 2
+        for layer in range(2):
+
+            @pl.when(s == layer)
+            def _():
+                first = sums[layer].at[kind, x] if h == layer else near[layer].at[kind]
+                a = pltpu.make_async_copy(first, left.at[slot], in_sem.at[0, slot])
+                b = pltpu.make_async_copy(far[layer].at[h, kind], right.at[slot], in_sem.at[1, slot])
+                if wait:
+                    a.wait()
+                    b.wait()
+                else:
+                    a.start()
+                    b.start()
+
+    def stores(u):
+        kind, h = units[u]
+        slot = u % 2
+        out = []
+        for j in range(EXP_DEV):
+            if kind < 2:
+                src = wide.at[slot, :, pl.ds(j * hidden, hidden)]
+                dst = (gate_out, up_out)[kind].at[j, pl.ds(h * quarter, quarter)]
+            else:
+                src = wide.at[slot, pl.ds(j * small, small)]
+                dst = down_out.at[j, pl.ds(h * small, small)]
+            out.append(pltpu.make_async_copy(src, dst, out_sem.at[slot, j]))
+        return out
+
+    rows = cols_out.shape[1]
+    block_width = blocks.shape[2]
+    half = blocks.shape[1] // 2
+    places = []
+    for i, ref in enumerate(wides):
+        for n in range(ref.shape[1] // block_width):
+            places.append((ref, n))
+
+    def col_load(b):
+        src = blocks.at[b // 2, pl.ds((b % 2) * half, rows)]
+        return pltpu.make_async_copy(src, cols_in.at[b % 2], col_in_sem.at[b % 2])
+
+    def col_store(b):
+        ref, n = places[b]
+        dst = ref.at[:, pl.ds(n * block_width, block_width)]
+        return pltpu.make_async_copy(cols_out.at[b % 2], dst, col_out_sem.at[b % 2])
+
+    load(0, False)
+    col_load(0).start()
+    for u in range(len(units)):
+        if u + 1 < len(units):
+            load(u + 1, False)
+        load(u, True)
+        if u >= 2:
+            for copy in stores(u - 2):
+                copy.wait()
+        wide[u % 2] = left[u % 2].astype(F32) + right[u % 2].astype(F32)
+        for copy in stores(u):
+            copy.start()
+    for b in range(len(places)):
+        if b + 1 < len(places):
+            col_load(b + 1).start()
+        col_load(b).wait()
+        if b >= 2:
+            col_store(b - 2).wait()
+        cols_out[b % 2] = cols_in[b % 2].astype(F32)
+        col_store(b).start()
+    for u in (len(units) - 2, len(units) - 1):
+        for copy in stores(u):
+            copy.wait()
+    for b in (len(places) - 2, len(places) - 1):
+        col_store(b).wait()
+
+
+def finish(sums, near, far, blocks, rows, hidden, widths):
+    quarter, width = near[0].shape[1:]
+    half = blocks.shape[1] // 2
+    block_width = blocks.shape[2]
+    down = hidden // 2
+    return pl.pallas_call(
+        finish_kernel,
+        out_shape=[
+            jax.ShapeDtypeStruct((EXP_DEV, rows, hidden), F32),
+            jax.ShapeDtypeStruct((EXP_DEV, rows, hidden), F32),
+            jax.ShapeDtypeStruct((EXP_DEV, down, width), F32),
+        ]
+        + [jax.ShapeDtypeStruct((rows, w), F32) for w in widths],
+        in_specs=[HB] * 7,
+        out_specs=[HB] * 7,
+        scratch_shapes=[
+            pltpu.VMEM((2, quarter, width), BF16),
+            pltpu.VMEM((2, quarter, width), BF16),
+            pltpu.VMEM((2, quarter, width), F32),
+            pltpu.VMEM((2, rows, block_width), BF16),
+            pltpu.VMEM((2, rows, block_width), F32),
+            DMA((2, 2)),
+            DMA((2, EXP_DEV)),
+            DMA((2,)),
+            DMA((2,)),
+        ],
+        compiler_params=pltpu.CompilerParams(vmem_limit_bytes=32 * MIB),
+        cost_estimate=pl.CostEstimate(flops=0, bytes_accessed=50 * MIB, transcendentals=0),
+        name="finish",
+    )(*sums, *near, *far, blocks)
 
 
 def rope_tables(length, head_dim):
@@ -1062,17 +1385,15 @@
     d_ins, act_list, gain_list, expert_list = [None] * 2, [None] * 2, [None] * 2, [None] * 2
     for k in (1, 0):
         kept = kept_list[k]
-        d_normed_two, d_gates, grads = experts_backward(
-            ls, k, 3 + k, d_out, mine, theirs, *kept["saved"]
-        )
-        mid = grads.shape[2] // 2
-        there = half_of(grads, 2, 1 - s, mid)
-        here = half_of(grads, 2, s, mid)
-        both = (here.astype(F32) + swap(there, "section").astype(F32)).astype(BF16)
-        gate_up = sum_over_dp(both[:2], 1, shard_rows)
-        down = both[2].reshape(EXP_DEV, -1, mid)
-        down = sum_over_dp(down, 1, down.shape[1] // n_dp)
-        expert_list[k] = (gate_up.astype(BF16), down.astype(BF16))
+        pair_up = n_dp == 2
+        sums = (expert_list[1],) if (pair_up and k == 0) else ()
+        got = experts_backward(
+            ls, k, 3 + k, d_out, mine, theirs, *kept["saved"], pair_up, sums
+        )
+        d_normed_two, d_gates = got[:2]
+        expert_list[k] = got[2]
+        if sums:
+            delivered = got[4:6]
 
         d_gates = d_gates[:, :n_experts] + d_gates[:, 32 : 32 + n_experts]
         d_out, acts, gain_grads = attention_backward(
@@ -1117,42 +1438,50 @@
     acts_mine = jnp.concatenate(own_layer(act_list[0], act_list[1]), axis=0)
     gain_mine = sum(own_layer(gain_list[0], gain_list[1]))
     lhs_rows = shard_rows if n_dp == 2 else width
-    lhs = [acts_mine[:, i * lhs_rows : (i + 1) * lhs_rows] for i in range(3)]
-    rhs = acts_mine[:, 3 * lhs_rows :]
-    n_qkv = own[0].shape[1] + own[1].shape[1] + own[2].shape[1]
-    parts = jnp.concatenate(
-        [
-            dot_tn(lhs[0], rhs[:, :n_qkv]),
-            dot_tn(lhs[1], rhs[:, n_qkv : n_qkv + width]),
-            dot_tn(lhs[2], rhs[:, n_qkv + width :]),
-        ],
-        axis=1,
-    ).astype(BF16)
-    if n_dp != 2:
-        parts = lax.psum_scatter(parts, "dp", scatter_dimension=0, tiled=True)
     gain_cols = jnp.pad(gain_mine.T, ((0, 0), (LANES - 2, 0)))
-    parts = jnp.concatenate(
-        [parts[:, :-LANES], (parts[:, -LANES:].astype(F32) + gain_cols).astype(BF16)], axis=1
-    )
+    widths = [w.shape[1] for w in own]
     if n_dp == 2:
-        block = shard_rows // n_exp
-        blocks = parts.reshape(LINE, 2 * block, -1)
-        spread = gather_all(ls, 6, sum_scattered(ls, 5, blocks))
-        spread = spread.reshape(shard_rows, -1).astype(F32)
+        lhs = acts_mine[:, : 3 * lhs_rows].reshape(-1, 3, lhs_rows).swapaxes(0, 1)
+        rhs = acts_mine[:, 3 * lhs_rows :]
+        blocks, near, far = shared_grads(ls, 5, lhs, rhs, gain_cols, expert_list[0])
+        gate_grad, up_grad, down_grad, *wide_grads = finish(
+            expert_list,
+            (near, delivered[0]),
+            (far, delivered[1]),
+            blocks,
+            shard_rows,
+            w_gate.shape[3],
+            widths,
+        )
+        half = blocks.shape[1] // 2
+        tail = blocks.reshape(2 * LINE, half, -1)[:, shard_rows : shard_rows + shard_rows // 32]
+        tail = tail.reshape(2 * LINE, -1, 4, LANES).swapaxes(1, 2).reshape(shard_rows, LANES)
+        tail = tail.astype(F32)
     else:
-        spread = lax.psum(parts, "expert").astype(F32)
-
-    def joined(zero, one):
-        kept_part, got = own_layer(zero, one)
-        return jnp.where(
-            first,
-            jnp.concatenate([kept_part, got], axis=-1),
-            jnp.concatenate([got, kept_part], axis=-1),
-        ).astype(F32)
-
-    gate_up = joined(expert_list[0][0], expert_list[1][0])
-    gate_up = gate_up.reshape(2, shard_rows, EXP_DEV, -1).swapaxes(1, 2)
-    down = joined(expert_list[0][1], expert_list[1][1])
+        lhs = [acts_mine[:, i * lhs_rows : (i + 1) * lhs_rows] for i in range(3)]
+        rhs = acts_mine[:, 3 * lhs_rows :]
+        n_qkv = sum(widths[:3])
+        parts = jnp.concatenate(
+            [
+                dot_tn(lhs[0], rhs[:, :n_qkv]),
+                dot_tn(lhs[1], rhs[:, n_qkv : n_qkv + width]),
+                dot_tn(lhs[2], rhs[:, n_qkv + width :]),
+            ],
+            axis=1,
+        ).astype(BF16)
+        parts = lax.psum_scatter(parts, "dp", scatter_dimension=0, tiled=True).astype(F32)
+        parts = parts + jnp.pad(gain_cols, ((0, 0), (parts.shape[1] - LANES, 0)))
+        spread = lax.psum(parts.astype(BF16), "expert").astype(F32)
+        cut = [sum(widths[:i]) for i in range(5)]
+        wide_grads = [spread[:, cut[i] : cut[i + 1]] for i in range(4)]
+        tail = spread[:, cut[4] :]
+        grads = sum(part.astype(F32) for part in own_layer(*expert_list)).astype(BF16)
+        gate_up = grads[:2].reshape(2, width, EXP_DEV, -1)
+        gate_up = lax.psum_scatter(gate_up, "dp", scatter_dimension=1, tiled=True)
+        gate_grad, up_grad = gate_up.swapaxes(1, 2).astype(F32)
+        down = grads[2].reshape(4, EXP_DEV, -1, width).swapaxes(0, 1)
+        down = down.reshape(EXP_DEV, -1, width)
+        down_grad = lax.psum_scatter(down, "dp", scatter_dimension=1, tiled=True).astype(F32)
 
     def both_micros(zero, one):
         kept_part, got = own_layer(zero, one)
@@ -1160,22 +1489,19 @@
 
     section_outputs = both_micros(outs[0], outs[1])
     section_input_grads = both_micros(d_ins[0], d_ins[1])
-    cut = [0]
-    for w in own:
-        cut.append(cut[-1] + w.shape[1])
     return (
         section_outputs[None],
         section_input_grads[None],
-        spread[:, -2][None],
-        spread[:, cut[0] : cut[1]][None],
-        spread[:, cut[1] : cut[2]][None],
-        spread[:, cut[2] : cut[3]][None],
-        spread[:, cut[3] : cut[4]][None],
-        spread[:, -1][None],
-        spread[:, cut[4] : cut[4] + n_experts][None],
-        gate_up[0][None],
-        gate_up[1][None],
-        down[None],
+        tail[:, -2][None],
+        wide_grads[0][None],
+        wide_grads[1][None],
+        wide_grads[2][None],
+        wide_grads[3][None],
+        tail[:, -1][None],
+        tail[:, :n_experts][None],
+        gate_grad[None],
+        up_grad[None],
+        down_grad[None],
     )
 
 

time: 1250 us -> 1070 us (0.86)
  blocking collectives: 153 us -> 35.7 us
  other arithmetic: 79.6 us -> 42.3 us
  local copies, waits for them, and re-layouts: 124 us -> 93.7 us
  Pallas kernels: 709 us -> 733 us
  waiting for transfers between devices: 91.9 us -> 73.4 us
    all_gather x1, blocking collectives: 143 us -> 26 us  [shards(): all_routes = lax.all_gather(routes[0], ('section', 'expert'), axis=0)]
    pallas_call x2, Pallas kernels: 294 us -> 241 us  [experts_forward(): pl.pallas_call(functools.partial(experts_forward_kernel, ls, layer, chunk...]
    pallas_call x2, Pallas kernels: 195 us -> 237 us  [experts_backward(): pl.pallas_call(functools.partial(experts_backward_kernel, ls, layer, chun...]
    pallas_call x2, Pallas kernels: 143 us -> 179 us  [the longest x1 164 us: shared_grads(): pl.pallas_call(functools.partial(shared_grads_kernel, ls, chunks), out_sh...]
    convert_element_type x6 -> x1, other arithmetic: 30.4 us -> 0.97 us  [shards(): tail = tail.astype(F32)]
    dynamic_slice x8 -> x2, local copies, waits for them, and re-layouts: 19.8 us -> 1.19 us  [half_of(): return lax.dynamic_slice_in_dim(value, index * size, size, axis)]
    ppermute x19 -> x11, waiting for transfers between devices: 91.9 us -> 73.4 us  [swap(): return lax.ppermute(value, axis, [(0, 1), (1, 0)])]
    slice x7 -> x2, local copies, waits for them, and re-layouts: 21.3 us -> 4.77 us  [the longest x1 4.27 us: shards(): lhs = acts_mine[:, :3 * lhs_rows].reshape(-1, 3, lhs_rows).swapaxes(0, 1)]
  transfers between devices with their start and end apart: 19 -> 11, of which waited for: 5 -> 5; matrix products, arithmetic and copies ran while one was open for 13% -> 6% of each run, Pallas kernels for 18% -> 7%
where the time goes in v2:
time: 1070 us; the launch traced here: 1060 us
  Pallas kernels  733 us (69%)
  local copies, waits for them, and re-layouts  93.7 us (9%)
  waiting for transfers between devices  73.4 us (7%)
  matrix products  58.2 us (5%)
  other arithmetic  42.3 us (4%)
  blocking collectives  35.7 us (3%)
  starting transfers between devices  17.4 us (2%)
    pallas_call x2, Pallas kernels, experts_forward(): pl.pallas_call(functools.partial(experts_forward_kernel, ls, layer, chunk...  241 us
    pallas_call x2, Pallas kernels, experts_backward(): pl.pallas_call(functools.partial(experts_backward_kernel, ls, layer, chun...  237 us
    pallas_call x1, Pallas kernels, shared_grads(): pl.pallas_call(functools.partial(shared_grads_kernel, ls, chunks), out_sh...  164 us
    pallas_call x1, Pallas kernels, spread_weights(): pl.pallas_call(functools.partial(spread_kernel, src, count), out_shape=sp...  75.8 us
    ppermute x11, waiting for transfers between devices, swap(): return lax.ppermute(value, axis, [(0, 1), (1, 0)])  73.4 us
    dot_general x20, matrix products, dot(): return jnp.dot(a, b, preferred_element_type=F32)  48 us
    unnamed x280, local copies, waits for them, and re-layouts  40.6 us
    all_gather x1, blocking collectives, shards(): all_routes = lax.all_gather(routes[0], ('section', 'expert'), axis=0)  26 us
  transfers between devices with their start and end apart: 11, of which 5 were waited for; matrix products, arithmetic and copies ran while one was open for 6% of the time, Pallas kernels for 7%

profile of v2, /device:TPU:17, one launch (start us, length us, event | category | flops | bytes accessed | tf_op | source)
XLA Modules:
  0.0 1056.1 jit_solution(10649884503490282596)
XLA Ops:
  2.7 9.7 all_gather.6
  20.8 75.8 %spread_weights.1 = (bf16[1536,1536]{1,0:T(8,128)(2,1)S(1)}, bf16[1536,512]{1,0:T(8,128)(2,1)S(1)}, bf16[1536,512]{1,0:T(8,128)(2,1)S(1)}, bf16[1536,1536]{1,0:T(8,128)(2,1)S(1)}) custom-call(bf16[768,1536]{1,0:T(8,128)(2,1)S(1)} %bitcast.279, bf16[768,512]{1,0:T(8,128)(2,1)S(1)} %bitcast.283, bf16[768,512]{1,0:T(8,128)(2,1)S(1)} %bitcast.285, ...), custom_call_target="tpu_custom_call" | custom-call | bytes 209715200 | tf_op jit(solution)/shard_map/spread_weights/pallas_call | solution.py:403
  96.7 2.2 copy-done.3
  98.8 2.2 copy-done.4
  101.0 7.2 copy.315
  111.7 2.9 fusion.56
  116.4 26.0 %all_gather.7 = s32[16,2,128,8]{2,3,1,0:T(8,128)S(1)} all-gather(s32[1,2,128,8]{2,3,1,0:T(8,128)S(1)} %copy-done.120), channel_id=1, replica_groups=mesh['section'=2,'expert'=8,'dp'=2] {'section','expert'}, dimensions={0}, use_global_device_ids=true | all-gather | bytes 139264 | tf_op jit(solution)/shard_map/all_gather | solution.py:1332
  150.2 1.9 pad.23.refs_3_
  154.7 3.8 fusion.54
  161.9 3.4 multiply_reduce_fusion.5
  175.2 1.8 dynamic-slice_bitcast_fusion.refs_0_
  178.1 124.0 %experts_forward.2 = (bf16[128,1536]{1,0:T(8,128)(2,1)}, bf16[4,256,1536]{2,1,0:T(8,128)(2,1)}, bf16[4,256,1536]{2,1,0:T(8,128)(2,1)}, bf16[4,256,1536]{2,1,0:T(...) custom-call(bf16[128,1536]{1,0:T(8,128)(2,1)} %copy-done.43, ...), custom_call_target="tpu_custom_call" | custom-call | flops 14495514624 | bytes 62914560 | tf_op jit(solution)/shard_map/experts_forward/pallas_call | solution.py:573
  304.5 2.3 fusion.88
  306.9 4.4 fusion.89
  316.3 3.4 multiply_reduce_fusion.4
  320.7 116.6 %experts_forward.3 = (bf16[128,1536]{1,0:T(8,128)(2,1)}, bf16[4,256,1536]{2,1,0:T(8,128)(2,1)}, bf16[4,256,1536]{2,1,0:T(8,128)(2,1)}, bf16[4,256,1536]{2,1,0:T(8,128)(2,1)}, f32[4,256,128]{2,1,0:T(8,128)}) custom-call(bf16[128,1536]{1,0:T(8,128)(2,1)} %copy-done.41, f32[128,1536]{1,0:T(8,128)} %copy-done.20, f32[4,256,128]{2,1,0:T(8,128)} %bitcast.343, ...), custom_call_target="tpu_custom_call" | custom-call | flops 14495514624 | bytes 62914560 | tf_op jit(solution)/shard_map/experts_forward/pallas_call | solution.py:573
  437.3 121.4 %experts_backward.2 = (f32[128,1536]{1,0:T(8,128)}, f32[128,128]{1,0:T(8,128)}, bf16[3,2,384,1536]{3,2,1,0:T(8,128)(2,1)}, bf16[3,2,384,1536]{3,2,1,0:T(8,128)(2,1)}) custom-call(bf16[128,1536]{1,0:T(8,128)(2,1)} %dynamic-slice_bitcast_fusion.refs_0_, bf16[3,1536,512]{2,1,0:T(8,128)(2,1)} %bitcast.354, bf16[3,1536,512]{2,1,0:T(8,128)(2,1)} %bitcast.359, ...), custom_call_target="tpu_custom_call" | custom-call | flops 28991029248 | bytes 104857600 | tf_op jit(solution)/shard_map/experts_backward/pallas_call | solution.py:905
  561.1 2.4 multiply_reduce_fusion
  564.7 4.9 convolution_convert_fusion.1
  569.6 1.9 copy.327
  578.2 2.4 fusion.43
  581.6 115.8 %experts_backward.3 = (f32[128,1536]{1,0:T(8,128)}, f32[128,128]{1,0:T(8,128)}, bf16[3,2,384,1536]{3,2,1,0:T(8,128)(2,1)}, bf16[3,2,384,1536]{3,2,1,0:T(8,128)(2...) custom-call(bf16[128,1536]{1,0:T(8,128)(2,1)} %fusion.42.refs_0_, bf16[3,1536,512]{2,1,0:T(8,128)(2,1)} %bitcast.355, ...), custom_call_target="tpu_custom_call" | custom-call | flops 28991029248 | bytes 104857600 | tf_op jit(solution)/shard_map/experts_backward/pallas_call | solution.py:905
  699.9 2.4 multiply_reduce_fusion.1
  702.6 5.1 convolution_convert_fusion
  707.7 1.9 copy.332
  709.6 2.1 fusion.1
  716.0 2.5 fusion.92
  719.4 2.0 copy.346
  721.5 1.9 copy.349
  730.1 2.8 convolution_add_fusion.1
  733.9 2.8 fusion.33
  741.2 2.1 collective-permute-start.5
  749.4 20.9 %collective-permute-done.5 = bf16[128,6528]{1,0:T(8,128)(2,1)} collective-permute-done((bf16[128,6528]{1,0:T(8,128)(2,1)}, bf16[128,6528]{1,0:T(8,128)(2,1)}, u32[]{:S(2)}, u32[]{:S(2)}) %collective-permute-start.5) | collective-permute-done | bytes 1671200 | tf_op jit(solution)/shard_map/ppermute | solution.py:1279
  770.3 35.7 %collective-permute-done.6 = bf16[128,6528]{1,0:T(8,128)(2,1)S(1)} collective-permute-done((bf16[128,6528]{1,0:T(8,128)(2,1)S(1)}, bf16[128,6528]{1,0:T(8,128)(2,1)S(1)}, u32[]{:S(2)}, u32[]{:S(2)}) %collective-permute-start.6) | collective-permute-done | bytes 1671200 | tf_op jit(solution)/shard_map/ppermute | solution.py:1279
  806.1 5.0 broadcast_select_fusion.1
  811.0 10.8 %collective-permute-start.7 = (bf16[256,6528]{1,0:T(8,128)(2,1)}, bf16[256,6528]{1,0:T(8,128)(2,1)}, u32[]{:S(2)}, u32[]{:S(2)}) collective-permute-start(bf16[256,6528]{1,0:T(8,128)(2,1)} %get-tuple-element.173), channel_id=1, source_target_pairs={{0,16},{16,0},{1,17},{17,1},{2,18},{18,2},{3,19},{19,3},{4,20},{20... | collective-permute-start | bytes 10027016 | tf_op jit(solution)/shard_map/ppermute | solution.py:1279
  825.9 7.1 collective-permute-done.8
  833.0 8.4 collective-permute-done.9
  846.8 2.8 pad_maximum_fusion.3
  849.6 4.3 copy.356
  853.9 4.5 copy.357
  858.4 4.6 pad_maximum_fusion.refs_1_
  863.0 163.6 %shared_grads.1 = (bf16[4,1600,512]{2,1,0:T(8,128)(2,1)}, bf16[3,384,1536]{2,1,0:T(8,128)(2,1)}, bf16[2,3,384,1536]{3,2,1,0:T(8,128)(2,1)}) custom-call(bf16[3,512,768]{2,1,0:T(8,128)(2,1)} %bitcast.289, bf16[512,4224]{1,0:T(8,128)(2,1)} %pad_maximum_fusion.refs_1_, f32[768,128]{1,0:T(8,128)} %pad.27.refs_2_, ...), custom_call_target="tpu_custom_call" | custom-call | bytes 419430400 | tf_op jit(solution)/shard_map/shared_grads/pallas_call | solution.py:1001
  1030.2 3.0 copy-done.2
  1033.2 2.9 copy-done.5
  1036.1 2.0 copy-done.8
  1038.1 2.0 copy-done.9
  1040.1 15.5 %finish.1 = (f32[3,768,512]{2,1,0:T(8,128)}, f32[3,768,512]{2,1,0:T(8,128)}, f32[3,256,1536]{2,1,0:T(8,128)}, f32[768,1536]{1,0:T(8,128)}, f32[768,512]{1,0:T(8,...) custom-call(bf16[3,2,384,1536]{3,2,1,0:T(8,128)(2,1)S(1)} %copy-done.2, ...), custom_call_target="tpu_custom_call" | custom-call | bytes 52428800 | tf_op jit(solution)/shard_map/finish/pallas_call | solution.py:1116
  (410 shorter events, 98.3 us)
Async XLA Ops:
  0.6 113.9 %copy-start = (s32[2,128]{1,0:T(2,128)S(1)}, s32[2,128]{1,0:T(2,128)}, u32[]{:S(2)}) copy-start(s32[2,128]{1,0:T(2,128)} %param.16) | copy-start | bytes 3076
  0.7 177.4 %collective-permute-start = (bf16[3,1536,512]{2,1,0:T(8,128)(2,1)}, bf16[3,1536,512]{2,1,0:T(8,128)(2,1)}, u32[]{:S(2)}, u32[]{:S(2)}) collective-permute-start(bf16[3,1536,512]{2,1,0:T(8,128)(2,1)} %bitcast.351), channel_id=1, source_target_pairs={{0,16},{16,0},{1,17},{17,1},{2,18},{18,2},{3,19},{19,3},{4,20},{20... | collective-permute-start | bytes 14155784 | tf_op jit(solution)/shard_map/ppermute | solution.py:1279
  1.4 176.7 %collective-permute-start.1 = (bf16[3,1536,512]{2,1,0:T(8,128)(2,1)}, bf16[3,1536,512]{2,1,0:T(8,128)(2,1)}, u32[]{:S(2)}, u32[]{:S(2)}) collective-permute-start(bf16[3,1536,512]{2,1,0:T(8,128)(2,1)} %bitcast.356), channel_id=1, source_target_pairs={{0,16},{16,0},{1,17},{17,1},{2,18},{18,2},{3,19},{19,3},{4,20},{20... | collective-permute-start | bytes 14155784 | tf_op jit(solution)/shard_map/ppermute | solution.py:1279
  1.5 176.6 %collective-permute-start.2 = (bf16[3,512,1536]{2,1,0:T(8,128)(2,1)}, bf16[3,512,1536]{2,1,0:T(8,128)(2,1)}, u32[]{:S(2)}, u32[]{:S(2)}) collective-permute-start(bf16[3,512,1536]{2,1,0:T(8,128)(2,1)} %bitcast.361), channel_id=1, source_target_pairs={{0,16},{16,0},{1,17},{17,1},{2,18},{18,2},{3,19},{19,3},{4,20},{20... | collective-permute-start | bytes 14155784 | tf_op jit(solution)/shard_map/ppermute | solution.py:1279
  101.0 7.9 copy-start.6
  144.7 7.4 copy-start.64
  147.4 6.2 copy-start.56
  147.4 6.2 copy-start.86
  148.1 6.5 copy-start.29
  154.7 4.6 copy-start.118
  178.1 125.2 %copy-start.106 = (f32[1536]{0:T(1024)S(1)}, f32[1536]{0:T(1024)}, u32[]{:S(2)}) copy-start(f32[1536]{0:T(1024)} %get-tuple-element.167) | copy-start | bytes 18436
  302.1 4.7 copy-start.57
  302.1 4.7 copy-start.87
  304.5 9.2 copy-start.27
  306.8 4.5 copy-start.99
  306.9 5.2 copy-start.119
  320.3 117.1 %copy-start.69 = (f32[128,24]{1,0:T(8,128)}, f32[128,24]{1,0:T(8,128)S(1)}, u32[]{:S(2)}) copy-start(f32[128,24]{1,0:T(8,128)S(1)} %get-tuple-element.240) | copy-start | bytes 36868
  558.7 4.8 copy-start.21
  558.7 4.8 copy-start.45
  558.7 4.8 copy-start.78
  564.7 6.8 copy-start.18
  581.6 115.9 %copy-start.123 = (f32[128]{0:T(128)S(1)}, f32[128]{0:T(128)}, u32[]{:S(2)}) copy-start(f32[128]{0:T(128)} %fusion.59) | copy-start | bytes 1540
  581.6 118.2 %copy-start.104 = (f32[1536]{0:T(1024)S(1)}, f32[1536]{0:T(1024)}, u32[]{:S(2)}) copy-start(f32[1536]{0:T(1024)} %get-tuple-element.168) | copy-start | bytes 18436
  581.6 118.3 %copy-start.122 = (f32[128]{0:T(128)S(1)}, f32[128]{0:T(128)}, u32[]{:S(2)}) copy-start(f32[128]{0:T(128)} %copy-done.121) | copy-start | bytes 1540
  697.5 4.8 copy-start.26
  697.5 4.8 copy-start.36
  697.5 4.8 copy-start.46
  702.6 5.1 copy-start.31
  702.6 7.0 copy-start.80
  702.6 7.0 copy-start.93
  702.6 13.3 %slice-start = ((s8[4718592]{0:T(1024)(128)(4,1)}), s8[524288]{0:T(1024)(128)(4,1)S(1)}, s32[]{:S(2)}) async-start(s8[4718592]{0:T(1024)(128)(4,1)} %bitcast.274), calls=%async_computation | async-start | bytes 1048576
  719.4 10.6 %copy-start.7 = (bf16[1536,512]{1,0:T(8,128)(2,1)S(1)}, bf16[1536,512]{1,0:T(8,128)(2,1)}, u32[]{:S(2)}) copy-start(bf16[1536,512]{1,0:T(8,128)(2,1)} %copy-done.6) | copy-start | bytes 4718596
  741.2 29.1 %collective-permute-start.5 = (bf16[128,6528]{1,0:T(8,128)(2,1)}, bf16[128,6528]{1,0:T(8,128)(2,1)}, u32[]{:S(2)}, u32[]{:S(2)}) collective-permute-start(bf16[128,6528]{1,0:T(8,128)(2,1)} %get-tuple-element.221), channel_id=1, source_target_pairs={{0,1},{1,0},{2,3},{3,2},{4,5},{5,4},{6,7},{7,6},{8,9},{9,8},{10,11... | collective-permute-start | bytes 5013512 | tf_op jit(solution)/shard_map/ppermute | solution.py:1279
  745.8 60.3 %copy-start.47 = (bf16[128,6528]{1,0:T(8,128)(2,1)S(1)}, bf16[128,6528]{1,0:T(8,128)(2,1)}, u32[]{:S(2)}) copy-start(bf16[128,6528]{1,0:T(8,128)(2,1)} %get-tuple-element.220) | copy-start | bytes 5013508
  749.4 56.7 %collective-permute-start.6 = (bf16[128,6528]{1,0:T(8,128)(2,1)S(1)}, bf16[128,6528]{1,0:T(8,128)(2,1)S(1)}, u32[]{:S(2)}, u32[]{:S(2)}) collective-permute-start(bf16[128,6528]{1,0:T(8,128)(2,1)S(1)} %get-tuple-element.223), channel_id=1, source_target_pairs={{0,1},{1,0},{2,3},{3,2},{4,5},{5,4},{6,7},{7,6},{8,9},{9,8},{10,11... | collective-permute-start | bytes 5013512 | tf_op jit(solution)/shard_map/ppermute | solution.py:1279
  806.0 15.8 %copy-start.116 = (f32[1536]{0:T(1024)S(1)}, f32[1536]{0:T(1024)}, u32[]{:S(2)}) copy-start(f32[1536]{0:T(1024)} %get-tuple-element.160) | copy-start | bytes 18436
  806.0 15.8 %copy-start.115 = (f32[1536]{0:T(1024)S(1)}, f32[1536]{0:T(1024)}, u32[]{:S(2)}) copy-start(f32[1536]{0:T(1024)} %get-tuple-element.156) | copy-start | bytes 18436
  806.0 17.7 %copy-start.117 = (f32[1536]{0:T(1024)S(1)}, f32[1536]{0:T(1024)}, u32[]{:S(2)}) copy-start(f32[1536]{0:T(1024)} %get-tuple-element.162) | copy-start | bytes 18436
  806.0 17.7 %copy-start.114 = (f32[1536]{0:T(1024)S(1)}, f32[1536]{0:T(1024)}, u32[]{:S(2)}) copy-start(f32[1536]{0:T(1024)} %get-tuple-element.158) | copy-start | bytes 18436
  806.1 18.1 %copy-start.50 = (bf16[128,1536]{1,0:T(8,128)(2,1)S(1)}, bf16[128,1536]{1,0:T(8,128)(2,1)}, u32[]{:S(2)}) copy-start(bf16[128,1536]{1,0:T(8,128)(2,1)} %get-tuple-element.189) | copy-start | bytes 1179652
  811.0 35.7 %collective-permute-start.7 = (bf16[256,6528]{1,0:T(8,128)(2,1)}, bf16[256,6528]{1,0:T(8,128)(2,1)}, u32[]{:S(2)}, u32[]{:S(2)}) collective-permute-start(bf16[256,6528]{1,0:T(8,128)(2,1)} %get-tuple-element.173), channel_id=1, source_target_pairs={{0,16},{16,0},{1,17},{17,1},{2,18},{18,2},{3,19},{19,3},{4,20},{20... | collective-permute-start | bytes 10027016 | tf_op jit(solution)/shard_map/ppermute | solution.py:1279
  822.2 10.8 %collective-permute-start.8 = (f32[2,768]{0,1:T(8,128)S(1)}, f32[2,768]{0,1:T(8,128)S(1)}, u32[]{:S(2)}, u32[]{:S(2)}) collective-permute-start(f32[2,768]{0,1:T(8,128)S(1)} %copy.392), channel_id=1, source_target_pairs={{0,1},{1,0},{2,3},{3,2},{4,5},{5,4},{6,7},{7,6},{8,9},{9,8},{10,11... | collective-permute-start | bytes 18440 | tf_op jit(solution)/shard_map/ppermute | solution.py:1279
  824.0 17.4 %collective-permute-start.9 = (f32[2,768]{0,1:T(8,128)S(1)}, f32[2,768]{0,1:T(8,128)S(1)}, u32[]{:S(2)}, u32[]{:S(2)}) collective-permute-start(f32[2,768]{0,1:T(8,128)S(1)} %copy.394), channel_id=1, source_target_pairs={{0,1},{1,0},{2,3},{3,2},{4,5},{5,4},{6,7},{7,6},{8,9},{9,8},{10,11... | collective-permute-start | bytes 18440 | tf_op jit(solution)/shard_map/ppermute | solution.py:1279
  824.9 17.4 %copy-start.88 = (bf16[128,1536]{1,0:T(8,128)(2,1)S(1)}, bf16[128,1536]{1,0:T(8,128)(2,1)}, u32[]{:S(2)}) copy-start(bf16[128,1536]{1,0:T(8,128)(2,1)} %get-tuple-element.57) | copy-start | bytes 1179652
  825.3 19.5 %collective-permute-start.4 = (bf16[128,1536]{1,0:T(8,128)(2,1)}, bf16[128,1536]{1,0:T(8,128)(2,1)S(1)}, u32[]{:S(2)}, u32[]{:S(2)}) collective-permute-start(bf16[128,1536]{1,0:T(8,128)(2,1)} %broadcast_select_fusion.2), channel_id=1, source_target_pairs={{0,16},{16,0},{1,17},{17,1},{2,18},{18,2},{3,19},{19,3},{4,20},{20... | collective-permute-start | bytes 1179656 | tf_op jit(solution)/shard_map/ppermute | solution.py:1279
  841.5 2.2 collective-permute-start.10
  842.4 3.3 collective-permute-start.3
  1040.1 15.5 %copy-start.1 = (s32[2,128]{1,0:T(2,128)S(1)}, s32[2,128]{1,0:T(2,128)}, u32[]{:S(2)}) copy-start(s32[2,128]{1,0:T(2,128)} %param.16) | copy-start | bytes 3076
  (93 other events, 200.3 us)

commit v3 on v2

--- a/solution.py
+++ b/solution.py
@@ -2,6 +2,7 @@
 
 import jax
 import jax.numpy as jnp
+import numpy as np
 from jax import lax
 from jax.experimental import pallas as pl
 from jax.experimental.pallas import tpu as pltpu
@@ -390,28 +391,50 @@
     return [jax.ShapeDtypeStruct((2 * w.shape[0], w.shape[1]), w.dtype) for w in shards]
 
 
-def spread_kernel(src, count, *refs):
-    shards, wholes, scratch = refs[:count], refs[count : 2 * count], refs[2 * count :]
-    spread = Spread(src, shards, wholes, scratch)
-    greet_all(spread.signals(), spread.waits())
+def start_kernel(ls, count, *refs):
+    picks_ref, shards = refs[0], refs[1 : 1 + count]
+    masks, wholes = refs[1 + count], refs[2 + count : 2 + 2 * count]
+    at = 2 + 2 * count
+    ag_sems, own_sem = refs[at : at + 6], refs[at + 6]
+    l, p = place(lax.axis_index("expert"), ls)
+    half = picks_ref.shape[0]
+    own = pltpu.make_async_copy(
+        picks_ref, masks.at[l, pl.ds(pl.multiple_of(p * half, half), half)], own_sem
+    )
+    own.start()
+    own.wait()
+    spread = Spread(0, shards, wholes, refs[at + 7 :])
+    greet(l, p, ls, spread.signals(), spread.waits())
     spread.begin()
+    gather = Gather(l, p, ls, masks, ag_sems, 1)
+    gather.begin()
+
+    def step(k, carry):
+        gather.arrive(k)
+        return carry
+
+    lax.fori_loop(1, LINE, step, 0)
+    for L in range(LINE):
+        gather.from_pair(L)
+    gather.end()
     spread.end()
 
 
-def spread_weights(src, shards, cid):
+def start(ls, cid, picks, shards):
     count = len(shards)
+    rows, width = picks.shape
     return pl.pallas_call(
-        functools.partial(spread_kernel, src, count),
-        out_shape=spread_shapes(shards),
-        in_specs=[HB] * count,
-        out_specs=[HB] * count,
-        scratch_shapes=spread_scratch(shards),
+        functools.partial(start_kernel, ls, count),
+        out_shape=[jax.ShapeDtypeStruct((LINE, 2 * rows, width), BF16)] + spread_shapes(shards),
+        in_specs=[VM] + [HB] * count,
+        out_specs=[VM] + [HB] * count,
+        scratch_shapes=link_sems(1) + [DMA(())] + spread_scratch(shards),
         compiler_params=pltpu.CompilerParams(
             collective_id=cid, has_side_effects=True, vmem_limit_bytes=32 * MIB
         ),
         cost_estimate=pl.CostEstimate(flops=0, bytes_accessed=200 * MIB, transcendentals=0),
-        name="spread_weights",
-    )(*shards)
+        name="start",
+    )(picks, *shards)
 
 
 def fetch(mine, theirs, own_layer, dst, sems, wait=False):
@@ -426,6 +449,18 @@
         @pl.when(jnp.logical_not(own_layer))
         def _():
             b.wait() if wait else b.start()
+
+
+def routed_softmax(logits, mask):
+    z = jnp.where(mask > 0, logits, NEG)
+    top = jnp.max(z, axis=-1, keepdims=True)
+    ex = jnp.exp(z - top) * mask
+    return ex / jnp.sum(ex, axis=-1, keepdims=True)
+
+
+def lane_of(value, lane):
+    lanes = lax.broadcasted_iota(jnp.int32, value.shape, 1)
+    return jnp.sum(jnp.where(lanes == lane, value, 0.0), axis=-1, keepdims=True)
 
 
 def dot(a, b):
@@ -493,12 +528,8 @@
         L = near_first(l, k)
         gather.from_pair(L)
         x = xb[L]
-        logits = dot(x, wr_ref[...])
-        mask = mask_ref[L]
-        z = jnp.where(mask > 0, logits, NEG)
-        top = jnp.max(z, axis=-1, keepdims=True)
-        ex = jnp.exp(z - top) * mask
-        gates = ex / jnp.sum(ex, axis=-1, keepdims=True)
+        mask = mask_ref[L, :, layer * LANES : (layer + 1) * LANES].astype(F32)
+        gates = routed_softmax(dot(x, wr_ref[...]), mask)
         gates_ref[L] = gates
         for j in range(EXP_DEV):
             width = wg.shape[2]
@@ -508,17 +539,18 @@
             gpb[L, :, cols] = gp.astype(BF16)
             upre[L, :, cols] = up.astype(BF16)
             a = gp * jax.nn.sigmoid(gp) * up
-            act[:, cols] = (gates[:, j : j + 1] * a).astype(BF16)
+            act[:, cols] = (lane_of(gates, EXP_DEV * e + j) * a).astype(BF16)
         for copy in save(L):
             copy.start()
         tile = 512
         for n in range(wd.shape[1] // tile):
             cols = slice(n * tile, (n + 1) * tile)
             part[L, :, cols] = dot(act[...], wd[:, cols]).astype(BF16)
-        total.give(L)
         return carry
 
     lax.fori_loop(0, LINE, step, 0)
+    for k in range(LINE):
+        total.give(near_first(l, LINE - 1 - k))
 
     def write(c, value):
         rows = pl.ds(c * (half // chunks), half // chunks)
@@ -744,7 +776,7 @@
             sig = jax.nn.sigmoid(gp)
             silu = gp * sig
             a = silu * up
-            gate = gates[:, j : j + 1]
+            gate = lane_of(gates, EXP_DEV * e + j)
             dgate = jnp.sum(a * da, axis=-1, keepdims=True)
             high = dgate.astype(BF16).astype(F32)
             dgates = dgates + jnp.where(lane == EXP_DEV * e + j, high, 0.0)
@@ -763,10 +795,11 @@
                 acc = acc + dot_nt(gpb[L, :, sub], wg[j, cols, :])
                 acc = acc + dot_nt(upre[L, :, sub], wu[j, cols, :])
             part[L, :, cols] = acc.astype(BF16)
-        total.give(L)
         return carry
 
     lax.fori_loop(0, LINE, step, 0)
+    for k in range(LINE):
+        total.give(near_first(l, LINE - 1 - k))
 
     def write(c, value):
         rows = pl.ds(c * (half // chunks), half // chunks)
@@ -919,19 +952,27 @@
 
 
 def shared_grads_kernel(ls, chunks, *refs):
-    lhs_ref, rhs_ref, gain_ref, sums_ref = refs[:4]
-    out, near, far = refs[4:7]
-    part, pairb, upb, dnb, small = refs[7:12]
-    ag_sems, rs_sems, deliver_sem = refs[12:18], refs[18:24], refs[24:]
+    inputs, sums_ref = refs[:6], refs[6]
+    out, near, far = refs[7:10]
+    part, pairb, upb, dnb, small, lhs_ref, rhs_ref, gain_ref, in_sem = refs[10:19]
+    ag_sems, rs_sems, deliver_sem = refs[19:25], refs[25:31], refs[31:]
+    s = lax.axis_index("section")
+    fetch(inputs[0:3], inputs[3:6], s == 0, (lhs_ref, rhs_ref, gain_ref), in_sem)
     l, p = place(lax.axis_index("expert"), ls)
     tokens, rows = lhs_ref.shape[1:]
     half, width = pairb.shape[1:]
     deliver = Deliver(0, sums_ref, near, far, deliver_sem)
     greet(l, p, ls, deliver.signals(False), deliver.waits(False))
+    fetch(inputs[0:3], inputs[3:6], s == 0, (lhs_ref, rhs_ref, gain_ref), in_sem, wait=True)
     gather = Gather(l, p, ls, out, ag_sems, chunks)
     total = Sum(l, p, ls, part, pairb, upb, dnb, rs_sems, chunks)
     n_first = 5
-    small[...] = dot_tn(lhs_ref[2], rhs_ref[:, 8 * width :]) + gain_ref[...]
+    row = lax.broadcasted_iota(jnp.int32, (gain_ref.shape[0], LANES), 0) % 16
+    lane = lax.broadcasted_iota(jnp.int32, (gain_ref.shape[0], LANES), 1)
+    chosen = ((row < 2) & (lane == LANES - 2)) | ((row >= 2) & (row < 4) & (lane == LANES - 1))
+    small[...] = dot_tn(lhs_ref[2], rhs_ref[:, 8 * width :]) + dot_tn(
+        gain_ref[...], jnp.where(chosen, 1.0, 0.0).astype(BF16)
+    )
     n_rows = rows // 8
     quarter = n_rows // 4
 
@@ -993,15 +1034,16 @@
     deliver.end()
 
 
-def shared_grads(ls, cid, lhs, rhs, gain_cols, sums, chunks=2):
-    _, tokens, rows = lhs.shape
+def shared_grads(ls, cid, acts, sums, chunks=2):
+    lhs, rhs, gains = acts[0]
+    rows = lhs.shape[2]
     width = 512
     half = rows + 32
     buf = pltpu.VMEM((LINE, half, width), BF16)
     return pl.pallas_call(
         functools.partial(shared_grads_kernel, ls, chunks),
         out_shape=[jax.ShapeDtypeStruct((LINE, 2 * half, width), BF16)] + deliver_shapes(sums),
-        in_specs=[VM, VM, VM, HB],
+        in_specs=[HB] * 7,
         out_specs=[VM, HB, HB],
         scratch_shapes=[
             pltpu.VMEM((LINE, 2 * half, width), BF16),
@@ -1009,6 +1051,10 @@
             buf,
             buf,
             pltpu.VMEM((rows, LANES), F32),
+            pltpu.VMEM(lhs.shape, BF16),
+            pltpu.VMEM(rhs.shape, BF16),
+            pltpu.VMEM(gains.shape, BF16),
+            DMA((3,)),
         ]
         + link_sems(chunks)
         + link_sems(chunks)
@@ -1018,7 +1064,7 @@
         ),
         cost_estimate=pl.CostEstimate(flops=0, bytes_accessed=400 * MIB, transcendentals=0),
         name="shared_grads",
-    )(lhs, rhs, gain_cols, sums)
+    )(*acts[0], *acts[1], sums)
 
 
 def finish_kernel(*refs):
@@ -1140,157 +1186,339 @@
     )(*sums, *near, *far, blocks)
 
 
-def rope_tables(length, head_dim):
-    places = jnp.arange(length, dtype=F32)
-    rates = THETA ** (-2.0 * jnp.arange(head_dim // 2, dtype=F32) / head_dim)
-    angle = places[:, None] * rates[None, :]
-    return (jnp.cos(angle)[:, None, :], jnp.sin(angle)[:, None, :])
-
-
-def apply_rotary(value_rows, cosine_table, sine_table):
-    half_size = value_rows.shape[-1] // 2
-    first = value_rows[..., :half_size]
-    second = value_rows[..., half_size:]
-    return jnp.concatenate(
-        [first * cosine_table - second * sine_table, second * cosine_table + first * sine_table],
-        axis=-1,
+def rope_tables(length):
+    half = HEAD_SIZE // 2
+    rates = THETA ** (-2.0 * np.arange(half, dtype=np.float32) / HEAD_SIZE)
+    angle = np.arange(length, dtype=np.float32)[:, None] * rates[None, :].astype(np.float32)
+    cosine, sine = np.cos(angle), np.sin(angle)
+    return np.stack(
+        [np.concatenate([cosine] * 4, axis=1), np.concatenate([-sine, sine] * 2, axis=1)]
+    ).astype(np.float32)
+
+
+def rotated(value, cosine, sine):
+    lane = lax.broadcasted_iota(jnp.int32, value.shape, 1)
+    half = HEAD_SIZE // 2
+    ahead = pltpu.roll(value, LANES - half, 1)
+    behind = pltpu.roll(value, half, 1)
+    partner = jnp.where(lane % HEAD_SIZE < half, ahead, behind)
+    return value * cosine + partner * sine
+
+
+def norm_scale(value):
+    return lax.rsqrt(jnp.mean(value * value, axis=-1, keepdims=True) + EPS)
+
+
+def gain_row(ref, i):
+    n = ref.shape[0] // 16
+    return jnp.concatenate([ref[16 * k + i : 16 * k + i + 1, :] for k in range(n)], axis=1).astype(
+        F32
     )
 
 
-def norm_scale(value_rows):
-    return lax.rsqrt(jnp.mean(value_rows * value_rows, axis=-1, keepdims=True) + EPS)
-
-
-def norm_back(grad_rows, value_rows, inverse, gain):
-    scaled = value_rows * inverse
-    weighted = grad_rows * gain
-    gain_grad = jnp.sum(grad_rows * scaled, axis=0)
-    value_grad = inverse * (weighted - scaled * jnp.mean(weighted * scaled, axis=-1, keepdims=True))
-    return (value_grad, gain_grad)
-
-
-def mask_for(seg_row):
-    places = jnp.arange(seg_row.shape[0])
-    return (seg_row[:, None] == seg_row[None, :]) & (places[:, None] >= places[None, :])
-
-
-def attend_scores(query_rows, key_rows, allowed):
+GROUP = QUERY_HEADS // KEY_VALUE_HEADS
+
+
+def head(ref, h):
+    return ref[:, h * HEAD_SIZE : (h + 1) * HEAD_SIZE]
+
+
+def group_rows(ref, j):
+    return jnp.concatenate([head(ref, GROUP * j + i) for i in range(GROUP)], axis=0)
+
+
+def group_probs(q_rows, keys, allowed):
+    scores = HEAD_SIZE ** (-0.5) * dot_nt(q_rows, keys)
+    scores = jnp.where(allowed, scores, NEG)
+    ex = jnp.exp(scores - jnp.max(scores, axis=-1, keepdims=True))
+    return ex / jnp.sum(ex, axis=-1, keepdims=True)
+
+
+def weight_copies(sources, targets, sems):
+    return [
+        pltpu.make_async_copy(a, b, sems.at[i]) for i, (a, b) in enumerate(zip(sources, targets))
+    ]
+
+
+def attention_forward_kernel(*refs):
+    h_ref, allowed_ref, rope_ref, gains_ref = refs[:4]
+    sources = refs[4:8]
+    n1_ref, q_ref, k_ref, v_ref, c_ref, h1_ref, n2_ref = refs[8:15]
+    wq, wk, wv, wo = refs[15:19]
+    copies = weight_copies(sources, (wq, wk, wv, wo), refs[19])
+    for copy in copies:
+        copy.start()
+    tokens = h_ref.shape[0]
+    h = h_ref[...].astype(F32)
+    n1_ref[...] = (h * norm_scale(h) * gain_row(gains_ref, 0)).astype(BF16)
+    cosine, sine = rope_ref[0], rope_ref[1]
+    for copy, w, out in ((copies[0], wq, q_ref), (copies[1], wk, k_ref)):
+        copy.wait()
+        for g in range(w.shape[1] // 256):
+            cols = slice(g * 256, (g + 1) * 256)
+            x = dot(n1_ref[...], w[:, cols])
+            out[:, cols] = jnp.concatenate(
+                [rotated(x[:, :LANES], cosine, sine), rotated(x[:, LANES:], cosine, sine)], axis=1
+            ).astype(BF16)
+    copies[2].wait()
+    v_ref[...] = dot(n1_ref[...], wv[...]).astype(BF16)
+    allowed = jnp.concatenate([allowed_ref[...]] * GROUP, axis=0) > 0
+    heads = []
+    for j in range(KEY_VALUE_HEADS):
+        probs = group_probs(group_rows(q_ref, j), head(k_ref, j), allowed)
+        context = dot(probs.astype(BF16), head(v_ref, j))
+        heads += [context[i * tokens : (i + 1) * tokens] for i in range(GROUP)]
+    for i in range(QUERY_HEADS // 2):
+        c_ref[:, i * LANES : (i + 1) * LANES] = jnp.concatenate(
+            heads[2 * i : 2 * i + 2], axis=1
+        ).astype(BF16)
+    copies[3].wait()
+    h1 = h + dot(c_ref[...], wo[...])
+    h1_ref[...] = h1
+    n2_ref[...] = (h1 * norm_scale(h1) * gain_row(gains_ref, 1)).astype(BF16)
+
+
+def attention_forward(h, allowed, rope, weights, gains):
+    tokens, width = h.shape
+    kv = weights[1].shape[1]
+    shape = jax.ShapeDtypeStruct
+    return pl.pallas_call(
+        attention_forward_kernel,
+        out_shape=[
+            shape((tokens, width), BF16),
+            shape((tokens, weights[0].shape[1]), BF16),
+            shape((tokens, kv), BF16),
+            shape((tokens, kv), BF16),
+            shape((tokens, weights[0].shape[1]), BF16),
+            shape((tokens, width), F32),
+            shape((tokens, width), BF16),
+        ],
+        in_specs=[VM] * 4 + [HB] * 4,
+        out_specs=[VM] * 7,
+        scratch_shapes=[pltpu.VMEM(w.shape, BF16) for w in weights] + [DMA((4,))],
+        compiler_params=pltpu.CompilerParams(vmem_limit_bytes=40 * MIB),
+        cost_estimate=pl.CostEstimate(
+            flops=2 * tokens * width * 4096, bytes_accessed=16 * MIB, transcendentals=0
+        ),
+        name="attention_forward",
+    )(h, allowed, rope, gains, *weights)
+
+
+class ActDeliver:
+    def __init__(self, layer, sources, targets, sems):
+        self.layer, self.sources, self.targets = layer, sources, targets
+        self.ns, self.nr, self.fs, self.fr = sems
+        self.s, self.x = lax.axis_index("section"), lax.axis_index("dp")
+        self.tokens = sources[0].shape[0]
+        self.part = targets[0].shape[2]
+
+    def signals(self):
+        owner = self.s == self.layer
+        return (
+            (owner, {"dp": 1 - self.x}),
+            (owner, {"dp": 1 - self.x, "section": 1 - self.layer}),
+            (owner, {"section": 1 - self.layer}),
+        )
+
+    def waits(self):
+        return (self.s >= 0, self.s != self.layer)
+
+    def src(self, i, x):
+        if i in (3, 4):
+            return self.sources[i]
+        return self.sources[i].at[:, pl.ds(pl.multiple_of(x * self.part, self.part), self.part)]
+
+    def dst(self, i, which):
+        lhs, rhs, gains = self.targets
+        rows = pl.ds(pl.multiple_of(which * self.tokens, self.tokens), self.tokens)
+        if i < 3:
+            return lhs.at[i, rows]
+        first = self.sources[4].shape[1]
+        if i == 3:
+            return rhs.at[rows, pl.ds(first, self.sources[3].shape[1])]
+        if i == 4:
+            return rhs.at[rows, pl.ds(0, first)]
+        return gains.at[pl.ds(pl.multiple_of(which * 16, 16), 16)]
+
+    def near(self, i, s):
+        return remote(
+            self.src(i, self.x),
+            self.dst(i, 2 * s + self.x),
+            self.ns.at[i],
+            self.nr.at[i],
+            section=self.layer,
+        )
+
+    def here(self, i):
+        return pltpu.make_async_copy(
+            self.src(i, self.x), self.dst(i, 2 * self.s + self.x), self.ns.at[i]
+        )
+
+    def far(self, i, s, x):
+        return remote(
+            self.src(i, 1 - x),
+            self.dst(i, 2 * s + x),
+            self.fs.at[i],
+            self.fr.at[s, i],
+            dp=1 - self.x,
+            section=self.layer,
+        )
+
+    def begin(self, pieces):
+        for i in pieces:
+            self.far(i, self.s, self.x).start()
+
+            @pl.when(self.s != self.layer)
+            def _():
+                self.near(i, self.s).start()
+
+            @pl.when(self.s == self.layer)
+            def _():
+                self.here(i).start()
+
+    def end(self, pieces):
+        for i in pieces:
+            self.far(i, self.s, self.x).wait_send()
+
+            @pl.when(self.s != self.layer)
+            def _():
+                self.near(i, self.s).wait_send()
+
+            @pl.when(self.s == self.layer)
+            def _():
+                self.here(i).wait()
+                self.near(i, 1 - self.s).wait_recv()
+                for s in range(2):
+                    self.far(i, s, 1 - self.x).wait_recv()
+
+
+def attention_backward_kernel(layer, deliver, n_experts, *refs):
+    (g_ref, dn2_ref, dgate_ref, mask_ref, allowed_ref, rope_ref, gains_ref, wr_ref) = refs[:8]
+    h_ref, n1_ref, q_ref, k_ref, v_ref, c_ref, h1_ref, n2_ref = refs[8:16]
+    sources = refs[16:20]
+    din_ref, dqkv_ref, datdr_ref, gain_out = refs[20:24]
+    at = 24
+    targets = refs[at : at + 3] if deliver else ()
+    at += len(targets)
+    wq, wk, wv, wo, dq, dc_ref = refs[at : at + 6]
+    copies = weight_copies((sources[3],) + tuple(sources[:3]), (wo, wq, wk, wv), refs[at + 6])
+    for copy in copies:
+        copy.start()
+    if deliver:
+        acts = ActDeliver(
+            layer, (n1_ref, c_ref, n2_ref, datdr_ref, dqkv_ref, gain_out), targets, refs[at + 7 :]
+        )
+        greet_all(acts.signals(), acts.waits())
+        acts.begin((0, 1, 2))
+    tokens, width = h_ref.shape
+    lane = lax.broadcasted_iota(jnp.int32, (tokens, LANES), 1)
+    gates = routed_softmax(
+        dot(n2_ref[...], wr_ref[...]), mask_ref[:, layer * LANES : (layer + 1) * LANES].astype(F32)
+    )
+    raw = dgate_ref[...]
+    dgates = jnp.where(lane < n_experts, raw + pltpu.roll(raw, LANES - 32, 1), 0.0)
+    dsel = gates * (dgates - jnp.sum(gates * dgates, axis=-1, keepdims=True))
+    dr = dsel.astype(BF16)
+    datdr_ref[:, width:] = dr
+    dn2 = dn2_ref[...] + dot_nt(dr, wr_ref[...])
+    h1 = h1_ref[...]
+    inv2 = norm_scale(h1)
+    z2 = h1 * inv2
+    w2 = dn2 * gain_row(gains_ref, 1)
+    gm = jnp.sum(dn2 * z2, axis=0, keepdims=True)
+    dh1 = g_ref[...].astype(F32) + inv2 * (w2 - z2 * jnp.mean(w2 * z2, axis=-1, keepdims=True))
+    datdr_ref[:, :width] = dh1.astype(BF16)
+    if deliver:
+        acts.begin((3,))
+    copies[0].wait()
+    dc_ref[...] = dot_nt(datdr_ref[:, :width], wo[...]).astype(BF16)
+    allowed = jnp.concatenate([allowed_ref[...]] * GROUP, axis=0) > 0
     scale = HEAD_SIZE ** (-0.5)
-    scores = scale * jnp.einsum("qkgd,pkd->kgqp", query_rows, key_rows, preferred_element_type=F32)
-    return jnp.where(allowed[None, None], scores, NEG)
-
-
-def attention_forward(hidden, allowed, gain_attn, gain_moe, weights):
-    w_query, key_matrix, value_matrix, w_out = weights
-    token_count = hidden.shape[0]
-    query_group = QUERY_HEADS // KEY_VALUE_HEADS
-    cosine_table, sine_table = rope_tables(token_count, HEAD_SIZE)
-    inv_one = norm_scale(hidden)
-    normed = (hidden * inv_one * gain_attn).astype(BF16)
-    query = dot(normed, w_query).reshape(token_count, QUERY_HEADS, HEAD_SIZE)
-    query = (
-        apply_rotary(query, cosine_table, sine_table)
-        .astype(BF16)
-        .reshape(token_count, KEY_VALUE_HEADS, query_group, HEAD_SIZE)
-    )
-    keys = dot(normed, key_matrix).reshape(token_count, KEY_VALUE_HEADS, HEAD_SIZE)
-    keys = apply_rotary(keys, cosine_table, sine_table).astype(BF16)
-    values = (
-        dot(normed, value_matrix).astype(BF16).reshape(token_count, KEY_VALUE_HEADS, HEAD_SIZE)
-    )
-    scores = attend_scores(query, keys, allowed)
-    highest = jnp.max(scores, axis=-1, keepdims=True)
-    exponent = jnp.exp(scores - highest)
-    row_total = jnp.sum(exponent, axis=-1, keepdims=True)
-    probs = exponent / row_total
-    log_total = highest + jnp.log(row_total)
-    context = jnp.einsum(
-        "kgqp,pkd->qkgd", probs.astype(BF16), values, preferred_element_type=F32
-    )
-    context = context.reshape(token_count, QUERY_HEADS * HEAD_SIZE).astype(BF16)
-    middle = hidden + dot(context, w_out)
-    inv_two = norm_scale(middle)
-    normed_two = (middle * inv_two * gain_moe).astype(BF16)
-    kept = dict(
-        hidden=hidden,
-        inv_one=inv_one,
-        normed=normed,
-        query=query,
-        keys=keys,
-        values=values,
-        log_total=log_total,
-        context=context,
-        middle=middle,
-        inv_two=inv_two,
-        normed_two=normed_two,
-    )
-    return middle, normed_two, kept
-
-
-def attention_backward(d_out, d_normed_two, d_gates, gates, kept, allowed, gains, weights, w_router):
-    gain_attn, gain_moe = gains
-    w_query, key_matrix, value_matrix, w_out = weights
-    token_count = d_out.shape[0]
-    query_group = QUERY_HEADS // KEY_VALUE_HEADS
-    d_logits = (gates * (d_gates - jnp.sum(gates * d_gates, axis=-1, keepdims=True))).astype(BF16)
-    d_normed_two = d_normed_two + dot(d_logits, w_router.T)
-    d_middle, grad_gain_moe = norm_back(d_normed_two, kept["middle"], kept["inv_two"], gain_moe)
-    d_middle = d_middle + d_out
-    d_attn = d_middle.astype(BF16)
-    d_context = (
-        dot(d_attn, w_out.T)
-        .astype(BF16)
-        .reshape(token_count, KEY_VALUE_HEADS, query_group, HEAD_SIZE)
-    )
-    query, keys, values = kept["query"], kept["keys"], kept["values"]
-    scores = attend_scores(query, keys, allowed)
-    probs = jnp.exp(scores - kept["log_total"])
-    d_probs = jnp.einsum("qkgd,pkd->kgqp", d_context, values, preferred_element_type=F32)
-    row_inner = jnp.sum(probs * d_probs, axis=-1, keepdims=True)
-    d_scores = (probs * (d_probs - row_inner)).astype(BF16)
-    scale = HEAD_SIZE ** (-0.5)
-    cosine_table, sine_table = rope_tables(token_count, HEAD_SIZE)
-    d_query = scale * jnp.einsum("kgqp,pkd->qkgd", d_scores, keys, preferred_element_type=F32)
-    d_query = (
-        apply_rotary(
-            d_query.reshape(token_count, QUERY_HEADS, HEAD_SIZE), cosine_table, -sine_table
-        )
-        .astype(BF16)
-        .reshape(token_count, QUERY_HEADS * HEAD_SIZE)
-    )
-    d_keys = scale * jnp.einsum("kgqp,qkgd->pkd", d_scores, query, preferred_element_type=F32)
-    d_keys = (
-        apply_rotary(d_keys, cosine_table, -sine_table)
-        .astype(BF16)
-        .reshape(token_count, KEY_VALUE_HEADS * HEAD_SIZE)
-    )
-    d_values = jnp.einsum(
-        "kgqp,qkgd->pkd", probs.astype(BF16), d_context, preferred_element_type=F32
-    )
-    d_values = d_values.astype(BF16).reshape(token_count, KEY_VALUE_HEADS * HEAD_SIZE)
-    d_normed = dot(d_query, w_query.T) + dot(d_keys, key_matrix.T) + dot(d_values, value_matrix.T)
-    d_hidden, grad_gain_attn = norm_back(d_normed, kept["hidden"], kept["inv_one"], gain_attn)
-    d_in = (d_hidden + d_middle).astype(BF16)
-    acts = dict(dq=d_query, dk=d_keys, dv=d_values, dat=d_attn, dr=d_logits)
-    return d_in, acts, (grad_gain_attn, grad_gain_moe)
+    dqs, dks, dvs = [], [], []
+    for j in range(KEY_VALUE_HEADS):
+        q_rows, dc_rows = group_rows(q_ref, j), group_rows(dc_ref, j)
+        keys, values = head(k_ref, j), head(v_ref, j)
+        probs = group_probs(q_rows, keys, allowed)
+        dprobs = dot_nt(dc_rows, values)
+        inner = jnp.sum(probs * dprobs, axis=-1, keepdims=True)
+        ds = (probs * (dprobs - inner)).astype(BF16)
+        dq_rows = scale * dot(ds, keys)
+        dqs += [dq_rows[i * tokens : (i + 1) * tokens] for i in range(GROUP)]
+        dks.append(scale * dot_tn(ds, q_rows))
+        dvs.append(dot_tn(probs.astype(BF16), dc_rows))
+    cosine, sine = rope_ref[0], -rope_ref[1]
+    n_q, n_kv = q_ref.shape[1], k_ref.shape[1]
+    for i in range(QUERY_HEADS // 2):
+        pair = jnp.concatenate(dqs[2 * i : 2 * i + 2], axis=1)
+        dqkv_ref[:, i * LANES : (i + 1) * LANES] = rotated(pair, cosine, sine).astype(BF16)
+    for i in range(KEY_VALUE_HEADS // 2):
+        pair = jnp.concatenate(dks[2 * i : 2 * i + 2], axis=1)
+        cols = slice(n_q + i * LANES, n_q + (i + 1) * LANES)
+        dqkv_ref[:, cols] = rotated(pair, cosine, sine).astype(BF16)
+        cols = slice(n_q + n_kv + i * LANES, n_q + n_kv + (i + 1) * LANES)
+        dqkv_ref[:, cols] = jnp.concatenate(dvs[2 * i : 2 * i + 2], axis=1).astype(BF16)
+    if deliver:
+        acts.begin((4,))
+    for copy in copies[1:]:
+        copy.wait()
+    dn1 = dot_nt(dqkv_ref[:, :n_q], wq[...])
+    dn1 = dn1 + dot_nt(dqkv_ref[:, n_q : n_q + n_kv], wk[...])
+    dn1 = dn1 + dot_nt(dqkv_ref[:, n_q + n_kv :], wv[...])
+    h = h_ref[...].astype(F32)
+    inv1 = norm_scale(h)
+    z1 = h * inv1
+    w1 = dn1 * gain_row(gains_ref, 0)
+    ga = jnp.sum(dn1 * z1, axis=0, keepdims=True)
+    din = dh1 + inv1 * (w1 - z1 * jnp.mean(w1 * z1, axis=-1, keepdims=True))
+    din_ref[...] = din.astype(BF16)
+    ga_high, gm_high = ga.astype(BF16).astype(F32), gm.astype(BF16).astype(F32)
+    gain_out[...] = jnp.concatenate(
+        [ga_high, ga - ga_high, gm_high, gm - gm_high, jnp.zeros((12, width), F32)], axis=0
+    ).astype(BF16)
+    if deliver:
+        acts.begin((5,))
+        acts.end(range(6))
+
+
+def attention_backward(
+    layer, cid, n_experts, g, dn2, dgates, mask, allowed, rope, gains, router, kept, weights, part
+):
+    tokens, width = g.shape
+    n_q, n_kv = weights[0].shape[1], weights[1].shape[1]
+    shape = jax.ShapeDtypeStruct
+    outs = [
+        shape((tokens, width), BF16),
+        shape((tokens, n_q + 2 * n_kv), BF16),
+        shape((tokens, width + LANES), BF16),
+        shape((16, width), BF16),
+    ]
+    scratch = [pltpu.VMEM(w.shape, BF16) for w in weights]
+    scratch += [pltpu.VMEM((tokens, n_q), F32), pltpu.VMEM((tokens, n_q), BF16), DMA((4,))]
+    params = dict(vmem_limit_bytes=48 * MIB)
+    if part:
+        outs += [
+            shape((3, 4 * tokens, part), BF16),
+            shape((4 * tokens, n_q + 2 * n_kv + width + LANES), BF16),
+            shape((64, part), BF16),
+        ]
+        scratch += [DMA((6,)), DMA((6,)), DMA((6,)), DMA((2, 6))]
+        params.update(collective_id=cid, has_side_effects=True)
+    return pl.pallas_call(
+        functools.partial(attention_backward_kernel, layer, bool(part), n_experts),
+        out_shape=outs,
+        in_specs=[VM] * 16 + [HB] * 4,
+        out_specs=[VM] * 4 + [HB] * (len(outs) - 4),
+        scratch_shapes=scratch,
+        compiler_params=pltpu.CompilerParams(**params),
+        cost_estimate=pl.CostEstimate(
+            flops=4 * tokens * width * 4096, bytes_accessed=20 * MIB, transcendentals=0
+        ),
+        name="attention_backward",
+    )(g, dn2, dgates, mask, allowed, rope, gains, router, *kept, *weights)
 
 
 def swap(value, axis):
     return lax.ppermute(value, axis, [(0, 1), (1, 0)])
-
-
-def half_of(value, axis, index, size):
-    return lax.dynamic_slice_in_dim(value, index * size, size, axis)
-
-
-def sum_over_dp(value, axis, size):
-    n = lax.axis_size("dp")
-    x = lax.axis_index("dp")
-    if n == 2:
-        there = half_of(value, axis, 1 - x, size)
-        here = half_of(value, axis, x, size)
-        return here.astype(F32) + swap(there, "dp").astype(F32)
-    return lax.psum_scatter(value, "dp", scatter_dimension=axis, tiled=True).astype(F32)
 
 
 def shards(
@@ -1311,139 +1539,108 @@
 ):
     n_dp = lax.axis_size("dp")
     n_exp = lax.axis_size("expert")
-    ls = 2 if n_dp == 2 else 1
+    paired = n_dp == 2
+    ls = 2 if paired else 1
     s = lax.axis_index("section")
-    e = lax.axis_index("expert")
-    x = lax.axis_index("dp")
+    first = s == 0
     tokens, width = layer_input.shape[1:]
     n_experts = EXP_DEV * n_exp
     shard_rows = width // n_dp
 
     def micro(value):
         return lax.dynamic_index_in_dim(value, s, 0, keepdims=False)
-
-    small = jnp.concatenate([w_router[0], gain_attn[0][:, None], gain_moe[0][:, None]], axis=1)
-    small = lax.all_gather(small, ("section", "dp"), axis=0, tiled=True).reshape(2, width, -1)
-    routers = small[:, :, :n_experts]
-    gains = [
-        (small[k, :, n_experts].astype(F32), small[k, :, n_experts + 1].astype(F32))
-        for k in range(2)
-    ]
-    all_routes = lax.all_gather(routes[0], ("section", "expert"), axis=0)
-    all_routes = all_routes.reshape(2, n_exp, 2, tokens, TOPK)
-    all_routes = lax.dynamic_index_in_dim(all_routes, s, 2, keepdims=False)
-    picks = jnp.max(
-        (all_routes[..., None] == jnp.arange(n_experts, dtype=jnp.int32)).astype(F32), axis=-2
-    )
-    own_picks = lax.dynamic_index_in_dim(picks, e, 1, keepdims=False)
-
-    def rolled(value):
-        twice = jnp.concatenate([value, value], axis=-1)
-        cut = lax.dynamic_slice_in_dim(twice, EXP_DEV * e, n_experts, value.ndim - 1)
-        pad = [(0, 0)] * (value.ndim - 1) + [(0, LANES - n_experts)]
-        return jnp.pad(cut, pad)
-
-    masks = rolled(picks)
-    if ls == 1:
-        masks = masks.reshape(2, 2, LINE, tokens, LANES).swapaxes(1, 2)
-    masks = masks.reshape(2, LINE, 2 * tokens, LANES)
-
-    mine = (w_gate[0], w_up[0], w_down[0])
-    theirs = tuple(swap(w, "section") for w in mine)
-    own = (w_query[0], key_matrix[0], value_matrix[0], w_out[0])
-    if n_dp == 2:
-        layer_weights = [spread_weights(0, own, 0), None]
-    else:
-        wholes = [
-            lax.all_gather(w, ("section", "dp"), axis=0, tiled=True).reshape(2, width, -1)
-            for w in own
-        ]
-        layer_weights = [tuple(w[k] for w in wholes) for k in range(2)]
-
-    allowed = mask_for(micro(segments))
-    current = micro(layer_input)
-    kept_list, outs = [], []
-    for k in range(2):
-        middle, normed_two, kept = attention_forward(
-            current.astype(F32), allowed, gains[k][0], gains[k][1], layer_weights[k]
-        )
-        logits = dot(normed_two, routers[k])
-        z = jnp.where(own_picks[k] > 0, logits, NEG)
-        kept["gates"] = jax.nn.softmax(z, axis=-1) * own_picks[k]
-        riders = own if (n_dp == 2 and k == 0) else ()
-        result = experts_forward(
-            ls, k, 1 + k, normed_two, middle, masks[k], rolled(routers[k]), mine, theirs, riders
-        )
-        current = result[0]
-        kept["saved"] = result[1:5]
-        if riders:
-            layer_weights[1] = result[5:]
-        kept_list.append(kept)
-        outs.append(current)
-
-    d_out = micro(cotangent)
-    d_ins, act_list, gain_list, expert_list = [None] * 2, [None] * 2, [None] * 2, [None] * 2
-    for k in (1, 0):
-        kept = kept_list[k]
-        pair_up = n_dp == 2
-        sums = (expert_list[1],) if (pair_up and k == 0) else ()
-        got = experts_backward(
-            ls, k, 3 + k, d_out, mine, theirs, *kept["saved"], pair_up, sums
-        )
-        d_normed_two, d_gates = got[:2]
-        expert_list[k] = got[2]
-        if sums:
-            delivered = got[4:6]
-
-        d_gates = d_gates[:, :n_experts] + d_gates[:, 32 : 32 + n_experts]
-        d_out, acts, gain_grads = attention_backward(
-            d_out.astype(F32),
-            d_normed_two,
-            d_gates,
-            kept["gates"],
-            kept,
-            allowed,
-            gains[k],
-            layer_weights[k],
-            routers[k],
-        )
-        d_ins[k] = d_out
-        lhs = jnp.concatenate(
-            [kept["normed"], kept["context"], kept["normed_two"]], axis=1
-        ).reshape(tokens, 3, width)
-        rhs = jnp.concatenate(
-            [acts["dq"], acts["dk"], acts["dv"], acts["dat"]]
-            + [jnp.pad(acts["dr"], ((0, 0), (0, LANES - n_experts)))],
-            axis=1,
-        )
-        gain_rows = jnp.stack(gain_grads)
-        if n_dp == 2:
-            pack_there = half_of(lhs, 2, 1 - x, shard_rows).reshape(tokens, -1)
-            pack_here = half_of(lhs, 2, x, shard_rows).reshape(tokens, -1)
-            sent = jnp.concatenate([pack_there, rhs], axis=1)
-            kept_here = jnp.concatenate([pack_here, rhs], axis=1)
-            pack = jnp.concatenate([kept_here, swap(sent, "dp")], axis=0)
-        else:
-            pack = jnp.concatenate([lhs.reshape(tokens, -1), rhs], axis=1)
-        act_list[k] = pack
-        gain_list[k] = sum_over_dp(gain_rows, 1, shard_rows)
-
-    first = s == 0
 
     def own_layer(zero, one):
         kept_part = jnp.where(first, zero, one)
         sent_part = jnp.where(first, one, zero)
         return kept_part, swap(sent_part, "section")
 
-    acts_mine = jnp.concatenate(own_layer(act_list[0], act_list[1]), axis=0)
-    gain_mine = sum(own_layer(gain_list[0], gain_list[1]))
-    lhs_rows = shard_rows if n_dp == 2 else width
-    gain_cols = jnp.pad(gain_mine.T, ((0, 0), (LANES - 2, 0)))
-    widths = [w.shape[1] for w in own]
-    if n_dp == 2:
-        lhs = acts_mine[:, : 3 * lhs_rows].reshape(-1, 3, lhs_rows).swapaxes(0, 1)
-        rhs = acts_mine[:, 3 * lhs_rows :]
-        blocks, near, far = shared_grads(ls, 5, lhs, rhs, gain_cols, expert_list[0])
+    own_routes = micro(routes[0])
+    other_routes = swap(
+        lax.dynamic_index_in_dim(routes[0], 1 - s, 0, keepdims=False), "section"
+    )
+    both_routes = jnp.where(
+        first, jnp.stack([own_routes, other_routes]), jnp.stack([other_routes, own_routes])
+    )
+    names = jnp.arange(LANES, dtype=jnp.int32)
+    picks = jnp.max((both_routes[..., None] == names).astype(BF16), axis=-2)
+    picks = jnp.concatenate([picks[0], picks[1]], axis=1)
+
+    mine = (w_gate[0], w_up[0], w_down[0])
+    theirs = tuple(swap(w, "section") for w in mine)
+    router = jnp.pad(w_router[0], ((0, 0), (0, LANES - n_experts)))
+    gains = jnp.concatenate([gain_attn, gain_moe, jnp.zeros((14, shard_rows), BF16)], axis=0)
+    own = (w_query[0], key_matrix[0], value_matrix[0], w_out[0], router, gains)
+    widths = [w.shape[1] for w in own[:4]]
+    if paired:
+        masks, *whole = start(ls, 0, picks, own)
+        layer_weights = [whole, None]
+    else:
+        wholes = [
+            lax.all_gather(w, ("section", "dp"), axis=0, tiled=True).reshape(2, -1, w.shape[1])
+            for w in own
+        ]
+        layer_weights = [tuple(w[k] for w in wholes) for k in range(2)]
+        masks = lax.all_gather(picks, "expert", axis=0).reshape(2, LINE, tokens, -1)
+        masks = masks.swapaxes(0, 1).reshape(LINE, 2 * tokens, -1)
+
+    seg_row = micro(segments)
+    places = jnp.arange(tokens)
+    allowed = (seg_row[:, None] == seg_row[None, :]) & (places[:, None] >= places[None, :])
+    allowed = allowed.astype(F32)
+    rope = jnp.asarray(rope_tables(tokens))
+    current = micro(layer_input)
+    kept_list, saved_list, outs = [], [], []
+    for k in range(2):
+        weights = layer_weights[k]
+        n1, q, keys, values, context, h1, n2 = attention_forward(
+            current, allowed, rope, weights[:4], weights[5]
+        )
+        kept_list.append((current, n1, q, keys, values, context, h1, n2))
+        riders = own if (paired and k == 0) else ()
+        result = experts_forward(
+            ls, k, 1 + k, n2, h1, masks, weights[4], mine, theirs, riders
+        )
+        current = result[0]
+        saved_list.append(result[1:5])
+        if riders:
+            layer_weights[1] = result[5:]
+        outs.append(current)
+
+    d_out = micro(cotangent)
+    d_ins, act_list, expert_list = [None] * 2, [None] * 2, [None] * 2
+    for k in (1, 0):
+        sums = (expert_list[1],) if (paired and k == 0) else ()
+        got = experts_backward(
+            ls, k, 3 + k, d_out, mine, theirs, *saved_list[k], paired, sums
+        )
+        expert_list[k] = got[2]
+        if sums:
+            delivered = got[4:6]
+        weights = layer_weights[k]
+        d_out, *acts = attention_backward(
+            k,
+            6 + k,
+            n_experts,
+            d_out,
+            got[0],
+            got[1],
+            picks,
+            allowed,
+            rope,
+            weights[5],
+            weights[4],
+            kept_list[k],
+            weights[:4],
+            shard_rows if paired else 0,
+        )
+        d_ins[k] = d_out
+        act_list[k] = acts
+
+    if paired:
+        blocks, near, far = shared_grads(
+            ls, 5, (act_list[0][3:], act_list[1][3:]), expert_list[0]
+        )
         gate_grad, up_grad, down_grad, *wide_grads = finish(
             expert_list,
             (near, delivered[0]),
@@ -1458,20 +1655,21 @@
         tail = tail.reshape(2 * LINE, -1, 4, LANES).swapaxes(1, 2).reshape(shard_rows, LANES)
         tail = tail.astype(F32)
     else:
-        lhs = [acts_mine[:, i * lhs_rows : (i + 1) * lhs_rows] for i in range(3)]
-        rhs = acts_mine[:, 3 * lhs_rows :]
-        n_qkv = sum(widths[:3])
-        parts = jnp.concatenate(
-            [
-                dot_tn(lhs[0], rhs[:, :n_qkv]),
-                dot_tn(lhs[1], rhs[:, n_qkv : n_qkv + width]),
-                dot_tn(lhs[2], rhs[:, n_qkv + width :]),
-            ],
-            axis=1,
-        ).astype(BF16)
-        parts = lax.psum_scatter(parts, "dp", scatter_dimension=0, tiled=True).astype(F32)
-        parts = parts + jnp.pad(gain_cols, ((0, 0), (parts.shape[1] - LANES, 0)))
-        spread = lax.psum(parts.astype(BF16), "expert").astype(F32)
+        parts = []
+        for k in range(2):
+            dqkv, datdr, gain_rows = act_list[k]
+            n1, context, n2 = kept_list[k][1], kept_list[k][5], kept_list[k][7]
+            gain_rows = gain_rows.astype(F32)
+            gain_cols = jnp.stack([gain_rows[0] + gain_rows[1], gain_rows[2] + gain_rows[3]], 1)
+            last = dot_tn(n2, datdr[:, width:]) + jnp.pad(gain_cols, ((0, 0), (LANES - 2, 0)))
+            parts.append(
+                jnp.concatenate(
+                    [dot_tn(n1, dqkv), dot_tn(context, datdr[:, :width]), last], axis=1
+                )
+            )
+        parts = sum(own_layer(*parts)).astype(BF16)
+        parts = lax.psum_scatter(parts, "dp", scatter_dimension=0, tiled=True)
+        spread = lax.psum(parts, "expert").astype(F32)
         cut = [sum(widths[:i]) for i in range(5)]
         wide_grads = [spread[:, cut[i] : cut[i + 1]] for i in range(4)]
         tail = spread[:, cut[4] :]

time: 1070 us -> 826 us (0.77)
  waiting for transfers between devices: 73.4 us -> 1.74 us
  matrix products: 58.2 us -> 0 us
  other arithmetic: 42.3 us -> 5.11 us
  blocking collectives: 35.7 us -> 0 us
  local copies, waits for them, and re-layouts: 93.7 us -> 62.2 us
  starting transfers between devices: 17.4 us -> 5.38 us
    pallas_call x1 -> x5, Pallas kernels: 75.8 us -> 174 us  [the longest x2 85.4 us: attention_backward(): pl.pallas_call(functools.partial(attention_backward_kernel, layer, bool(p...]
    ppermute x11 -> x6, waiting for transfers between devices: 73.4 us -> 1.74 us  [swap(): return lax.ppermute(value, axis, [(0, 1), (1, 0)])]
    dot_general x32 -> x0, matrix products: 58.2 us -> none  [the longest x20 48 us: dot(): return jnp.dot(a, b, preferred_element_type=F32)]
    pallas_call x2, Pallas kernels: 241 us -> 191 us  [experts_forward(): pl.pallas_call(functools.partial(experts_forward_kernel, ls, layer, chunk...]
    all_gather x2 -> x0, blocking collectives: 35.7 us -> none  [the longest x1 26 us: shards(): all_routes = lax.all_gather(routes[0], ('section', 'expert'), axis=0)]
    pallas_call x2, Pallas kernels: 237 us -> 206 us  [experts_backward(): pl.pallas_call(functools.partial(experts_backward_kernel, ls, layer, chun...]
    unnamed x280 -> x132, local copies, waits for them, and re-layouts: 40.6 us -> 56.8 us
    convert_element_type x10 -> x0, local copies, waits for them, and re-layouts: 14.5 us -> none  [the longest x2 3.83 us: attention_backward(): d_context = dot(d_attn, w_out.T).astype(BF16).reshape(token_count, KEY_VA...]
  transfers between devices with their start and end apart: 11 -> 6, of which waited for: 5 -> 1; matrix products, arithmetic and copies ran while one was open for 6% -> 1% of each run, Pallas kernels for 7% -> 31%
where the time goes in v3:
time: 826 us; the launch traced here: 816 us
  Pallas kernels  740 us (90%)
  local copies, waits for them, and re-layouts  62.2 us (8%)
    pallas_call x2, Pallas kernels, experts_backward(): pl.pallas_call(functools.partial(experts_backward_kernel, ls, layer, chun...  206 us
    pallas_call x2, Pallas kernels, experts_forward(): pl.pallas_call(functools.partial(experts_forward_kernel, ls, layer, chunk...  191 us
    pallas_call x1, Pallas kernels, shared_grads(): pl.pallas_call(functools.partial(shared_grads_kernel, ls, chunks), out_sh...  152 us
    pallas_call x2, Pallas kernels, attention_backward(): pl.pallas_call(functools.partial(attention_backward_kernel, layer, bool(p...  85.4 us
    pallas_call x1, Pallas kernels, start(): pl.pallas_call(functools.partial(start_kernel, ls, count), out_shape=[jax...  77.5 us
    unnamed x132, local copies, waits for them, and re-layouts  56.8 us
  transfers between devices with their start and end apart: 6, of which 1 were waited for; matrix products, arithmetic and copies ran while one was open for 1% of the time, Pallas kernels for 31%

profile of v3, /device:TPU:17, one launch (start us, length us, event | category | flops | bytes accessed | tf_op | source)
XLA Modules:
  0.0 815.7 jit_solution(228538878683534345)
XLA Ops:
  3.6 1.8 dynamic-slice_bitcast_fusion.refs_0_
  6.2 0.9 copy.40
  7.2 1.7 collective-permute-done
  9.5 1.7 copy-done.15
  11.2 1.7 copy-done.16
  12.9 1.1 copy-done.26
  14.0 1.1 copy-done.27
  15.1 77.5 %start.1 = (bf16[4,256,256]{2,1,0:T(8,128)(2,1)S(1)}, bf16[1536,1536]{1,0:T(8,128)(2,1)S(1)}, bf16[1536,512]{1,0:T(8,128)(2,1)S(1)}, bf16[1536,512]{1,0:T(8,128)...) custom-call(bf16[128,256]{1,0:T(8,128)(2,1)S(1)} %pad_maximum_fusion.refs_0_.r, ...), custom_call_target="tpu_custom_call" | custom-call | bytes 209715200 | tf_op jit(solution)/shard_map/start/pallas_call | solution.py:426
  92.6 2.2 copy-done.4
  95.6 6.1 attention_forward.2
  106.4 99.6 %experts_forward.2 = (bf16[128,1536]{1,0:T(8,128)(2,1)}, bf16[4,256,1536]{2,1,0:T(8,128)(2,1)}, bf16[4,256,1536]{2,1,0:T(8,128)(2,1)}, bf16[4,256,1536]{2,1,0:T(...) custom-call(bf16[128,1536]{1,0:T(8,128)(2,1)} %copy-done.36, ...), custom_call_target="tpu_custom_call" | custom-call | flops 14495514624 | bytes 62914560 | tf_op jit(solution)/shard_map/experts_forward/pallas_call | solution.py:605
  206.0 2.3 copy-done.5
  208.3 1.4 copy-done.9
  209.7 1.4 copy-done.10
  211.1 1.0 copy-done.13
  212.9 5.4 attention_forward.3
  223.5 91.9 %experts_forward.3 = (bf16[128,1536]{1,0:T(8,128)(2,1)}, bf16[4,256,1536]{2,1,0:T(8,128)(2,1)}, bf16[4,256,1536]{2,1,0:T(8,128)(2,1)}, bf16[4,256,1536]{2,1,0:T(8,128)(2,1)}, f32[4,256,128]{2,1,0:T(8,128)}) custom-call(bf16[128,1536]{1,0:T(8,128)(2,1)} %copy-done.45, f32[128,1536]{1,0:T(8,128)} %copy-done.22, bf16[4,256,256]{2,1,0:T(8,128)(2,1)} %copy-done.62, ...), custom_call_target="tpu_custom_call" | custom-call | flops 14495514624 | bytes 62914560 | tf_op jit(solution)/shard_map/experts_forward/pallas_call | solution.py:605
  315.4 103.2 %experts_backward.2 = (f32[128,1536]{1,0:T(8,128)}, f32[128,128]{1,0:T(8,128)}, bf16[3,2,384,1536]{3,2,1,0:T(8,128)(2,1)}, bf16[3,2,384,1536]{3,2,1,0:T(8,128)(2,1)}) custom-call(bf16[128,1536]{1,0:T(8,128)(2,1)} %dynamic-slice_bitcast_fusion.refs_0_, bf16[3,1536,512]{2,1,0:T(8,128)(2,1)} %bitcast.62, bf16[3,1536,512]{2,1,0:T(8,128)(2,1)} %bitcast.67, ...), custom_call_target="tpu_custom_call" | custom-call | flops 28991029248 | bytes 104857600 | tf_op jit(solution)/shard_map/experts_backward/pallas_call | solution.py:938
  418.7 1.0 copy-done.18
  419.6 1.1 copy-done.24
  420.8 1.0 copy-done.38
  421.8 1.0 copy-done.40
  422.8 1.0 copy-done.42
  423.8 1.0 copy-done.44
  424.8 1.0 copy-done.46
  425.8 0.9 copy-done.54
  426.7 0.9 copy-done.56
  428.4 41.4 %attention_backward.2 = (bf16[128,1536]{1,0:T(8,128)(2,1)S(1)}, bf16[128,2560]{1,0:T(8,128)(2,1)}, bf16[128,1664]{1,0:T(8,128)(2,1)}, bf16[16,1536]{1,0:T(8,128)...) custom-call(bf16[128,1536]{1,0:T(8,128)(2,1)S(1)} %copy-done.18, ...), custom_call_target="tpu_custom_call" | custom-call | flops 3221225472 | bytes 20971520 | tf_op jit(solution)/shard_map/attention_backward/pallas_call | solution.py:1506
  471.2 102.7 %experts_backward.3 = (f32[128,1536]{1,0:T(8,128)}, f32[128,128]{1,0:T(8,128)}, bf16[3,2,384,1536]{3,2,1,0:T(8,128)(2,1)}, bf16[3,2,384,1536]{3,2,1,0:T(8,128)(2...) custom-call(bf16[128,1536]{1,0:T(8,128)(2,1)} %copy-done.19, bf16[3,1536,512]{2,1,0:T(8,128)(2,1)} %bitcast.63, ...), custom_call_target="tpu_custom_call" | custom-call | flops 28991029248 | bytes 104857600 | tf_op jit(solution)/shard_map/experts_backward/pallas_call | solution.py:938
  573.9 1.0 copy-done.20
  574.9 1.1 copy-done.23
  576.0 1.0 copy-done.29
  577.0 1.0 copy-done.31
  578.0 1.0 copy-done.33
  579.0 1.0 copy-done.35
  580.0 1.0 copy-done.37
  582.8 44.1 %attention_backward.3 = (bf16[128,1536]{1,0:T(8,128)(2,1)S(1)}, bf16[128,2560]{1,0:T(8,128)(2,1)}, bf16[128,1664]{1,0:T(8,128)(2,1)}, bf16[16,1536]{1,0:T(8,128)...) custom-call(bf16[128,1536]{1,0:T(8,128)(2,1)S(1)} %copy-done.20, ...), custom_call_target="tpu_custom_call" | custom-call | flops 3221225472 | bytes 20971520 | tf_op jit(solution)/shard_map/attention_backward/pallas_call | solution.py:1506
  626.9 3.0 collective-permute-start.5
  630.7 152.4 %shared_grads.1 = (bf16[4,1600,512]{2,1,0:T(8,128)(2,1)}, bf16[3,384,1536]{2,1,0:T(8,128)(2,1)}, bf16[2,3,384,1536]{3,2,1,0:T(8,128)(2,1)}) custom-call(bf16[3,512,768]{2,1,0:T(8,128)(2,1)} %get-tuple-element.119.refs_0_, bf16[512,4224]{1,0:T(8,128)(2,1)} %get-tuple-element.120.refs_1_, bf16[64,768]{1,0:T(8,128)(2,1)} %copy-done.58, ...), custom_call_target="tpu_custom_call" | custom-call | bytes 419430400 | tf_op jit(solution)/shard_map/shared_grads/pallas_call | solution.py:1043
  783.1 1.0 slice_convert_fusion
  784.2 1.1 collective-permute-start.4
  787.8 3.0 copy-done.2
  790.8 2.9 copy-done.6
  793.7 2.0 copy-done.11
  795.7 2.0 copy-done.12
  797.7 15.5 %finish.1 = (f32[3,768,512]{2,1,0:T(8,128)}, f32[3,768,512]{2,1,0:T(8,128)}, f32[3,256,1536]{2,1,0:T(8,128)}, f32[768,1536]{1,0:T(8,128)}, f32[768,512]{1,0:T(8,...) custom-call(bf16[3,2,384,1536]{3,2,1,0:T(8,128)(2,1)S(1)} %copy-done.2, ...), custom_call_target="tpu_custom_call" | custom-call | bytes 52428800 | tf_op jit(solution)/shard_map/finish/pallas_call | solution.py:1162
  813.2 1.0 maximum_select_fusion.1
  814.2 1.0 maximum_select_fusion
  (132 shorter events, 23.2 us)
Async XLA Ops:
  0.6 2.9 copy-start
  0.7 105.7 %collective-permute-start.1 = (bf16[3,1536,512]{2,1,0:T(8,128)(2,1)}, bf16[3,1536,512]{2,1,0:T(8,128)(2,1)}, u32[]{:S(2)}, u32[]{:S(2)}) collective-permute-start(bf16[3,1536,512]{2,1,0:T(8,128)(2,1)} %bitcast.59), channel_id=1, source_target_pairs={{0,16},{16,0},{1,17},{17,1},{2,18},{18,2},{3,19},{19,3},{4,20},{20... | collective-permute-start | bytes 14155784 | tf_op jit(solution)/shard_map/ppermute | solution.py:1521
  1.4 104.9 %collective-permute-start.2 = (bf16[3,1536,512]{2,1,0:T(8,128)(2,1)}, bf16[3,1536,512]{2,1,0:T(8,128)(2,1)}, u32[]{:S(2)}, u32[]{:S(2)}) collective-permute-start(bf16[3,1536,512]{2,1,0:T(8,128)(2,1)} %bitcast.64), channel_id=1, source_target_pairs={{0,16},{16,0},{1,17},{17,1},{2,18},{18,2},{3,19},{19,3},{4,20},{20... | collective-permute-start | bytes 14155784 | tf_op jit(solution)/shard_map/ppermute | solution.py:1521
  1.5 104.9 %collective-permute-start.3 = (bf16[3,512,1536]{2,1,0:T(8,128)(2,1)}, bf16[3,512,1536]{2,1,0:T(8,128)(2,1)}, u32[]{:S(2)}, u32[]{:S(2)}) collective-permute-start(bf16[3,512,1536]{2,1,0:T(8,128)(2,1)} %bitcast.69), channel_id=1, source_target_pairs={{0,16},{16,0},{1,17},{17,1},{2,18},{18,2},{3,19},{19,3},{4,20},{20... | collective-permute-start | bytes 14155784 | tf_op jit(solution)/shard_map/ppermute | solution.py:1521
  2.6 6.3 collective-permute-start
  3.6 92.0 %copy-start.17 = (f32[2,128,128]{2,1,0:T(8,128)S(1)}, f32[2,128,128]{2,1,0:T(8,128)}, u32[]{:S(2)}) copy-start(f32[2,128,128]{2,1,0:T(8,128)} %constant.38.clone.refs_2_.refs_5_) | copy-start | bytes 393220
  6.2 95.5 %copy-start.59 = (bf16[16,768]{1,0:T(8,128)(2,1)}, bf16[16,768]{1,0:T(8,128)(2,1)S(1)}, u32[]{:S(2)}) copy-start(bf16[16,768]{1,0:T(8,128)(2,1)S(1)} %maximum_maximum_fusion.refs_6_.refs_15_) | copy-start | bytes 73732
  7.2 94.5 %copy-start.25 = (bf16[768,128]{1,0:T(8,128)(2,1)}, bf16[768,128]{1,0:T(8,128)(2,1)S(1)}, u32[]{:S(2)}) copy-start(bf16[768,128]{1,0:T(8,128)(2,1)S(1)} %pad.4.refs_5_.refs_14_) | copy-start | bytes 589828
  9.5 1.7 copy-start.15
  11.2 1.7 copy-start.16
  12.9 1.1 copy-start.26
  14.0 1.1 copy-start.27
  92.6 2.2 copy-start.4
  95.6 6.2 copy-start.3
  95.6 6.2 copy-start.7
  95.6 6.2 copy-start.8
  95.6 6.2 copy-start.28
  106.3 99.6 %copy-start.49 = (bf16[128,512]{1,0:T(8,128)(2,1)}, bf16[128,512]{1,0:T(8,128)(2,1)S(1)}, u32[]{:S(2)}) copy-start(bf16[128,512]{1,0:T(8,128)(2,1)S(1)} %get-tuple-element.115.refs_11_) | copy-start | bytes 393220
  206.0 2.3 copy-start.5
  208.3 1.4 copy-start.9
  209.7 1.4 copy-start.10
  211.1 1.0 copy-start.13
  315.4 103.2 %copy-start.14 = (bf16[128,1536]{1,0:T(8,128)(2,1)S(1)}, bf16[128,1536]{1,0:T(8,128)(2,1)}, u32[]{:S(2)}) copy-start(bf16[128,1536]{1,0:T(8,128)(2,1)} %get-tuple-element.84.refs_0_.refs_8_) | copy-start | bytes 1179652
  315.4 103.2 %copy-start.48 = (bf16[32,768]{1,0:T(8,128)(2,1)S(1)}, bf16[32,768]{1,0:T(8,128)(2,1)}, u32[]{:S(2)}) copy-start(bf16[32,768]{1,0:T(8,128)(2,1)} %get-tuple-element.85.refs_3_.refs_6_) | copy-start | bytes 147460
  418.6 1.0 copy-start.18
  419.6 1.1 copy-start.24
  420.8 1.0 copy-start.38
  421.8 1.0 copy-start.40
  422.8 1.0 copy-start.42
  423.8 1.0 copy-start.44
  424.8 1.0 copy-start.46
  471.2 102.7 %copy-start.50 = (bf16[128,512]{1,0:T(8,128)(2,1)S(1)}, bf16[128,512]{1,0:T(8,128)(2,1)}, u32[]{:S(2)}) copy-start(bf16[128,512]{1,0:T(8,128)(2,1)} %copy-done.49) | copy-start | bytes 393220
  573.9 1.0 copy-start.20
  574.9 1.1 copy-start.23
  576.0 1.0 copy-start.29
  577.0 1.0 copy-start.31
  578.0 1.0 copy-start.33
  579.0 1.0 copy-start.35
  582.8 47.1 %copy-start.63 = (bf16[128,1536]{1,0:T(8,128)(2,1)S(1)}, bf16[128,1536]{1,0:T(8,128)(2,1)}, u32[]{:S(2)}) copy-start(bf16[128,1536]{1,0:T(8,128)(2,1)} %get-tuple-element.93) | copy-start | bytes 1179652
  626.8 3.8 copy-start.58
  626.9 186.2 %collective-permute-start.5 = (bf16[128,1536]{1,0:T(8,128)(2,1)S(1)}, bf16[128,1536]{1,0:T(8,128)(2,1)S(1)}, u32[]{:S(2)}, u32[]{:S(2)}) collective-permute-start(bf16[128,1536]{1,0:T(8,128)(2,1)S(1)} %get-tuple-element.177), channel_id=1, source_target_pairs={{0,16},{16,0},{1,17},{17,1},{2,18},{18,2},{3,19},{19,3},{4,20},{20... | collective-permute-start | bytes 1179656 | tf_op jit(solution)/shard_map/ppermute | solution.py:1521
  630.7 153.5 %copy-start.64 = (bf16[128,1536]{1,0:T(8,128)(2,1)S(1)}, bf16[128,1536]{1,0:T(8,128)(2,1)}, u32[]{:S(2)}) copy-start(bf16[128,1536]{1,0:T(8,128)(2,1)} %get-tuple-element.179) | copy-start | bytes 1179652
  784.2 30.0 %collective-permute-start.4 = (bf16[128,1536]{1,0:T(8,128)(2,1)S(1)}, bf16[128,1536]{1,0:T(8,128)(2,1)S(1)}, u32[]{:S(2)}, u32[]{:S(2)}) collective-permute-start(bf16[128,1536]{1,0:T(8,128)(2,1)S(1)} %copy-done.64), channel_id=1, source_target_pairs={{0,16},{16,0},{1,17},{17,1},{2,18},{18,2},{3,19},{19,3},{4,20},{20... | collective-permute-start | bytes 1179656 | tf_op jit(solution)/shard_map/ppermute | solution.py:1521
  787.8 3.0 copy-start.2
  790.8 2.9 copy-start.6
  793.7 2.0 copy-start.11
  795.7 2.0 copy-start.12
  797.7 17.5 %copy-start.1 = (bf16[2,128,1536]{2,1,0:T(8,128)(2,1)S(1)}, bf16[2,128,1536]{2,1,0:T(8,128)(2,1)}, u32[]{:S(2)}) copy-start(bf16[2,128,1536]{2,1,0:T(8,128)(2,1)} %param.15) | copy-start | bytes 2359300
  (23 other events, 18.1 us)

commit v4 on v3

--- a/solution.py
+++ b/solution.py
@@ -20,6 +20,9 @@
 THETA = 10000.0
 NEG = -1e30
 
+EARLY = (0, 1)
+LATE = (2,)
+
 MESH = pl.DeviceIdType.MESH
 DMA = pltpu.SemaphoreType.DMA
 VM = pl.BlockSpec(memory_space=pltpu.VMEM)
@@ -73,6 +76,20 @@
         (l < LINE - 1, {"expert": index_of(l + 1, p, ls)}),
     )
     greet_all(near + tuple(signals), tuple(w for w, _ in near) + tuple(waits))
+
+
+def around():
+    s, x = lax.axis_index("section"), lax.axis_index("dp")
+    signals = (
+        (s >= 0, {"dp": 1 - x}),
+        (s >= 0, {"dp": 1 - x, "section": 1 - s}),
+        (s >= 0, {"section": 1 - s}),
+    )
+    return signals, (s >= 0,) * 3
+
+
+def moves(pairs, sems):
+    return [pltpu.make_async_copy(a, b, sems.at[i]) for i, (a, b) in enumerate(pairs)]
 
 
 def remote(src, dst, ssem, rsem, **where):
@@ -395,44 +412,154 @@
     picks_ref, shards = refs[0], refs[1 : 1 + count]
     masks, wholes = refs[1 + count], refs[2 + count : 2 + 2 * count]
     at = 2 + 2 * count
-    ag_sems, own_sem = refs[at : at + 6], refs[at + 6]
-    l, p = place(lax.axis_index("expert"), ls)
+    sems = [refs[at + 6 * i : at + 6 * i + 6] for i in range(3)]
+    own_sem, in_sem, out_sem, xs, xr, cs, cr, far_sem = refs[at + 18 : at + 26]
+    bounce, big = refs[at + 26 : at + 26 + count], refs[at + 26 + count :]
+    e = lax.axis_index("expert")
+    s, x = lax.axis_index("section"), lax.axis_index("dp")
+    l, p = place(e, ls)
+    src = s == 0
+    large = (0, 3)
+
+    def whole(i, x):
+        size = shards[i].shape[0]
+        return wholes[i].at[pl.ds(pl.multiple_of(x * size, size), size)]
+
+    def across(i):
+        if i in large:
+            buf = big[large.index(i)]
+            size = buf.shape[1] // 2
+            from_rows = shards[i].at[pl.ds(pl.multiple_of(e * size, size), size)]
+            to_rows = buf.at[l, pl.ds(pl.multiple_of(p * size, size), size)]
+            return remote(from_rows, to_rows, xs.at[i], xr.at[i], dp=1 - x)
+        return remote(shards[i], whole(i, x), xs.at[i], xr.at[i], dp=1 - x)
+
+    def core_own(i):
+        return remote(shards[i], whole(i, x), cs.at[0, i], cr.at[0, i], section=1 - s)
+
+    def far_rows(i, L):
+        rows = big[large.index(i)].shape[1]
+        start = pl.multiple_of((1 - x) * LINE * rows + L * rows, rows)
+        return wholes[i].at[pl.ds(start, rows)]
+
+    def core_large(i, L):
+        j = large.index(i)
+        return remote(
+            big[j].at[L],
+            far_rows(i, L),
+            far_sem.at[0, j, L],
+            far_sem.at[1, j, L],
+            section=1 - s,
+        )
+
+    def core_small(i):
+        v = whole(i, 1 - x)
+        return remote(v, v, cs.at[1, i], cr.at[1, i], section=1 - s)
+
+    def kept(i, L):
+        j = large.index(i)
+        return pltpu.make_async_copy(big[j].at[L], far_rows(i, L), far_sem.at[2, j, L])
+
+    loads = moves(list(zip(shards, bounce)), in_sem)
+    stores = moves([(bounce[i], whole(i, x)) for i in range(count)], out_sem)
     half = picks_ref.shape[0]
     own = pltpu.make_async_copy(
         picks_ref, masks.at[l, pl.ds(pl.multiple_of(p * half, half), half)], own_sem
     )
     own.start()
     own.wait()
-    spread = Spread(0, shards, wholes, refs[at + 7 :])
-    greet(l, p, ls, spread.signals(), spread.waits())
-    spread.begin()
-    gather = Gather(l, p, ls, masks, ag_sems, 1)
-    gather.begin()
+    greet(l, p, ls, *around())
+    order = large + tuple(i for i in range(count) if i not in large)
+    gathers = [Gather(l, p, ls, big[i], sems[i], 2) for i in range(2)]
+    picked = Gather(l, p, ls, masks, sems[2], 1)
+    picked.begin()
+
+    @pl.when(src)
+    def _():
+        for i in order:
+            across(i).start()
+        for i in order:
+            loads[i].start()
+            core_own(i).start()
+        for g, i in enumerate(large):
+            across(i).wait_recv()
+            gathers[g].begin()
+        for i in order:
+            loads[i].wait()
+            stores[i].start()
 
     def step(k, carry):
-        gather.arrive(k)
+        picked.arrive(k)
+
+        @pl.when(src)
+        def _():
+            for g in gathers:
+                g.arrive(k)
+
         return carry
 
     lax.fori_loop(1, LINE, step, 0)
     for L in range(LINE):
-        gather.from_pair(L)
-    gather.end()
-    spread.end()
+        picked.from_pair(L)
+    picked.end()
+
+    @pl.when(src)
+    def _():
+        for i in order[2:]:
+            across(i).wait_recv()
+            core_small(i).start()
+        for g, i in enumerate(large):
+            for L in range(LINE):
+                gathers[g].from_pair(L)
+                core_large(i, L).start()
+                kept(i, L).start()
+        for g in gathers:
+            g.end()
+        for i in order:
+            across(i).wait_send()
+            core_own(i).wait_send()
+            stores[i].wait()
+        for i in order[2:]:
+            core_small(i).wait_send()
+        for i in large:
+            for L in range(LINE):
+                core_large(i, L).wait_send()
+                kept(i, L).wait()
+
+    @pl.when(jnp.logical_not(src))
+    def _():
+        for i in order:
+            core_own(i).wait_recv()
+        for i in order[2:]:
+            core_small(i).wait_recv()
+        for i in large:
+            for L in range(LINE):
+                core_large(i, L).wait_recv()
 
 
 def start(ls, cid, picks, shards):
     count = len(shards)
     rows, width = picks.shape
+    shard_rows, wide = shards[0].shape
+    buf = pltpu.VMEM((LINE, shard_rows // LINE, wide), BF16)
     return pl.pallas_call(
         functools.partial(start_kernel, ls, count),
         out_shape=[jax.ShapeDtypeStruct((LINE, 2 * rows, width), BF16)] + spread_shapes(shards),
         in_specs=[VM] + [HB] * count,
         out_specs=[VM] + [HB] * count,
-        scratch_shapes=link_sems(1) + [DMA(())] + spread_scratch(shards),
+        scratch_shapes=link_sems(2)
+        + link_sems(2)
+        + link_sems(1)
+        + [DMA(())]
+        + [DMA((count,))] * 4
+        + [DMA((2, count))] * 2
+        + [DMA((3, 2, LINE))]
+        + [pltpu.VMEM(w.shape, w.dtype) for w in shards]
+        + [buf, buf],
         compiler_params=pltpu.CompilerParams(
-            collective_id=cid, has_side_effects=True, vmem_limit_bytes=32 * MIB
+            collective_id=cid, has_side_effects=True, vmem_limit_bytes=60 * MIB
         ),
-        cost_estimate=pl.CostEstimate(flops=0, bytes_accessed=200 * MIB, transcendentals=0),
+        cost_estimate=pl.CostEstimate(flops=0, bytes_accessed=100 * MIB, transcendentals=0),
         name="start",
     )(picks, *shards)
 
@@ -476,41 +603,48 @@
 
 
 def experts_forward_kernel(ls, layer, chunks, n_spread, *refs):
-    n2_ref, h1_ref, mask_ref, wr_ref = refs[:4]
+    inputs = refs[:4]
     mine, theirs = refs[4:7], refs[7:10]
     shards = refs[10 : 10 + n_spread]
     at = 10 + n_spread
-    out_ref, x_out, gp_out, up_out, gates_ref = refs[at : at + 5]
+    out_hbm, x_out, gp_out, up_out, gates_out = refs[at : at + 5]
     wholes = refs[at + 5 : at + 5 + n_spread]
     at = at + 5 + n_spread
     xb, gpb, upre, part, pairb, upb, dnb, wg, wu, wd, act = refs[at : at + 11]
     at += 11
     ag_sems, rs_sems = refs[at : at + 6], refs[at + 6 : at + 12]
     at += 12
-    w_sem, own_sem, save_sem = refs[at : at + 3]
-    spread_sem = refs[at + 3 :]
+    w_sem, own_sem, save_sem, in_sem, out_sem = refs[at : at + 5]
+    h1_ref, mask_ref, wr_ref, gates_ref, out_ref = refs[at + 5 : at + 10]
+    spread_sem = refs[at + 10 :]
 
     e = lax.axis_index("expert")
     s = lax.axis_index("section")
     l, p = place(e, ls)
-    half = n2_ref.shape[0]
+    half = out_ref.shape[0]
     own_layer = s == layer
-    fetch(mine, theirs, own_layer, (wg, wu, wd), w_sem)
     own = pltpu.make_async_copy(
-        n2_ref, xb.at[l, pl.ds(pl.multiple_of(p * half, half), half)], own_sem
+        inputs[0], xb.at[l, pl.ds(pl.multiple_of(p * half, half), half)], own_sem
     )
     own.start()
+    loads = moves(list(zip(inputs[1:], (h1_ref, mask_ref, wr_ref))), in_sem)
+    for copy in loads[1:]:
+        copy.start()
+    fetch(mine, theirs, own_layer, (wg, wu, wd), w_sem)
+    loads[0].start()
     own.wait()
     signals = waits = ()
     if n_spread:
         spread = Spread(1 - layer, shards, wholes, spread_sem)
-        signals, waits = spread.signals(), spread.waits()
+        signals, waits = around()
     greet(l, p, ls, signals, waits)
     gather = Gather(l, p, ls, xb, ag_sems, chunks)
     total = Sum(l, p, ls, part, pairb, upb, dnb, rs_sems, chunks)
     gather.begin()
     if n_spread:
         spread.begin()
+    for copy in loads:
+        copy.wait()
     fetch(mine, theirs, own_layer, (wg, wu, wd), w_sem, wait=True)
 
     def save(L):
@@ -561,6 +695,9 @@
         return carry
 
     lax.fori_loop(0, LINE, back, 0)
+    last = moves([(out_ref, out_hbm), (gates_ref, gates_out)], out_sem)
+    for copy in last:
+        copy.start()
     if n_spread:
         spread.end()
     gather.end()
@@ -568,6 +705,8 @@
     for L in range(LINE):
         for copy in save(L):
             copy.wait()
+    for copy in last:
+        copy.wait()
 
 
 def experts_forward(ls, layer, cid, n2, h1, mask, wr, mine, theirs, shards=(), chunks=2):
@@ -599,14 +738,21 @@
         pltpu.VMEM((two, wide), BF16),
     ]
     scratch += link_sems(chunks) + link_sems(chunks)
-    scratch += [DMA((3,)), DMA(()), DMA((3, LINE))]
+    scratch += [DMA((3,)), DMA(()), DMA((3, LINE)), DMA((3,)), DMA((2,))]
+    scratch += [
+        pltpu.VMEM((tokens, width), F32),
+        pltpu.VMEM(mask.shape, BF16),
+        pltpu.VMEM(wr.shape, BF16),
+        pltpu.VMEM((LINE, two, LANES), F32),
+        pltpu.VMEM((tokens, width), BF16),
+    ]
     if n:
         scratch += spread_scratch(shards)
     return pl.pallas_call(
         functools.partial(experts_forward_kernel, ls, layer, chunks, n),
         out_shape=outs,
-        in_specs=[VM] * 4 + [HB] * (6 + n),
-        out_specs=[VM, HB, HB, HB, VM] + [HB] * n,
+        in_specs=[HB] * (10 + n),
+        out_specs=[HB] * (5 + n),
         scratch_shapes=scratch,
         compiler_params=pltpu.CompilerParams(
             collective_id=cid, has_side_effects=True, vmem_limit_bytes=60 * MIB
@@ -619,47 +765,15 @@
 
 
 class Deliver:
-    def __init__(self, layer, sums, near, far, sems):
-        self.layer, self.sums, self.near, self.far = layer, sums, near, far
+    def __init__(self, layer, kinds, sums, near, far, sems):
+        self.layer, self.kinds = layer, kinds
+        self.sums, self.near, self.far = sums, near, far
         self.ns, self.nr, self.fs, self.fr = sems
         self.s, self.x = lax.axis_index("section"), lax.axis_index("dp")
 
-    def signals(self, met_section):
-        owner = self.s == self.layer
-        out = [
-            (owner, {"dp": 1 - self.x}),
-            (owner, {"dp": 1 - self.x, "section": 1 - self.layer}),
-        ]
-        if not met_section:
-            out.append((owner, {"section": 1 - self.layer}))
-        return tuple(out)
-
-    def waits(self, met_section):
-        away = self.s != self.layer
-        return (self.s >= 0,) + (() if met_section else (away,))
-
-    def to_far(self, i):
+    def to_far(self, i, h):
         return remote(
-            self.sums.at[i, 1 - self.x],
-            self.far.at[self.s, i],
-            self.fs.at[i],
-            self.fr.at[self.s, i],
-            dp=1 - self.x,
-            section=self.layer,
-        )
-
-    def to_near(self, i):
-        return remote(
-            self.sums.at[i, self.x],
-            self.near.at[i],
-            self.ns.at[i],
-            self.nr.at[i],
-            section=self.layer,
-        )
-
-    def from_far(self, h, i):
-        return remote(
-            self.sums.at[i, 1 - self.x],
+            self.sums.at[self.kinds[i], 1 - self.x],
             self.far.at[h, i],
             self.fs.at[i],
             self.fr.at[h, i],
@@ -667,93 +781,212 @@
             section=self.layer,
         )
 
+    def to_near(self, i):
+        return remote(
+            self.sums.at[self.kinds[i], self.x],
+            self.near.at[i],
+            self.ns.at[i],
+            self.nr.at[i],
+            section=self.layer,
+        )
+
     def begin(self):
-        for i in range(3):
-            self.to_far(i).start()
+        for i in range(len(self.kinds)):
+            self.to_far(i, self.s).start()
 
         @pl.when(self.s != self.layer)
         def _():
-            for i in range(3):
+            for i in range(len(self.kinds)):
                 self.to_near(i).start()
 
     def end(self):
-        for i in range(3):
-            self.to_far(i).wait_send()
+        count = len(self.kinds)
+        for i in range(count):
+            self.to_far(i, self.s).wait_send()
 
         @pl.when(self.s != self.layer)
         def _():
-            for i in range(3):
+            for i in range(count):
                 self.to_near(i).wait_send()
 
         @pl.when(self.s == self.layer)
         def _():
-            for i in range(3):
+            for i in range(count):
                 self.to_near(i).wait_recv()
                 for h in range(2):
-                    self.from_far(h, i).wait_recv()
-
-
-def deliver_sems():
-    return [DMA((3,)), DMA((3,)), DMA((3,)), DMA((2, 3))]
-
-
-def deliver_shapes(sums):
-    kinds, _, rows, width = sums.shape
+                    self.to_far(i, h).wait_recv()
+
+
+def deliver_sems(kinds):
+    n = len(kinds)
+    return [DMA((n,)), DMA((n,)), DMA((n,)), DMA((2, n))]
+
+
+def deliver_shapes(kinds, sums):
+    _, _, rows, width = sums.shape
     return [
-        jax.ShapeDtypeStruct((kinds, rows, width), BF16),
-        jax.ShapeDtypeStruct((2, kinds, rows, width), BF16),
+        jax.ShapeDtypeStruct((len(kinds), rows, width), BF16),
+        jax.ShapeDtypeStruct((2, len(kinds), rows, width), BF16),
     ]
 
 
-def experts_backward_kernel(ls, layer, chunks, exchange, n_deliver, *refs):
-    g_ref = refs[0]
-    mine, theirs = refs[1:4], refs[4:7]
-    x_in, gp_in, up_in, gates_ref = refs[7:11]
-    sums_in = refs[11 : 11 + n_deliver]
-    at = 11 + n_deliver
-    dn_ref, dgate_ref, grads, got = refs[at : at + 4]
-    near_far = refs[at + 4 : at + 4 + 2 * n_deliver]
-    at = at + 4 + 2 * n_deliver
-    (xb, gb, gpb, upre, act, part, pairb, upb, dnb, wg, wu, wd, stage, extra) = refs[at : at + 14]
-    at += 14
-    ag_sems, rs_sems = refs[at : at + 6], refs[at + 6 : at + 12]
-    at += 12
-    w_sem, own_sem, load_sem, stage_sem, got_sem, extra_sem = refs[at : at + 6]
-    deliver_sem = refs[at + 6 :]
+class ActDeliver:
+    def __init__(self, layer, pieces, sems):
+        self.layer, self.pieces = layer, pieces
+        self.ns, self.nr, self.fs, self.fr = sems
+        self.s, self.x = lax.axis_index("section"), lax.axis_index("dp")
+
+    def near(self, i, s):
+        src, dst = self.pieces[i]
+        return remote(
+            src(self.x), dst(2 * s + self.x), self.ns.at[i], self.nr.at[i], section=self.layer
+        )
+
+    def here(self, i):
+        src, dst = self.pieces[i]
+        return pltpu.make_async_copy(src(self.x), dst(2 * self.s + self.x), self.ns.at[i])
+
+    def far(self, i, s, x):
+        src, dst = self.pieces[i]
+        return remote(
+            src(1 - x),
+            dst(2 * s + x),
+            self.fs.at[i],
+            self.fr.at[s, i],
+            dp=1 - self.x,
+            section=self.layer,
+        )
+
+    def begin(self, which):
+        for i in which:
+            self.far(i, self.s, self.x).start()
+
+            @pl.when(self.s != self.layer)
+            def _():
+                self.near(i, self.s).start()
+
+            @pl.when(self.s == self.layer)
+            def _():
+                self.here(i).start()
+
+    def end(self):
+        for i in range(len(self.pieces)):
+            self.far(i, self.s, self.x).wait_send()
+
+            @pl.when(self.s != self.layer)
+            def _():
+                self.near(i, self.s).wait_send()
+
+            @pl.when(self.s == self.layer)
+            def _():
+                self.here(i).wait()
+                self.near(i, 1 - self.s).wait_recv()
+                for s in range(2):
+                    self.far(i, s, 1 - self.x).wait_recv()
+
+
+def act_sems(count):
+    return [DMA((count,)), DMA((count,)), DMA((count,)), DMA((2, count))]
+
+
+def columns_for(ref, part):
+    return lambda x: ref.at[:, pl.ds(pl.multiple_of(x * part, part), part)]
+
+
+def rows_of(ref, size, cols=None):
+    def at(which):
+        rows = pl.ds(pl.multiple_of(which * size, size), size)
+        return ref.at[rows] if cols is None else ref.at[rows, cols]
+
+    return at
+
+
+def left_pieces(sources, lhs):
+    part = lhs.shape[2]
+    tokens = lhs.shape[1] // 4
+    return [
+        (columns_for(src, part), rows_of(lhs.at[i], tokens)) for i, src in enumerate(sources)
+    ]
+
+
+def right_pieces(datdr, dqkv, gains, rhs, gain_target):
+    tokens, first = dqkv.shape
+    return [
+        (lambda x: datdr, rows_of(rhs, tokens, pl.ds(first, datdr.shape[1]))),
+        (lambda x: dqkv, rows_of(rhs, tokens, pl.ds(0, first))),
+        (columns_for(gains, gain_target.shape[1]), rows_of(gain_target, 16)),
+    ]
+
+
+def left_shape(tokens, part):
+    return jax.ShapeDtypeStruct((3, 4 * tokens, part), BF16)
+
+
+def right_shapes(tokens, total, part):
+    return [
+        jax.ShapeDtypeStruct((4 * tokens, total), BF16),
+        jax.ShapeDtypeStruct((64, part), BF16),
+    ]
+
+
+def experts_backward_kernel(ls, layer, chunks, exchange, riders, *refs):
+    refs = list(refs)
+
+    def take(count):
+        out = refs[:count]
+        del refs[:count]
+        return out
+
+    g_in = take(1)[0]
+    mine, theirs = take(3), take(3)
+    x_in, gp_in, up_in, gates_in = take(4)
+    rider_in = take({"": 0, "left": 6, "right": 4}[riders])
+    dn_out, dgate_out, grads, got = take(4)
+    rider_out = take({"": 0, "left": 2, "right": 4}[riders])
+    (xb, gb, gpb, upre, act, part, pairb, upb, dnb, wg, wu, wd, stage, extra) = take(14)
+    gates_ref, dn_ref, dgate_ref = take(3)
+    ag_sems, rs_sems = take(6), take(6)
+    w_sem, own_sem, load_sem, stage_sem, got_sem, extra_sem, out_sem = take(7)
+    rider_sems = refs
 
     e = lax.axis_index("expert")
     s = lax.axis_index("section")
     l, p = place(e, ls)
-    half, width = g_ref.shape
+    half, width = g_in.shape
     hidden = wg.shape[2]
     two = 2 * half
     own_layer = s == layer
+    own = pltpu.make_async_copy(
+        g_in, gb.at[l, pl.ds(pl.multiple_of(p * half, half), half)], own_sem
+    )
+    own.start()
     fetch(mine, theirs, own_layer, (wg, wu, wd), w_sem)
-    loads = (
-        pltpu.make_async_copy(x_in, xb, load_sem.at[0]),
-        pltpu.make_async_copy(gp_in, gpb, load_sem.at[1]),
-        pltpu.make_async_copy(up_in, upre, load_sem.at[2]),
+    loads = moves(
+        [(gates_in, gates_ref), (gp_in, gpb), (up_in, upre), (x_in, xb)], load_sem
     )
     for copy in loads:
         copy.start()
-    own = pltpu.make_async_copy(
-        g_ref, gb.at[l, pl.ds(pl.multiple_of(p * half, half), half)], own_sem
-    )
-    own.start()
     own.wait()
-    signals = waits = ()
-    if exchange:
-        signals, waits = ((s >= 0, {"section": 1 - s}),), (s >= 0,)
-    if n_deliver:
-        deliver = Deliver(1 - layer, sums_in[0], *near_far, deliver_sem)
-        signals += deliver.signals(True)
-        waits += deliver.waits(True)
-    greet(l, p, ls, signals, waits)
+    couriers = []
+    if riders == "left":
+        for k in (1, 0):
+            pieces = left_pieces(rider_in[3 * k : 3 * k + 3], rider_out[k])
+            couriers.append(ActDeliver(k, pieces, rider_sems[4 * k : 4 * k + 4]))
+    if riders == "right":
+        pieces = right_pieces(*rider_in[1:], *rider_out[2:])
+        couriers.append(ActDeliver(1 - layer, pieces, rider_sems[4:8]))
+        couriers.append(
+            Deliver(1 - layer, EARLY, rider_in[0], *rider_out[:2], rider_sems[:4])
+        )
+    greet(l, p, ls, *(around() if exchange else ()))
     gather = Gather(l, p, ls, gb, ag_sems, chunks)
     total = Sum(l, p, ls, part, pairb, upb, dnb, rs_sems, chunks)
     gather.begin()
-    if n_deliver:
-        deliver.begin()
+    for courier in couriers:
+        if isinstance(courier, ActDeliver):
+            courier.begin(range(3))
+        else:
+            courier.begin()
     fetch(mine, theirs, own_layer, (wg, wu, wd), w_sem, wait=True)
     for copy in loads:
         copy.wait()
@@ -888,16 +1121,21 @@
         return carry
 
     lax.fori_loop(0, LINE, back, 0)
+    last = moves([(dn_ref, dn_out), (dgate_ref, dgate_out)], out_sem)
+    for copy in last:
+        copy.start()
     for kind in range(3):
         stored(kind, 3).wait()
     gather.end()
     total.end()
-    if n_deliver:
-        deliver.end()
+    for courier in couriers:
+        courier.end()
+    for copy in last:
+        copy.wait()
 
 
 def experts_backward(
-    ls, layer, cid, g, mine, theirs, x, gp, up, gates, exchange, sums=(), chunks=2
+    ls, layer, cid, g, mine, theirs, x, gp, up, gates, exchange, riders="", carried=(), chunks=2
 ):
     tokens, width = g.shape
     hidden = mine[0].shape[2]
@@ -922,24 +1160,31 @@
         pltpu.VMEM(mine[2].shape, BF16),
         pltpu.VMEM((3, quarter, width), BF16),
         pltpu.VMEM((quarter, width), BF16),
+        pltpu.VMEM(gates.shape, F32),
+        pltpu.VMEM((tokens, width), F32),
+        pltpu.VMEM((tokens, LANES), F32),
     ]
     scratch += link_sems(chunks) + link_sems(chunks)
-    scratch += [DMA((3,)), DMA(()), DMA((3,)), DMA((2, 3)), DMA((3, 2)), DMA(())]
-    n = len(sums)
+    scratch += [DMA((3,)), DMA(()), DMA((4,)), DMA((2, 3)), DMA((3, 2)), DMA(()), DMA((2,))]
     shapes = [
         jax.ShapeDtypeStruct((tokens, width), F32),
         jax.ShapeDtypeStruct((tokens, LANES), F32),
         jax.ShapeDtypeStruct((3, 2 if exchange else 4, quarter, width), BF16),
         jax.ShapeDtypeStruct((3, 2, quarter, width), BF16),
     ]
-    if n:
-        shapes += deliver_shapes(sums[0])
-        scratch += deliver_sems()
+    if riders == "left":
+        shapes += [left_shape(tokens, width // 2)] * 2
+        scratch += act_sems(3) + act_sems(3)
+    if riders == "right":
+        sums, datdr, dqkv, gains = carried
+        shapes += deliver_shapes(EARLY, sums)
+        shapes += right_shapes(tokens, dqkv.shape[1] + datdr.shape[1], width // 2)
+        scratch += deliver_sems(EARLY) + act_sems(3)
     return pl.pallas_call(
-        functools.partial(experts_backward_kernel, ls, layer, chunks, exchange, n),
+        functools.partial(experts_backward_kernel, ls, layer, chunks, exchange, riders),
         out_shape=shapes,
-        in_specs=[VM] + [HB] * 9 + [VM] + [HB] * n,
-        out_specs=[VM, VM, HB, HB] + [HB] * (2 * n),
+        in_specs=[HB] * (11 + len(carried)),
+        out_specs=[HB] * len(shapes),
         scratch_shapes=scratch,
         compiler_params=pltpu.CompilerParams(
             collective_id=cid, has_side_effects=True, vmem_limit_bytes=62 * MIB
@@ -948,21 +1193,24 @@
             flops=12 * LINE * two * width * wide, bytes_accessed=100 * MIB, transcendentals=0
         ),
         name="experts_backward",
-    )(g, *mine, *theirs, x, gp, up, gates, *sums)
+    )(g, *mine, *theirs, x, gp, up, gates, *carried)
 
 
 def shared_grads_kernel(ls, chunks, *refs):
-    inputs, sums_ref = refs[:6], refs[6]
-    out, near, far = refs[7:10]
-    part, pairb, upb, dnb, small, lhs_ref, rhs_ref, gain_ref, in_sem = refs[10:19]
-    ag_sems, rs_sems, deliver_sem = refs[19:25], refs[25:31], refs[31:]
+    inputs, sums = refs[:6], refs[6:8]
+    out_hbm, near, far, near_late, far_late = refs[8:13]
+    part, pairb, upb, dnb, small, lhs_ref, rhs_ref, gain_ref, out, in_sem, out_sem = refs[13:24]
+    ag_sems, rs_sems = refs[24:30], refs[30:36]
     s = lax.axis_index("section")
     fetch(inputs[0:3], inputs[3:6], s == 0, (lhs_ref, rhs_ref, gain_ref), in_sem)
     l, p = place(lax.axis_index("expert"), ls)
     tokens, rows = lhs_ref.shape[1:]
     half, width = pairb.shape[1:]
-    deliver = Deliver(0, sums_ref, near, far, deliver_sem)
-    greet(l, p, ls, deliver.signals(False), deliver.waits(False))
+    couriers = (
+        Deliver(0, (0, 1, 2), sums[0], near, far, refs[36:40]),
+        Deliver(1, LATE, sums[1], near_late, far_late, refs[40:44]),
+    )
+    greet(l, p, ls, *around())
     fetch(inputs[0:3], inputs[3:6], s == 0, (lhs_ref, rhs_ref, gain_ref), in_sem, wait=True)
     gather = Gather(l, p, ls, out, ag_sems, chunks)
     total = Sum(l, p, ls, part, pairb, upb, dnb, rs_sems, chunks)
@@ -1004,7 +1252,8 @@
 
         @pl.when(k == 0)
         def _():
-            deliver.begin()
+            for courier in couriers:
+                courier.begin()
 
         return carry
 
@@ -1027,11 +1276,16 @@
         return carry
 
     lax.fori_loop(1, LINE, step, 0)
+    saves = moves([(out.at[L], out_hbm.at[L]) for L in range(LINE)], out_sem)
     for L in range(LINE):
         gather.from_pair(L)
+        saves[L].start()
     gather.end()
     total.end()
-    deliver.end()
+    for courier in couriers:
+        courier.end()
+    for copy in saves:
+        copy.wait()
 
 
 def shared_grads(ls, cid, acts, sums, chunks=2):
@@ -1040,13 +1294,17 @@
     width = 512
     half = rows + 32
     buf = pltpu.VMEM((LINE, half, width), BF16)
+    both = pltpu.VMEM((LINE, 2 * half, width), BF16)
+    every = (0, 1, 2)
+    shapes = [jax.ShapeDtypeStruct((LINE, 2 * half, width), BF16)]
+    shapes += deliver_shapes(every, sums[0]) + deliver_shapes(LATE, sums[1])
     return pl.pallas_call(
         functools.partial(shared_grads_kernel, ls, chunks),
-        out_shape=[jax.ShapeDtypeStruct((LINE, 2 * half, width), BF16)] + deliver_shapes(sums),
-        in_specs=[HB] * 7,
-        out_specs=[VM, HB, HB],
+        out_shape=shapes,
+        in_specs=[HB] * 8,
+        out_specs=[HB] * 5,
         scratch_shapes=[
-            pltpu.VMEM((LINE, 2 * half, width), BF16),
+            both,
             buf,
             buf,
             buf,
@@ -1054,25 +1312,27 @@
             pltpu.VMEM(lhs.shape, BF16),
             pltpu.VMEM(rhs.shape, BF16),
             pltpu.VMEM(gains.shape, BF16),
+            both,
             DMA((3,)),
+            DMA((LINE,)),
         ]
         + link_sems(chunks)
         + link_sems(chunks)
-        + deliver_sems(),
+        + deliver_sems(every)
+        + deliver_sems(LATE),
         compiler_params=pltpu.CompilerParams(
-            collective_id=cid, has_side_effects=True, vmem_limit_bytes=60 * MIB
+            collective_id=cid, has_side_effects=True, vmem_limit_bytes=62 * MIB
         ),
         cost_estimate=pl.CostEstimate(flops=0, bytes_accessed=400 * MIB, transcendentals=0),
         name="shared_grads",
-    )(*acts[0], *acts[1], sums)
+    )(*acts[0], *acts[1], *sums)
 
 
 def finish_kernel(*refs):
-    sums, near, far = refs[0:2], refs[2:4], refs[4:6]
-    blocks = refs[6]
-    gate_out, up_out, down_out = refs[7:10]
-    wides = refs[10:14]
-    left, right, wide, cols_in, cols_out, in_sem, out_sem, col_in_sem, col_out_sem = refs[14:]
+    sums, arrived, blocks = refs[0:2], (refs[2:4], refs[4:8]), refs[8]
+    gate_out, up_out, down_out = refs[9:12]
+    wides = refs[12:16]
+    left, right, wide, cols_in, cols_out, in_sem, out_sem, col_in_sem, col_out_sem = refs[16:]
     s, x = lax.axis_index("section"), lax.axis_index("dp")
     quarter, width = left.shape[1:]
     hidden = gate_out.shape[2]
@@ -1086,9 +1346,14 @@
 
             @pl.when(s == layer)
             def _():
-                first = sums[layer].at[kind, x] if h == layer else near[layer].at[kind]
+                near, far = arrived[layer][:2]
+                i = kind
+                if layer == 1 and kind in LATE:
+                    near, far = arrived[layer][2:]
+                    i = LATE.index(kind)
+                first = sums[layer].at[kind, x] if h == layer else near.at[i]
                 a = pltpu.make_async_copy(first, left.at[slot], in_sem.at[0, slot])
-                b = pltpu.make_async_copy(far[layer].at[h, kind], right.at[slot], in_sem.at[1, slot])
+                b = pltpu.make_async_copy(far.at[h, i], right.at[slot], in_sem.at[1, slot])
                 if wait:
                     a.wait()
                     b.wait()
@@ -1154,8 +1419,8 @@
         col_store(b).wait()
 
 
-def finish(sums, near, far, blocks, rows, hidden, widths):
-    quarter, width = near[0].shape[1:]
+def finish(sums, arrived, blocks, rows, hidden, widths):
+    quarter, width = sums[0].shape[2:]
     half = blocks.shape[1] // 2
     block_width = blocks.shape[2]
     down = hidden // 2
@@ -1167,7 +1432,7 @@
             jax.ShapeDtypeStruct((EXP_DEV, down, width), F32),
         ]
         + [jax.ShapeDtypeStruct((rows, w), F32) for w in widths],
-        in_specs=[HB] * 7,
+        in_specs=[HB] * 9,
         out_specs=[HB] * 7,
         scratch_shapes=[
             pltpu.VMEM((2, quarter, width), BF16),
@@ -1180,10 +1445,10 @@
             DMA((2,)),
             DMA((2,)),
         ],
-        compiler_params=pltpu.CompilerParams(vmem_limit_bytes=32 * MIB),
+        compiler_params=pltpu.CompilerParams(vmem_limit_bytes=60 * MIB),
         cost_estimate=pl.CostEstimate(flops=0, bytes_accessed=50 * MIB, transcendentals=0),
         name="finish",
-    )(*sums, *near, *far, blocks)
+    )(*sums, *arrived, blocks)
 
 
 def rope_tables(length):
@@ -1234,34 +1499,34 @@
     return ex / jnp.sum(ex, axis=-1, keepdims=True)
 
 
-def weight_copies(sources, targets, sems):
-    return [
-        pltpu.make_async_copy(a, b, sems.at[i]) for i, (a, b) in enumerate(zip(sources, targets))
-    ]
-
-
 def attention_forward_kernel(*refs):
-    h_ref, allowed_ref, rope_ref, gains_ref = refs[:4]
-    sources = refs[4:8]
-    n1_ref, q_ref, k_ref, v_ref, c_ref, h1_ref, n2_ref = refs[8:15]
-    wq, wk, wv, wo = refs[15:19]
-    copies = weight_copies(sources, (wq, wk, wv, wo), refs[19])
-    for copy in copies:
+    ins, outs, vmem_in, vmem_out = refs[:8], refs[8:15], refs[15:23], refs[23:30]
+    loads, stores = moves(list(zip(ins, vmem_in)), refs[30]), moves(
+        list(zip(vmem_out, outs)), refs[31]
+    )
+    for copy in loads:
         copy.start()
+    h_ref, gains_ref, rope_ref, allowed_ref, wq, wk, wv, wo = vmem_in
+    n1_ref, q_ref, k_ref, v_ref, c_ref, h1_ref, n2_ref = vmem_out
+    for copy in loads[:4]:
+        copy.wait()
     tokens = h_ref.shape[0]
     h = h_ref[...].astype(F32)
     n1_ref[...] = (h * norm_scale(h) * gain_row(gains_ref, 0)).astype(BF16)
+    stores[0].start()
     cosine, sine = rope_ref[0], rope_ref[1]
-    for copy, w, out in ((copies[0], wq, q_ref), (copies[1], wk, k_ref)):
-        copy.wait()
+    for i, (w, out) in enumerate(((wq, q_ref), (wk, k_ref))):
+        loads[4 + i].wait()
         for g in range(w.shape[1] // 256):
             cols = slice(g * 256, (g + 1) * 256)
             x = dot(n1_ref[...], w[:, cols])
             out[:, cols] = jnp.concatenate(
                 [rotated(x[:, :LANES], cosine, sine), rotated(x[:, LANES:], cosine, sine)], axis=1
             ).astype(BF16)
-    copies[2].wait()
+        stores[1 + i].start()
+    loads[6].wait()
     v_ref[...] = dot(n1_ref[...], wv[...]).astype(BF16)
+    stores[3].start()
     allowed = jnp.concatenate([allowed_ref[...]] * GROUP, axis=0) > 0
     heads = []
     for j in range(KEY_VALUE_HEADS):
@@ -1272,144 +1537,73 @@
         c_ref[:, i * LANES : (i + 1) * LANES] = jnp.concatenate(
             heads[2 * i : 2 * i + 2], axis=1
         ).astype(BF16)
-    copies[3].wait()
+    stores[4].start()
+    loads[7].wait()
     h1 = h + dot(c_ref[...], wo[...])
     h1_ref[...] = h1
+    stores[5].start()
     n2_ref[...] = (h1 * norm_scale(h1) * gain_row(gains_ref, 1)).astype(BF16)
+    stores[6].start()
+    for copy in stores:
+        copy.wait()
+
+
+def in_vmem(values):
+    return [pltpu.VMEM(v.shape, v.dtype) for v in values]
 
 
 def attention_forward(h, allowed, rope, weights, gains):
     tokens, width = h.shape
-    kv = weights[1].shape[1]
+    n_q, kv = weights[0].shape[1], weights[1].shape[1]
     shape = jax.ShapeDtypeStruct
+    args = (h, gains, rope, allowed) + tuple(weights)
+    outs = [
+        shape((tokens, width), BF16),
+        shape((tokens, n_q), BF16),
+        shape((tokens, kv), BF16),
+        shape((tokens, kv), BF16),
+        shape((tokens, n_q), BF16),
+        shape((tokens, width), F32),
+        shape((tokens, width), BF16),
+    ]
     return pl.pallas_call(
         attention_forward_kernel,
-        out_shape=[
-            shape((tokens, width), BF16),
-            shape((tokens, weights[0].shape[1]), BF16),
-            shape((tokens, kv), BF16),
-            shape((tokens, kv), BF16),
-            shape((tokens, weights[0].shape[1]), BF16),
-            shape((tokens, width), F32),
-            shape((tokens, width), BF16),
-        ],
-        in_specs=[VM] * 4 + [HB] * 4,
-        out_specs=[VM] * 7,
-        scratch_shapes=[pltpu.VMEM(w.shape, BF16) for w in weights] + [DMA((4,))],
-        compiler_params=pltpu.CompilerParams(vmem_limit_bytes=40 * MIB),
+        out_shape=outs,
+        in_specs=[HB] * 8,
+        out_specs=[HB] * 7,
+        scratch_shapes=in_vmem(args) + in_vmem(outs) + [DMA((8,)), DMA((7,))],
+        compiler_params=pltpu.CompilerParams(vmem_limit_bytes=60 * MIB),
         cost_estimate=pl.CostEstimate(
             flops=2 * tokens * width * 4096, bytes_accessed=16 * MIB, transcendentals=0
         ),
         name="attention_forward",
-    )(h, allowed, rope, gains, *weights)
-
-
-class ActDeliver:
-    def __init__(self, layer, sources, targets, sems):
-        self.layer, self.sources, self.targets = layer, sources, targets
-        self.ns, self.nr, self.fs, self.fr = sems
-        self.s, self.x = lax.axis_index("section"), lax.axis_index("dp")
-        self.tokens = sources[0].shape[0]
-        self.part = targets[0].shape[2]
-
-    def signals(self):
-        owner = self.s == self.layer
-        return (
-            (owner, {"dp": 1 - self.x}),
-            (owner, {"dp": 1 - self.x, "section": 1 - self.layer}),
-            (owner, {"section": 1 - self.layer}),
-        )
-
-    def waits(self):
-        return (self.s >= 0, self.s != self.layer)
-
-    def src(self, i, x):
-        if i in (3, 4):
-            return self.sources[i]
-        return self.sources[i].at[:, pl.ds(pl.multiple_of(x * self.part, self.part), self.part)]
-
-    def dst(self, i, which):
-        lhs, rhs, gains = self.targets
-        rows = pl.ds(pl.multiple_of(which * self.tokens, self.tokens), self.tokens)
-        if i < 3:
-            return lhs.at[i, rows]
-        first = self.sources[4].shape[1]
-        if i == 3:
-            return rhs.at[rows, pl.ds(first, self.sources[3].shape[1])]
-        if i == 4:
-            return rhs.at[rows, pl.ds(0, first)]
-        return gains.at[pl.ds(pl.multiple_of(which * 16, 16), 16)]
-
-    def near(self, i, s):
-        return remote(
-            self.src(i, self.x),
-            self.dst(i, 2 * s + self.x),
-            self.ns.at[i],
-            self.nr.at[i],
-            section=self.layer,
-        )
-
-    def here(self, i):
-        return pltpu.make_async_copy(
-            self.src(i, self.x), self.dst(i, 2 * self.s + self.x), self.ns.at[i]
-        )
-
-    def far(self, i, s, x):
-        return remote(
-            self.src(i, 1 - x),
-            self.dst(i, 2 * s + x),
-            self.fs.at[i],
-            self.fr.at[s, i],
-            dp=1 - self.x,
-            section=self.layer,
-        )
-
-    def begin(self, pieces):
-        for i in pieces:
-            self.far(i, self.s, self.x).start()
-
-            @pl.when(self.s != self.layer)
-            def _():
-                self.near(i, self.s).start()
-
-            @pl.when(self.s == self.layer)
-            def _():
-                self.here(i).start()
-
-    def end(self, pieces):
-        for i in pieces:
-            self.far(i, self.s, self.x).wait_send()
-
-            @pl.when(self.s != self.layer)
-            def _():
-                self.near(i, self.s).wait_send()
-
-            @pl.when(self.s == self.layer)
-            def _():
-                self.here(i).wait()
-                self.near(i, 1 - self.s).wait_recv()
-                for s in range(2):
-                    self.far(i, s, 1 - self.x).wait_recv()
+    )(*args)
 
 
 def attention_backward_kernel(layer, deliver, n_experts, *refs):
-    (g_ref, dn2_ref, dgate_ref, mask_ref, allowed_ref, rope_ref, gains_ref, wr_ref) = refs[:8]
-    h_ref, n1_ref, q_ref, k_ref, v_ref, c_ref, h1_ref, n2_ref = refs[8:16]
-    sources = refs[16:20]
-    din_ref, dqkv_ref, datdr_ref, gain_out = refs[20:24]
-    at = 24
-    targets = refs[at : at + 3] if deliver else ()
+    n_in, n_out = 20, 4
+    ins, outs = refs[:n_in], refs[n_in : n_in + n_out]
+    at = n_in + n_out
+    targets = refs[at : at + 2] if deliver else ()
     at += len(targets)
-    wq, wk, wv, wo, dq, dc_ref = refs[at : at + 6]
-    copies = weight_copies((sources[3],) + tuple(sources[:3]), (wo, wq, wk, wv), refs[at + 6])
-    for copy in copies:
+    vmem_in, vmem_out = refs[at : at + n_in], refs[at + n_in : at + n_in + n_out]
+    at += n_in + n_out
+    dc_ref = refs[at]
+    loads = moves(list(zip(ins, vmem_in)), refs[at + 1])
+    kept = 1 if deliver else n_out
+    stores = moves(list(zip(vmem_out[:kept], outs)), refs[at + 2])
+    for copy in loads:
         copy.start()
+    (n2_ref, wr_ref, mask_ref, dgate_ref, dn2_ref, h1_ref, g_ref, gains_ref) = vmem_in[:8]
+    wo, allowed_ref, q_ref, k_ref, v_ref, c_ref, rope_ref = vmem_in[8:15]
+    wq, wk, wv, h_ref, n1_ref = vmem_in[15:20]
+    din_ref, dqkv_ref, datdr_ref, gain_out = vmem_out
     if deliver:
-        acts = ActDeliver(
-            layer, (n1_ref, c_ref, n2_ref, datdr_ref, dqkv_ref, gain_out), targets, refs[at + 7 :]
-        )
-        greet_all(acts.signals(), acts.waits())
-        acts.begin((0, 1, 2))
+        pieces = right_pieces(datdr_ref, dqkv_ref, gain_out, *targets)
+        acts = ActDeliver(layer, pieces, refs[at + 3 :])
+        greet_all(*around())
+    for copy in loads[:8]:
+        copy.wait()
     tokens, width = h_ref.shape
     lane = lax.broadcasted_iota(jnp.int32, (tokens, LANES), 1)
     gates = routed_softmax(
@@ -1429,8 +1623,11 @@
     dh1 = g_ref[...].astype(F32) + inv2 * (w2 - z2 * jnp.mean(w2 * z2, axis=-1, keepdims=True))
     datdr_ref[:, :width] = dh1.astype(BF16)
     if deliver:
-        acts.begin((3,))
-    copies[0].wait()
+        acts.begin((0,))
+    else:
+        stores[2].start()
+    for copy in loads[8:15]:
+        copy.wait()
     dc_ref[...] = dot_nt(datdr_ref[:, :width], wo[...]).astype(BF16)
     allowed = jnp.concatenate([allowed_ref[...]] * GROUP, axis=0) > 0
     scale = HEAD_SIZE ** (-0.5)
@@ -1458,8 +1655,10 @@
         cols = slice(n_q + n_kv + i * LANES, n_q + n_kv + (i + 1) * LANES)
         dqkv_ref[:, cols] = jnp.concatenate(dvs[2 * i : 2 * i + 2], axis=1).astype(BF16)
     if deliver:
-        acts.begin((4,))
-    for copy in copies[1:]:
+        acts.begin((1,))
+    else:
+        stores[1].start()
+    for copy in loads[15:]:
         copy.wait()
     dn1 = dot_nt(dqkv_ref[:, :n_q], wq[...])
     dn1 = dn1 + dot_nt(dqkv_ref[:, n_q : n_q + n_kv], wk[...])
@@ -1475,16 +1674,26 @@
     gain_out[...] = jnp.concatenate(
         [ga_high, ga - ga_high, gm_high, gm - gm_high, jnp.zeros((12, width), F32)], axis=0
     ).astype(BF16)
+    stores[0].start()
     if deliver:
-        acts.begin((5,))
-        acts.end(range(6))
+        acts.begin((2,))
+        acts.end()
+    else:
+        stores[3].start()
+        for copy in stores[1:]:
+            copy.wait()
+    stores[0].wait()
 
 
 def attention_backward(
     layer, cid, n_experts, g, dn2, dgates, mask, allowed, rope, gains, router, kept, weights, part
 ):
     tokens, width = g.shape
-    n_q, n_kv = weights[0].shape[1], weights[1].shape[1]
+    h, n1, q, keys, values, context, h1, n2 = kept
+    wq, wk, wv, wo = weights
+    args = (n2, router, mask, dgates, dn2, h1, g, gains, wo, allowed, q, keys, values, context)
+    args += (rope, wq, wk, wv, h, n1)
+    n_q, n_kv = wq.shape[1], wk.shape[1]
     shape = jax.ShapeDtypeStruct
     outs = [
         shape((tokens, width), BF16),
@@ -1492,29 +1701,25 @@
         shape((tokens, width + LANES), BF16),
         shape((16, width), BF16),
     ]
-    scratch = [pltpu.VMEM(w.shape, BF16) for w in weights]
-    scratch += [pltpu.VMEM((tokens, n_q), F32), pltpu.VMEM((tokens, n_q), BF16), DMA((4,))]
-    params = dict(vmem_limit_bytes=48 * MIB)
+    scratch = in_vmem(args) + in_vmem(outs)
+    scratch += [pltpu.VMEM((tokens, n_q), BF16), DMA((len(args),)), DMA((4,))]
+    params = dict(vmem_limit_bytes=60 * MIB)
     if part:
-        outs += [
-            shape((3, 4 * tokens, part), BF16),
-            shape((4 * tokens, n_q + 2 * n_kv + width + LANES), BF16),
-            shape((64, part), BF16),
-        ]
-        scratch += [DMA((6,)), DMA((6,)), DMA((6,)), DMA((2, 6))]
+        outs += right_shapes(tokens, n_q + 2 * n_kv + width + LANES, part)
+        scratch += act_sems(3)
         params.update(collective_id=cid, has_side_effects=True)
     return pl.pallas_call(
         functools.partial(attention_backward_kernel, layer, bool(part), n_experts),
         out_shape=outs,
-        in_specs=[VM] * 16 + [HB] * 4,
-        out_specs=[VM] * 4 + [HB] * (len(outs) - 4),
+        in_specs=[HB] * len(args),
+        out_specs=[HB] * len(outs),
         scratch_shapes=scratch,
         compiler_params=pltpu.CompilerParams(**params),
         cost_estimate=pl.CostEstimate(
             flops=4 * tokens * width * 4096, bytes_accessed=20 * MIB, transcendentals=0
         ),
         name="attention_backward",
-    )(g, dn2, dgates, mask, allowed, rope, gains, router, *kept, *weights)
+    )(*args)
 
 
 def swap(value, axis):
@@ -1610,17 +1815,26 @@
     d_out = micro(cotangent)
     d_ins, act_list, expert_list = [None] * 2, [None] * 2, [None] * 2
     for k in (1, 0):
-        sums = (expert_list[1],) if (paired and k == 0) else ()
+        riders, carried = "", ()
+        if paired and k == 1:
+            riders = "left"
+            carried = [kept_list[j][i] for j in range(2) for i in (1, 5, 7)]
+        if paired and k == 0:
+            riders = "right"
+            dqkv, datdr, gain_rows = act_list[1]
+            carried = [expert_list[1], datdr, dqkv, gain_rows]
         got = experts_backward(
-            ls, k, 3 + k, d_out, mine, theirs, *saved_list[k], paired, sums
+            ls, k, 3 + k, d_out, mine, theirs, *saved_list[k], paired, riders, carried
         )
         expert_list[k] = got[2]
-        if sums:
-            delivered = got[4:6]
+        if riders == "left":
+            lefts = got[4:6]
+        if riders == "right":
+            early, rights = got[4:6], got[6:8]
         weights = layer_weights[k]
         d_out, *acts = attention_backward(
             k,
-            6 + k,
+            6,
             n_experts,
             d_out,
             got[0],
@@ -1632,19 +1846,17 @@
             weights[4],
             kept_list[k],
             weights[:4],
-            shard_rows if paired else 0,
+            shard_rows if (paired and k == 0) else 0,
         )
         d_ins[k] = d_out
         act_list[k] = acts
 
     if paired:
-        blocks, near, far = shared_grads(
-            ls, 5, (act_list[0][3:], act_list[1][3:]), expert_list[0]
-        )
+        acts = ((lefts[0], *act_list[0][3:]), (lefts[1], *rights))
+        blocks, *arrived = shared_grads(ls, 5, acts, expert_list)
         gate_grad, up_grad, down_grad, *wide_grads = finish(
             expert_list,
-            (near, delivered[0]),
-            (far, delivered[1]),
+            (*arrived[:2], *early, *arrived[2:]),
             blocks,
             shard_rows,
             w_gate.shape[3],

time: 826 us -> 736 us (0.89)
  local copies, waits for them, and re-layouts: 62.2 us -> 8.45 us
  Pallas kernels: 740 us -> 703 us
    unnamed x132 -> x12, local copies, waits for them, and re-layouts: 56.8 us -> 1.73 us
    pallas_call x2, Pallas kernels: 85.4 us -> 46 us  [attention_backward(): pl.pallas_call(functools.partial(attention_backward_kernel, layer, bool(p...]
    pallas_call x1, Pallas kernels: 77.5 us -> 46.6 us  [start(): pl.pallas_call(functools.partial(start_kernel, ls, count), out_shape=[jax...]
    pallas_call x2, Pallas kernels: 206 us -> 225 us  [experts_backward(): pl.pallas_call(functools.partial(experts_backward_kernel, ls, layer, chun...]
  transfers between devices with their start and end apart: 6 -> 6, of which waited for: 1 -> 0; matrix products, arithmetic and copies ran while one was open for 1% -> 2% of each run, Pallas kernels for 31% -> 31%
where the time goes in v4:
time: 736 us; the launch traced here: 727 us
  Pallas kernels  703 us (96%)
  other arithmetic  9.07 us (1%)
  local copies, waits for them, and re-layouts  8.45 us (1%)
    pallas_call x2, Pallas kernels, experts_backward(): pl.pallas_call(functools.partial(experts_backward_kernel, ls, layer, chun...  225 us
    pallas_call x2, Pallas kernels, experts_forward(): pl.pallas_call(functools.partial(experts_forward_kernel, ls, layer, chunk...  198 us
    pallas_call x1, Pallas kernels, shared_grads(): pl.pallas_call(functools.partial(shared_grads_kernel, ls, chunks), out_sh...  152 us
    pallas_call x1, Pallas kernels, start(): pl.pallas_call(functools.partial(start_kernel, ls, count), out_shape=[jax...  46.6 us
    pallas_call x2, Pallas kernels, attention_backward(): pl.pallas_call(functools.partial(attention_backward_kernel, layer, bool(p...  46 us
    pallas_call x1, Pallas kernels, finish(): pl.pallas_call(finish_kernel, out_shape=[jax.ShapeDtypeStruct((EXP_DEV, r...  17.9 us
    pallas_call x2, Pallas kernels, attention_forward(): pl.pallas_call(attention_forward_kernel, out_shape=outs, in_specs=[HB] *...  16.8 us
  transfers between devices with their start and end apart: 6, of which 0 were waited for; matrix products, arithmetic and copies ran while one was open for 2% of the time, Pallas kernels for 31%

profile of v4, /device:TPU:17, one launch (start us, length us, event | category | flops | bytes accessed | tf_op | source)
XLA Modules:
  0.0 726.9 jit_solution(14504554241920392983)
XLA Ops:
  0.6 0.0 copy-start
  0.7 0.7 collective-permute-start.1
  1.4 0.1 collective-permute-start.2
  1.5 0.4 collective-permute-start.3
  1.9 0.7 dynamic-slice_bitcast_fusion.3
  2.6 0.1 collective-permute-start
  2.7 0.1 pad.15.clone
  2.8 0.7 fusion.4
  3.5 0.7 fusion.3.refs_3_.refs_9_
  4.2 0.8 dynamic-slice_bitcast_fusion.1.refs_0_.refs_18_
  4.9 1.8 dynamic-slice_bitcast_fusion.refs_0_.refs_6_
  6.7 1.4 maximum_maximum_fusion.refs_6_.refs_15_
  8.1 0.9 copy.40
  9.0 0.7 pad.4.refs_5_.refs_14_
  9.8 0.0 collective-permute-done
  9.8 0.1 copy.39
  9.9 0.4 fusion.1
  10.3 0.6 pad_maximum_fusion.refs_0_.refs_2_
  11.0 46.6 %start.1 = (bf16[4,256,256]{2,1,0:T(8,128)(2,1)}, bf16[1536,1536]{1,0:T(8,128)(2,1)}, bf16[1536,512]{1,0:T(8,128)(2,1)}, bf16[1536,512]{1,0:T(8,128)(2,1)}, bf16...) custom-call(bf16[128,256]{1,0:T(8,128)(2,1)} %pad_maximum_fusion.refs_0_.refs_2_, ...), custom_call_target="tpu_custom_call" | custom-call | bytes 104857600 | tf_op jit(solution)/shard_map/start/pallas_call | solution.py:545
  57.6 8.4 %attention_forward.2 = (bf16[128,1536]{1,0:T(8,128)(2,1)}, bf16[128,1536]{1,0:T(8,128)(2,1)}, bf16[128,512]{1,0:T(8,128)(2,1)}, bf16[128,512]{1,0:T(8,128)(2,1)}...) custom-call(bf16[128,1536]{1,0:T(8,128)(2,1)} %dynamic-slice_bitcast_fusion.1.refs_0_.refs_18_, ...), custom_call_target="tpu_custom_call" | custom-call | flops 1610612736 | bytes 16777216 | tf_op jit(solution)/shard_map/attention_forward/pallas_call | solution.py:1569
  66.0 0.0 collective-permute-done.1.refs_7_.refs_4_
  66.0 0.0 collective-permute-done.2.refs_8_.refs_5_
  66.0 0.0 collective-permute-done.3
  66.0 102.2 %experts_forward.2 = (bf16[128,1536]{1,0:T(8,128)(2,1)}, bf16[4,256,1536]{2,1,0:T(8,128)(2,1)}, bf16[4,256,1536]{2,1,0:T(8,128)(2,1)}, bf16[4,256,1536]{2,1,0:T(...) custom-call(bf16[128,1536]{1,0:T(8,128)(2,1)} %get-tuple-element.85., ...), custom_call_target="tpu_custom_call" | custom-call | flops 14495514624 | bytes 62914560 | tf_op jit(solution)/shard_map/experts_forward/pallas_call | solution.py:751
  168.3 8.4 %attention_forward.3 = (bf16[128,1536]{1,0:T(8,128)(2,1)}, bf16[128,1536]{1,0:T(8,128)(2,1)}, bf16[128,512]{1,0:T(8,128)(2,1)}, bf16[128,512]{1,0:T(8,128)(2,1)}...) custom-call(bf16[128,1536]{1,0:T(8,128)(2,1)} %get-tuple-element.89.refs_0_.refs_18_, ...), custom_call_target="tpu_custom_call" | custom-call | flops 1610612736 | bytes 16777216 | tf_op jit(solution)/shard_map/attention_forward/pallas_call | solution.py:1569
  176.7 95.8 %experts_forward.3 = (bf16[128,1536]{1,0:T(8,128)(2,1)}, bf16[4,256,1536]{2,1,0:T(8,128)(2,1)}, bf16[4,256,1536]{2,1,0:T(8,128)(2,1)}, bf16[4,256,1536]{2,1,0:T(8,128)(2,1)}, f32[4,256,128]{2,1,0:T(8,128)}) custom-call(bf16[128,1536]{1,0:T(8,128)(2,1)} %get-tuple-element.95.refs_0_.refs_16_, f32[128,1536]{1,0:T(8,128)} %get-tuple-element.96.refs_1_.refs_5_, ...), custom_call_target="tpu_custom_call" | custom-call | flops 14495514624 | bytes 62914560 | tf_op jit(solution)/shard_map/experts_forward/pallas_call | solution.py:751
  272.5 111.4 %experts_backward.2 = (f32[128,1536]{1,0:T(8,128)}, f32[128,128]{1,0:T(8,128)}, bf16[3,2,384,1536]{3,2,1,0:T(8,128)(2,1)}, bf16[3,2,384,1536]{3,2,1,0:T(8,128)(2...) custom-call(bf16[128,1536]{1,0:T(8,128)(2,1)} %dynamic-slice_bitcast_fusion.refs_0_.refs_6_, ...), custom_call_target="tpu_custom_call" | custom-call | flops 28991029248 | bytes 104857600 | tf_op jit(solution)/shard_map/experts_backward/pallas_call | solution.py:1183
  383.9 14.7 %attention_backward.2 = (bf16[128,1536]{1,0:T(8,128)(2,1)}, bf16[128,2560]{1,0:T(8,128)(2,1)}, bf16[128,1664]{1,0:T(8,128)(2,1)}, bf16[16,1536]{1,0:T(8,128)(2,1)}) custom-call(bf16[128,1536]{1,0:T(8,128)(2,1)} %get-tuple-element.95.refs_0_.refs_16_, bf16[1536,128]{1,0:T(8,128)(2,1)} %get-tuple-element.97.refs_3_.refs_1_, ...), custom_call_target="tpu_custom_call" | custom-call | flops 3221225472 | bytes 20971520 | tf_op jit(solution)/shard_map/attention_backward/pallas_call | solution.py:1711
  398.7 114.0 %experts_backward.3 = (f32[128,1536]{1,0:T(8,128)}, f32[128,128]{1,0:T(8,128)}, bf16[3,2,384,1536]{3,2,1,0:T(8,128)(2,1)}, bf16[3,2,384,1536]{3,2,1,0:T(8,128)(2...) custom-call(bf16[128,1536]{1,0:T(8,128)(2,1)} %get-tuple-element.112, ...), custom_call_target="tpu_custom_call" | custom-call | flops 28991029248 | bytes 104857600 | tf_op jit(solution)/shard_map/experts_backward/pallas_call | solution.py:1183
  512.6 0.0 copy-start.3
  512.6 0.0 copy-start.2
  512.7 31.2 %attention_backward.3 = (bf16[128,1536]{1,0:T(8,128)(2,1)}, bf16[128,2560]{1,0:T(8,128)(2,1)}, bf16[128,1664]{1,0:T(8,128)(2,1)}, bf16[16,1536]{1,0:T(8,128)(2,1...) custom-call(bf16[128,1536]{1,0:T(8,128)(2,1)} %get-tuple-element.85.refs_0_.refs_13_, ...), custom_call_target="tpu_custom_call" | custom-call | flops 3221225472 | bytes 20971520 | tf_op jit(solution)/shard_map/attention_backward/pallas_call | solution.py:1711
  543.9 1.1 select_bitcast_fusion
  545.0 2.4 collective-permute-start.5
  547.4 0.8 select_bitcast_fusion.1
  548.2 152.4 %shared_grads.1 = (bf16[4,1600,512]{2,1,0:T(8,128)(2,1)}, bf16[3,384,1536]{2,1,0:T(8,128)(2,1)}, bf16[2,3,384,1536]{3,2,1,0:T(8,128)(2,1)}, bf16[1,384,1536]{2,1,0:T(8,128)(2,1)}, bf16[2,1,384,1536]{3,2,1,0:T(8,128)(2,1)}) custom-call(bf16[3,512,768]{2,1,0:T(8,128)(2,1)} %get-tuple-element.127.refs_0_, bf16[512,4224]{1,0:T(8,128)(2,1)} %get-tuple-element.128.refs_1_, ...), custom_call_target="tpu_custom_call" | custom-call | bytes 419430400 | tf_op jit(solution)/shard_map/shared_grads/pallas_call | solution.py:1301
  700.6 1.0 slice_convert_fusion
  701.6 0.1 reshape.198
  701.8 1.1 collective-permute-start.4
  702.9 0.8 copy.42
  703.7 0.5 slice_reduce_fusion
  704.2 0.6 broadcast_in_dim_squeeze.6
  704.8 0.6 broadcast_in_dim_squeeze.7
  705.3 17.9 %finish.1 = (f32[3,768,512]{2,1,0:T(8,128)}, f32[3,768,512]{2,1,0:T(8,128)}, f32[3,256,1536]{2,1,0:T(8,128)}, f32[768,1536]{1,0:T(8,128)}, f32[768,512]{1,0:T(8,...) custom-call(bf16[3,2,384,1536]{3,2,1,0:T(8,128)(2,1)} %get-tuple-element.133.refs_6_.refs_0_, ...), custom_call_target="tpu_custom_call" | custom-call | bytes 52428800 | tf_op jit(solution)/shard_map/finish/pallas_call | solution.py:1427
  723.2 0.0 collective-permute-done.5
  723.2 2.1 maximum_select_fusion.1
  725.4 0.0 collective-permute-done.4
  725.4 1.0 maximum_select_fusion
  (12 shorter events, 0.1 us)
Async XLA Ops:
  0.6 3.5 copy-start
  0.7 65.4 %collective-permute-start.1 = (bf16[3,1536,512]{2,1,0:T(8,128)(2,1)}, bf16[3,1536,512]{2,1,0:T(8,128)(2,1)}, u32[]{:S(2)}, u32[]{:S(2)}) collective-permute-start(bf16[3,1536,512]{2,1,0:T(8,128)(2,1)} %bitcast.58), channel_id=1, source_target_pairs={{0,16},{16,0},{1,17},{17,1},{2,18},{18,2},{3,19},{19,3},{4,20},{20... | collective-permute-start | bytes 14155784 | tf_op jit(solution)/shard_map/ppermute | solution.py:1726
  1.4 64.6 %collective-permute-start.2 = (bf16[3,1536,512]{2,1,0:T(8,128)(2,1)}, bf16[3,1536,512]{2,1,0:T(8,128)(2,1)}, u32[]{:S(2)}, u32[]{:S(2)}) collective-permute-start(bf16[3,1536,512]{2,1,0:T(8,128)(2,1)} %bitcast.63), channel_id=1, source_target_pairs={{0,16},{16,0},{1,17},{17,1},{2,18},{18,2},{3,19},{19,3},{4,20},{20... | collective-permute-start | bytes 14155784 | tf_op jit(solution)/shard_map/ppermute | solution.py:1726
  1.5 64.5 %collective-permute-start.3 = (bf16[3,512,1536]{2,1,0:T(8,128)(2,1)}, bf16[3,512,1536]{2,1,0:T(8,128)(2,1)}, u32[]{:S(2)}, u32[]{:S(2)}) collective-permute-start(bf16[3,512,1536]{2,1,0:T(8,128)(2,1)} %bitcast.68), channel_id=1, source_target_pairs={{0,16},{16,0},{1,17},{17,1},{2,18},{18,2},{3,19},{19,3},{4,20},{20... | collective-permute-start | bytes 14155784 | tf_op jit(solution)/shard_map/ppermute | solution.py:1726
  2.6 7.1 collective-permute-start
  512.6 31.3 %copy-start.3 = (bf16[128,1536]{1,0:T(8,128)(2,1)S(1)}, bf16[128,1536]{1,0:T(8,128)(2,1)}, u32[]{:S(2)}) copy-start(bf16[128,1536]{1,0:T(8,128)(2,1)} %get-tuple-element.112.refs_0_.refs_6_) | copy-start | bytes 1179652
  512.6 34.8 %copy-start.2 = (bf16[128,1536]{1,0:T(8,128)(2,1)S(1)}, bf16[128,1536]{1,0:T(8,128)(2,1)}, u32[]{:S(2)}) copy-start(bf16[128,1536]{1,0:T(8,128)(2,1)} %get-tuple-element.89.refs_0_.refs_18_) | copy-start | bytes 1179652
  512.7 34.8 %copy-start.4 = (bf16[128,1536]{1,0:T(8,128)(2,1)S(1)}, bf16[128,1536]{1,0:T(8,128)(2,1)}, u32[]{:S(2)}) copy-start(bf16[128,1536]{1,0:T(8,128)(2,1)} %get-tuple-element.98) | copy-start | bytes 1179652
  545.0 178.3 %collective-permute-start.5 = (bf16[128,1536]{1,0:T(8,128)(2,1)S(1)}, bf16[128,1536]{1,0:T(8,128)(2,1)}, u32[]{:S(2)}, u32[]{:S(2)}) collective-permute-start(bf16[128,1536]{1,0:T(8,128)(2,1)S(1)} %get-tuple-element.187), channel_id=1, source_target_pairs={{0,16},{16,0},{1,17},{17,1},{2,18},{18,2},{3,19},{19,3},{4,20},{20... | collective-permute-start | bytes 1179656 | tf_op jit(solution)/shard_map/ppermute | solution.py:1726
  701.8 23.6 %collective-permute-start.4 = (bf16[128,1536]{1,0:T(8,128)(2,1)}, bf16[128,1536]{1,0:T(8,128)(2,1)S(1)}, u32[]{:S(2)}, u32[]{:S(2)}) collective-permute-start(bf16[128,1536]{1,0:T(8,128)(2,1)} %get-tuple-element.189), channel_id=1, source_target_pairs={{0,16},{16,0},{1,17},{17,1},{2,18},{18,2},{3,19},{19,3},{4,20},{20... | collective-permute-start | bytes 1179656 | tf_op jit(solution)/shard_map/ppermute | solution.py:1726
  705.3 21.0 %copy-start.1 = (bf16[2,128,1536]{2,1,0:T(8,128)(2,1)S(1)}, bf16[2,128,1536]{2,1,0:T(8,128)(2,1)}, u32[]{:S(2)}) copy-start(bf16[2,128,1536]{2,1,0:T(8,128)(2,1)} %param.15) | copy-start | bytes 2359300

commit v5 on v4

--- a/solution.py
+++ b/solution.py
@@ -49,19 +49,26 @@
     )
 
 
+def sum_order(l, j):
+    inner = jnp.where(j == 0, 3, jnp.where(j == 1, 1, jnp.where(j == 2, 2, 0)))
+    return near_first(l, jnp.where((l == 0) | (l == LINE - 1), LINE - 1 - j, inner))
+
+
 def signal(**where):
     pl.semaphore_signal(
         pltpu.get_barrier_semaphore(), inc=1, device_id=where, device_id_type=MESH
     )
 
 
-def greet_all(signals, waits):
+def send_greetings(signals):
     for wanted, where in signals:
 
         @pl.when(wanted)
         def _(where=where):
             signal(**where)
 
+
+def await_greetings(waits):
     count = sum(jnp.where(wanted, 1, 0) for wanted in waits)
 
     @pl.when(count > 0)
@@ -69,13 +76,19 @@
         pl.semaphore_wait(pltpu.get_barrier_semaphore(), count)
 
 
-def greet(l, p, ls, signals=(), waits=()):
+def neighbours(l, p, ls, signals=(), waits=()):
     near = (
         (l >= 0, {"expert": index_of(l, 1 - p, ls)}),
         (l > 0, {"expert": index_of(l - 1, p, ls)}),
         (l < LINE - 1, {"expert": index_of(l + 1, p, ls)}),
     )
-    greet_all(near + tuple(signals), tuple(w for w, _ in near) + tuple(waits))
+    return near + tuple(signals), tuple(w for w, _ in near) + tuple(waits)
+
+
+def greet(l, p, ls, signals=(), waits=()):
+    signals, waits = neighbours(l, p, ls, signals, waits)
+    send_greetings(signals)
+    await_greetings(waits)
 
 
 def around():
@@ -246,60 +259,65 @@
         ].astype(F32)
 
     def pass_on(self, L, write):
+        for c in range(self.chunks):
+            self.pass_chunk(L, c, write)
+
+    def pass_chunk(self, L, c, write):
         l = self.l
-        for c in range(self.chunks):
-            self.pair(L, c).wait_recv()
-
-            @pl.when(L > l)
+        self.pair(L, c).wait_recv()
+        mine = self.mine(self.p, c)
+        part = self.part(c)
+
+        @pl.when(L > l)
+        def _():
+            @pl.when(l == 0)
             def _():
-                @pl.when(l == 0)
-                def _():
-                    self.buf[L, self.mine(self.p, c)] = self.total(L, c).astype(BF16)
-
-                @pl.when(l > 0)
-                def _():
-                    self.up(L, c).wait_recv()
-                    here = self.total(L, c) + self.upb[L, self.part(c)].astype(F32)
-                    self.buf[L, self.mine(self.p, c)] = here.astype(BF16)
-
-                self.up(L, c).start()
-
-            @pl.when(L < l)
+                self.buf[L, mine] = self.total(L, c).astype(BF16)
+
+            @pl.when(l > 0)
             def _():
-                @pl.when(l == LINE - 1)
-                def _():
-                    self.buf[L, self.mine(self.p, c)] = self.total(L, c).astype(BF16)
-
-                @pl.when(l < LINE - 1)
-                def _():
-                    self.dn(L, c).wait_recv()
-                    here = self.total(L, c) + self.dnb[L, self.part(c)].astype(F32)
-                    self.buf[L, self.mine(self.p, c)] = here.astype(BF16)
-
-                self.dn(L, c).start()
-
-            @pl.when(L == l)
+                self.up(L, c).wait_recv()
+                here = self.total(L, c) + self.upb[L, part].astype(F32)
+                self.buf[L, mine] = here.astype(BF16)
+
+            self.up(L, c).start()
+
+        @pl.when(L < l)
+        def _():
+            @pl.when(l == LINE - 1)
             def _():
-                @pl.when(l == 0)
-                def _():
-                    self.dn(L, c).wait_recv()
-                    write(c, self.total(L, c) + self.dnb[L, self.part(c)].astype(F32))
-
-                @pl.when(l == LINE - 1)
-                def _():
-                    self.up(L, c).wait_recv()
-                    write(c, self.total(L, c) + self.upb[L, self.part(c)].astype(F32))
-
-                @pl.when((l > 0) & (l < LINE - 1))
-                def _():
-                    self.up(L, c).wait_recv()
-                    self.dn(L, c).wait_recv()
-                    write(
-                        c,
-                        self.total(L, c)
-                        + self.upb[L, self.part(c)].astype(F32)
-                        + self.dnb[L, self.part(c)].astype(F32),
-                    )
+                self.buf[L, mine] = self.total(L, c).astype(BF16)
+
+            @pl.when(l < LINE - 1)
+            def _():
+                self.dn(L, c).wait_recv()
+                here = self.total(L, c) + self.dnb[L, part].astype(F32)
+                self.buf[L, mine] = here.astype(BF16)
+
+            self.dn(L, c).start()
+
+        @pl.when(L == l)
+        def _():
+            @pl.when(l == 0)
+            def _():
+                self.dn(L, c).wait_recv()
+                write(c, self.total(L, c) + self.dnb[L, part].astype(F32))
+
+            @pl.when(l == LINE - 1)
+            def _():
+                self.up(L, c).wait_recv()
+                write(c, self.total(L, c) + self.upb[L, part].astype(F32))
+
+            @pl.when((l > 0) & (l < LINE - 1))
+            def _():
+                self.up(L, c).wait_recv()
+                self.dn(L, c).wait_recv()
+                write(
+                    c,
+                    self.total(L, c)
+                    + self.upb[L, part].astype(F32)
+                    + self.dnb[L, part].astype(F32),
+                )
 
     def end(self):
         l = self.l
@@ -409,12 +427,13 @@
 
 
 def start_kernel(ls, count, *refs):
-    picks_ref, shards = refs[0], refs[1 : 1 + count]
-    masks, wholes = refs[1 + count], refs[2 + count : 2 + 2 * count]
-    at = 2 + 2 * count
-    sems = [refs[at + 6 * i : at + 6 * i + 6] for i in range(3)]
-    own_sem, in_sem, out_sem, xs, xr, cs, cr, far_sem = refs[at + 18 : at + 26]
-    bounce, big = refs[at + 26 : at + 26 + count], refs[at + 26 + count :]
+    picks_ref, cot_ref, shards = refs[0], refs[1], refs[2 : 2 + count]
+    masks, cot_out, wholes = refs[2 + count], refs[3 + count], refs[4 + count : 4 + 2 * count]
+    at = 4 + 2 * count
+    sems = [refs[at + 6 * i : at + 6 * i + 6] for i in range(4)]
+    own_sem, in_sem, out_sem, xs, xr, cs, cr, far_sem, cot_sem = refs[at + 24 : at + 33]
+    bounce, big = refs[at + 33 : at + 33 + count], refs[at + 33 + count : at + 35 + count]
+    cots = refs[at + 35 + count]
     e = lax.axis_index("expert")
     s, x = lax.axis_index("section"), lax.axis_index("dp")
     l, p = place(e, ls)
@@ -467,12 +486,18 @@
         picks_ref, masks.at[l, pl.ds(pl.multiple_of(p * half, half), half)], own_sem
     )
     own.start()
+    own_cot = pltpu.make_async_copy(
+        cot_ref, cots.at[l, pl.ds(pl.multiple_of(p * half, half), half)], cot_sem.at[0]
+    )
+    own_cot.start()
     own.wait()
+    own_cot.wait()
     greet(l, p, ls, *around())
     order = large + tuple(i for i in range(count) if i not in large)
     gathers = [Gather(l, p, ls, big[i], sems[i], 2) for i in range(2)]
     picked = Gather(l, p, ls, masks, sems[2], 1)
     picked.begin()
+    cot = Gather(l, p, ls, cots, sems[3], 2)
 
     @pl.when(src)
     def _():
@@ -488,6 +513,10 @@
             loads[i].wait()
             stores[i].start()
 
+    @pl.when(jnp.logical_not(src))
+    def _():
+        cot.begin()
+
     def step(k, carry):
         picked.arrive(k)
 
@@ -496,12 +525,26 @@
             for g in gathers:
                 g.arrive(k)
 
+        @pl.when(jnp.logical_not(src))
+        def _():
+            cot.arrive(k)
+
+        return carry
+
+    def cot_step(k, carry):
+        cot.arrive(k)
         return carry
 
     lax.fori_loop(1, LINE, step, 0)
     for L in range(LINE):
         picked.from_pair(L)
     picked.end()
+
+    @pl.when(src)
+    def _():
+        cot.begin()
+
+    cot_save = pltpu.make_async_copy(cots, cot_out, cot_sem.at[1])
 
     @pl.when(src)
     def _():
@@ -513,6 +556,7 @@
                 gathers[g].from_pair(L)
                 core_large(i, L).start()
                 kept(i, L).start()
+        lax.fori_loop(1, LINE, cot_step, 0)
         for g in gathers:
             g.end()
         for i in order:
@@ -536,32 +580,44 @@
             for L in range(LINE):
                 core_large(i, L).wait_recv()
 
-
-def start(ls, cid, picks, shards):
+    for L in range(LINE):
+        cot.from_pair(L)
+    cot_save.start()
+    cot.end()
+    cot_save.wait()
+
+
+def start(ls, cid, picks, cot, shards):
     count = len(shards)
     rows, width = picks.shape
     shard_rows, wide = shards[0].shape
+    gathered = (LINE, 2 * rows, cot.shape[1])
     buf = pltpu.VMEM((LINE, shard_rows // LINE, wide), BF16)
     return pl.pallas_call(
         functools.partial(start_kernel, ls, count),
-        out_shape=[jax.ShapeDtypeStruct((LINE, 2 * rows, width), BF16)] + spread_shapes(shards),
-        in_specs=[VM] + [HB] * count,
-        out_specs=[VM] + [HB] * count,
+        out_shape=[
+            jax.ShapeDtypeStruct((LINE, 2 * rows, width), BF16),
+            jax.ShapeDtypeStruct(gathered, BF16),
+        ]
+        + spread_shapes(shards),
+        in_specs=[VM] + [HB] * (1 + count),
+        out_specs=[VM] + [HB] * (1 + count),
         scratch_shapes=link_sems(2)
         + link_sems(2)
         + link_sems(1)
+        + link_sems(2)
         + [DMA(())]
         + [DMA((count,))] * 4
         + [DMA((2, count))] * 2
-        + [DMA((3, 2, LINE))]
+        + [DMA((3, 2, LINE)), DMA((2,))]
         + [pltpu.VMEM(w.shape, w.dtype) for w in shards]
-        + [buf, buf],
+        + [buf, buf, pltpu.VMEM(gathered, BF16)],
         compiler_params=pltpu.CompilerParams(
             collective_id=cid, has_side_effects=True, vmem_limit_bytes=60 * MIB
         ),
         cost_estimate=pl.CostEstimate(flops=0, bytes_accessed=100 * MIB, transcendentals=0),
         name="start",
-    )(picks, *shards)
+    )(picks, cot, *shards)
 
 
 def fetch(mine, theirs, own_layer, dst, sems, wait=False):
@@ -602,48 +658,52 @@
     return lax.dot_general(a, b, (((0,), (0,)), ((), ())), preferred_element_type=F32)
 
 
-def experts_forward_kernel(ls, layer, chunks, n_spread, *refs):
-    inputs = refs[:4]
-    mine, theirs = refs[4:7], refs[7:10]
-    shards = refs[10 : 10 + n_spread]
-    at = 10 + n_spread
-    out_hbm, x_out, gp_out, up_out, gates_out = refs[at : at + 5]
-    wholes = refs[at + 5 : at + 5 + n_spread]
-    at = at + 5 + n_spread
-    xb, gpb, upre, part, pairb, upb, dnb, wg, wu, wd, act = refs[at : at + 11]
-    at += 11
-    ag_sems, rs_sems = refs[at : at + 6], refs[at + 6 : at + 12]
-    at += 12
-    w_sem, own_sem, save_sem, in_sem, out_sem = refs[at : at + 5]
-    h1_ref, mask_ref, wr_ref, gates_ref, out_ref = refs[at + 5 : at + 10]
-    spread_sem = refs[at + 10 :]
+def forward_kernel(ls, layer, chunks, n_spread, *refs):
+    refs = list(refs)
+
+    def take(count):
+        out = refs[:count]
+        del refs[:count]
+        return out
+
+    ins, mine, theirs, shards = take(10), take(3), take(3), take(n_spread)
+    outs = take(7)
+    out_hbm, x_out, gp_out, up_out, gates_out = take(5)
+    wholes = take(n_spread)
+    vmem_in, vmem_out = take(10), take(7)
+    in_sem, keep_sem = take(2)
+    xb, gpb, upre, part, pairb, upb, dnb, wg, wu, wd, act = take(11)
+    ag_sems, rs_sems = take(6), take(6)
+    w_sem, save_sem, out_sem, gates_ref, out_ref = take(5)
+    spread_scratch = refs
 
     e = lax.axis_index("expert")
     s = lax.axis_index("section")
     l, p = place(e, ls)
     half = out_ref.shape[0]
     own_layer = s == layer
-    own = pltpu.make_async_copy(
-        inputs[0], xb.at[l, pl.ds(pl.multiple_of(p * half, half), half)], own_sem
-    )
-    own.start()
-    loads = moves(list(zip(inputs[1:], (h1_ref, mask_ref, wr_ref))), in_sem)
-    for copy in loads[1:]:
+    signals, waits = neighbours(l, p, ls, *(around() if n_spread else ()))
+    send_greetings(signals)
+    loads = moves(list(zip(ins, vmem_in)), in_sem)
+    for copy in loads:
         copy.start()
     fetch(mine, theirs, own_layer, (wg, wu, wd), w_sem)
-    loads[0].start()
-    own.wait()
-    signals = waits = ()
+    stores = moves(list(zip(vmem_out, outs)), keep_sem)
+    n2_ref, h1_ref = vmem_out[6], vmem_out[5]
+    mask_ref, wr_ref = vmem_in[8:]
     if n_spread:
-        spread = Spread(1 - layer, shards, wholes, spread_sem)
-        signals, waits = around()
-    greet(l, p, ls, signals, waits)
+        spread = Spread(1 - layer, shards, wholes, spread_scratch)
+        await_greetings(waits)
+        spread.begin()
+    attend_forward(vmem_in[:8], vmem_out, loads, stores)
+    own = pl.ds(pl.multiple_of(p * half, half), half)
+    xb[l, own, :] = n2_ref[...]
+    if not n_spread:
+        await_greetings(waits)
     gather = Gather(l, p, ls, xb, ag_sems, chunks)
     total = Sum(l, p, ls, part, pairb, upb, dnb, rs_sems, chunks)
     gather.begin()
-    if n_spread:
-        spread.begin()
-    for copy in loads:
+    for copy in loads[8:]:
         copy.wait()
     fetch(mine, theirs, own_layer, (wg, wu, wd), w_sem, wait=True)
 
@@ -683,15 +743,15 @@
         return carry
 
     lax.fori_loop(0, LINE, step, 0)
-    for k in range(LINE):
-        total.give(near_first(l, LINE - 1 - k))
+    for j in range(LINE):
+        total.give(sum_order(l, j))
 
     def write(c, value):
         rows = pl.ds(c * (half // chunks), half // chunks)
         out_ref[rows, :] = (h1_ref[rows, :] + value).astype(BF16)
 
     def back(j, carry):
-        total.pass_on(near_first(l, LINE - 1 - j), write)
+        total.pass_on(sum_order(l, j), write)
         return carry
 
     lax.fori_loop(0, LINE, back, 0)
@@ -705,63 +765,81 @@
     for L in range(LINE):
         for copy in save(L):
             copy.wait()
+    for copy in stores:
+        copy.wait()
     for copy in last:
         copy.wait()
 
 
-def experts_forward(ls, layer, cid, n2, h1, mask, wr, mine, theirs, shards=(), chunks=2):
-    tokens, width = n2.shape
+def in_vmem(values):
+    return [pltpu.VMEM(v.shape, v.dtype) for v in values]
+
+
+def forward(
+    ls, layer, cid, h, allowed, rope, weights, masks, mine, theirs, riders=(), chunks=2
+):
+    wq, wk, wv, wo, router, gains = weights
+    tokens, width = h.shape
     hidden = mine[0].shape[2]
     wide = EXP_DEV * hidden
     two = 2 * tokens
     mine = (mine[0], mine[1], mine[2].reshape(wide, width))
     theirs = (theirs[0], theirs[1], theirs[2].reshape(wide, width))
-    n = len(shards)
-    outs = [
-        jax.ShapeDtypeStruct((tokens, width), BF16),
-        jax.ShapeDtypeStruct((LINE, two, width), BF16),
-        jax.ShapeDtypeStruct((LINE, two, wide), BF16),
-        jax.ShapeDtypeStruct((LINE, two, wide), BF16),
-        jax.ShapeDtypeStruct((LINE, two, LANES), F32),
-    ] + spread_shapes(shards)
-    scratch = [
+    n = len(riders)
+    shape = jax.ShapeDtypeStruct
+    args = (h, gains, rope, allowed, wq, wk, wv, wo, masks, router)
+    kept = [
+        shape((tokens, width), BF16),
+        shape((tokens, wq.shape[1]), BF16),
+        shape((tokens, wk.shape[1]), BF16),
+        shape((tokens, wv.shape[1]), BF16),
+        shape((tokens, wq.shape[1]), BF16),
+        shape((tokens, width), F32),
+        shape((tokens, width), BF16),
+    ]
+    saved = [
+        shape((tokens, width), BF16),
+        shape((LINE, two, width), BF16),
+        shape((LINE, two, wide), BF16),
+        shape((LINE, two, wide), BF16),
+        shape((LINE, two, LANES), F32),
+    ]
+    buf = pltpu.VMEM((LINE, tokens, width), BF16)
+    scratch = in_vmem(args) + in_vmem(kept) + [DMA((10,)), DMA((7,))]
+    scratch += [
         pltpu.VMEM((LINE, two, width), BF16),
         pltpu.VMEM((LINE, two, wide), BF16),
         pltpu.VMEM((LINE, two, wide), BF16),
         pltpu.VMEM((LINE, two, width), BF16),
-        pltpu.VMEM((LINE, tokens, width), BF16),
-        pltpu.VMEM((LINE, tokens, width), BF16),
-        pltpu.VMEM((LINE, tokens, width), BF16),
-        pltpu.VMEM(mine[0].shape, BF16),
-        pltpu.VMEM(mine[1].shape, BF16),
-        pltpu.VMEM(mine[2].shape, BF16),
-        pltpu.VMEM((two, wide), BF16),
+        buf,
+        buf,
+        buf,
     ]
+    scratch += in_vmem(mine) + [pltpu.VMEM((two, wide), BF16)]
     scratch += link_sems(chunks) + link_sems(chunks)
-    scratch += [DMA((3,)), DMA(()), DMA((3, LINE)), DMA((3,)), DMA((2,))]
     scratch += [
-        pltpu.VMEM((tokens, width), F32),
-        pltpu.VMEM(mask.shape, BF16),
-        pltpu.VMEM(wr.shape, BF16),
+        DMA((3,)),
+        DMA((3, LINE)),
+        DMA((2,)),
         pltpu.VMEM((LINE, two, LANES), F32),
         pltpu.VMEM((tokens, width), BF16),
     ]
     if n:
-        scratch += spread_scratch(shards)
+        scratch += spread_scratch(riders)
     return pl.pallas_call(
-        functools.partial(experts_forward_kernel, ls, layer, chunks, n),
-        out_shape=outs,
-        in_specs=[HB] * (10 + n),
-        out_specs=[HB] * (5 + n),
+        functools.partial(forward_kernel, ls, layer, chunks, n),
+        out_shape=kept + saved + spread_shapes(riders),
+        in_specs=[HB] * (16 + n),
+        out_specs=[HB] * (12 + n),
         scratch_shapes=scratch,
         compiler_params=pltpu.CompilerParams(
-            collective_id=cid, has_side_effects=True, vmem_limit_bytes=60 * MIB
+            collective_id=cid, has_side_effects=True, vmem_limit_bytes=62 * MIB
         ),
         cost_estimate=pl.CostEstimate(
             flops=6 * LINE * two * width * wide, bytes_accessed=60 * MIB, transcendentals=0
         ),
-        name="experts_forward",
-    )(n2, h1, mask, wr, *mine, *theirs, *shards)
+        name="forward",
+    )(*args, *mine, *theirs, *riders)
 
 
 class Deliver:
@@ -869,7 +947,7 @@
             def _():
                 self.here(i).start()
 
-    def end(self):
+    def sent(self):
         for i in range(len(self.pieces)):
             self.far(i, self.s, self.x).wait_send()
 
@@ -877,12 +955,18 @@
             def _():
                 self.near(i, self.s).wait_send()
 
-            @pl.when(self.s == self.layer)
-            def _():
+    def received(self):
+        @pl.when(self.s == self.layer)
+        def _():
+            for i in range(len(self.pieces)):
                 self.here(i).wait()
                 self.near(i, 1 - self.s).wait_recv()
                 for s in range(2):
                     self.far(i, s, 1 - self.x).wait_recv()
+
+    def end(self):
+        self.sent()
+        self.received()
 
 
 def act_sems(count):
@@ -929,7 +1013,7 @@
     ]
 
 
-def experts_backward_kernel(ls, layer, chunks, exchange, riders, *refs):
+def backward_kernel(ls, layer, chunks, exchange, riders, gathered, n_experts, *refs):
     refs = list(refs)
 
     def take(count):
@@ -940,32 +1024,53 @@
     g_in = take(1)[0]
     mine, theirs = take(3), take(3)
     x_in, gp_in, up_in, gates_in = take(4)
+    ins, weights = take(12), take(4)
     rider_in = take({"": 0, "left": 6, "right": 4}[riders])
-    dn_out, dgate_out, grads, got = take(4)
+    grads, got = take(2)
+    outs = take(4)
     rider_out = take({"": 0, "left": 2, "right": 4}[riders])
     (xb, gb, gpb, upre, act, part, pairb, upb, dnb, wg, wu, wd, stage, extra) = take(14)
     gates_ref, dn_ref, dgate_ref = take(3)
     ag_sems, rs_sems = take(6), take(6)
-    w_sem, own_sem, load_sem, stage_sem, got_sem, extra_sem, out_sem = take(7)
+    w_sem, own_sem, load_sem, stage_sem, got_sem, extra_sem = take(6)
+    vmem_in, vmem_out, dc_ref = take(12), take(4), take(1)[0]
+    in_sem, keep_sem, att_sem = take(3)
     rider_sems = refs
 
     e = lax.axis_index("expert")
     s = lax.axis_index("section")
     l, p = place(e, ls)
-    half, width = g_in.shape
+    half, width = dn_ref.shape
     hidden = wg.shape[2]
     two = 2 * half
     own_layer = s == layer
-    own = pltpu.make_async_copy(
-        g_in, gb.at[l, pl.ds(pl.multiple_of(p * half, half), half)], own_sem
-    )
+    if gathered:
+        own = pltpu.make_async_copy(g_in, gb, own_sem)
+    else:
+        own = pltpu.make_async_copy(
+            g_in, gb.at[l, pl.ds(pl.multiple_of(p * half, half), half)], own_sem
+        )
     own.start()
+    signals, waits = neighbours(l, p, ls, *(around() if exchange else ()))
+    send_greetings(signals)
     fetch(mine, theirs, own_layer, (wg, wu, wd), w_sem)
     loads = moves(
         [(gates_in, gates_ref), (gp_in, gpb), (up_in, upre), (x_in, xb)], load_sem
     )
     for copy in loads:
         copy.start()
+    kept = moves(list(zip(ins, vmem_in)), in_sem)
+    for copy in kept:
+        copy.start()
+    stores = moves(list(zip(vmem_out, outs)), keep_sem)
+    attention = moves(
+        [
+            (weights[0].at[:, pl.ds(j * hidden, hidden)], wg.at[j])
+            for j in range(weights[0].shape[1] // hidden)
+        ]
+        + [(weights[1], wu.at[0]), (weights[2], wu.at[1]), (weights[3], wd)],
+        att_sem,
+    )
     own.wait()
     couriers = []
     if riders == "left":
@@ -978,10 +1083,12 @@
         couriers.append(
             Deliver(1 - layer, EARLY, rider_in[0], *rider_out[:2], rider_sems[:4])
         )
-    greet(l, p, ls, *(around() if exchange else ()))
-    gather = Gather(l, p, ls, gb, ag_sems, chunks)
+    await_greetings(waits)
+    if not gathered:
+        gather = Gather(l, p, ls, gb, ag_sems, chunks)
     total = Sum(l, p, ls, part, pairb, upb, dnb, rs_sems, chunks)
-    gather.begin()
+    if not gathered:
+        gather.begin()
     for courier in couriers:
         if isinstance(courier, ActDeliver):
             courier.begin(range(3))
@@ -992,12 +1099,16 @@
         copy.wait()
 
     def step(k, carry):
-        @pl.when(k > 0)
-        def _():
-            gather.arrive(k)
-
-        L = near_first(l, k)
-        gather.from_pair(L)
+        if not gathered:
+
+            @pl.when(k > 0)
+            def _():
+                gather.arrive(k)
+
+        L = sum_order(l, k) if gathered else near_first(l, k)
+        if not gathered:
+            gather.from_pair(L)
+
         gates = gates_ref[L]
         lane = lax.broadcasted_iota(jnp.int32, (two, LANES), 1)
         dgates = jnp.zeros((two, LANES), F32)
@@ -1030,14 +1141,30 @@
             part[L, :, cols] = acc.astype(BF16)
         return carry
 
-    lax.fori_loop(0, LINE, step, 0)
-    for k in range(LINE):
-        total.give(near_first(l, LINE - 1 - k))
-
     def write(c, value):
         rows = pl.ds(c * (half // chunks), half // chunks)
         dn_ref[rows, :] = value[:, :width]
         dgate_ref[rows, :] = value[:, width:]
+
+    def early(k, carry):
+        step(k, carry)
+        total.give(sum_order(l, k))
+
+        @pl.when(k > 0)
+        def _():
+            total.pass_on(sum_order(l, k - 1), write)
+
+        return carry
+
+    if gathered:
+        lax.fori_loop(0, LINE, early, 0)
+    else:
+        lax.fori_loop(0, LINE, step, 0)
+        for j in range(LINE):
+            total.give(sum_order(l, j))
+
+    for copy in attention:
+        copy.start()
 
     def stored(kind, t):
         if exchange:
@@ -1113,31 +1240,62 @@
 
                 stage[kind] = acc.astype(BF16)
                 stored(kind, t).start()
+            if kind < chunks:
+                if gathered:
+
+                    @pl.when(t == 0)
+                    def _():
+                        total.pass_chunk(sum_order(l, LINE - 1), kind, write)
+
+                else:
+                    total.pass_chunk(sum_order(l, t), kind, write)
         return carry
 
-    def back(j, carry):
-        weight_grads(j, carry)
-        total.pass_on(near_first(l, LINE - 1 - j), write)
-        return carry
-
-    lax.fori_loop(0, LINE, back, 0)
-    last = moves([(dn_ref, dn_out), (dgate_ref, dgate_out)], out_sem)
-    for copy in last:
-        copy.start()
+    lax.fori_loop(0, LINE, weight_grads, 0)
+    for copy in kept + attention:
+        copy.wait()
+    g_rows = gb[l, pl.ds(pl.multiple_of(p * half, half), half), :]
+    attend_backward(
+        layer,
+        n_experts,
+        g_rows,
+        dn_ref,
+        dgate_ref,
+        vmem_in,
+        vmem_out,
+        (wg, wu, wd, dc_ref),
+        stores,
+    )
     for kind in range(3):
         stored(kind, 3).wait()
-    gather.end()
+    if not gathered:
+        gather.end()
     total.end()
     for courier in couriers:
         courier.end()
-    for copy in last:
+    for copy in stores:
         copy.wait()
 
 
-def experts_backward(
-    ls, layer, cid, g, mine, theirs, x, gp, up, gates, exchange, riders="", carried=(), chunks=2
+def backward(
+    ls,
+    layer,
+    cid,
+    n_experts,
+    g,
+    mine,
+    theirs,
+    saved,
+    kept,
+    common,
+    weights,
+    exchange,
+    riders="",
+    carried=(),
+    chunks=2,
 ):
-    tokens, width = g.shape
+    gathered = g.ndim == 3
+    tokens, width = (g.shape[1] // 2, g.shape[2]) if gathered else g.shape
     hidden = mine[0].shape[2]
     wide = EXP_DEV * hidden
     two = 2 * tokens
@@ -1145,6 +1303,19 @@
     theirs = (theirs[0], theirs[1], theirs[2].reshape(wide, width))
     sent = width + LANES
     quarter = width // 4
+    x, gp, up, gates = saved
+    h, n1, q, keys, values, context, h1, n2 = kept
+    picks, allowed, rope = common
+    wq, wk, wv, wo, router, gains = weights
+    ins = (n2, router, picks, h1, gains, allowed, q, keys, values, context, rope, h)
+    n_q, n_kv = wq.shape[1], wk.shape[1]
+    shape = jax.ShapeDtypeStruct
+    outs = [
+        shape((tokens, width), BF16),
+        shape((tokens, n_q + 2 * n_kv), BF16),
+        shape((tokens, width + LANES), BF16),
+        shape((16, width), BF16),
+    ]
     scratch = [
         pltpu.VMEM((LINE, two, width), BF16),
         pltpu.VMEM((LINE, two, width), BF16),
@@ -1155,9 +1326,9 @@
         pltpu.VMEM((LINE, tokens, sent), BF16),
         pltpu.VMEM((LINE, tokens, sent), BF16),
         pltpu.VMEM((LINE, tokens, sent), BF16),
-        pltpu.VMEM(mine[0].shape, BF16),
-        pltpu.VMEM(mine[1].shape, BF16),
-        pltpu.VMEM(mine[2].shape, BF16),
+    ]
+    scratch += in_vmem(mine)
+    scratch += [
         pltpu.VMEM((3, quarter, width), BF16),
         pltpu.VMEM((quarter, width), BF16),
         pltpu.VMEM(gates.shape, F32),
@@ -1165,53 +1336,71 @@
         pltpu.VMEM((tokens, LANES), F32),
     ]
     scratch += link_sems(chunks) + link_sems(chunks)
-    scratch += [DMA((3,)), DMA(()), DMA((4,)), DMA((2, 3)), DMA((3, 2)), DMA(()), DMA((2,))]
+    scratch += [DMA((3,)), DMA(()), DMA((4,)), DMA((2, 3)), DMA((3, 2)), DMA(())]
+    scratch += in_vmem(ins) + in_vmem(outs) + [pltpu.VMEM((tokens, n_q), BF16)]
+    scratch += [DMA((12,)), DMA((4,)), DMA((6,))]
     shapes = [
-        jax.ShapeDtypeStruct((tokens, width), F32),
-        jax.ShapeDtypeStruct((tokens, LANES), F32),
-        jax.ShapeDtypeStruct((3, 2 if exchange else 4, quarter, width), BF16),
-        jax.ShapeDtypeStruct((3, 2, quarter, width), BF16),
-    ]
+        shape((3, 2 if exchange else 4, quarter, width), BF16),
+        shape((3, 2, quarter, width), BF16),
+    ] + outs
     if riders == "left":
         shapes += [left_shape(tokens, width // 2)] * 2
         scratch += act_sems(3) + act_sems(3)
     if riders == "right":
-        sums, datdr, dqkv, gains = carried
+        sums, datdr, dqkv, gain_rows = carried
         shapes += deliver_shapes(EARLY, sums)
         shapes += right_shapes(tokens, dqkv.shape[1] + datdr.shape[1], width // 2)
         scratch += deliver_sems(EARLY) + act_sems(3)
     return pl.pallas_call(
-        functools.partial(experts_backward_kernel, ls, layer, chunks, exchange, riders),
+        functools.partial(
+            backward_kernel, ls, layer, chunks, exchange, riders, gathered, n_experts
+        ),
         out_shape=shapes,
-        in_specs=[HB] * (11 + len(carried)),
+        in_specs=[HB] * (27 + len(carried)),
         out_specs=[HB] * len(shapes),
         scratch_shapes=scratch,
         compiler_params=pltpu.CompilerParams(
-            collective_id=cid, has_side_effects=True, vmem_limit_bytes=62 * MIB
+            collective_id=cid, has_side_effects=True, vmem_limit_bytes=63 * MIB
         ),
         cost_estimate=pl.CostEstimate(
             flops=12 * LINE * two * width * wide, bytes_accessed=100 * MIB, transcendentals=0
         ),
-        name="experts_backward",
-    )(g, *mine, *theirs, x, gp, up, gates, *carried)
+        name="backward",
+    )(g, *mine, *theirs, x, gp, up, gates, *ins, wq, wk, wv, wo, *carried)
 
 
 def shared_grads_kernel(ls, chunks, *refs):
-    inputs, sums = refs[:6], refs[6:8]
-    out_hbm, near, far, near_late, far_late = refs[8:13]
-    part, pairb, upb, dnb, small, lhs_ref, rhs_ref, gain_ref, out, in_sem, out_sem = refs[13:24]
-    ag_sems, rs_sems = refs[24:30], refs[30:36]
+    lefts, rights, sent, sums = refs[:2], refs[2:4], refs[4:7], refs[7:9]
+    out_hbm, near, far, near_late, far_late = refs[9:14]
+    part, pairb, upb, dnb, small, lhs_ref, rhs_ref, gain_ref, out, in_sem, out_sem = refs[14:25]
+    ag_sems, rs_sems = refs[25:31], refs[31:37]
     s = lax.axis_index("section")
-    fetch(inputs[0:3], inputs[3:6], s == 0, (lhs_ref, rhs_ref, gain_ref), in_sem)
+    fetch(lefts[:1], lefts[1:], s == 0, (lhs_ref,), in_sem)
+    second = moves([(rights[0], rhs_ref), (rights[1], gain_ref)], in_sem.at[pl.ds(1, 2)])
+
+    @pl.when(s == 1)
+    def _():
+        for copy in second:
+            copy.start()
+
+    acts = ActDeliver(0, right_pieces(*sent, rhs_ref, gain_ref), refs[45:49])
     l, p = place(lax.axis_index("expert"), ls)
     tokens, rows = lhs_ref.shape[1:]
     half, width = pairb.shape[1:]
     couriers = (
-        Deliver(0, (0, 1, 2), sums[0], near, far, refs[36:40]),
-        Deliver(1, LATE, sums[1], near_late, far_late, refs[40:44]),
+        Deliver(0, (0, 1, 2), sums[0], near, far, refs[37:41]),
+        Deliver(1, LATE, sums[1], near_late, far_late, refs[41:45]),
     )
     greet(l, p, ls, *around())
-    fetch(inputs[0:3], inputs[3:6], s == 0, (lhs_ref, rhs_ref, gain_ref), in_sem, wait=True)
+    acts.begin((1, 0, 2))
+    fetch(lefts[:1], lefts[1:], s == 0, (lhs_ref,), in_sem, wait=True)
+    acts.received()
+
+    @pl.when(s == 1)
+    def _():
+        for copy in second:
+            copy.wait()
+
     gather = Gather(l, p, ls, out, ag_sems, chunks)
     total = Sum(l, p, ls, part, pairb, upb, dnb, rs_sems, chunks)
     n_first = 5
@@ -1225,7 +1414,7 @@
     quarter = n_rows // 4
 
     def fill(k, carry):
-        L = near_first(l, LINE - 1 - k)
+        L = sum_order(l, k)
 
         def one(q, carry):
             b = 2 * L + q
@@ -1249,15 +1438,12 @@
 
         lax.fori_loop(0, 2, one, 0)
         total.give(L)
-
-        @pl.when(k == 0)
-        def _():
-            for courier in couriers:
-                courier.begin()
-
         return carry
 
     lax.fori_loop(0, LINE, fill, 0)
+    acts.sent()
+    for courier in couriers:
+        courier.begin()
 
     def write(c, value):
         size = half // chunks
@@ -1265,7 +1451,7 @@
         out[l, pl.ds(start, size), :] = value.astype(BF16)
 
     def back(j, carry):
-        total.pass_on(near_first(l, LINE - 1 - j), write)
+        total.pass_on(sum_order(l, j), write)
         return carry
 
     lax.fori_loop(0, LINE, back, 0)
@@ -1288,8 +1474,9 @@
         copy.wait()
 
 
-def shared_grads(ls, cid, acts, sums, chunks=2):
-    lhs, rhs, gains = acts[0]
+def shared_grads(ls, cid, lefts, rights, sent, sums, chunks=2):
+    lhs = lefts[0]
+    rhs, gains = rights
     rows = lhs.shape[2]
     width = 512
     half = rows + 32
@@ -1301,7 +1488,7 @@
     return pl.pallas_call(
         functools.partial(shared_grads_kernel, ls, chunks),
         out_shape=shapes,
-        in_specs=[HB] * 8,
+        in_specs=[HB] * 9,
         out_specs=[HB] * 5,
         scratch_shapes=[
             both,
@@ -1319,13 +1506,14 @@
         + link_sems(chunks)
         + link_sems(chunks)
         + deliver_sems(every)
-        + deliver_sems(LATE),
+        + deliver_sems(LATE)
+        + act_sems(3),
         compiler_params=pltpu.CompilerParams(
             collective_id=cid, has_side_effects=True, vmem_limit_bytes=62 * MIB
         ),
         cost_estimate=pl.CostEstimate(flops=0, bytes_accessed=400 * MIB, transcendentals=0),
         name="shared_grads",
-    )(*acts[0], *acts[1], *sums)
+    )(*lefts, *rights, *sent, *sums)
 
 
 def finish_kernel(*refs):
@@ -1499,13 +1687,7 @@
     return ex / jnp.sum(ex, axis=-1, keepdims=True)
 
 
-def attention_forward_kernel(*refs):
-    ins, outs, vmem_in, vmem_out = refs[:8], refs[8:15], refs[15:23], refs[23:30]
-    loads, stores = moves(list(zip(ins, vmem_in)), refs[30]), moves(
-        list(zip(vmem_out, outs)), refs[31]
-    )
-    for copy in loads:
-        copy.start()
+def attend_forward(vmem_in, vmem_out, loads, stores):
     h_ref, gains_ref, rope_ref, allowed_ref, wq, wk, wv, wo = vmem_in
     n1_ref, q_ref, k_ref, v_ref, c_ref, h1_ref, n2_ref = vmem_out
     for copy in loads[:4]:
@@ -1544,66 +1726,13 @@
     stores[5].start()
     n2_ref[...] = (h1 * norm_scale(h1) * gain_row(gains_ref, 1)).astype(BF16)
     stores[6].start()
-    for copy in stores:
-        copy.wait()
-
-
-def in_vmem(values):
-    return [pltpu.VMEM(v.shape, v.dtype) for v in values]
-
-
-def attention_forward(h, allowed, rope, weights, gains):
-    tokens, width = h.shape
-    n_q, kv = weights[0].shape[1], weights[1].shape[1]
-    shape = jax.ShapeDtypeStruct
-    args = (h, gains, rope, allowed) + tuple(weights)
-    outs = [
-        shape((tokens, width), BF16),
-        shape((tokens, n_q), BF16),
-        shape((tokens, kv), BF16),
-        shape((tokens, kv), BF16),
-        shape((tokens, n_q), BF16),
-        shape((tokens, width), F32),
-        shape((tokens, width), BF16),
-    ]
-    return pl.pallas_call(
-        attention_forward_kernel,
-        out_shape=outs,
-        in_specs=[HB] * 8,
-        out_specs=[HB] * 7,
-        scratch_shapes=in_vmem(args) + in_vmem(outs) + [DMA((8,)), DMA((7,))],
-        compiler_params=pltpu.CompilerParams(vmem_limit_bytes=60 * MIB),
-        cost_estimate=pl.CostEstimate(
-            flops=2 * tokens * width * 4096, bytes_accessed=16 * MIB, transcendentals=0
-        ),
-        name="attention_forward",
-    )(*args)
-
-
-def attention_backward_kernel(layer, deliver, n_experts, *refs):
-    n_in, n_out = 20, 4
-    ins, outs = refs[:n_in], refs[n_in : n_in + n_out]
-    at = n_in + n_out
-    targets = refs[at : at + 2] if deliver else ()
-    at += len(targets)
-    vmem_in, vmem_out = refs[at : at + n_in], refs[at + n_in : at + n_in + n_out]
-    at += n_in + n_out
-    dc_ref = refs[at]
-    loads = moves(list(zip(ins, vmem_in)), refs[at + 1])
-    kept = 1 if deliver else n_out
-    stores = moves(list(zip(vmem_out[:kept], outs)), refs[at + 2])
-    for copy in loads:
-        copy.start()
-    (n2_ref, wr_ref, mask_ref, dgate_ref, dn2_ref, h1_ref, g_ref, gains_ref) = vmem_in[:8]
-    wo, allowed_ref, q_ref, k_ref, v_ref, c_ref, rope_ref = vmem_in[8:15]
-    wq, wk, wv, h_ref, n1_ref = vmem_in[15:20]
+
+
+def attend_backward(layer, n_experts, g_rows, dn2_ref, dgate_ref, vmem_in, vmem_out, work, stores):
+    (n2_ref, wr_ref, mask_ref, h1_ref, gains_ref, allowed_ref) = vmem_in[:6]
+    q_ref, k_ref, v_ref, c_ref, rope_ref, h_ref = vmem_in[6:12]
     din_ref, dqkv_ref, datdr_ref, gain_out = vmem_out
-    if deliver:
-        pieces = right_pieces(datdr_ref, dqkv_ref, gain_out, *targets)
-        acts = ActDeliver(layer, pieces, refs[at + 3 :])
-        greet_all(*around())
-    for copy in loads[:8]:
-        copy.wait()
+    wg, wu, wd, dc_ref = work
     tokens, width = h_ref.shape
     lane = lax.broadcasted_iota(jnp.int32, (tokens, LANES), 1)
     gates = routed_softmax(
@@ -1620,15 +1749,10 @@
     z2 = h1 * inv2
     w2 = dn2 * gain_row(gains_ref, 1)
     gm = jnp.sum(dn2 * z2, axis=0, keepdims=True)
-    dh1 = g_ref[...].astype(F32) + inv2 * (w2 - z2 * jnp.mean(w2 * z2, axis=-1, keepdims=True))
+    dh1 = g_rows.astype(F32) + inv2 * (w2 - z2 * jnp.mean(w2 * z2, axis=-1, keepdims=True))
     datdr_ref[:, :width] = dh1.astype(BF16)
-    if deliver:
-        acts.begin((0,))
-    else:
-        stores[2].start()
-    for copy in loads[8:15]:
-        copy.wait()
-    dc_ref[...] = dot_nt(datdr_ref[:, :width], wo[...]).astype(BF16)
+    stores[2].start()
+    dc_ref[...] = dot_nt(datdr_ref[:, :width], wd[...]).astype(BF16)
     allowed = jnp.concatenate([allowed_ref[...]] * GROUP, axis=0) > 0
     scale = HEAD_SIZE ** (-0.5)
     dqs, dks, dvs = [], [], []
@@ -1654,15 +1778,14 @@
         dqkv_ref[:, cols] = rotated(pair, cosine, sine).astype(BF16)
         cols = slice(n_q + n_kv + i * LANES, n_q + n_kv + (i + 1) * LANES)
         dqkv_ref[:, cols] = jnp.concatenate(dvs[2 * i : 2 * i + 2], axis=1).astype(BF16)
-    if deliver:
-        acts.begin((1,))
-    else:
-        stores[1].start()
-    for copy in loads[15:]:
-        copy.wait()
-    dn1 = dot_nt(dqkv_ref[:, :n_q], wq[...])
-    dn1 = dn1 + dot_nt(dqkv_ref[:, n_q : n_q + n_kv], wk[...])
-    dn1 = dn1 + dot_nt(dqkv_ref[:, n_q + n_kv :], wv[...])
+    stores[1].start()
+    block = wg.shape[2]
+    dn1 = dot_nt(dqkv_ref[:, :block], wg[0])
+    for j in range(1, n_q // block):
+        dn1 = dn1 + dot_nt(dqkv_ref[:, j * block : (j + 1) * block], wg[j])
+    for j in range(2 * n_kv // block):
+        cols = slice(n_q + j * block, n_q + (j + 1) * block)
+        dn1 = dn1 + dot_nt(dqkv_ref[:, cols], wu[j])
     h = h_ref[...].astype(F32)
     inv1 = norm_scale(h)
     z1 = h * inv1
@@ -1675,51 +1798,7 @@
         [ga_high, ga - ga_high, gm_high, gm - gm_high, jnp.zeros((12, width), F32)], axis=0
     ).astype(BF16)
     stores[0].start()
-    if deliver:
-        acts.begin((2,))
-        acts.end()
-    else:
-        stores[3].start()
-        for copy in stores[1:]:
-            copy.wait()
-    stores[0].wait()
-
-
-def attention_backward(
-    layer, cid, n_experts, g, dn2, dgates, mask, allowed, rope, gains, router, kept, weights, part
-):
-    tokens, width = g.shape
-    h, n1, q, keys, values, context, h1, n2 = kept
-    wq, wk, wv, wo = weights
-    args = (n2, router, mask, dgates, dn2, h1, g, gains, wo, allowed, q, keys, values, context)
-    args += (rope, wq, wk, wv, h, n1)
-    n_q, n_kv = wq.shape[1], wk.shape[1]
-    shape = jax.ShapeDtypeStruct
-    outs = [
-        shape((tokens, width), BF16),
-        shape((tokens, n_q + 2 * n_kv), BF16),
-        shape((tokens, width + LANES), BF16),
-        shape((16, width), BF16),
-    ]
-    scratch = in_vmem(args) + in_vmem(outs)
-    scratch += [pltpu.VMEM((tokens, n_q), BF16), DMA((len(args),)), DMA((4,))]
-    params = dict(vmem_limit_bytes=60 * MIB)
-    if part:
-        outs += right_shapes(tokens, n_q + 2 * n_kv + width + LANES, part)
-        scratch += act_sems(3)
-        params.update(collective_id=cid, has_side_effects=True)
-    return pl.pallas_call(
-        functools.partial(attention_backward_kernel, layer, bool(part), n_experts),
-        out_shape=outs,
-        in_specs=[HB] * len(args),
-        out_specs=[HB] * len(outs),
-        scratch_shapes=scratch,
-        compiler_params=pltpu.CompilerParams(**params),
-        cost_estimate=pl.CostEstimate(
-            flops=4 * tokens * width * 4096, bytes_accessed=20 * MIB, transcendentals=0
-        ),
-        name="attention_backward",
-    )(*args)
+    stores[3].start()
 
 
 def swap(value, axis):
@@ -1778,7 +1857,7 @@
     own = (w_query[0], key_matrix[0], value_matrix[0], w_out[0], router, gains)
     widths = [w.shape[1] for w in own[:4]]
     if paired:
-        masks, *whole = start(ls, 0, picks, own)
+        masks, d_out, *whole = start(ls, 0, picks, micro(cotangent), own)
         layer_weights = [whole, None]
     else:
         wholes = [
@@ -1797,22 +1876,19 @@
     current = micro(layer_input)
     kept_list, saved_list, outs = [], [], []
     for k in range(2):
-        weights = layer_weights[k]
-        n1, q, keys, values, context, h1, n2 = attention_forward(
-            current, allowed, rope, weights[:4], weights[5]
+        riders = own if (paired and k == 0) else ()
+        result = forward(
+            ls, k, 1 + k, current, allowed, rope, layer_weights[k], masks, mine, theirs, riders
         )
-        kept_list.append((current, n1, q, keys, values, context, h1, n2))
-        riders = own if (paired and k == 0) else ()
-        result = experts_forward(
-            ls, k, 1 + k, n2, h1, masks, weights[4], mine, theirs, riders
-        )
-        current = result[0]
-        saved_list.append(result[1:5])
+        kept_list.append((current, *result[:7]))
+        current = result[7]
+        saved_list.append(result[8:12])
         if riders:
-            layer_weights[1] = result[5:]
+            layer_weights[1] = result[12:]
         outs.append(current)
 
-    d_out = micro(cotangent)
+    if not paired:
+        d_out = micro(cotangent)
     d_ins, act_list, expert_list = [None] * 2, [None] * 2, [None] * 2
     for k in (1, 0):
         riders, carried = "", ()
@@ -1823,37 +1899,35 @@
             riders = "right"
             dqkv, datdr, gain_rows = act_list[1]
             carried = [expert_list[1], datdr, dqkv, gain_rows]
-        got = experts_backward(
-            ls, k, 3 + k, d_out, mine, theirs, *saved_list[k], paired, riders, carried
-        )
-        expert_list[k] = got[2]
-        if riders == "left":
-            lefts = got[4:6]
-        if riders == "right":
-            early, rights = got[4:6], got[6:8]
-        weights = layer_weights[k]
-        d_out, *acts = attention_backward(
+        grads, _, d_out, dqkv, datdr, gain_rows, *got = backward(
+            ls,
             k,
-            6,
+            3 + k,
             n_experts,
             d_out,
-            got[0],
-            got[1],
-            picks,
-            allowed,
-            rope,
-            weights[5],
-            weights[4],
+            mine,
+            theirs,
+            saved_list[k],
             kept_list[k],
-            weights[:4],
-            shard_rows if (paired and k == 0) else 0,
+            (picks, allowed, rope),
+            layer_weights[k],
+            paired,
+            riders,
+            carried,
         )
+        expert_list[k] = grads
         d_ins[k] = d_out
-        act_list[k] = acts
+        act_list[k] = (dqkv, datdr, gain_rows)
+        if riders == "left":
+            lefts = got
+        if riders == "right":
+            early, rights = got[:2], got[2:]
 
     if paired:
-        acts = ((lefts[0], *act_list[0][3:]), (lefts[1], *rights))
-        blocks, *arrived = shared_grads(ls, 5, acts, expert_list)
+        dqkv, datdr, gain_rows = act_list[0]
+        blocks, *arrived = shared_grads(
+            ls, 5, lefts, rights, (datdr, dqkv, gain_rows), expert_list
+        )
         gate_grad, up_grad, down_grad, *wide_grads = finish(
             expert_list,
             (*arrived[:2], *early, *arrived[2:]),

time: 736 us -> 683 us (0.928)
  Pallas kernels: 703 us -> 623 us
  starting transfers between devices: 4.89 us -> 29 us
    pallas_call x8 -> x4, Pallas kernels: 486 us -> 410 us  [the longest x2 215 us: forward(): pl.pallas_call(functools.partial(forward_kernel, ls, layer, chunks, n), o...]
    ppermute x6, starting transfers between devices: 4.89 us -> 29 us  [swap(): return lax.ppermute(value, axis, [(0, 1), (1, 0)])]
    pallas_call x1, Pallas kernels: 152 us -> 132 us  [shared_grads(): pl.pallas_call(functools.partial(shared_grads_kernel, ls, chunks), out_sh...]
    pallas_call x1, Pallas kernels: 46.6 us -> 63 us  [start(): pl.pallas_call(functools.partial(start_kernel, ls, count), out_shape=[jax...]
  transfers between devices with their start and end apart: 6 -> 6, of which waited for: 0 -> 0; matrix products, arithmetic and copies ran while one was open for 2% -> 2% of each run, Pallas kernels for 31% -> 32%
where the time goes in v5:
time: 683 us; the launch traced here: 671 us
  Pallas kernels  623 us (91%)
  starting transfers between devices  29 us (4%)
  other arithmetic  9.24 us (1%)
  local copies, waits for them, and re-layouts  8.44 us (1%)
    pallas_call x2, Pallas kernels, forward(): pl.pallas_call(functools.partial(forward_kernel, ls, layer, chunks, n), o...  215 us
    pallas_call x2, Pallas kernels, backward(): pl.pallas_call(functools.partial(backward_kernel, ls, layer, chunks, exch...  196 us
    pallas_call x1, Pallas kernels, shared_grads(): pl.pallas_call(functools.partial(shared_grads_kernel, ls, chunks), out_sh...  132 us
    pallas_call x1, Pallas kernels, start(): pl.pallas_call(functools.partial(start_kernel, ls, count), out_shape=[jax...  63 us
    ppermute x6, starting transfers between devices, swap(): return lax.ppermute(value, axis, [(0, 1), (1, 0)])  29 us
    pallas_call x1, Pallas kernels, finish(): pl.pallas_call(finish_kernel, out_shape=[jax.ShapeDtypeStruct((EXP_DEV, r...  17.9 us
  transfers between devices with their start and end apart: 6, of which 0 were waited for; matrix products, arithmetic and copies ran while one was open for 2% of the time, Pallas kernels for 32%

profile of v5, /device:TPU:17, one launch (start us, length us, event | category | flops | bytes accessed | tf_op | source)
XLA Modules:
  0.0 671.1 jit_solution(25586984833177563)
XLA Ops:
  0.6 0.0 copy-start
  0.7 0.7 collective-permute-start.1
  1.4 0.1 collective-permute-start.2
  1.5 0.4 collective-permute-start.3
  1.9 0.7 dynamic-slice_bitcast_fusion.3
  2.6 0.1 collective-permute-start
  2.7 0.1 pad.15.clone
  2.8 0.7 fusion.4
  3.5 0.7 fusion.3.refs_3_.refs_16_
  4.2 0.0 copy-done
  4.2 0.8 dynamic-slice_bitcast_fusion.refs_1_
  5.0 1.8 dynamic-slice_bitcast_fusion.1.refs_0_.refs_22_
  6.7 1.4 maximum_maximum_fusion.refs_7_.refs_21_
  8.1 0.9 copy.40
  9.0 0.7 pad.4.refs_6_.refs_20_
  9.8 0.0 collective-permute-done
  9.8 0.1 copy.39
  9.9 0.4 fusion.1
  10.3 0.6 pad_maximum_fusion.refs_0_.refs_13_
  11.0 63.0 %start.1 = (bf16[4,256,256]{2,1,0:T(8,128)(2,1)}, bf16[4,256,1536]{2,1,0:T(8,128)(2,1)}, bf16[1536,1536]{1,0:T(8,128)(2,1)}, bf16[1536,512]{1,0:T(8,128)(2,1)}, ...) custom-call(bf16[128,256]{1,0:T(8,128)(2,1)} %pad_maximum_fusion.ref, ...), custom_call_target="tpu_custom_call" | custom-call | bytes 104857600 | tf_op jit(solution)/shard_map/start/pallas_call | solution.py:596
  74.0 0.0 collective-permute-done.1.refs_13_.refs_4_
  74.0 0.0 collective-permute-done.2.refs_14_.refs_5_
  74.0 0.0 collective-permute-done.3
  74.0 113.7 %forward.2 = (bf16[128,1536]{1,0:T(8,128)(2,1)}, bf16[128,1536]{1,0:T(8,128)(2,1)}, bf16[128,512]{1,0:T(8,128)(2,1)}, bf16[128,512]{1,0:T(8,128)(2,1)}, bf16[128...) custom-call(bf16[128,1536]{1,0:T(8,128)(2,1)} %dynamic-slice_bitcast, ...), custom_call_target="tpu_custom_call" | custom-call | flops 14495514624 | bytes 62914560 | tf_op jit(solution)/shard_map/forward/pallas_call | solution.py:829
  187.7 101.0 %forward.3 = (bf16[128,1536]{1,0:T(8,128)(2,1)}, bf16[128,1536]{1,0:T(8,128)(2,1)}, bf16[128,512]{1,0:T(8,128)(2,1)}, bf16[128,512]{1,0:T(8,128)(2,1)}, bf16[128...) custom-call(bf16[128,1536]{1,0:T(8,128)(2,1)} %get-tuple-element.85., ...), custom_call_target="tpu_custom_call" | custom-call | flops 14495514624 | bytes 62914560 | tf_op jit(solution)/shard_map/forward/pallas_call | solution.py:829
  288.7 86.9 %backward.2 = (bf16[3,2,384,1536]{3,2,1,0:T(8,128)(2,1)}, bf16[3,2,384,1536]{3,2,1,0:T(8,128)(2,1)}, bf16[128,1536]{1,0:T(8,128)(2,1)}, bf16[128,2560]{1,0:T(8,1...) custom-call(bf16[4,256,1536]{2,1,0:T(8,128)(2,1)} %get-tuple-element, ...), custom_call_target="tpu_custom_call" | custom-call | flops 28991029248 | bytes 104857600 | tf_op jit(solution)/shard_map/backward/pallas_call | solution.py:1354
  375.6 0.0 copy-start.2
  375.6 0.0 copy-start.3
  375.6 108.8 %backward.3 = (bf16[3,2,384,1536]{3,2,1,0:T(8,128)(2,1)}, bf16[3,2,384,1536]{3,2,1,0:T(8,128)(2,1)}, bf16[128,1536]{1,0:T(8,128)(2,1)}, bf16[128,2560]{1,0:T(8,1...) custom-call(bf16[128,1536]{1,0:T(8,128)(2,1)} %get-tuple-element.108, ...), custom_call_target="tpu_custom_call" | custom-call | flops 28991029248 | bytes 104857600 | tf_op jit(solution)/shard_map/backward/pallas_call | solution.py:1354
  484.4 1.2 select_bitcast_fusion
  485.6 9.9 %collective-permute-start.5 = (bf16[128,1536]{1,0:T(8,128)(2,1)S(1)}, bf16[128,1536]{1,0:T(8,128)(2,1)}, u32[]{:S(2)}, u32[]{:S(2)}) collective-permute-start(bf16[128,1536]{1,0:T(8,128)(2,1)S(1)} %get-tuple-element.183), channel_id=1, source_target_pairs={{0,16},{16,0},{1,17},{17,1},{2,18},{18,2},{3,19},{19,3},{4,20},{20... | collective-permute-start | bytes 1179656 | tf_op jit(solution)/shard_map/ppermute | solution.py:1805
  495.5 0.0 copy-done.2
  495.5 0.0 copy-done.3
  495.5 0.8 select_bitcast_fusion.1
  496.3 131.9 %shared_grads.1 = (bf16[4,1600,512]{2,1,0:T(8,128)(2,1)}, bf16[3,384,1536]{2,1,0:T(8,128)(2,1)}, bf16[2,3,384,1536]{3,2,1,0:T(8,128)(2,1)}, bf16[1,384,1536]{2,1,0:T(8,128)(2,1)}, bf16[2,1,384,1536]{3,2,1,0:T(8,128)(2,1)}) custom-call(bf16[3,512,768]{2,1,0:T(8,128)(2,1)} %get-tuple-element.122.refs_0_, bf16[3,512,768]{2,1,0:T(8,128)(2,1)} %get-tuple-element.123.refs_1_, ...), custom_call_target="tpu_custom_call" | custom-call | bytes 419430400 | tf_op jit(solution)/shard_map/shared_grads/pallas_call | solution.py:1488
  628.1 1.0 slice_convert_fusion
  629.1 0.1 reshape.198
  629.3 17.8 %collective-permute-start.4 = (bf16[128,1536]{1,0:T(8,128)(2,1)}, bf16[128,1536]{1,0:T(8,128)(2,1)S(1)}, u32[]{:S(2)}, u32[]{:S(2)}) collective-permute-start(bf16[128,1536]{1,0:T(8,128)(2,1)} %get-tuple-element.185), channel_id=1, source_target_pairs={{0,16},{16,0},{1,17},{17,1},{2,18},{18,2},{3,19},{19,3},{4,20},{20... | collective-permute-start | bytes 1179656 | tf_op jit(solution)/shard_map/ppermute | solution.py:1805
  647.1 0.8 copy.42
  647.9 0.5 slice_reduce_fusion
  648.4 0.6 broadcast_in_dim_squeeze.6
  648.9 0.6 broadcast_in_dim_squeeze.7
  649.5 17.9 %finish.1 = (f32[3,768,512]{2,1,0:T(8,128)}, f32[3,768,512]{2,1,0:T(8,128)}, f32[3,256,1536]{2,1,0:T(8,128)}, f32[768,1536]{1,0:T(8,128)}, f32[768,512]{1,0:T(8,...) custom-call(bf16[3,2,384,1536]{3,2,1,0:T(8,128)(2,1)} %get-tuple-element.129.refs_7_.refs_0_, ...), custom_call_target="tpu_custom_call" | custom-call | bytes 52428800 | tf_op jit(solution)/shard_map/finish/pallas_call | solution.py:1615
  667.4 0.0 collective-permute-done.5
  667.4 2.2 maximum_select_fusion.1
  669.6 0.0 collective-permute-done.4
  669.6 1.0 maximum_select_fusion
  670.6 0.0 copy-done.1
  (6 shorter events, 0.1 us)
Async XLA Ops:
  0.6 3.5 copy-start
  0.7 73.3 %collective-permute-start.1 = (bf16[3,1536,512]{2,1,0:T(8,128)(2,1)}, bf16[3,1536,512]{2,1,0:T(8,128)(2,1)}, u32[]{:S(2)}, u32[]{:S(2)}) collective-permute-start(bf16[3,1536,512]{2,1,0:T(8,128)(2,1)} %bitcast.58), channel_id=1, source_target_pairs={{0,16},{16,0},{1,17},{17,1},{2,18},{18,2},{3,19},{19,3},{4,20},{20... | collective-permute-start | bytes 14155784 | tf_op jit(solution)/shard_map/ppermute | solution.py:1805
  1.4 72.6 %collective-permute-start.2 = (bf16[3,1536,512]{2,1,0:T(8,128)(2,1)}, bf16[3,1536,512]{2,1,0:T(8,128)(2,1)}, u32[]{:S(2)}, u32[]{:S(2)}) collective-permute-start(bf16[3,1536,512]{2,1,0:T(8,128)(2,1)} %bitcast.63), channel_id=1, source_target_pairs={{0,16},{16,0},{1,17},{17,1},{2,18},{18,2},{3,19},{19,3},{4,20},{20... | collective-permute-start | bytes 14155784 | tf_op jit(solution)/shard_map/ppermute | solution.py:1805
  1.5 72.5 %collective-permute-start.3 = (bf16[3,512,1536]{2,1,0:T(8,128)(2,1)}, bf16[3,512,1536]{2,1,0:T(8,128)(2,1)}, u32[]{:S(2)}, u32[]{:S(2)}) collective-permute-start(bf16[3,512,1536]{2,1,0:T(8,128)(2,1)} %bitcast.68), channel_id=1, source_target_pairs={{0,16},{16,0},{1,17},{17,1},{2,18},{18,2},{3,19},{19,3},{4,20},{20... | collective-permute-start | bytes 14155784 | tf_op jit(solution)/shard_map/ppermute | solution.py:1805
  2.6 7.1 %collective-permute-start = (s32[128,8]{0,1:T(8,128)S(1)}, s32[128,8]{0,1:T(8,128)S(1)}, u32[]{:S(2)}, u32[]{:S(2)}) collective-permute-start(s32[128,8]{0,1:T(8,128)S(1)} %get-tuple-element.189), channel_id=1, source_target_pairs={{0,16},{16,0},{1,17},{17,1},{2,18},{18,2},{3,19},{19,3},{4,20},{20... | collective-permute-start | bytes 12296 | tf_op jit(solution)/shard_map/ppermute | solution.py:1805
  375.6 119.9 %copy-start.2 = (bf16[128,1536]{1,0:T(8,128)(2,1)S(1)}, bf16[128,1536]{1,0:T(8,128)(2,1)}, u32[]{:S(2)}) copy-start(bf16[128,1536]{1,0:T(8,128)(2,1)} %get-tuple-element.85.refs_0_.refs_22_) | copy-start | bytes 1179652
  375.6 119.9 %copy-start.3 = (bf16[128,1536]{1,0:T(8,128)(2,1)S(1)}, bf16[128,1536]{1,0:T(8,128)(2,1)}, u32[]{:S(2)}) copy-start(bf16[128,1536]{1,0:T(8,128)(2,1)} %get-tuple-element.92) | copy-start | bytes 1179652
  485.6 181.8 %collective-permute-start.5 = (bf16[128,1536]{1,0:T(8,128)(2,1)S(1)}, bf16[128,1536]{1,0:T(8,128)(2,1)}, u32[]{:S(2)}, u32[]{:S(2)}) collective-permute-start(bf16[128,1536]{1,0:T(8,128)(2,1)S(1)} %get-tuple-element.183), channel_id=1, source_target_pairs={{0,16},{16,0},{1,17},{17,1},{2,18},{18,2},{3,19},{19,3},{4,20},{20... | collective-permute-start | bytes 1179656 | tf_op jit(solution)/shard_map/ppermute | solution.py:1805
  629.3 40.3 %collective-permute-start.4 = (bf16[128,1536]{1,0:T(8,128)(2,1)}, bf16[128,1536]{1,0:T(8,128)(2,1)S(1)}, u32[]{:S(2)}, u32[]{:S(2)}) collective-permute-start(bf16[128,1536]{1,0:T(8,128)(2,1)} %get-tuple-element.185), channel_id=1, source_target_pairs={{0,16},{16,0},{1,17},{17,1},{2,18},{18,2},{3,19},{19,3},{4,20},{20... | collective-permute-start | bytes 1179656 | tf_op jit(solution)/shard_map/ppermute | solution.py:1805
  649.5 21.1 %copy-start.1 = (bf16[2,128,1536]{2,1,0:T(8,128)(2,1)S(1)}, bf16[2,128,1536]{2,1,0:T(8,128)(2,1)}, u32[]{:S(2)}) copy-start(bf16[2,128,1536]{2,1,0:T(8,128)(2,1)} %param.16) | copy-start | bytes 2359300

commit v6 on v5

--- a/solution.py
+++ b/solution.py
@@ -20,8 +20,10 @@
 THETA = 10000.0
 NEG = -1e30
 
-EARLY = (0, 1)
-LATE = (2,)
+KINDS = (0, 1, 2)
+
+SIDES = 16
+WIDE_SIDES = 128
 
 MESH = pl.DeviceIdType.MESH
 DMA = pltpu.SemaphoreType.DMA
@@ -111,28 +113,43 @@
     )
 
 
+def cuts_of(half, chunks, sides):
+    rest = half - sides
+    size = -(-rest // (16 * chunks)) * 16
+    edges = [min(c * size, rest) for c in range(chunks + 1)]
+    return [(a, b - a) for a, b in zip(edges[:-1], edges[1:])], (rest, sides)
+
+
 class Gather:
-    def __init__(self, l, p, ls, buf, sems, chunks):
+    def __init__(self, l, p, ls, buf, sems, chunks, sides=0):
         self.l, self.p, self.ls, self.buf, self.chunks = l, p, ls, buf, chunks
         self.us, self.ur, self.ds, self.dr, self.ps, self.pr = sems
         self.half = buf.shape[1] // 2
-        self.rows = self.half // chunks
+        self.cuts, self.side = cuts_of(self.half, chunks, sides)
+        self.sides = sides
 
     def view(self, L, p, c):
-        start = pl.multiple_of(p * self.half + c * self.rows, self.rows)
-        return self.buf.at[L, pl.ds(start, self.rows)]
+        first, size = self.side if c >= self.chunks else self.cuts[c]
+        step = 16 if size % 16 == 0 else 8
+        start = pl.multiple_of(p * self.half + first, step)
+        return self.buf.at[L, pl.ds(start, size)]
 
     def copy(self, L, p, c, ssem, rsem, dev):
         v = self.view(L, p, c)
         return remote(v, v, ssem, rsem, expert=dev)
 
+    def column(self, c):
+        return 1 - self.p if c == self.chunks + 1 else self.p
+
     def up(self, s, c):
         dev = index_of(self.l + 1, self.p, self.ls)
-        return self.copy(self.l - s, self.p, c, self.us.at[s, c], self.ur.at[s, c], dev)
+        L = self.l - s
+        return self.copy(L, self.column(c), c, self.us.at[s, c], self.ur.at[s, c], dev)
 
     def dn(self, s, c):
         dev = index_of(self.l - 1, self.p, self.ls)
-        return self.copy(self.l + s, self.p, c, self.ds.at[s, c], self.dr.at[s, c], dev)
+        L = self.l + s
+        return self.copy(L, self.column(c), c, self.ds.at[s, c], self.dr.at[s, c], dev)
 
     def pair(self, L, c):
         dev = index_of(self.l, 1 - self.p, self.ls)
@@ -140,33 +157,46 @@
 
     def up_in(self, s, c):
         dev = index_of(self.l, self.p, self.ls)
-        return self.copy(self.l - 1 - s, self.p, c, self.us.at[s, c], self.ur.at[s, c], dev)
+        L = self.l - 1 - s
+        return self.copy(L, self.column(c), c, self.us.at[s, c], self.ur.at[s, c], dev)
 
     def dn_in(self, s, c):
         dev = index_of(self.l, self.p, self.ls)
-        return self.copy(self.l + 1 + s, self.p, c, self.ds.at[s, c], self.dr.at[s, c], dev)
+        L = self.l + 1 + s
+        return self.copy(L, self.column(c), c, self.ds.at[s, c], self.dr.at[s, c], dev)
 
     def pair_in(self, L, c):
         dev = index_of(self.l, self.p, self.ls)
         return self.copy(L, 1 - self.p, c, self.ps.at[L, c], self.pr.at[L, c], dev)
 
+    def both(self, s, c):
+        l = self.l
+
+        @pl.when(l < LINE - 1)
+        def _():
+            self.up(s, c).start()
+
+        @pl.when(l > 0)
+        def _():
+            self.dn(s, c).start()
+
     def begin(self):
-        l = self.l
+        if self.sides:
+            self.pair(self.l, self.chunks).start()
         for c in range(self.chunks):
-
-            @pl.when(l < LINE - 1)
-            def _():
-                self.up(0, c).start()
-
-            @pl.when(l > 0)
-            def _():
-                self.dn(0, c).start()
-
-            self.pair(l, c).start()
+            self.both(0, c)
+            self.pair(self.l, c).start()
+        if self.sides:
+            self.both(0, self.chunks)
+
+    def begin_sides(self):
+        if self.sides:
+            self.pair_in(self.l, self.chunks).wait_recv()
+            self.both(0, self.chunks + 1)
 
     def arrive(self, s):
         l = self.l
-        for c in range(self.chunks):
+        for c in range(self.chunks + (2 if self.sides else 0)):
 
             @pl.when(l - s >= 0)
             def _():
@@ -176,7 +206,8 @@
                 def _():
                     self.up(s, c).start()
 
-                self.pair(l - s, c).start()
+                if c < self.chunks:
+                    self.pair(l - s, c).start()
 
             @pl.when(l + s < LINE)
             def _():
@@ -186,7 +217,8 @@
                 def _():
                     self.dn(s, c).start()
 
-                self.pair(l + s, c).start()
+                if c < self.chunks:
+                    self.pair(l + s, c).start()
 
     def from_pair(self, L):
         for c in range(self.chunks):
@@ -194,9 +226,12 @@
 
     def end(self):
         l = self.l
+        if self.sides:
+            self.pair(l, self.chunks).wait_send()
         for c in range(self.chunks):
             for L in range(LINE):
                 self.pair(L, c).wait_send()
+        for c in range(self.chunks + (2 if self.sides else 0)):
             for s in range(LINE - 1):
 
                 @pl.when((l - s >= 0) & (l < LINE - 1))
@@ -209,18 +244,29 @@
 
 
 class Sum:
-    def __init__(self, l, p, ls, buf, pairb, upb, dnb, sems, chunks):
+    def __init__(self, l, p, ls, buf, pairb, upb, dnb, sems, chunks, sides=0):
         self.l, self.p, self.ls, self.buf, self.chunks = l, p, ls, buf, chunks
         self.pairb, self.upb, self.dnb = pairb, upb, dnb
         self.us, self.ur, self.ds, self.dr, self.ps, self.pr = sems
         self.half = buf.shape[1] // 2
-        self.rows = self.half // chunks
+        self.cuts, self.side = cuts_of(self.half, chunks, sides)
+        self.sides = sides
+
+    def column(self, c):
+        return 1 - self.p if c == self.chunks + 1 else self.p
+
+    def cut(self, c):
+        return self.side if c >= self.chunks else self.cuts[c]
 
     def mine(self, p, c):
-        return pl.ds(pl.multiple_of(p * self.half + c * self.rows, self.rows), self.rows)
+        first, size = self.cut(c)
+        return pl.ds(pl.multiple_of(p * self.half + first, 16), size)
 
     def part(self, c):
-        return pl.ds(c * self.rows, self.rows)
+        first, size = self.cut(c)
+        if c == self.chunks + 1:
+            first = first + size
+        return pl.ds(first, size)
 
     def pair(self, L, c):
         return remote(
@@ -233,7 +279,7 @@
 
     def up(self, L, c):
         return remote(
-            self.buf.at[L, self.mine(self.p, c)],
+            self.buf.at[L, self.mine(self.column(c), c)],
             self.upb.at[L, self.part(c)],
             self.us.at[L, c],
             self.ur.at[L, c],
@@ -242,7 +288,7 @@
 
     def dn(self, L, c):
         return remote(
-            self.buf.at[L, self.mine(self.p, c)],
+            self.buf.at[L, self.mine(self.column(c), c)],
             self.dnb.at[L, self.part(c)],
             self.ds.at[L, c],
             self.dr.at[L, c],
@@ -254,25 +300,42 @@
             self.pair(L, c).start()
 
     def total(self, L, c):
-        return self.buf[L, self.mine(self.p, c)].astype(F32) + self.pairb[
-            L, self.part(c)
-        ].astype(F32)
+        here = self.buf[L, self.mine(self.column(c), c)].astype(F32)
+        if c < self.chunks:
+            here = here + self.pairb[L, self.part(c)].astype(F32)
+        return here
 
     def pass_on(self, L, write):
         for c in range(self.chunks):
             self.pass_chunk(L, c, write)
 
     def pass_chunk(self, L, c, write):
+        if c == 0 and self.sides:
+            self.travel(L, self.chunks, None)
+            self.travel(L, self.chunks + 1, None)
+        self.pair(L, c).wait_recv()
+        self.travel(L, c, write)
+        if c == self.chunks - 1 and self.sides:
+
+            @pl.when(L == self.l)
+            def _():
+                c = self.chunks
+                self.pair(L, c).wait_recv()
+                here = self.buf[L, self.mine(self.p, c)].astype(F32)
+                write(self.cut(c), here + self.pairb[L, self.part(c)].astype(F32))
+
+    def travel(self, L, c, write):
         l = self.l
-        self.pair(L, c).wait_recv()
-        mine = self.mine(self.p, c)
+        mine = self.mine(self.column(c), c)
         part = self.part(c)
 
         @pl.when(L > l)
         def _():
-            @pl.when(l == 0)
-            def _():
-                self.buf[L, mine] = self.total(L, c).astype(BF16)
+            if c < self.chunks:
+
+                @pl.when(l == 0)
+                def _():
+                    self.buf[L, mine] = self.total(L, c).astype(BF16)
 
             @pl.when(l > 0)
             def _():
@@ -284,9 +347,11 @@
 
         @pl.when(L < l)
         def _():
-            @pl.when(l == LINE - 1)
-            def _():
-                self.buf[L, mine] = self.total(L, c).astype(BF16)
+            if c < self.chunks:
+
+                @pl.when(l == LINE - 1)
+                def _():
+                    self.buf[L, mine] = self.total(L, c).astype(BF16)
 
             @pl.when(l < LINE - 1)
             def _():
@@ -296,34 +361,46 @@
 
             self.dn(L, c).start()
 
+        def done(value):
+            if c < self.chunks:
+                write(self.cut(c), value)
+            else:
+                self.buf[L, mine] = value.astype(BF16)
+
         @pl.when(L == l)
         def _():
             @pl.when(l == 0)
             def _():
                 self.dn(L, c).wait_recv()
-                write(c, self.total(L, c) + self.dnb[L, part].astype(F32))
+                done(self.total(L, c) + self.dnb[L, part].astype(F32))
 
             @pl.when(l == LINE - 1)
             def _():
                 self.up(L, c).wait_recv()
-                write(c, self.total(L, c) + self.upb[L, part].astype(F32))
+                done(self.total(L, c) + self.upb[L, part].astype(F32))
 
             @pl.when((l > 0) & (l < LINE - 1))
             def _():
                 self.up(L, c).wait_recv()
                 self.dn(L, c).wait_recv()
-                write(
-                    c,
+                done(
                     self.total(L, c)
                     + self.upb[L, part].astype(F32)
-                    + self.dnb[L, part].astype(F32),
+                    + self.dnb[L, part].astype(F32)
                 )
+
+            if c == self.chunks + 1:
+                self.pair(L, self.chunks).start()
 
     def end(self):
         l = self.l
+        if self.sides:
+            self.pair(l, self.chunks).wait_send()
         for c in range(self.chunks):
             for L in range(LINE):
                 self.pair(L, c).wait_send()
+        for c in range(self.chunks + (2 if self.sides else 0)):
+            for L in range(LINE):
                 if L > 0:
 
                     @pl.when(l < L)
@@ -338,7 +415,7 @@
 
 
 def link_sems(chunks):
-    return [DMA((LINE, chunks))] * 6
+    return [DMA((LINE, chunks + 2))] * 6
 
 
 class Spread:
@@ -430,15 +507,15 @@
     picks_ref, cot_ref, shards = refs[0], refs[1], refs[2 : 2 + count]
     masks, cot_out, wholes = refs[2 + count], refs[3 + count], refs[4 + count : 4 + 2 * count]
     at = 4 + 2 * count
-    sems = [refs[at + 6 * i : at + 6 * i + 6] for i in range(4)]
-    own_sem, in_sem, out_sem, xs, xr, cs, cr, far_sem, cot_sem = refs[at + 24 : at + 33]
-    bounce, big = refs[at + 33 : at + 33 + count], refs[at + 33 + count : at + 35 + count]
-    cots = refs[at + 35 + count]
+    sems = [refs[at + 6 * i : at + 6 * i + 6] for i in range(3)]
+    own_sem, in_sem, out_sem, xs, xr, cs, cr, far_sem, cot_sem = refs[at + 18 : at + 27]
+    bounce, big = refs[at + 27 : at + 27 + count], refs[at + 27 + count : at + 28 + count]
+    cots = refs[at + 28 + count]
     e = lax.axis_index("expert")
     s, x = lax.axis_index("section"), lax.axis_index("dp")
     l, p = place(e, ls)
     src = s == 0
-    large = (0, 3)
+    large = (3,)
 
     def whole(i, x):
         size = shards[i].shape[0]
@@ -494,10 +571,10 @@
     own_cot.wait()
     greet(l, p, ls, *around())
     order = large + tuple(i for i in range(count) if i not in large)
-    gathers = [Gather(l, p, ls, big[i], sems[i], 2) for i in range(2)]
-    picked = Gather(l, p, ls, masks, sems[2], 1)
+    gathers = [Gather(l, p, ls, big[0], sems[0], 2)]
+    picked = Gather(l, p, ls, masks, sems[1], 1)
     picked.begin()
-    cot = Gather(l, p, ls, cots, sems[3], 2)
+    cot = Gather(l, p, ls, cots, sems[2], 2, SIDES)
 
     @pl.when(src)
     def _():
@@ -513,9 +590,8 @@
             loads[i].wait()
             stores[i].start()
 
-    @pl.when(jnp.logical_not(src))
-    def _():
-        cot.begin()
+    cot.begin()
+    cot.begin_sides()
 
     def step(k, carry):
         picked.arrive(k)
@@ -525,13 +601,6 @@
             for g in gathers:
                 g.arrive(k)
 
-        @pl.when(jnp.logical_not(src))
-        def _():
-            cot.arrive(k)
-
-        return carry
-
-    def cot_step(k, carry):
         cot.arrive(k)
         return carry
 
@@ -539,31 +608,25 @@
     for L in range(LINE):
         picked.from_pair(L)
     picked.end()
+    cot_save = pltpu.make_async_copy(cots, cot_out, cot_sem.at[1])
 
     @pl.when(src)
     def _():
-        cot.begin()
-
-    cot_save = pltpu.make_async_copy(cots, cot_out, cot_sem.at[1])
-
-    @pl.when(src)
-    def _():
-        for i in order[2:]:
-            across(i).wait_recv()
-            core_small(i).start()
         for g, i in enumerate(large):
             for L in range(LINE):
                 gathers[g].from_pair(L)
                 core_large(i, L).start()
                 kept(i, L).start()
-        lax.fori_loop(1, LINE, cot_step, 0)
+        for i in order[len(large) :]:
+            across(i).wait_recv()
+            core_small(i).start()
         for g in gathers:
             g.end()
         for i in order:
             across(i).wait_send()
             core_own(i).wait_send()
             stores[i].wait()
-        for i in order[2:]:
+        for i in order[len(large) :]:
             core_small(i).wait_send()
         for i in large:
             for L in range(LINE):
@@ -574,7 +637,7 @@
     def _():
         for i in order:
             core_own(i).wait_recv()
-        for i in order[2:]:
+        for i in order[len(large) :]:
             core_small(i).wait_recv()
         for i in large:
             for L in range(LINE):
@@ -603,15 +666,14 @@
         in_specs=[VM] + [HB] * (1 + count),
         out_specs=[VM] + [HB] * (1 + count),
         scratch_shapes=link_sems(2)
-        + link_sems(2)
         + link_sems(1)
         + link_sems(2)
         + [DMA(())]
         + [DMA((count,))] * 4
         + [DMA((2, count))] * 2
-        + [DMA((3, 2, LINE)), DMA((2,))]
+        + [DMA((3, 1, LINE)), DMA((2,))]
         + [pltpu.VMEM(w.shape, w.dtype) for w in shards]
-        + [buf, buf, pltpu.VMEM(gathered, BF16)],
+        + [buf, pltpu.VMEM(gathered, BF16)],
         compiler_params=pltpu.CompilerParams(
             collective_id=cid, has_side_effects=True, vmem_limit_bytes=60 * MIB
         ),
@@ -700,8 +762,8 @@
     xb[l, own, :] = n2_ref[...]
     if not n_spread:
         await_greetings(waits)
-    gather = Gather(l, p, ls, xb, ag_sems, chunks)
-    total = Sum(l, p, ls, part, pairb, upb, dnb, rs_sems, chunks)
+    gather = Gather(l, p, ls, xb, ag_sems, chunks, SIDES)
+    total = Sum(l, p, ls, part, pairb, upb, dnb, rs_sems, chunks, SIDES)
     gather.begin()
     for copy in loads[8:]:
         copy.wait()
@@ -718,6 +780,10 @@
         @pl.when(k > 0)
         def _():
             gather.arrive(k)
+
+        @pl.when(k == 0)
+        def _():
+            gather.begin_sides()
 
         L = near_first(l, k)
         gather.from_pair(L)
@@ -746,8 +812,8 @@
     for j in range(LINE):
         total.give(sum_order(l, j))
 
-    def write(c, value):
-        rows = pl.ds(c * (half // chunks), half // chunks)
+    def write(cut, value):
+        rows = pl.ds(*cut)
         out_ref[rows, :] = (h1_ref[rows, :] + value).astype(BF16)
 
     def back(j, carry):
@@ -804,7 +870,7 @@
         shape((LINE, two, wide), BF16),
         shape((LINE, two, LANES), F32),
     ]
-    buf = pltpu.VMEM((LINE, tokens, width), BF16)
+    buf = pltpu.VMEM((LINE, tokens + SIDES, width), BF16)
     scratch = in_vmem(args) + in_vmem(kept) + [DMA((10,)), DMA((7,))]
     scratch += [
         pltpu.VMEM((LINE, two, width), BF16),
@@ -1081,12 +1147,12 @@
         pieces = right_pieces(*rider_in[1:], *rider_out[2:])
         couriers.append(ActDeliver(1 - layer, pieces, rider_sems[4:8]))
         couriers.append(
-            Deliver(1 - layer, EARLY, rider_in[0], *rider_out[:2], rider_sems[:4])
+            Deliver(1 - layer, KINDS, rider_in[0], *rider_out[:2], rider_sems[:4])
         )
     await_greetings(waits)
     if not gathered:
-        gather = Gather(l, p, ls, gb, ag_sems, chunks)
-    total = Sum(l, p, ls, part, pairb, upb, dnb, rs_sems, chunks)
+        gather = Gather(l, p, ls, gb, ag_sems, chunks, SIDES)
+    total = Sum(l, p, ls, part, pairb, upb, dnb, rs_sems, chunks, SIDES)
     if not gathered:
         gather.begin()
     for courier in couriers:
@@ -1104,6 +1170,10 @@
             @pl.when(k > 0)
             def _():
                 gather.arrive(k)
+
+            @pl.when(k == 0)
+            def _():
+                gather.begin_sides()
 
         L = sum_order(l, k) if gathered else near_first(l, k)
         if not gathered:
@@ -1141,8 +1211,8 @@
             part[L, :, cols] = acc.astype(BF16)
         return carry
 
-    def write(c, value):
-        rows = pl.ds(c * (half // chunks), half // chunks)
+    def write(cut, value):
+        rows = pl.ds(*cut)
         dn_ref[rows, :] = value[:, :width]
         dgate_ref[rows, :] = value[:, width:]
 
@@ -1324,8 +1394,8 @@
         pltpu.VMEM((LINE, two, wide), BF16),
         pltpu.VMEM((LINE, two, sent), BF16),
         pltpu.VMEM((LINE, tokens, sent), BF16),
-        pltpu.VMEM((LINE, tokens, sent), BF16),
-        pltpu.VMEM((LINE, tokens, sent), BF16),
+        pltpu.VMEM((LINE, tokens + SIDES, sent), BF16),
+        pltpu.VMEM((LINE, tokens + SIDES, sent), BF16),
     ]
     scratch += in_vmem(mine)
     scratch += [
@@ -1348,9 +1418,9 @@
         scratch += act_sems(3) + act_sems(3)
     if riders == "right":
         sums, datdr, dqkv, gain_rows = carried
-        shapes += deliver_shapes(EARLY, sums)
+        shapes += deliver_shapes(KINDS, sums)
         shapes += right_shapes(tokens, dqkv.shape[1] + datdr.shape[1], width // 2)
-        scratch += deliver_sems(EARLY) + act_sems(3)
+        scratch += deliver_sems(KINDS) + act_sems(3)
     return pl.pallas_call(
         functools.partial(
             backward_kernel, ls, layer, chunks, exchange, riders, gathered, n_experts
@@ -1370,10 +1440,10 @@
 
 
 def shared_grads_kernel(ls, chunks, *refs):
-    lefts, rights, sent, sums = refs[:2], refs[2:4], refs[4:7], refs[7:9]
-    out_hbm, near, far, near_late, far_late = refs[9:14]
-    part, pairb, upb, dnb, small, lhs_ref, rhs_ref, gain_ref, out, in_sem, out_sem = refs[14:25]
-    ag_sems, rs_sems = refs[25:31], refs[31:37]
+    lefts, rights, sent, sums = refs[:2], refs[2:4], refs[4:7], refs[7]
+    out_hbm, near, far = refs[8:11]
+    part, pairb, upb, dnb, small, lhs_ref, rhs_ref, gain_ref, out, in_sem, out_sem = refs[11:22]
+    ag_sems, rs_sems = refs[22:28], refs[28:34]
     s = lax.axis_index("section")
     fetch(lefts[:1], lefts[1:], s == 0, (lhs_ref,), in_sem)
     second = moves([(rights[0], rhs_ref), (rights[1], gain_ref)], in_sem.at[pl.ds(1, 2)])
@@ -1383,14 +1453,11 @@
         for copy in second:
             copy.start()
 
-    acts = ActDeliver(0, right_pieces(*sent, rhs_ref, gain_ref), refs[45:49])
+    acts = ActDeliver(0, right_pieces(*sent, rhs_ref, gain_ref), refs[38:42])
     l, p = place(lax.axis_index("expert"), ls)
     tokens, rows = lhs_ref.shape[1:]
-    half, width = pairb.shape[1:]
-    couriers = (
-        Deliver(0, (0, 1, 2), sums[0], near, far, refs[37:41]),
-        Deliver(1, LATE, sums[1], near_late, far_late, refs[41:45]),
-    )
+    half, width = out.shape[1] // 2, out.shape[2]
+    courier = Deliver(0, KINDS, sums, near, far, refs[34:38])
     greet(l, p, ls, *around())
     acts.begin((1, 0, 2))
     fetch(lefts[:1], lefts[1:], s == 0, (lhs_ref,), in_sem, wait=True)
@@ -1401,8 +1468,8 @@
         for copy in second:
             copy.wait()
 
-    gather = Gather(l, p, ls, out, ag_sems, chunks)
-    total = Sum(l, p, ls, part, pairb, upb, dnb, rs_sems, chunks)
+    gather = Gather(l, p, ls, out, ag_sems, chunks, WIDE_SIDES)
+    total = Sum(l, p, ls, part, pairb, upb, dnb, rs_sems, chunks, WIDE_SIDES)
     n_first = 5
     row = lax.broadcasted_iota(jnp.int32, (gain_ref.shape[0], LANES), 0) % 16
     lane = lax.broadcasted_iota(jnp.int32, (gain_ref.shape[0], LANES), 1)
@@ -1442,12 +1509,11 @@
 
     lax.fori_loop(0, LINE, fill, 0)
     acts.sent()
-    for courier in couriers:
-        courier.begin()
-
-    def write(c, value):
-        size = half // chunks
-        start = pl.multiple_of(p * half + c * size, size)
+    courier.begin()
+
+    def write(cut, value):
+        first, size = cut
+        start = pl.multiple_of(p * half + first, 16)
         out[l, pl.ds(start, size), :] = value.astype(BF16)
 
     def back(j, carry):
@@ -1456,6 +1522,7 @@
 
     lax.fori_loop(0, LINE, back, 0)
     gather.begin()
+    gather.begin_sides()
 
     def step(k, carry):
         gather.arrive(k)
@@ -1468,8 +1535,7 @@
         saves[L].start()
     gather.end()
     total.end()
-    for courier in couriers:
-        courier.end()
+    courier.end()
     for copy in saves:
         copy.wait()
 
@@ -1480,16 +1546,15 @@
     rows = lhs.shape[2]
     width = 512
     half = rows + 32
-    buf = pltpu.VMEM((LINE, half, width), BF16)
+    buf = pltpu.VMEM((LINE, half + WIDE_SIDES, width), BF16)
     both = pltpu.VMEM((LINE, 2 * half, width), BF16)
-    every = (0, 1, 2)
     shapes = [jax.ShapeDtypeStruct((LINE, 2 * half, width), BF16)]
-    shapes += deliver_shapes(every, sums[0]) + deliver_shapes(LATE, sums[1])
+    shapes += deliver_shapes(KINDS, sums)
     return pl.pallas_call(
         functools.partial(shared_grads_kernel, ls, chunks),
         out_shape=shapes,
-        in_specs=[HB] * 9,
-        out_specs=[HB] * 5,
+        in_specs=[HB] * 8,
+        out_specs=[HB] * 3,
         scratch_shapes=[
             both,
             buf,
@@ -1505,22 +1570,21 @@
         ]
         + link_sems(chunks)
         + link_sems(chunks)
-        + deliver_sems(every)
-        + deliver_sems(LATE)
+        + deliver_sems(KINDS)
         + act_sems(3),
         compiler_params=pltpu.CompilerParams(
             collective_id=cid, has_side_effects=True, vmem_limit_bytes=62 * MIB
         ),
         cost_estimate=pl.CostEstimate(flops=0, bytes_accessed=400 * MIB, transcendentals=0),
         name="shared_grads",
-    )(*lefts, *rights, *sent, *sums)
+    )(*lefts, *rights, *sent, sums)
 
 
 def finish_kernel(*refs):
-    sums, arrived, blocks = refs[0:2], (refs[2:4], refs[4:8]), refs[8]
-    gate_out, up_out, down_out = refs[9:12]
-    wides = refs[12:16]
-    left, right, wide, cols_in, cols_out, in_sem, out_sem, col_in_sem, col_out_sem = refs[16:]
+    sums, arrived, blocks = refs[0:2], (refs[2:4], refs[4:6]), refs[6]
+    gate_out, up_out, down_out = refs[7:10]
+    wides = refs[10:14]
+    left, right, wide, cols_in, cols_out, in_sem, out_sem, col_in_sem, col_out_sem = refs[14:]
     s, x = lax.axis_index("section"), lax.axis_index("dp")
     quarter, width = left.shape[1:]
     hidden = gate_out.shape[2]
@@ -1534,14 +1598,10 @@
 
             @pl.when(s == layer)
             def _():
-                near, far = arrived[layer][:2]
-                i = kind
-                if layer == 1 and kind in LATE:
-                    near, far = arrived[layer][2:]
-                    i = LATE.index(kind)
-                first = sums[layer].at[kind, x] if h == layer else near.at[i]
+                near, far = arrived[layer]
+                first = sums[layer].at[kind, x] if h == layer else near.at[kind]
                 a = pltpu.make_async_copy(first, left.at[slot], in_sem.at[0, slot])
-                b = pltpu.make_async_copy(far.at[h, i], right.at[slot], in_sem.at[1, slot])
+                b = pltpu.make_async_copy(far.at[h, kind], right.at[slot], in_sem.at[1, slot])
                 if wait:
                     a.wait()
                     b.wait()
@@ -1620,7 +1680,7 @@
             jax.ShapeDtypeStruct((EXP_DEV, down, width), F32),
         ]
         + [jax.ShapeDtypeStruct((rows, w), F32) for w in widths],
-        in_specs=[HB] * 9,
+        in_specs=[HB] * 7,
         out_specs=[HB] * 7,
         scratch_shapes=[
             pltpu.VMEM((2, quarter, width), BF16),
@@ -1926,11 +1986,11 @@
     if paired:
         dqkv, datdr, gain_rows = act_list[0]
         blocks, *arrived = shared_grads(
-            ls, 5, lefts, rights, (datdr, dqkv, gain_rows), expert_list
+            ls, 5, lefts, rights, (datdr, dqkv, gain_rows), expert_list[0]
         )
         gate_grad, up_grad, down_grad, *wide_grads = finish(
             expert_list,
-            (*arrived[:2], *early, *arrived[2:]),
+            (*arrived, *early),
             blocks,
             shard_rows,
             w_gate.shape[3],

time: 683 us -> 662 us (0.969)
  Pallas kernels: 623 us -> 607 us
    pallas_call x2, Pallas kernels: 215 us -> 196 us  [forward(): pl.pallas_call(functools.partial(forward_kernel, ls, layer, chunks, n), o...]
  transfers between devices with their start and end apart: 6 -> 6, of which waited for: 0 -> 0; matrix products, arithmetic and copies ran while one was open for 2% -> 2% of each run, Pallas kernels for 32% -> 33%
where the time goes in v6:
time: 662 us; the launch traced here: 649 us
  Pallas kernels  607 us (92%)
  starting transfers between devices  23.6 us (4%)
  other arithmetic  9.21 us (1%)
  local copies, waits for them, and re-layouts  8.44 us (1%)
    pallas_call x2, Pallas kernels, forward(): pl.pallas_call(functools.partial(forward_kernel, ls, layer, chunks, n), o...  196 us
    pallas_call x2, Pallas kernels, backward(): pl.pallas_call(functools.partial(backward_kernel, ls, layer, chunks, exch...  194 us
    pallas_call x1, Pallas kernels, shared_grads(): pl.pallas_call(functools.partial(shared_grads_kernel, ls, chunks), out_sh...  132 us
    pallas_call x1, Pallas kernels, start(): pl.pallas_call(functools.partial(start_kernel, ls, count), out_shape=[jax...  67.2 us
    ppermute x6, starting transfers between devices, swap(): return lax.ppermute(value, axis, [(0, 1), (1, 0)])  23.6 us
    pallas_call x1, Pallas kernels, finish(): pl.pallas_call(finish_kernel, out_shape=[jax.ShapeDtypeStruct((EXP_DEV, r...  17.9 us
  transfers between devices with their start and end apart: 6, of which 0 were waited for; matrix products, arithmetic and copies ran while one was open for 2% of the time, Pallas kernels for 33%

profile of v6, /device:TPU:17, one launch (start us, length us, event | category | flops | bytes accessed | tf_op | source)
XLA Modules:
  0.0 649.5 jit_solution(5671323758560840876)
XLA Ops:
  0.6 0.0 copy-start
  0.7 0.7 collective-permute-start.1
  1.4 0.1 collective-permute-start.2
  1.5 0.4 collective-permute-start.3
  1.9 0.7 dynamic-slice_bitcast_fusion.3
  2.6 0.1 collective-permute-start
  2.7 0.1 pad.15.clone
  2.8 0.7 fusion.4
  3.5 0.7 fusion.3.refs_3_.refs_16_
  4.2 0.0 copy-done
  4.2 0.8 dynamic-slice_bitcast_fusion.refs_1_
  5.0 1.8 dynamic-slice_bitcast_fusion.1.refs_0_.refs_22_
  6.7 1.4 maximum_maximum_fusion.refs_7_.refs_21_
  8.1 0.9 copy.40
  9.0 0.7 pad.4.refs_6_.refs_20_
  9.8 0.0 collective-permute-done
  9.8 0.1 copy.39
  9.9 0.4 fusion.1
  10.3 0.6 pad_maximum_fusion.refs_0_.refs_13_
  11.0 67.2 %start.1 = (bf16[4,256,256]{2,1,0:T(8,128)(2,1)}, bf16[4,256,1536]{2,1,0:T(8,128)(2,1)}, bf16[1536,1536]{1,0:T(8,128)(2,1)}, bf16[1536,512]{1,0:T(8,128)(2,1)}, ...) custom-call(bf16[128,256]{1,0:T(8,128)(2,1)} %pad_maximum_fusion.ref, ...), custom_call_target="tpu_custom_call" | custom-call | bytes 104857600 | tf_op jit(solution)/shard_map/start/pallas_call | solution.py:659
  78.2 0.0 collective-permute-done.1.refs_13_.refs_4_
  78.2 0.0 collective-permute-done.2.refs_14_.refs_5_
  78.2 0.0 collective-permute-done.3
  78.2 99.0 %forward.2 = (bf16[128,1536]{1,0:T(8,128)(2,1)}, bf16[128,1536]{1,0:T(8,128)(2,1)}, bf16[128,512]{1,0:T(8,128)(2,1)}, bf16[128,512]{1,0:T(8,128)(2,1)}, bf16[128...) custom-call(bf16[128,1536]{1,0:T(8,128)(2,1)} %dynamic-slice_bitcast, ...), custom_call_target="tpu_custom_call" | custom-call | flops 14495514624 | bytes 62914560 | tf_op jit(solution)/shard_map/forward/pallas_call | solution.py:895
  177.2 96.7 %forward.3 = (bf16[128,1536]{1,0:T(8,128)(2,1)}, bf16[128,1536]{1,0:T(8,128)(2,1)}, bf16[128,512]{1,0:T(8,128)(2,1)}, bf16[128,512]{1,0:T(8,128)(2,1)}, bf16[128...) custom-call(bf16[128,1536]{1,0:T(8,128)(2,1)} %get-tuple-element.83., ...), custom_call_target="tpu_custom_call" | custom-call | flops 14495514624 | bytes 62914560 | tf_op jit(solution)/shard_map/forward/pallas_call | solution.py:895
  273.9 84.3 %backward.2 = (bf16[3,2,384,1536]{3,2,1,0:T(8,128)(2,1)}, bf16[3,2,384,1536]{3,2,1,0:T(8,128)(2,1)}, bf16[128,1536]{1,0:T(8,128)(2,1)}, bf16[128,2560]{1,0:T(8,1...) custom-call(bf16[4,256,1536]{2,1,0:T(8,128)(2,1)} %get-tuple-element, ...), custom_call_target="tpu_custom_call" | custom-call | flops 28991029248 | bytes 104857600 | tf_op jit(solution)/shard_map/backward/pallas_call | solution.py:1424
  358.3 0.0 copy-start.2
  358.3 0.0 copy-start.3
  358.3 109.7 %backward.3 = (bf16[3,2,384,1536]{3,2,1,0:T(8,128)(2,1)}, bf16[3,2,384,1536]{3,2,1,0:T(8,128)(2,1)}, bf16[128,1536]{1,0:T(8,128)(2,1)}, bf16[128,2560]{1,0:T(8,1...) custom-call(bf16[128,1536]{1,0:T(8,128)(2,1)} %get-tuple-element.106, ...), custom_call_target="tpu_custom_call" | custom-call | flops 28991029248 | bytes 104857600 | tf_op jit(solution)/shard_map/backward/pallas_call | solution.py:1424
  468.0 1.2 select_bitcast_fusion
  469.2 4.8 collective-permute-start.5
  474.0 0.0 copy-done.2
  474.0 0.0 copy-done.3
  474.0 0.8 select_bitcast_fusion.1
  474.8 132.1 %shared_grads.1 = (bf16[4,1600,512]{2,1,0:T(8,128)(2,1)}, bf16[3,384,1536]{2,1,0:T(8,128)(2,1)}, bf16[2,3,384,1536]{3,2,1,0:T(8,128)(2,1)}) custom-call(bf16[3,512,768]{2,1,0:T(8,128)(2,1)} %get-tuple-element.120.refs_0_, bf16[3,512,768]{2,1,0:T(8,128)(2,1)} %get-tuple-element.121.refs_1_, bf16[512,4224]{1,0:T(8,128)(2,1)} %get-tuple-element.122.refs_2_, ...), custom_call_target="tpu_custom_call" | custom-call | bytes 419430400 | tf_op jit(solution)/shard_map/shared_grads/pallas_call | solution.py:1553
  606.9 1.0 slice_convert_fusion
  607.9 0.1 reshape.198
  608.0 17.5 %collective-permute-start.4 = (bf16[128,1536]{1,0:T(8,128)(2,1)}, bf16[128,1536]{1,0:T(8,128)(2,1)S(1)}, u32[]{:S(2)}, u32[]{:S(2)}) collective-permute-start(bf16[128,1536]{1,0:T(8,128)(2,1)} %get-tuple-element.181), channel_id=1, source_target_pairs={{0,16},{16,0},{1,17},{17,1},{2,18},{18,2},{3,19},{19,3},{4,20},{20... | collective-permute-start | bytes 1179656 | tf_op jit(solution)/shard_map/ppermute | solution.py:1865
  625.5 0.8 copy.42
  626.3 0.5 slice_reduce_fusion
  626.8 0.6 broadcast_in_dim_squeeze.6
  627.4 0.6 broadcast_in_dim_squeeze.7
  628.0 17.9 %finish.1 = (f32[3,768,512]{2,1,0:T(8,128)}, f32[3,768,512]{2,1,0:T(8,128)}, f32[3,256,1536]{2,1,0:T(8,128)}, f32[768,1536]{1,0:T(8,128)}, f32[768,512]{1,0:T(8,...) custom-call(bf16[3,2,384,1536]{3,2,1,0:T(8,128)(2,1)} %get-tuple-element.127.refs_7_.refs_0_, ...), custom_call_target="tpu_custom_call" | custom-call | bytes 52428800 | tf_op jit(solution)/shard_map/finish/pallas_call | solution.py:1675
  645.9 0.0 collective-permute-done.5
  645.9 2.1 maximum_select_fusion.1
  648.0 0.0 collective-permute-done.4
  648.0 1.0 maximum_select_fusion
  649.0 0.0 copy-done.1
  (6 shorter events, 0.1 us)
Async XLA Ops:
  0.6 3.5 copy-start
  0.7 77.5 %collective-permute-start.1 = (bf16[3,1536,512]{2,1,0:T(8,128)(2,1)}, bf16[3,1536,512]{2,1,0:T(8,128)(2,1)}, u32[]{:S(2)}, u32[]{:S(2)}) collective-permute-start(bf16[3,1536,512]{2,1,0:T(8,128)(2,1)} %bitcast.58), channel_id=1, source_target_pairs={{0,16},{16,0},{1,17},{17,1},{2,18},{18,2},{3,19},{19,3},{4,20},{20... | collective-permute-start | bytes 14155784 | tf_op jit(solution)/shard_map/ppermute | solution.py:1865
  1.4 76.8 %collective-permute-start.2 = (bf16[3,1536,512]{2,1,0:T(8,128)(2,1)}, bf16[3,1536,512]{2,1,0:T(8,128)(2,1)}, u32[]{:S(2)}, u32[]{:S(2)}) collective-permute-start(bf16[3,1536,512]{2,1,0:T(8,128)(2,1)} %bitcast.63), channel_id=1, source_target_pairs={{0,16},{16,0},{1,17},{17,1},{2,18},{18,2},{3,19},{19,3},{4,20},{20... | collective-permute-start | bytes 14155784 | tf_op jit(solution)/shard_map/ppermute | solution.py:1865
  1.5 76.7 %collective-permute-start.3 = (bf16[3,512,1536]{2,1,0:T(8,128)(2,1)}, bf16[3,512,1536]{2,1,0:T(8,128)(2,1)}, u32[]{:S(2)}, u32[]{:S(2)}) collective-permute-start(bf16[3,512,1536]{2,1,0:T(8,128)(2,1)} %bitcast.68), channel_id=1, source_target_pairs={{0,16},{16,0},{1,17},{17,1},{2,18},{18,2},{3,19},{19,3},{4,20},{20... | collective-permute-start | bytes 14155784 | tf_op jit(solution)/shard_map/ppermute | solution.py:1865
  2.6 7.1 %collective-permute-start = (s32[128,8]{0,1:T(8,128)S(1)}, s32[128,8]{0,1:T(8,128)S(1)}, u32[]{:S(2)}, u32[]{:S(2)}) collective-permute-start(s32[128,8]{0,1:T(8,128)S(1)} %get-tuple-element.185), channel_id=1, source_target_pairs={{0,16},{16,0},{1,17},{17,1},{2,18},{18,2},{3,19},{19,3},{4,20},{20... | collective-permute-start | bytes 12296 | tf_op jit(solution)/shard_map/ppermute | solution.py:1865
  358.3 115.7 %copy-start.2 = (bf16[128,1536]{1,0:T(8,128)(2,1)S(1)}, bf16[128,1536]{1,0:T(8,128)(2,1)}, u32[]{:S(2)}) copy-start(bf16[128,1536]{1,0:T(8,128)(2,1)} %get-tuple-element.83.refs_0_.refs_22_) | copy-start | bytes 1179652
  358.3 115.7 %copy-start.3 = (bf16[128,1536]{1,0:T(8,128)(2,1)S(1)}, bf16[128,1536]{1,0:T(8,128)(2,1)}, u32[]{:S(2)}) copy-start(bf16[128,1536]{1,0:T(8,128)(2,1)} %get-tuple-element.90) | copy-start | bytes 1179652
  469.2 176.7 %collective-permute-start.5 = (bf16[128,1536]{1,0:T(8,128)(2,1)S(1)}, bf16[128,1536]{1,0:T(8,128)(2,1)}, u32[]{:S(2)}, u32[]{:S(2)}) collective-permute-start(bf16[128,1536]{1,0:T(8,128)(2,1)S(1)} %get-tuple-element.179), channel_id=1, source_target_pairs={{0,16},{16,0},{1,17},{17,1},{2,18},{18,2},{3,19},{19,3},{4,20},{20... | collective-permute-start | bytes 1179656 | tf_op jit(solution)/shard_map/ppermute | solution.py:1865
  608.0 39.9 %collective-permute-start.4 = (bf16[128,1536]{1,0:T(8,128)(2,1)}, bf16[128,1536]{1,0:T(8,128)(2,1)S(1)}, u32[]{:S(2)}, u32[]{:S(2)}) collective-permute-start(bf16[128,1536]{1,0:T(8,128)(2,1)} %get-tuple-element.181), channel_id=1, source_target_pairs={{0,16},{16,0},{1,17},{17,1},{2,18},{18,2},{3,19},{19,3},{4,20},{20... | collective-permute-start | bytes 1179656 | tf_op jit(solution)/shard_map/ppermute | solution.py:1865
  628.0 21.0 %copy-start.1 = (bf16[2,128,1536]{2,1,0:T(8,128)(2,1)S(1)}, bf16[2,128,1536]{2,1,0:T(8,128)(2,1)}, u32[]{:S(2)}) copy-start(bf16[2,128,1536]{2,1,0:T(8,128)(2,1)} %param.16) | copy-start | bytes 2359300

commit v7 on v6

--- a/solution.py
+++ b/solution.py
@@ -20,7 +20,8 @@
 THETA = 10000.0
 NEG = -1e30
 
-KINDS = (0, 1, 2)
+EARLY = (0, 1)
+LATE = (2,)
 
 SIDES = 16
 WIDE_SIDES = 128
@@ -682,8 +683,8 @@
     )(picks, cot, *shards)
 
 
-def fetch(mine, theirs, own_layer, dst, sems, wait=False):
-    for i in range(len(dst)):
+def fetch(mine, theirs, own_layer, dst, sems, wait=False, which=None):
+    for i in range(len(dst)) if which is None else which:
         a = pltpu.make_async_copy(mine[i], dst[i], sems.at[i])
         b = pltpu.make_async_copy(theirs[i], dst[i], sems.at[i])
 
@@ -765,9 +766,6 @@
     gather = Gather(l, p, ls, xb, ag_sems, chunks, SIDES)
     total = Sum(l, p, ls, part, pairb, upb, dnb, rs_sems, chunks, SIDES)
     gather.begin()
-    for copy in loads[8:]:
-        copy.wait()
-    fetch(mine, theirs, own_layer, (wg, wu, wd), w_sem, wait=True)
 
     def save(L):
         return (
@@ -777,16 +775,22 @@
         )
 
     def step(k, carry):
-        @pl.when(k > 0)
-        def _():
-            gather.arrive(k)
-
         @pl.when(k == 0)
         def _():
             gather.begin_sides()
 
+        @pl.when(k < LINE - 1)
+        def _():
+            gather.arrive(k + 1)
+
         L = near_first(l, k)
         gather.from_pair(L)
+        @pl.when(k == 0)
+        def _():
+            for copy in loads[8:]:
+                copy.wait()
+            fetch(mine, theirs, own_layer, (wg, wu, wd), w_sem, wait=True)
+
         x = xb[L]
         mask = mask_ref[L, :, layer * LANES : (layer + 1) * LANES].astype(F32)
         gates = routed_softmax(dot(x, wr_ref[...]), mask)
@@ -1119,12 +1123,14 @@
     own.start()
     signals, waits = neighbours(l, p, ls, *(around() if exchange else ()))
     send_greetings(signals)
-    fetch(mine, theirs, own_layer, (wg, wu, wd), w_sem)
+    fetch(mine, theirs, own_layer, (wg, wu, wd), w_sem, which=(2,))
     loads = moves(
         [(gates_in, gates_ref), (gp_in, gpb), (up_in, upre), (x_in, xb)], load_sem
     )
-    for copy in loads:
+    for copy in loads[:3]:
         copy.start()
+    fetch(mine, theirs, own_layer, (wg, wu, wd), w_sem, which=(0, 1))
+    loads[3].start()
     kept = moves(list(zip(ins, vmem_in)), in_sem)
     for copy in kept:
         copy.start()
@@ -1147,7 +1153,7 @@
         pieces = right_pieces(*rider_in[1:], *rider_out[2:])
         couriers.append(ActDeliver(1 - layer, pieces, rider_sems[4:8]))
         couriers.append(
-            Deliver(1 - layer, KINDS, rider_in[0], *rider_out[:2], rider_sems[:4])
+            Deliver(1 - layer, EARLY, rider_in[0], *rider_out[:2], rider_sems[:4])
         )
     await_greetings(waits)
     if not gathered:
@@ -1160,24 +1166,27 @@
             courier.begin(range(3))
         else:
             courier.begin()
-    fetch(mine, theirs, own_layer, (wg, wu, wd), w_sem, wait=True)
-    for copy in loads:
-        copy.wait()
 
     def step(k, carry):
         if not gathered:
-
-            @pl.when(k > 0)
-            def _():
-                gather.arrive(k)
 
             @pl.when(k == 0)
             def _():
                 gather.begin_sides()
 
+            @pl.when(k < LINE - 1)
+            def _():
+                gather.arrive(k + 1)
+
         L = sum_order(l, k) if gathered else near_first(l, k)
         if not gathered:
             gather.from_pair(L)
+
+        @pl.when(k == 0)
+        def _():
+            fetch(mine, theirs, own_layer, (wg, wu, wd), w_sem, wait=True, which=(2,))
+            for copy in loads[:3]:
+                copy.wait()
 
         gates = gates_ref[L]
         lane = lax.broadcasted_iota(jnp.int32, (two, LANES), 1)
@@ -1200,6 +1209,10 @@
             gpb[L, :, cols] = (da * up * sig * (1.0 + gp * (1.0 - sig))).astype(BF16)
             upre[L, :, cols] = (da * silu).astype(BF16)
         part[L, :, width:] = dgates.astype(BF16)
+        @pl.when(k == 0)
+        def _():
+            fetch(mine, theirs, own_layer, (wg, wu, wd), w_sem, wait=True, which=(0, 1))
+
         tile = 512
         for n in range(width // tile):
             cols = slice(n * tile, (n + 1) * tile)
@@ -1232,6 +1245,8 @@
         lax.fori_loop(0, LINE, step, 0)
         for j in range(LINE):
             total.give(sum_order(l, j))
+
+    loads[3].wait()
 
     for copy in attention:
         copy.start()
@@ -1418,9 +1433,9 @@
         scratch += act_sems(3) + act_sems(3)
     if riders == "right":
         sums, datdr, dqkv, gain_rows = carried
-        shapes += deliver_shapes(KINDS, sums)
+        shapes += deliver_shapes(EARLY, sums)
         shapes += right_shapes(tokens, dqkv.shape[1] + datdr.shape[1], width // 2)
-        scratch += deliver_sems(KINDS) + act_sems(3)
+        scratch += deliver_sems(EARLY) + act_sems(3)
     return pl.pallas_call(
         functools.partial(
             backward_kernel, ls, layer, chunks, exchange, riders, gathered, n_experts
@@ -1440,10 +1455,10 @@
 
 
 def shared_grads_kernel(ls, chunks, *refs):
-    lefts, rights, sent, sums = refs[:2], refs[2:4], refs[4:7], refs[7]
-    out_hbm, near, far = refs[8:11]
-    part, pairb, upb, dnb, small, lhs_ref, rhs_ref, gain_ref, out, in_sem, out_sem = refs[11:22]
-    ag_sems, rs_sems = refs[22:28], refs[28:34]
+    lefts, rights, sent, sums = refs[:2], refs[2:4], refs[4:7], refs[7:9]
+    out_hbm, near, far, near_late, far_late = refs[9:14]
+    part, pairb, upb, dnb, small, lhs_ref, rhs_ref, gain_ref, out, in_sem, out_sem = refs[14:25]
+    ag_sems, rs_sems = refs[25:31], refs[31:37]
     s = lax.axis_index("section")
     fetch(lefts[:1], lefts[1:], s == 0, (lhs_ref,), in_sem)
     second = moves([(rights[0], rhs_ref), (rights[1], gain_ref)], in_sem.at[pl.ds(1, 2)])
@@ -1453,11 +1468,14 @@
         for copy in second:
             copy.start()
 
-    acts = ActDeliver(0, right_pieces(*sent, rhs_ref, gain_ref), refs[38:42])
+    acts = ActDeliver(0, right_pieces(*sent, rhs_ref, gain_ref), refs[45:49])
     l, p = place(lax.axis_index("expert"), ls)
     tokens, rows = lhs_ref.shape[1:]
     half, width = out.shape[1] // 2, out.shape[2]
-    courier = Deliver(0, KINDS, sums, near, far, refs[34:38])
+    couriers = (
+        Deliver(0, (0, 1, 2), sums[0], near, far, refs[37:41]),
+        Deliver(1, LATE, sums[1], near_late, far_late, refs[41:45]),
+    )
     greet(l, p, ls, *around())
     acts.begin((1, 0, 2))
     fetch(lefts[:1], lefts[1:], s == 0, (lhs_ref,), in_sem, wait=True)
@@ -1509,7 +1527,8 @@
 
     lax.fori_loop(0, LINE, fill, 0)
     acts.sent()
-    courier.begin()
+    for courier in couriers:
+        courier.begin()
 
     def write(cut, value):
         first, size = cut
@@ -1535,7 +1554,8 @@
         saves[L].start()
     gather.end()
     total.end()
-    courier.end()
+    for courier in couriers:
+        courier.end()
     for copy in saves:
         copy.wait()
 
@@ -1548,13 +1568,14 @@
     half = rows + 32
     buf = pltpu.VMEM((LINE, half + WIDE_SIDES, width), BF16)
     both = pltpu.VMEM((LINE, 2 * half, width), BF16)
+    every = (0, 1, 2)
     shapes = [jax.ShapeDtypeStruct((LINE, 2 * half, width), BF16)]
-    shapes += deliver_shapes(KINDS, sums)
+    shapes += deliver_shapes(every, sums[0]) + deliver_shapes(LATE, sums[1])
     return pl.pallas_call(
         functools.partial(shared_grads_kernel, ls, chunks),
         out_shape=shapes,
-        in_specs=[HB] * 8,
-        out_specs=[HB] * 3,
+        in_specs=[HB] * 9,
+        out_specs=[HB] * 5,
         scratch_shapes=[
             both,
             buf,
@@ -1570,21 +1591,22 @@
         ]
         + link_sems(chunks)
         + link_sems(chunks)
-        + deliver_sems(KINDS)
+        + deliver_sems(every)
+        + deliver_sems(LATE)
         + act_sems(3),
         compiler_params=pltpu.CompilerParams(
             collective_id=cid, has_side_effects=True, vmem_limit_bytes=62 * MIB
         ),
         cost_estimate=pl.CostEstimate(flops=0, bytes_accessed=400 * MIB, transcendentals=0),
         name="shared_grads",
-    )(*lefts, *rights, *sent, sums)
+    )(*lefts, *rights, *sent, *sums)
 
 
 def finish_kernel(*refs):
-    sums, arrived, blocks = refs[0:2], (refs[2:4], refs[4:6]), refs[6]
-    gate_out, up_out, down_out = refs[7:10]
-    wides = refs[10:14]
-    left, right, wide, cols_in, cols_out, in_sem, out_sem, col_in_sem, col_out_sem = refs[14:]
+    sums, arrived, blocks = refs[0:2], (refs[2:4], refs[4:8]), refs[8]
+    gate_out, up_out, down_out = refs[9:12]
+    wides = refs[12:16]
+    left, right, wide, cols_in, cols_out, in_sem, out_sem, col_in_sem, col_out_sem = refs[16:]
     s, x = lax.axis_index("section"), lax.axis_index("dp")
     quarter, width = left.shape[1:]
     hidden = gate_out.shape[2]
@@ -1598,10 +1620,14 @@
 
             @pl.when(s == layer)
             def _():
-                near, far = arrived[layer]
-                first = sums[layer].at[kind, x] if h == layer else near.at[kind]
+                near, far = arrived[layer][:2]
+                i = kind
+                if layer == 1 and kind in LATE:
+                    near, far = arrived[layer][2:]
+                    i = LATE.index(kind)
+                first = sums[layer].at[kind, x] if h == layer else near.at[i]
                 a = pltpu.make_async_copy(first, left.at[slot], in_sem.at[0, slot])
-                b = pltpu.make_async_copy(far.at[h, kind], right.at[slot], in_sem.at[1, slot])
+                b = pltpu.make_async_copy(far.at[h, i], right.at[slot], in_sem.at[1, slot])
                 if wait:
                     a.wait()
                     b.wait()
@@ -1680,7 +1706,7 @@
             jax.ShapeDtypeStruct((EXP_DEV, down, width), F32),
         ]
         + [jax.ShapeDtypeStruct((rows, w), F32) for w in widths],
-        in_specs=[HB] * 7,
+        in_specs=[HB] * 9,
         out_specs=[HB] * 7,
         scratch_shapes=[
             pltpu.VMEM((2, quarter, width), BF16),
@@ -1986,11 +2012,11 @@
     if paired:
         dqkv, datdr, gain_rows = act_list[0]
         blocks, *arrived = shared_grads(
-            ls, 5, lefts, rights, (datdr, dqkv, gain_rows), expert_list[0]
+            ls, 5, lefts, rights, (datdr, dqkv, gain_rows), expert_list
         )
         gate_grad, up_grad, down_grad, *wide_grads = finish(
             expert_list,
-            (*arrived, *early),
+            (*arrived[:2], *early, *arrived[2:]),
             blocks,
             shard_rows,
             w_gate.shape[3],

time: 662 us -> 625 us (0.944)
  Pallas kernels: 607 us -> 575 us
    pallas_call x2, Pallas kernels: 196 us -> 177 us  [forward(): pl.pallas_call(functools.partial(forward_kernel, ls, layer, chunks, n), o...]
    pallas_call x2, Pallas kernels: 194 us -> 179 us  [backward(): pl.pallas_call(functools.partial(backward_kernel, ls, layer, chunks, exch...]
  transfers between devices with their start and end apart: 6 -> 6, of which waited for: 0 -> 0; matrix products, arithmetic and copies ran while one was open for 2% -> 3% of each run, Pallas kernels for 33% -> 36%
where the time goes in v7:
time: 625 us; the launch traced here: 614 us
  Pallas kernels  575 us (92%)
  starting transfers between devices  20.5 us (3%)
  other arithmetic  9.24 us (1%)
  local copies, waits for them, and re-layouts  8.44 us (1%)
    pallas_call x2, Pallas kernels, backward(): pl.pallas_call(functools.partial(backward_kernel, ls, layer, chunks, exch...  179 us
    pallas_call x2, Pallas kernels, forward(): pl.pallas_call(functools.partial(forward_kernel, ls, layer, chunks, n), o...  177 us
    pallas_call x1, Pallas kernels, shared_grads(): pl.pallas_call(functools.partial(shared_grads_kernel, ls, chunks), out_sh...  134 us
    pallas_call x1, Pallas kernels, start(): pl.pallas_call(functools.partial(start_kernel, ls, count), out_shape=[jax...  67.1 us
    ppermute x6, starting transfers between devices, swap(): return lax.ppermute(value, axis, [(0, 1), (1, 0)])  20.5 us
    pallas_call x1, Pallas kernels, finish(): pl.pallas_call(finish_kernel, out_shape=[jax.ShapeDtypeStruct((EXP_DEV, r...  17.9 us
  transfers between devices with their start and end apart: 6, of which 0 were waited for; matrix products, arithmetic and copies ran while one was open for 3% of the time, Pallas kernels for 36%

profile of v7, /device:TPU:17, one launch (start us, length us, event | category | flops | bytes accessed | tf_op | source)
XLA Modules:
  0.0 614.3 jit_solution(6859617272551302667)
XLA Ops:
  0.6 0.0 copy-start
  0.7 0.7 collective-permute-start.1
  1.4 0.1 collective-permute-start.2
  1.5 0.4 collective-permute-start.3
  1.9 0.7 dynamic-slice_bitcast_fusion.3
  2.6 0.1 collective-permute-start
  2.7 0.1 pad.15.clone
  2.8 0.7 fusion.4
  3.5 0.7 fusion.3.refs_3_.refs_16_
  4.2 0.0 copy-done
  4.2 0.8 dynamic-slice_bitcast_fusion.refs_1_
  5.0 1.8 dynamic-slice_bitcast_fusion.1.refs_0_.refs_22_
  6.7 1.4 maximum_maximum_fusion.refs_7_.refs_21_
  8.1 0.9 copy.40
  9.0 0.7 pad.4.refs_6_.refs_20_
  9.8 0.0 collective-permute-done
  9.8 0.1 copy.39
  9.9 0.4 fusion.1
  10.3 0.6 pad_maximum_fusion.refs_0_.refs_13_
  11.0 67.1 %start.1 = (bf16[4,256,256]{2,1,0:T(8,128)(2,1)}, bf16[4,256,1536]{2,1,0:T(8,128)(2,1)}, bf16[1536,1536]{1,0:T(8,128)(2,1)}, bf16[1536,512]{1,0:T(8,128)(2,1)}, ...) custom-call(bf16[128,256]{1,0:T(8,128)(2,1)} %pad_maximum_fusion.ref, ...), custom_call_target="tpu_custom_call" | custom-call | bytes 104857600 | tf_op jit(solution)/shard_map/start/pallas_call | solution.py:660
  78.0 0.0 collective-permute-done.1.refs_13_.refs_4_
  78.1 0.0 collective-permute-done.2.refs_14_.refs_5_
  78.1 0.0 collective-permute-done.3
  78.1 90.9 %forward.2 = (bf16[128,1536]{1,0:T(8,128)(2,1)}, bf16[128,1536]{1,0:T(8,128)(2,1)}, bf16[128,512]{1,0:T(8,128)(2,1)}, bf16[128,512]{1,0:T(8,128)(2,1)}, bf16[128...) custom-call(bf16[128,1536]{1,0:T(8,128)(2,1)} %dynamic-slice_bitcast, ...), custom_call_target="tpu_custom_call" | custom-call | flops 14495514624 | bytes 62914560 | tf_op jit(solution)/shard_map/forward/pallas_call | solution.py:899
  169.0 86.0 %forward.3 = (bf16[128,1536]{1,0:T(8,128)(2,1)}, bf16[128,1536]{1,0:T(8,128)(2,1)}, bf16[128,512]{1,0:T(8,128)(2,1)}, bf16[128,512]{1,0:T(8,128)(2,1)}, bf16[128...) custom-call(bf16[128,1536]{1,0:T(8,128)(2,1)} %get-tuple-element.85., ...), custom_call_target="tpu_custom_call" | custom-call | flops 14495514624 | bytes 62914560 | tf_op jit(solution)/shard_map/forward/pallas_call | solution.py:899
  255.0 85.5 %backward.2 = (bf16[3,2,384,1536]{3,2,1,0:T(8,128)(2,1)}, bf16[3,2,384,1536]{3,2,1,0:T(8,128)(2,1)}, bf16[128,1536]{1,0:T(8,128)(2,1)}, bf16[128,2560]{1,0:T(8,1...) custom-call(bf16[4,256,1536]{2,1,0:T(8,128)(2,1)} %get-tuple-element, ...), custom_call_target="tpu_custom_call" | custom-call | flops 28991029248 | bytes 104857600 | tf_op jit(solution)/shard_map/backward/pallas_call | solution.py:1439
  340.5 0.0 copy-start.2
  340.5 0.0 copy-start.3
  340.6 93.7 %backward.3 = (bf16[3,2,384,1536]{3,2,1,0:T(8,128)(2,1)}, bf16[3,2,384,1536]{3,2,1,0:T(8,128)(2,1)}, bf16[128,1536]{1,0:T(8,128)(2,1)}, bf16[128,2560]{1,0:T(8,1...) custom-call(bf16[128,1536]{1,0:T(8,128)(2,1)} %get-tuple-element.108, ...), custom_call_target="tpu_custom_call" | custom-call | flops 28991029248 | bytes 104857600 | tf_op jit(solution)/shard_map/backward/pallas_call | solution.py:1439
  434.3 1.2 select_bitcast_fusion
  435.4 2.7 collective-permute-start.5
  438.1 0.0 copy-done.2
  438.1 0.0 copy-done.3
  438.1 0.8 select_bitcast_fusion.1
  438.9 133.7 %shared_grads.1 = (bf16[4,1600,512]{2,1,0:T(8,128)(2,1)}, bf16[3,384,1536]{2,1,0:T(8,128)(2,1)}, bf16[2,3,384,1536]{3,2,1,0:T(8,128)(2,1)}, bf16[1,384,1536]{2,1,0:T(8,128)(2,1)}, bf16[2,1,384,1536]{3,2,1,0:T(8,128)(2,1)}) custom-call(bf16[3,512,768]{2,1,0:T(8,128)(2,1)} %get-tuple-element.122.refs_0_, bf16[3,512,768]{2,1,0:T(8,128)(2,1)} %get-tuple-element.123.refs_1_, ...), custom_call_target="tpu_custom_call" | custom-call | bytes 419430400 | tf_op jit(solution)/shard_map/shared_grads/pallas_call | solution.py:1574
  572.7 1.0 slice_convert_fusion
  573.7 0.1 reshape.198
  573.8 16.5 %collective-permute-start.4 = (bf16[128,1536]{1,0:T(8,128)(2,1)}, bf16[128,1536]{1,0:T(8,128)(2,1)S(1)}, u32[]{:S(2)}, u32[]{:S(2)}) collective-permute-start(bf16[128,1536]{1,0:T(8,128)(2,1)} %get-tuple-element.185), channel_id=1, source_target_pairs={{0,16},{16,0},{1,17},{17,1},{2,18},{18,2},{3,19},{19,3},{4,20},{20... | collective-permute-start | bytes 1179656 | tf_op jit(solution)/shard_map/ppermute | solution.py:1891
  590.3 0.8 copy.42
  591.1 0.5 slice_reduce_fusion
  591.6 0.6 broadcast_in_dim_squeeze.6
  592.2 0.6 broadcast_in_dim_squeeze.7
  592.8 17.9 %finish.1 = (f32[3,768,512]{2,1,0:T(8,128)}, f32[3,768,512]{2,1,0:T(8,128)}, f32[3,256,1536]{2,1,0:T(8,128)}, f32[768,1536]{1,0:T(8,128)}, f32[768,512]{1,0:T(8,...) custom-call(bf16[3,2,384,1536]{3,2,1,0:T(8,128)(2,1)} %get-tuple-element.129.refs_7_.refs_0_, ...), custom_call_target="tpu_custom_call" | custom-call | bytes 52428800 | tf_op jit(solution)/shard_map/finish/pallas_call | solution.py:1701
  610.6 0.0 collective-permute-done.5
  610.7 2.2 maximum_select_fusion.1
  612.8 0.0 collective-permute-done.4
  612.8 1.0 maximum_select_fusion
  613.8 0.0 copy-done.1
  (6 shorter events, 0.1 us)
Async XLA Ops:
  0.6 3.5 copy-start
  0.7 77.4 %collective-permute-start.1 = (bf16[3,1536,512]{2,1,0:T(8,128)(2,1)}, bf16[3,1536,512]{2,1,0:T(8,128)(2,1)}, u32[]{:S(2)}, u32[]{:S(2)}) collective-permute-start(bf16[3,1536,512]{2,1,0:T(8,128)(2,1)} %bitcast.58), channel_id=1, source_target_pairs={{0,16},{16,0},{1,17},{17,1},{2,18},{18,2},{3,19},{19,3},{4,20},{20... | collective-permute-start | bytes 14155784 | tf_op jit(solution)/shard_map/ppermute | solution.py:1891
  1.4 76.7 %collective-permute-start.2 = (bf16[3,1536,512]{2,1,0:T(8,128)(2,1)}, bf16[3,1536,512]{2,1,0:T(8,128)(2,1)}, u32[]{:S(2)}, u32[]{:S(2)}) collective-permute-start(bf16[3,1536,512]{2,1,0:T(8,128)(2,1)} %bitcast.63), channel_id=1, source_target_pairs={{0,16},{16,0},{1,17},{17,1},{2,18},{18,2},{3,19},{19,3},{4,20},{20... | collective-permute-start | bytes 14155784 | tf_op jit(solution)/shard_map/ppermute | solution.py:1891
  1.5 76.6 %collective-permute-start.3 = (bf16[3,512,1536]{2,1,0:T(8,128)(2,1)}, bf16[3,512,1536]{2,1,0:T(8,128)(2,1)}, u32[]{:S(2)}, u32[]{:S(2)}) collective-permute-start(bf16[3,512,1536]{2,1,0:T(8,128)(2,1)} %bitcast.68), channel_id=1, source_target_pairs={{0,16},{16,0},{1,17},{17,1},{2,18},{18,2},{3,19},{19,3},{4,20},{20... | collective-permute-start | bytes 14155784 | tf_op jit(solution)/shard_map/ppermute | solution.py:1891
  2.6 7.1 %collective-permute-start = (s32[128,8]{0,1:T(8,128)S(1)}, s32[128,8]{0,1:T(8,128)S(1)}, u32[]{:S(2)}, u32[]{:S(2)}) collective-permute-start(s32[128,8]{0,1:T(8,128)S(1)} %get-tuple-element.189), channel_id=1, source_target_pairs={{0,16},{16,0},{1,17},{17,1},{2,18},{18,2},{3,19},{19,3},{4,20},{20... | collective-permute-start | bytes 12296 | tf_op jit(solution)/shard_map/ppermute | solution.py:1891
  340.5 97.6 %copy-start.2 = (bf16[128,1536]{1,0:T(8,128)(2,1)S(1)}, bf16[128,1536]{1,0:T(8,128)(2,1)}, u32[]{:S(2)}) copy-start(bf16[128,1536]{1,0:T(8,128)(2,1)} %get-tuple-element.85.refs_0_.refs_22_) | copy-start | bytes 1179652
  340.5 97.6 %copy-start.3 = (bf16[128,1536]{1,0:T(8,128)(2,1)S(1)}, bf16[128,1536]{1,0:T(8,128)(2,1)}, u32[]{:S(2)}) copy-start(bf16[128,1536]{1,0:T(8,128)(2,1)} %get-tuple-element.92) | copy-start | bytes 1179652
  435.4 175.2 %collective-permute-start.5 = (bf16[128,1536]{1,0:T(8,128)(2,1)S(1)}, bf16[128,1536]{1,0:T(8,128)(2,1)}, u32[]{:S(2)}, u32[]{:S(2)}) collective-permute-start(bf16[128,1536]{1,0:T(8,128)(2,1)S(1)} %get-tuple-element.183), channel_id=1, source_target_pairs={{0,16},{16,0},{1,17},{17,1},{2,18},{18,2},{3,19},{19,3},{4,20},{20... | collective-permute-start | bytes 1179656 | tf_op jit(solution)/shard_map/ppermute | solution.py:1891
  573.8 39.0 %collective-permute-start.4 = (bf16[128,1536]{1,0:T(8,128)(2,1)}, bf16[128,1536]{1,0:T(8,128)(2,1)S(1)}, u32[]{:S(2)}, u32[]{:S(2)}) collective-permute-start(bf16[128,1536]{1,0:T(8,128)(2,1)} %get-tuple-element.185), channel_id=1, source_target_pairs={{0,16},{16,0},{1,17},{17,1},{2,18},{18,2},{3,19},{19,3},{4,20},{20... | collective-permute-start | bytes 1179656 | tf_op jit(solution)/shard_map/ppermute | solution.py:1891
  592.8 21.1 %copy-start.1 = (bf16[2,128,1536]{2,1,0:T(8,128)(2,1)S(1)}, bf16[2,128,1536]{2,1,0:T(8,128)(2,1)}, u32[]{:S(2)}) copy-start(bf16[2,128,1536]{2,1,0:T(8,128)(2,1)} %param.16) | copy-start | bytes 2359300

commit v8 on v7

--- a/solution.py
+++ b/solution.py
@@ -24,6 +24,7 @@
 LATE = (2,)
 
 SIDES = 16
+SECOND = 32
 WIDE_SIDES = 128
 
 MESH = pl.DeviceIdType.MESH
@@ -613,12 +614,15 @@
 
     @pl.when(src)
     def _():
+        first = order[len(large)]
+        across(first).wait_recv()
+        core_small(first).start()
         for g, i in enumerate(large):
             for L in range(LINE):
                 gathers[g].from_pair(L)
                 core_large(i, L).start()
                 kept(i, L).start()
-        for i in order[len(large) :]:
+        for i in order[len(large) + 1 :]:
             across(i).wait_recv()
             core_small(i).start()
         for g in gathers:
@@ -697,6 +701,14 @@
             b.wait() if wait else b.start()
 
 
+def layer_picks(picks, layer):
+    picks = picks.astype(F32)
+    if layer:
+        picks = pltpu.roll(picks, LANES - SECOND, 1)
+    lane = lax.broadcasted_iota(jnp.int32, picks.shape, 1)
+    return jnp.where(lane < SECOND, picks, 0.0)
+
+
 def routed_softmax(logits, mask):
     z = jnp.where(mask > 0, logits, NEG)
     top = jnp.max(z, axis=-1, keepdims=True)
@@ -792,7 +804,7 @@
             fetch(mine, theirs, own_layer, (wg, wu, wd), w_sem, wait=True)
 
         x = xb[L]
-        mask = mask_ref[L, :, layer * LANES : (layer + 1) * LANES].astype(F32)
+        mask = layer_picks(mask_ref[L], layer)
         gates = routed_softmax(dot(x, wr_ref[...]), mask)
         gates_ref[L] = gates
         for j in range(EXP_DEV):
@@ -1822,7 +1834,7 @@
     tokens, width = h_ref.shape
     lane = lax.broadcasted_iota(jnp.int32, (tokens, LANES), 1)
     gates = routed_softmax(
-        dot(n2_ref[...], wr_ref[...]), mask_ref[:, layer * LANES : (layer + 1) * LANES].astype(F32)
+        dot(n2_ref[...], wr_ref[...]), layer_picks(mask_ref[...], layer)
     )
     raw = dgate_ref[...]
     dgates = jnp.where(lane < n_experts, raw + pltpu.roll(raw, LANES - 32, 1), 0.0)
@@ -1934,7 +1946,7 @@
     )
     names = jnp.arange(LANES, dtype=jnp.int32)
     picks = jnp.max((both_routes[..., None] == names).astype(BF16), axis=-2)
-    picks = jnp.concatenate([picks[0], picks[1]], axis=1)
+    picks = picks[0] + jnp.roll(picks[1], SECOND, axis=-1)
 
     mine = (w_gate[0], w_up[0], w_down[0])
     theirs = tuple(swap(w, "section") for w in mine)

time: 625 us -> 621 us (level)
  transfers between devices with their start and end apart: 6 -> 6, of which waited for: 0 -> 0; matrix products, arithmetic and copies ran while one was open for 3% -> 3% of each run, Pallas kernels for 36% -> 35%
where the time goes in v8:
time: 621 us; the launch traced here: 609 us
  Pallas kernels  570 us (92%)
  starting transfers between devices  20 us (3%)
  other arithmetic  9.27 us (1%)
  local copies, waits for them, and re-layouts  8.51 us (1%)
    pallas_call x2, Pallas kernels, backward(): pl.pallas_call(functools.partial(backward_kernel, ls, layer, chunks, exch...  179 us
    pallas_call x2, Pallas kernels, forward(): pl.pallas_call(functools.partial(forward_kernel, ls, layer, chunks, n), o...  178 us
    pallas_call x1, Pallas kernels, shared_grads(): pl.pallas_call(functools.partial(shared_grads_kernel, ls, chunks), out_sh...  134 us
    pallas_call x1, Pallas kernels, start(): pl.pallas_call(functools.partial(start_kernel, ls, count), out_shape=[jax...  61.1 us
    ppermute x6, starting transfers between devices, swap(): return lax.ppermute(value, axis, [(0, 1), (1, 0)])  20 us
    pallas_call x1, Pallas kernels, finish(): pl.pallas_call(finish_kernel, out_shape=[jax.ShapeDtypeStruct((EXP_DEV, r...  17.9 us
  transfers between devices with their start and end apart: 6, of which 0 were waited for; matrix products, arithmetic and copies ran while one was open for 3% of the time, Pallas kernels for 35%

profile of v8, /device:TPU:17, one launch (start us, length us, event | category | flops | bytes accessed | tf_op | source)
XLA Modules:
  0.0 609.0 jit_solution(13318880924580689065)
XLA Ops:
  0.6 0.0 copy-start
  0.7 0.7 collective-permute-start.1
  1.4 0.1 collective-permute-start.2
  1.5 0.4 collective-permute-start.3
  1.9 0.7 dynamic-slice_bitcast_fusion.3
  2.6 0.1 collective-permute-start
  2.7 0.1 pad.15.clone
  2.8 0.7 fusion.5
  3.5 0.7 fusion.3.refs_3_.refs_16_
  4.2 0.0 copy-done
  4.2 0.8 dynamic-slice_bitcast_fusion.refs_1_
  5.0 1.8 dynamic-slice_bitcast_fusion.1.refs_0_.refs_22_
  6.7 1.4 maximum_maximum_fusion.refs_7_.refs_21_
  8.1 0.9 copy.40
  9.0 0.7 pad.4.refs_6_.refs_20_
  9.8 0.0 collective-permute-done
  9.8 0.1 copy.39
  9.9 0.4 fusion.1
  10.3 0.1 slice.36
  10.4 0.7 fusion.4.refs_0_.refs_13_
  11.1 61.1 %start.1 = (bf16[4,256,128]{2,1,0:T(8,128)(2,1)}, bf16[4,256,1536]{2,1,0:T(8,128)(2,1)}, bf16[1536,1536]{1,0:T(8,128)(2,1)}, bf16[1536,512]{1,0:T(8,128)(2,1)}, ...) custom-call(bf16[128,128]{1,0:T(8,128)(2,1)} %fusion.4.refs_0_.refs_, ...), custom_call_target="tpu_custom_call" | custom-call | bytes 104857600 | tf_op jit(solution)/shard_map/start/pallas_call | solution.py:664
  72.2 0.0 collective-permute-done.1.refs_13_.refs_4_
  72.2 0.0 collective-permute-done.2.refs_14_.refs_5_
  72.2 0.0 collective-permute-done.3
  72.2 92.0 %forward.2 = (bf16[128,1536]{1,0:T(8,128)(2,1)}, bf16[128,1536]{1,0:T(8,128)(2,1)}, bf16[128,512]{1,0:T(8,128)(2,1)}, bf16[128,512]{1,0:T(8,128)(2,1)}, bf16[128...) custom-call(bf16[128,1536]{1,0:T(8,128)(2,1)} %dynamic-slice_bitcast, ...), custom_call_target="tpu_custom_call" | custom-call | flops 14495514624 | bytes 62914560 | tf_op jit(solution)/shard_map/forward/pallas_call | solution.py:911
  164.3 85.8 %forward.3 = (bf16[128,1536]{1,0:T(8,128)(2,1)}, bf16[128,1536]{1,0:T(8,128)(2,1)}, bf16[128,512]{1,0:T(8,128)(2,1)}, bf16[128,512]{1,0:T(8,128)(2,1)}, bf16[128...) custom-call(bf16[128,1536]{1,0:T(8,128)(2,1)} %get-tuple-element.85., ...), custom_call_target="tpu_custom_call" | custom-call | flops 14495514624 | bytes 62914560 | tf_op jit(solution)/shard_map/forward/pallas_call | solution.py:911
  250.1 85.9 %backward.2 = (bf16[3,2,384,1536]{3,2,1,0:T(8,128)(2,1)}, bf16[3,2,384,1536]{3,2,1,0:T(8,128)(2,1)}, bf16[128,1536]{1,0:T(8,128)(2,1)}, bf16[128,2560]{1,0:T(8,1...) custom-call(bf16[4,256,1536]{2,1,0:T(8,128)(2,1)} %get-tuple-element, ...), custom_call_target="tpu_custom_call" | custom-call | flops 28991029248 | bytes 104857600 | tf_op jit(solution)/shard_map/backward/pallas_call | solution.py:1451
  335.9 0.0 copy-start.2
  335.9 0.0 copy-start.3
  335.9 93.3 %backward.3 = (bf16[3,2,384,1536]{3,2,1,0:T(8,128)(2,1)}, bf16[3,2,384,1536]{3,2,1,0:T(8,128)(2,1)}, bf16[128,1536]{1,0:T(8,128)(2,1)}, bf16[128,2560]{1,0:T(8,1...) custom-call(bf16[128,1536]{1,0:T(8,128)(2,1)} %get-tuple-element.108, ...), custom_call_target="tpu_custom_call" | custom-call | flops 28991029248 | bytes 104857600 | tf_op jit(solution)/shard_map/backward/pallas_call | solution.py:1451
  429.3 1.2 select_bitcast_fusion
  430.5 2.4 collective-permute-start.5
  432.9 0.0 copy-done.2
  432.9 0.0 copy-done.3
  432.9 0.8 select_bitcast_fusion.1
  433.7 133.9 %shared_grads.1 = (bf16[4,1600,512]{2,1,0:T(8,128)(2,1)}, bf16[3,384,1536]{2,1,0:T(8,128)(2,1)}, bf16[2,3,384,1536]{3,2,1,0:T(8,128)(2,1)}, bf16[1,384,1536]{2,1,0:T(8,128)(2,1)}, bf16[2,1,384,1536]{3,2,1,0:T(8,128)(2,1)}) custom-call(bf16[3,512,768]{2,1,0:T(8,128)(2,1)} %get-tuple-element.122.refs_0_, bf16[3,512,768]{2,1,0:T(8,128)(2,1)} %get-tuple-element.123.refs_1_, ...), custom_call_target="tpu_custom_call" | custom-call | bytes 419430400 | tf_op jit(solution)/shard_map/shared_grads/pallas_call | solution.py:1586
  567.5 1.0 slice_convert_fusion
  568.5 0.1 reshape.198
  568.7 16.3 %collective-permute-start.4 = (bf16[128,1536]{1,0:T(8,128)(2,1)}, bf16[128,1536]{1,0:T(8,128)(2,1)S(1)}, u32[]{:S(2)}, u32[]{:S(2)}) collective-permute-start(bf16[128,1536]{1,0:T(8,128)(2,1)} %get-tuple-element.185), channel_id=1, source_target_pairs={{0,16},{16,0},{1,17},{17,1},{2,18},{18,2},{3,19},{19,3},{4,20},{20... | collective-permute-start | bytes 1179656 | tf_op jit(solution)/shard_map/ppermute | solution.py:1903
  585.0 0.8 copy.42
  585.8 0.5 slice_reduce_fusion
  586.3 0.6 broadcast_in_dim_squeeze.6
  586.9 0.6 broadcast_in_dim_squeeze.7
  587.5 17.9 %finish.1 = (f32[3,768,512]{2,1,0:T(8,128)}, f32[3,768,512]{2,1,0:T(8,128)}, f32[3,256,1536]{2,1,0:T(8,128)}, f32[768,1536]{1,0:T(8,128)}, f32[768,512]{1,0:T(8,...) custom-call(bf16[3,2,384,1536]{3,2,1,0:T(8,128)(2,1)} %get-tuple-element.129.refs_7_.refs_0_, ...), custom_call_target="tpu_custom_call" | custom-call | bytes 52428800 | tf_op jit(solution)/shard_map/finish/pallas_call | solution.py:1713
  605.3 0.0 collective-permute-done.5
  605.4 2.1 maximum_select_fusion.1
  607.5 0.0 collective-permute-done.4
  607.5 1.0 maximum_select_fusion
  (7 shorter events, 0.1 us)
Async XLA Ops:
  0.6 3.5 copy-start
  0.7 71.6 %collective-permute-start.1 = (bf16[3,1536,512]{2,1,0:T(8,128)(2,1)}, bf16[3,1536,512]{2,1,0:T(8,128)(2,1)}, u32[]{:S(2)}, u32[]{:S(2)}) collective-permute-start(bf16[3,1536,512]{2,1,0:T(8,128)(2,1)} %bitcast.62), channel_id=1, source_target_pairs={{0,16},{16,0},{1,17},{17,1},{2,18},{18,2},{3,19},{19,3},{4,20},{20... | collective-permute-start | bytes 14155784 | tf_op jit(solution)/shard_map/ppermute | solution.py:1903
  1.4 70.8 %collective-permute-start.2 = (bf16[3,1536,512]{2,1,0:T(8,128)(2,1)}, bf16[3,1536,512]{2,1,0:T(8,128)(2,1)}, u32[]{:S(2)}, u32[]{:S(2)}) collective-permute-start(bf16[3,1536,512]{2,1,0:T(8,128)(2,1)} %bitcast.67), channel_id=1, source_target_pairs={{0,16},{16,0},{1,17},{17,1},{2,18},{18,2},{3,19},{19,3},{4,20},{20... | collective-permute-start | bytes 14155784 | tf_op jit(solution)/shard_map/ppermute | solution.py:1903
  1.5 70.8 %collective-permute-start.3 = (bf16[3,512,1536]{2,1,0:T(8,128)(2,1)}, bf16[3,512,1536]{2,1,0:T(8,128)(2,1)}, u32[]{:S(2)}, u32[]{:S(2)}) collective-permute-start(bf16[3,512,1536]{2,1,0:T(8,128)(2,1)} %bitcast.72), channel_id=1, source_target_pairs={{0,16},{16,0},{1,17},{17,1},{2,18},{18,2},{3,19},{19,3},{4,20},{20... | collective-permute-start | bytes 14155784 | tf_op jit(solution)/shard_map/ppermute | solution.py:1903
  2.6 7.1 %collective-permute-start = (s32[128,8]{0,1:T(8,128)S(1)}, s32[128,8]{0,1:T(8,128)S(1)}, u32[]{:S(2)}, u32[]{:S(2)}) collective-permute-start(s32[128,8]{0,1:T(8,128)S(1)} %get-tuple-element.187), channel_id=1, source_target_pairs={{0,16},{16,0},{1,17},{17,1},{2,18},{18,2},{3,19},{19,3},{4,20},{20... | collective-permute-start | bytes 12296 | tf_op jit(solution)/shard_map/ppermute | solution.py:1903
  335.9 96.9 %copy-start.2 = (bf16[128,1536]{1,0:T(8,128)(2,1)S(1)}, bf16[128,1536]{1,0:T(8,128)(2,1)}, u32[]{:S(2)}) copy-start(bf16[128,1536]{1,0:T(8,128)(2,1)} %get-tuple-element.85.refs_0_.refs_22_) | copy-start | bytes 1179652
  335.9 96.9 %copy-start.3 = (bf16[128,1536]{1,0:T(8,128)(2,1)S(1)}, bf16[128,1536]{1,0:T(8,128)(2,1)}, u32[]{:S(2)}) copy-start(bf16[128,1536]{1,0:T(8,128)(2,1)} %get-tuple-element.92) | copy-start | bytes 1179652
  430.5 174.9 %collective-permute-start.5 = (bf16[128,1536]{1,0:T(8,128)(2,1)S(1)}, bf16[128,1536]{1,0:T(8,128)(2,1)}, u32[]{:S(2)}, u32[]{:S(2)}) collective-permute-start(bf16[128,1536]{1,0:T(8,128)(2,1)S(1)} %get-tuple-element.183), channel_id=1, source_target_pairs={{0,16},{16,0},{1,17},{17,1},{2,18},{18,2},{3,19},{19,3},{4,20},{20... | collective-permute-start | bytes 1179656 | tf_op jit(solution)/shard_map/ppermute | solution.py:1903
  568.7 38.8 %collective-permute-start.4 = (bf16[128,1536]{1,0:T(8,128)(2,1)}, bf16[128,1536]{1,0:T(8,128)(2,1)S(1)}, u32[]{:S(2)}, u32[]{:S(2)}) collective-permute-start(bf16[128,1536]{1,0:T(8,128)(2,1)} %get-tuple-element.185), channel_id=1, source_target_pairs={{0,16},{16,0},{1,17},{17,1},{2,18},{18,2},{3,19},{19,3},{4,20},{20... | collective-permute-start | bytes 1179656 | tf_op jit(solution)/shard_map/ppermute | solution.py:1903
  587.5 21.0 %copy-start.1 = (bf16[2,128,1536]{2,1,0:T(8,128)(2,1)S(1)}, bf16[2,128,1536]{2,1,0:T(8,128)(2,1)}, u32[]{:S(2)}) copy-start(bf16[2,128,1536]{2,1,0:T(8,128)(2,1)} %param.16) | copy-start | bytes 2359300

commit v9 on v8

--- a/solution.py
+++ b/solution.py
@@ -144,12 +144,12 @@
         return 1 - self.p if c == self.chunks + 1 else self.p
 
     def up(self, s, c):
-        dev = index_of(self.l + 1, self.p, self.ls)
+        dev = index_of(jnp.minimum(self.l + 1, LINE - 1), self.p, self.ls)
         L = self.l - s
         return self.copy(L, self.column(c), c, self.us.at[s, c], self.ur.at[s, c], dev)
 
     def dn(self, s, c):
-        dev = index_of(self.l - 1, self.p, self.ls)
+        dev = index_of(jnp.maximum(self.l - 1, 0), self.p, self.ls)
         L = self.l + s
         return self.copy(L, self.column(c), c, self.ds.at[s, c], self.dr.at[s, c], dev)
 
@@ -285,7 +285,7 @@
             self.upb.at[L, self.part(c)],
             self.us.at[L, c],
             self.ur.at[L, c],
-            expert=index_of(self.l + 1, self.p, self.ls),
+            expert=index_of(jnp.minimum(self.l + 1, LINE - 1), self.p, self.ls),
         )
 
     def dn(self, L, c):
@@ -294,7 +294,7 @@
             self.dnb.at[L, self.part(c)],
             self.ds.at[L, c],
             self.dr.at[L, c],
-            expert=index_of(self.l - 1, self.p, self.ls),
+            expert=index_of(jnp.maximum(self.l - 1, 0), self.p, self.ls),
         )
 
     def give(self, L):

time: 621 us -> 621 us (level)
  no operation moved by 1% of the time
where the time goes in v9:
time: 621 us; the launch traced here: 609 us
  Pallas kernels  571 us (92%)
  starting transfers between devices  19.6 us (3%)
  other arithmetic  9.27 us (1%)
  local copies, waits for them, and re-layouts  8.51 us (1%)
    pallas_call x2, Pallas kernels, backward(): pl.pallas_call(functools.partial(backward_kernel, ls, layer, chunks, exch...  180 us
    pallas_call x2, Pallas kernels, forward(): pl.pallas_call(functools.partial(forward_kernel, ls, layer, chunks, n), o...  178 us
    pallas_call x1, Pallas kernels, shared_grads(): pl.pallas_call(functools.partial(shared_grads_kernel, ls, chunks), out_sh...  134 us
    pallas_call x1, Pallas kernels, start(): pl.pallas_call(functools.partial(start_kernel, ls, count), out_shape=[jax...  61.1 us
    ppermute x6, starting transfers between devices, swap(): return lax.ppermute(value, axis, [(0, 1), (1, 0)])  19.6 us
    pallas_call x1, Pallas kernels, finish(): pl.pallas_call(finish_kernel, out_shape=[jax.ShapeDtypeStruct((EXP_DEV, r...  17.9 us
  transfers between devices with their start and end apart: 6, of which 0 were waited for; matrix products, arithmetic and copies ran while one was open for 3% of the time, Pallas kernels for 35%

profile of v9, /device:TPU:17, one launch (start us, length us, event | category | flops | bytes accessed | tf_op | source)
XLA Modules:
  0.0 609.2 jit_solution(13947789431594980925)
XLA Ops:
  0.6 0.0 copy-start
  0.7 0.7 collective-permute-start.1
  1.4 0.1 collective-permute-start.2
  1.5 0.4 collective-permute-start.3
  1.9 0.7 dynamic-slice_bitcast_fusion.3
  2.6 0.1 collective-permute-start
  2.7 0.1 pad.15.clone
  2.8 0.7 fusion.5
  3.5 0.7 fusion.3.refs_3_.refs_16_
  4.2 0.0 copy-done
  4.2 0.8 dynamic-slice_bitcast_fusion.refs_1_
  5.0 1.8 dynamic-slice_bitcast_fusion.1.refs_0_.refs_22_
  6.7 1.4 maximum_maximum_fusion.refs_7_.refs_21_
  8.1 0.9 copy.40
  9.0 0.7 pad.4.refs_6_.refs_20_
  9.8 0.0 collective-permute-done
  9.8 0.1 copy.39
  9.9 0.4 fusion.1
  10.3 0.1 slice.36
  10.4 0.7 fusion.4.refs_0_.refs_13_
  11.1 61.1 %start.1 = (bf16[4,256,128]{2,1,0:T(8,128)(2,1)}, bf16[4,256,1536]{2,1,0:T(8,128)(2,1)}, bf16[1536,1536]{1,0:T(8,128)(2,1)}, bf16[1536,512]{1,0:T(8,128)(2,1)}, ...) custom-call(bf16[128,128]{1,0:T(8,128)(2,1)} %fusion.4.refs_0_.refs_, ...), custom_call_target="tpu_custom_call" | custom-call | bytes 104857600 | tf_op jit(solution)/shard_map/start/pallas_call | solution.py:664
  72.2 0.0 collective-permute-done.1.refs_13_.refs_4_
  72.2 0.0 collective-permute-done.2.refs_14_.refs_5_
  72.2 0.0 collective-permute-done.3
  72.2 92.0 %forward.2 = (bf16[128,1536]{1,0:T(8,128)(2,1)}, bf16[128,1536]{1,0:T(8,128)(2,1)}, bf16[128,512]{1,0:T(8,128)(2,1)}, bf16[128,512]{1,0:T(8,128)(2,1)}, bf16[128...) custom-call(bf16[128,1536]{1,0:T(8,128)(2,1)} %dynamic-slice_bitcast, ...), custom_call_target="tpu_custom_call" | custom-call | flops 14495514624 | bytes 62914560 | tf_op jit(solution)/shard_map/forward/pallas_call | solution.py:911
  164.3 85.8 %forward.3 = (bf16[128,1536]{1,0:T(8,128)(2,1)}, bf16[128,1536]{1,0:T(8,128)(2,1)}, bf16[128,512]{1,0:T(8,128)(2,1)}, bf16[128,512]{1,0:T(8,128)(2,1)}, bf16[128...) custom-call(bf16[128,1536]{1,0:T(8,128)(2,1)} %get-tuple-element.85., ...), custom_call_target="tpu_custom_call" | custom-call | flops 14495514624 | bytes 62914560 | tf_op jit(solution)/shard_map/forward/pallas_call | solution.py:911
  250.1 85.8 %backward.2 = (bf16[3,2,384,1536]{3,2,1,0:T(8,128)(2,1)}, bf16[3,2,384,1536]{3,2,1,0:T(8,128)(2,1)}, bf16[128,1536]{1,0:T(8,128)(2,1)}, bf16[128,2560]{1,0:T(8,1...) custom-call(bf16[4,256,1536]{2,1,0:T(8,128)(2,1)} %get-tuple-element, ...), custom_call_target="tpu_custom_call" | custom-call | flops 28991029248 | bytes 104857600 | tf_op jit(solution)/shard_map/backward/pallas_call | solution.py:1451
  335.9 0.0 copy-start.2
  335.9 0.0 copy-start.3
  335.9 93.7 %backward.3 = (bf16[3,2,384,1536]{3,2,1,0:T(8,128)(2,1)}, bf16[3,2,384,1536]{3,2,1,0:T(8,128)(2,1)}, bf16[128,1536]{1,0:T(8,128)(2,1)}, bf16[128,2560]{1,0:T(8,1...) custom-call(bf16[128,1536]{1,0:T(8,128)(2,1)} %get-tuple-element.108, ...), custom_call_target="tpu_custom_call" | custom-call | flops 28991029248 | bytes 104857600 | tf_op jit(solution)/shard_map/backward/pallas_call | solution.py:1451
  429.6 1.2 select_bitcast_fusion
  430.8 2.2 collective-permute-start.5
  433.0 0.0 copy-done.2
  433.0 0.0 copy-done.3
  433.0 0.8 select_bitcast_fusion.1
  433.8 134.2 %shared_grads.1 = (bf16[4,1600,512]{2,1,0:T(8,128)(2,1)}, bf16[3,384,1536]{2,1,0:T(8,128)(2,1)}, bf16[2,3,384,1536]{3,2,1,0:T(8,128)(2,1)}, bf16[1,384,1536]{2,1,0:T(8,128)(2,1)}, bf16[2,1,384,1536]{3,2,1,0:T(8,128)(2,1)}) custom-call(bf16[3,512,768]{2,1,0:T(8,128)(2,1)} %get-tuple-element.122.refs_0_, bf16[3,512,768]{2,1,0:T(8,128)(2,1)} %get-tuple-element.123.refs_1_, ...), custom_call_target="tpu_custom_call" | custom-call | bytes 419430400 | tf_op jit(solution)/shard_map/shared_grads/pallas_call | solution.py:1586
  568.0 1.0 slice_convert_fusion
  569.0 0.1 reshape.198
  569.1 16.1 %collective-permute-start.4 = (bf16[128,1536]{1,0:T(8,128)(2,1)}, bf16[128,1536]{1,0:T(8,128)(2,1)S(1)}, u32[]{:S(2)}, u32[]{:S(2)}) collective-permute-start(bf16[128,1536]{1,0:T(8,128)(2,1)} %get-tuple-element.185), channel_id=1, source_target_pairs={{0,16},{16,0},{1,17},{17,1},{2,18},{18,2},{3,19},{19,3},{4,20},{20... | collective-permute-start | bytes 1179656 | tf_op jit(solution)/shard_map/ppermute | solution.py:1903
  585.3 0.8 copy.42
  586.0 0.5 slice_reduce_fusion
  586.5 0.6 broadcast_in_dim_squeeze.6
  587.1 0.6 broadcast_in_dim_squeeze.7
  587.7 17.9 %finish.1 = (f32[3,768,512]{2,1,0:T(8,128)}, f32[3,768,512]{2,1,0:T(8,128)}, f32[3,256,1536]{2,1,0:T(8,128)}, f32[768,1536]{1,0:T(8,128)}, f32[768,512]{1,0:T(8,...) custom-call(bf16[3,2,384,1536]{3,2,1,0:T(8,128)(2,1)} %get-tuple-element.129.refs_7_.refs_0_, ...), custom_call_target="tpu_custom_call" | custom-call | bytes 52428800 | tf_op jit(solution)/shard_map/finish/pallas_call | solution.py:1713
  605.6 0.0 collective-permute-done.5
  605.6 2.1 maximum_select_fusion.1
  607.7 0.0 collective-permute-done.4
  607.7 1.0 maximum_select_fusion
  (7 shorter events, 0.1 us)
Async XLA Ops:
  0.6 3.5 copy-start
  0.7 71.6 %collective-permute-start.1 = (bf16[3,1536,512]{2,1,0:T(8,128)(2,1)}, bf16[3,1536,512]{2,1,0:T(8,128)(2,1)}, u32[]{:S(2)}, u32[]{:S(2)}) collective-permute-start(bf16[3,1536,512]{2,1,0:T(8,128)(2,1)} %bitcast.62), channel_id=1, source_target_pairs={{0,16},{16,0},{1,17},{17,1},{2,18},{18,2},{3,19},{19,3},{4,20},{20... | collective-permute-start | bytes 14155784 | tf_op jit(solution)/shard_map/ppermute | solution.py:1903
  1.4 70.8 %collective-permute-start.2 = (bf16[3,1536,512]{2,1,0:T(8,128)(2,1)}, bf16[3,1536,512]{2,1,0:T(8,128)(2,1)}, u32[]{:S(2)}, u32[]{:S(2)}) collective-permute-start(bf16[3,1536,512]{2,1,0:T(8,128)(2,1)} %bitcast.67), channel_id=1, source_target_pairs={{0,16},{16,0},{1,17},{17,1},{2,18},{18,2},{3,19},{19,3},{4,20},{20... | collective-permute-start | bytes 14155784 | tf_op jit(solution)/shard_map/ppermute | solution.py:1903
  1.5 70.8 %collective-permute-start.3 = (bf16[3,512,1536]{2,1,0:T(8,128)(2,1)}, bf16[3,512,1536]{2,1,0:T(8,128)(2,1)}, u32[]{:S(2)}, u32[]{:S(2)}) collective-permute-start(bf16[3,512,1536]{2,1,0:T(8,128)(2,1)} %bitcast.72), channel_id=1, source_target_pairs={{0,16},{16,0},{1,17},{17,1},{2,18},{18,2},{3,19},{19,3},{4,20},{20... | collective-permute-start | bytes 14155784 | tf_op jit(solution)/shard_map/ppermute | solution.py:1903
  2.6 7.1 %collective-permute-start = (s32[128,8]{0,1:T(8,128)S(1)}, s32[128,8]{0,1:T(8,128)S(1)}, u32[]{:S(2)}, u32[]{:S(2)}) collective-permute-start(s32[128,8]{0,1:T(8,128)S(1)} %get-tuple-element.187), channel_id=1, source_target_pairs={{0,16},{16,0},{1,17},{17,1},{2,18},{18,2},{3,19},{19,3},{4,20},{20... | collective-permute-start | bytes 12296 | tf_op jit(solution)/shard_map/ppermute | solution.py:1903
  335.9 97.1 %copy-start.2 = (bf16[128,1536]{1,0:T(8,128)(2,1)S(1)}, bf16[128,1536]{1,0:T(8,128)(2,1)}, u32[]{:S(2)}) copy-start(bf16[128,1536]{1,0:T(8,128)(2,1)} %get-tuple-element.85.refs_0_.refs_22_) | copy-start | bytes 1179652
  335.9 97.0 %copy-start.3 = (bf16[128,1536]{1,0:T(8,128)(2,1)S(1)}, bf16[128,1536]{1,0:T(8,128)(2,1)}, u32[]{:S(2)}) copy-start(bf16[128,1536]{1,0:T(8,128)(2,1)} %get-tuple-element.92) | copy-start | bytes 1179652
  430.8 174.8 %collective-permute-start.5 = (bf16[128,1536]{1,0:T(8,128)(2,1)S(1)}, bf16[128,1536]{1,0:T(8,128)(2,1)}, u32[]{:S(2)}, u32[]{:S(2)}) collective-permute-start(bf16[128,1536]{1,0:T(8,128)(2,1)S(1)} %get-tuple-element.183), channel_id=1, source_target_pairs={{0,16},{16,0},{1,17},{17,1},{2,18},{18,2},{3,19},{19,3},{4,20},{20... | collective-permute-start | bytes 1179656 | tf_op jit(solution)/shard_map/ppermute | solution.py:1903
  569.1 38.6 %collective-permute-start.4 = (bf16[128,1536]{1,0:T(8,128)(2,1)}, bf16[128,1536]{1,0:T(8,128)(2,1)S(1)}, u32[]{:S(2)}, u32[]{:S(2)}) collective-permute-start(bf16[128,1536]{1,0:T(8,128)(2,1)} %get-tuple-element.185), channel_id=1, source_target_pairs={{0,16},{16,0},{1,17},{17,1},{2,18},{18,2},{3,19},{19,3},{4,20},{20... | collective-permute-start | bytes 1179656 | tf_op jit(solution)/shard_map/ppermute | solution.py:1903
  587.7 21.0 %copy-start.1 = (bf16[2,128,1536]{2,1,0:T(8,128)(2,1)S(1)}, bf16[2,128,1536]{2,1,0:T(8,128)(2,1)}, u32[]{:S(2)}) copy-start(bf16[2,128,1536]{2,1,0:T(8,128)(2,1)} %param.16) | copy-start | bytes 2359300
